TPU v7x, 32 devices: a whole 2x2x4 slice. The times are simulated.
32 devices in a mesh: parts: 2 (over y), dap: 4 (over z), sub: 4 (over x, core).
Axes of the slice: x: 2, y: 2, z: 4, core: 2. Of those that a mesh axis runs over, the one named last changes fastest.
Arguments:
- alignment: bfloat16 [512, 64, 256], P('parts', 'dap'), parts along dimension 0, may hold values from -6 to 6
- alignment_mask: int32 [512, 64], P('parts'), parts along dimension 0, may hold values from 0 to 1, as said below
- pair_input: bfloat16 [128, 64, 128], P(('parts', 'dap'), 'sub'), parts along dimension 0, may hold values from -6 to 6
- residue_mask: int32 [128], P('parts'), parts along dimension 0, may hold values from 0 to 1, as said below
- chain_index: int32 [128], P('parts'), parts along dimension 0, may hold values from 0 to 3, as said below
- outer_left: bfloat16 [256, 32], replicated, may hold values from -0.375 to 0.375
- outer_right: bfloat16 [256, 32], replicated, may hold values from -0.375 to 0.375
- outer_proj: float32 [32, 32, 128], replicated, may hold values from -1 to 1
- triangle_left: bfloat16 [128, 256], replicated, may hold values from -0.5 to 0.5
- triangle_right: bfloat16 [128, 256], replicated, may hold values from -0.5 to 0.5
- triangle_gate: bfloat16 [128, 128], replicated, may hold values from -0.5 to 0.5
- triangle_out: bfloat16 [128, 128], replicated, may hold values from -0.5 to 0.5
- relative_table: bfloat16 [66, 128], replicated, may hold values from -5 to 5
- transition_up: bfloat16 [128, 512], replicated, may hold values from -0.5 to 0.5
- transition_down: bfloat16 [512, 128], replicated, may hold values from -0.25 to 0.25
Outputs:
- pair_output: bfloat16 [128, 64, 128], P(('parts', 'dap'), 'sub'), parts along dimension 0
There are 2 independent parts, one for each index of `parts`. A program takes and returns all parts, laid end to end along the dimension named above; an argument that names none is the same for every part. Nothing has to cross between parts.
Inputs may be any that keep to these rules, and one draw needn't show every extreme that they name: `residue_mask`: the first residue is live and the last residue is padding. `chain_index`: never falls along the residues; the first residue is in chain 0 and the last in chain 3. `alignment_mask`: for each chain, a leading run of alignment rows, at least 32 long, is 1 at that chain's live residues; every other entry is 0.
All inputs are finite; a program needn't handle non-finite values.
Results may differ from a plain program's by a relative error of at most 0.012.
Values may be sent and summed in bfloat16 or wider, within the bound.
No kernel may reach another device: no remote copies, remote signals or barrier semaphores. Data moves between devices by JAX's collectives and lax.ppermute only.
A program may use at most 64 MiB of HBM per device.

v0:
```python
import jax
import jax.numpy as jnp
from jax import lax
from jax.sharding import PartitionSpec as P

REL_CLIP = 32
RELBINS = 66


epsilon = 1e-05


def layer_norm(values, along):
    average = jnp.mean(values, axis=along, keepdims=True)
    centered = values - average
    spread = jnp.mean(centered * centered, axis=along, keepdims=True)
    return centered * lax.rsqrt(spread + epsilon)


def relative_bias(row_ids, col_ids, row_chain, col_chain, relative_table):
    offset = jnp.clip(row_ids[:, None] - col_ids[None, :] + REL_CLIP, 0, 2 * REL_CLIP)
    bucket = jnp.where(row_chain[:, None] == col_chain[None, :], offset, 2 * REL_CLIP + 1)
    classes = jnp.arange(RELBINS, dtype=jnp.int32)
    onehot = (bucket[:, :, None] == classes[None, None, :]).astype(jnp.bfloat16)
    return jnp.dot(onehot, relative_table, preferred_element_type=jnp.float32)


def outer_factor(normed, weight, seq_mask):
    product = jnp.einsum("sic,ce->sei", normed, weight, preferred_element_type=jnp.float32)
    return (product * seq_mask[:, None, :]).astype(jnp.bfloat16)


def per_device(
    alignment,
    alignment_mask,
    pair_input,
    residue_mask,
    chain_index,
    outer_left,
    outer_right,
    outer_proj,
    triangle_left,
    triangle_right,
    triangle_gate,
    triangle_out,
    relative_table,
    transition_up,
    transition_down,
):
    highest = lax.Precision.HIGHEST
    sub_count = lax.axis_size("sub")
    local_rows = alignment.shape[1]
    residues = alignment_mask.shape[1]
    local_cols = residues // sub_count
    sequences = alignment.shape[0]
    share_count = sequences // sub_count
    row_start = lax.axis_index("dap") * local_rows
    col_start = lax.axis_index("sub") * local_cols
    seq_start = lax.axis_index("sub") * share_count
    seq_mask = alignment_mask.astype(jnp.float32)
    row_mask = lax.dynamic_slice_in_dim(seq_mask, row_start, local_rows, 1)
    col_mask = lax.dynamic_slice_in_dim(seq_mask, col_start, local_cols, 1)
    share_mask = lax.dynamic_slice_in_dim(row_mask, seq_start, share_count, 0)
    share_rows = lax.dynamic_slice_in_dim(alignment, seq_start, share_count, 0)
    share_norm = layer_norm(share_rows.astype(jnp.float32), -1).astype(jnp.bfloat16)
    right_share = outer_factor(share_norm, outer_right, share_mask)
    right_all = lax.all_gather(right_share, "dap", axis=2, tiled=True)
    aligned = layer_norm(alignment.astype(jnp.float32), -1).astype(jnp.bfloat16)
    left_full = outer_factor(aligned, outer_left, row_mask)
    right_cols = lax.all_to_all(right_all, "sub", split_axis=2, concat_axis=0, tiled=True)
    outer = jnp.einsum("sci,sej->icej", left_full, right_cols, preferred_element_type=jnp.float32)
    projected = jnp.einsum("icej,ced->ijd", outer, outer_proj, precision=highest)
    counts = jnp.dot(row_mask.T, col_mask, precision=highest)
    outer_mean = projected / jnp.maximum(counts, 1.0)[:, :, None]
    row_ids = row_start + jnp.arange(local_rows, dtype=jnp.int32)
    col_ids = col_start + jnp.arange(local_cols, dtype=jnp.int32)
    row_chain = lax.dynamic_slice_in_dim(chain_index, row_start, local_rows, 0)
    col_chain = lax.dynamic_slice_in_dim(chain_index, col_start, local_cols, 0)
    relative = relative_bias(row_ids, col_ids, row_chain, col_chain, relative_table)
    pair_one = (pair_input.astype(jnp.float32) + relative + outer_mean).astype(jnp.bfloat16)
    tri_norm = layer_norm(pair_one.astype(jnp.float32), -1).astype(jnp.bfloat16)
    live = residue_mask.astype(jnp.float32)
    row_live = lax.dynamic_slice_in_dim(live, row_start, local_rows, 0)
    col_live = lax.dynamic_slice_in_dim(live, col_start, local_cols, 0)
    pair_mask = row_live[:, None] * col_live[None, :]

    def gated(weight):
        halves = weight.shape[1] // 2
        both = jnp.einsum("ijd,dc->cij", tri_norm, weight, preferred_element_type=jnp.float32)
        return (jax.nn.sigmoid(both[:halves]) * both[halves:] * pair_mask[None, :, :]).astype(
            jnp.bfloat16
        )

    left_tri = gated(triangle_left)
    right_tri = gated(triangle_right)
    left_split, right_split = (
        lax.all_to_all(left_tri, "sub", split_axis=0, concat_axis=2, tiled=True),
        lax.all_to_all(right_tri, "sub", split_axis=0, concat_axis=2, tiled=True),
    )
    tri_sum = jnp.einsum(
        "cik,cjk->cij",
        left_split,
        lax.all_gather(right_split, "dap", axis=1, tiled=True),
        preferred_element_type=jnp.float32,
    ).astype(jnp.bfloat16)
    tri_back = lax.all_to_all(tri_sum, "sub", split_axis=2, concat_axis=0, tiled=True)
    tri_hidden = layer_norm(tri_back.astype(jnp.float32), 0).astype(jnp.bfloat16)
    update = jnp.einsum("cij,cd->ijd", tri_hidden, triangle_out, preferred_element_type=jnp.float32)
    gate = jax.nn.sigmoid(jnp.dot(tri_norm, triangle_gate, preferred_element_type=jnp.float32))
    pair_two = (pair_one.astype(jnp.float32) + gate * update).astype(jnp.bfloat16)
    trans_norm = layer_norm(pair_two.astype(jnp.float32), -1).astype(jnp.bfloat16)
    trans_hidden = jax.nn.relu(
        jnp.dot(trans_norm, transition_up, preferred_element_type=jnp.float32)
    ).astype(jnp.bfloat16)
    result = pair_two.astype(jnp.float32) + jnp.dot(
        trans_hidden, transition_down, preferred_element_type=jnp.float32
    )
    return result.astype(jnp.bfloat16)


def solution(mesh):
    in_specs = (
        P("parts", "dap", None),
        P("parts", None),
        P(("parts", "dap"), "sub", None),
        P("parts"),
        P("parts"),
        P(),
        P(),
        P(),
        P(),
        P(),
        P(),
        P(),
        P(),
        P(),
        P(),
    )
    out_specs = P(("parts", "dap"), "sub", None)
    return jax.shard_map(
        per_device, mesh=mesh, in_specs=in_specs, out_specs=out_specs, check_vma=False
    )
```

profile of v0, /device:TPU:1, one launch (start us, length us, event | category | flops | bytes accessed | tf_op | source)
XLA Modules:
  0.0 92.0 jit_solution(3672275457018215455)
XLA Ops:
  0.0 1.4 %convert_reduce_fusion.1 = f32[64,16]{1,0:T(8,128)S(1)} fusion(bf16[256,16,256]{2,1,0:T(8,128)(2,1)} %param.15, s32[]{:T(128)S(6)} %select_n.29), kind=kLoop, calls=%fused_computation.14 | loop fusion | flops 523264 | bytes 528388 | tf_op jit(solution)/shard_map/reduce_sum | solution.py:14
  1.4 1.4 %fusion.39 = f32[64,16]{1,0:T(8,128)S(1)} fusion(f32[64,16]{1,0:T(8,128)S(1)} %broadcast_multiply_fusion.1, bf16[256,16,256]{2,1,0:T(8,128)(2,1)} %param.15, s32[]{:T(128)S(6)} %select_n.29), kind=kLoop, calls=%fused_computation.43 | loop fusion | flops 1047552 | bytes 532484 | tf_op jit(solution)/shard_map/reduce_sum | solution.py:16
  2.8 0.0 copy-start.12
  2.9 0.0 copy-start.7
  2.9 0.9 convert_element_type.93
  3.7 0.1 dynamic_slice.27
  3.8 0.1 copy.55
  3.9 1.5 %fusion.19 = bf16[64,32,16]{1,2,0:T(8,128)(2,1)S(1)} fusion(f32[64,16]{1,0:T(8,128)S(1)} %add_rsqrt_fusion.1, f32[64,16]{1,0:T(8,128)S(1)} %broadcast_multiply_fusion.1, bf16[256,16,256]{2,1,0:T(8,128)(2,1)} %param.15, s32[]{:T(128)S(6)} %select_n.29, f32[64,16]{1,0:T(8,128)S(1)} %copy.55, bf16[256,32]{0,1:T(8,128)(2,1)} %param.21), kind=kOutput, calls=%fused_computation.21 | convolution fusion | flops 17891328 | bytes 618500 | tf_op jit(solution)/shard_map/sic,ce->sei/dot_general | solution.py:29
  5.4 21.1 %all_gather.6 = bf16[64,32,64]{1,2,0:T(8,128)(2,1)} all-gather(bf16[64,32,16]{1,2,0:T(8,128)(2,1)S(1)} %fusion.19), channel_id=1, replica_groups=mesh['parts'=2,'dap'=4,'sub'=4] {'dap'}, dimensions={2}, use_global_device_ids=true | all-gather | bytes 327680 | tf_op jit(solution)/shard_map/all_gather | solution.py:67
  26.5 2.3 %copy.56 = bf16[64,32,64]{0,1,2:T(8,128)(2,1)S(1)} copy(bf16[64,32,64]{1,2,0:T(8,128)(2,1)} %all_gather.6) | data formatting | bytes 524288 | tf_op jit(solution)/shard_map/all_gather | solution.py:67
  28.8 1.1 %reshape.178 = bf16[4,2,16384]{2,1,0:T(2,128)(2,1)} reshape(bf16[64,32,64]{2,1,0:T(8,128)(2,1)S(1)} %bitcast.93) | data formatting | bytes 524288
  29.9 6.9 %all-to-all-start = ((bf16[4,2,16384]{2,1,0:T(2,128)(2,1)}), bf16[4,2,16384]{2,1,0:T(2,128)(2,1)S(1)}, u32[]{:S(2)}, u32[]{:S(2)}) async-start(bf16[4,2,16384]{2,1,0:T(2,128)(2,1)} %reshape.178), calls=%async_computation | async-start | bytes 524288 | tf_op jit(solution)/shard_map/all_to_all | solution.py:70
  36.9 0.6 convert_reduce_fusion
  37.5 0.1 copy.58
  37.6 0.1 convolution_maximum_fusion.1
  37.8 0.1 fusion.84
  37.9 0.1 fusion.85
  38.0 1.3 %fusion.2 = f32[256,16]{1,0:T(8,128)S(1)} fusion(bf16[256,16,256]{2,1,0:T(8,128)(2,1)S(1)} %copy-done.1, f32[256,16]{1,0:T(8,128)S(1)} %broadcast_multiply_fusion), kind=kLoop, calls=%fused_computation.4 | loop fusion | flops 4190208 | bytes 2129920 | tf_op jit(solution)/shard_map/reduce_sum | solution.py:16
  39.3 2.9 %fusion.12 = bf16[256,32,16]{1,2,0:T(8,128)(2,1)} fusion(bf16[256,16,256]{2,1,0:T(8,128)(2,1)S(1)} %copy-done.1, f32[256,16]{1,0:T(8,128)S(1)} %add_rsqrt_fusion, f32[256,16]{1,0:T(8,128)S(1)} %broadcast_multiply_fusion, f32[256,16]{1,0:T(8,128)S(1)} %copy.58, bf16[256,32]{0,1:T(8,128)(2,1)S(1)} %copy-done.11), kind=kOutput, calls=%fused_computation.12 | convolution fusion | flops 71565312 | bytes 2424832 | tf_op jit(solution)/shard_map/sic,ce->sei/dot_general | solution.py:29
  42.2 2.0 %copy.59 = bf16[256,32,16]{0,1,2:T(8,128)(2,1)S(1)} copy(bf16[256,32,16]{1,2,0:T(8,128)(2,1)} %fusion.12) | data formatting | bytes 524288 | tf_op jit(solution)/shard_map/convert_element_type | solution.py:30
  44.1 0.1 clamp_select_fusion
  44.2 0.1 broadcast_multiply_fusion.2
  44.3 0.4 reshape.179
  44.7 0.4 copy.79
  45.1 0.3 reshape.167
  45.4 0.0 copy-start.2
  45.4 0.0 copy-start.6
  45.4 0.0 copy-start.3
  45.4 0.0 copy-start.4
  45.5 0.7 fusion.47
  46.2 3.8 %fusion.31 = f32[16,16,128]{2,1,0:T(8,128)S(1)} fusion(f32[32,16,32,16]{2,1,3,0:T(8,128)S(1)} %fusion.47, f32[32,32,128,1]{2,1,0,3:T(8,128)S(1)} %bitcast.90, f32[16,16]{1,0:T(8,128)S(1)} %convolution_maximum_fusion.1), kind=kOutput, calls=%fused_computation.36 | convolution fusion | flops 402685952 | bytes 1704960 | tf_op jit(solution)/shard_map/icej,ced->ijd/dot_general | solution.py:72
  50.0 0.3 fusion.86
  50.3 0.2 multiply_reduce_fusion.2
  50.5 0.3 convolution_bitcast_fusion.1
  50.8 0.3 convolution_bitcast_fusion
  51.0 0.1 fusion.52
  51.1 0.4 copy.63
  51.6 1.2 %reshape.182 = bf16[4,2,4096]{2,1,0:T(2,128)(2,1)} reshape(bf16[128,16,16]{2,1,0:T(8,128)(2,1)S(1)} %copy.63) | data formatting | bytes 131072
  52.7 3.5 %all-to-all-start.2 = ((bf16[4,2,4096]{2,1,0:T(2,128)(2,1)}), bf16[4,2,4096]{2,1,0:T(2,128)(2,1)S(1)}, u32[]{:S(2)}, u32[]{:S(2)}) async-start(bf16[4,2,4096]{2,1,0:T(2,128)(2,1)} %reshape.182), calls=%async_computation.2 | async-start | bytes 131072 | tf_op jit(solution)/shard_map/all_to_all | solution.py:98
  56.2 0.4 copy.61
  56.7 1.2 %reshape.180 = bf16[4,2,4096]{2,1,0:T(2,128)(2,1)} reshape(bf16[128,16,16]{2,1,0:T(8,128)(2,1)S(1)} %copy.61) | data formatting | bytes 131072
  57.8 1.7 %all-to-all-done.2 = bf16[4,2,4096]{2,1,0:T(2,128)(2,1)S(1)} async-done(((bf16[4,2,4096]{2,1,0:T(2,128)(2,1)}), bf16[4,2,4096]{2,1,0:T(2,128)(2,1)S(1)}, u32[]{:S(2)}, u32[]{:S(2)}) %all-to-all-start.2) | async-done | bytes 65568 | tf_op jit(solution)/shard_map/all_to_all | solution.py:98
  59.5 4.1 %all-to-all-start.1 = ((bf16[4,2,4096]{2,1,0:T(2,128)(2,1)}), bf16[4,2,4096]{2,1,0:T(2,128)(2,1)S(1)}, u32[]{:S(2)}, u32[]{:S(2)}) async-start(bf16[4,2,4096]{2,1,0:T(2,128)(2,1)} %reshape.180), calls=%async_computation.1 | async-start | bytes 131072 | tf_op jit(solution)/shard_map/all_to_all | solution.py:97
  63.6 0.4 reshape.183
  64.0 0.5 copy.64
  64.5 0.2 copy.65
  64.7 14.1 %all_gather.7 = bf16[32,64,64]{2,1,0:T(8,128)(2,1)S(1)} all-gather(bf16[32,16,64]{2,1,0:T(8,128)(2,1)S(1)} %copy.65), channel_id=1, replica_groups=mesh['parts'=2,'dap'=4,'sub'=4] {'dap'}, dimensions={1}, use_global_device_ids=true | all-gather | bytes 327680 | tf_op jit(solution)/shard_map/all_gather | solution.py:103
  78.8 0.4 reshape.181
  79.2 0.5 copy.62
  79.8 0.2 copy.66
  79.9 0.4 convolution_convert_fusion
  80.3 0.3 copy.67
  80.6 0.3 reshape.184
  80.9 8.1 %all_to_all.63 = bf16[4,2,4096]{2,1,0:T(2,128)(2,1)S(1)} all-to-all(bf16[4,2,4096]{2,1,0:T(2,128)(2,1)S(1)} %reshape.184), channel_id=1, replica_groups=mesh['parts'=2,'dap'=4,'sub'=4] {'sub'}, dimensions={0} | all-to-all | bytes 131072 | tf_op jit(solution)/shard_map/all_to_all | solution.py:106
  89.0 0.2 reshape.185
  89.2 0.1 fusion.83
  89.2 0.1 fusion.46
  89.4 0.2 multiply_reduce_fusion
  89.6 0.2 copy.69
  89.8 0.3 reshape.161
  90.1 0.2 fusion.64
  90.4 0.3 fusion.87
  90.7 0.2 multiply_reduce_fusion.1
  91.0 1.0 %fusion.37 = bf16[16,16,128]{2,1,0:T(8,128)(2,1)} fusion(f32[16,16,128]{2,1,0:T(8,128)S(1)} %get-tuple-element.16, bf16[512,128]{1,0:T(8,128)(2,1)S(1)} %copy-done.8, bf16[128,512]{1,0:T(8,128)(2,1)S(1)} %copy-done.9, f32[16,16]{1,0:T(8,128)S(1)} %add_rsqrt_fusion.2, f32[16,16]{1,0:T(8,128)S(1)} %broadcast_multiply_fusion.3), kind=kOutput, calls=%fused_computation.40 | convolution fusion | flops 67534848 | bytes 460800 | tf_op jit(solution)/shard_map/dot_general | solution.py:115
  (35 shorter events, 0.1 us)
Async XLA Ops:
  0.0 46.2 %copy-start = (f32[32,32,128]{2,1,0:T(8,128)S(1)}, f32[32,32,128]{2,1,0:T(8,128)}, u32[]{:S(2)}) copy-start(f32[32,32,128]{2,1,0:T(8,128)} %param.22) | copy-start | bytes 1572868
  0.0 36.9 %copy-start.1 = (bf16[256,16,256]{2,1,0:T(8,128)(2,1)S(1)}, bf16[256,16,256]{2,1,0:T(8,128)(2,1)}, u32[]{:S(2)}) copy-start(bf16[256,16,256]{2,1,0:T(8,128)(2,1)} %param.15) | copy-start | bytes 6291460
  2.8 34.7 %copy-start.12 = (s32[64]{0:T(128)S(1)}, s32[64]{0:T(128)}, u32[]{:S(2)}) copy-start(s32[64]{0:T(128)} %param.18) | copy-start | bytes 772
  2.9 35.0 %copy-start.7 = (s32[64]{0:T(128)S(1)}, s32[64]{0:T(128)}, u32[]{:S(2)}) copy-start(s32[64]{0:T(128)} %param.19) | copy-start | bytes 772
  26.5 12.7 %copy-start.11 = (bf16[256,32]{0,1:T(8,128)(2,1)S(1)}, bf16[256,32]{0,1:T(8,128)(2,1)}, u32[]{:S(2)}) copy-start(bf16[256,32]{0,1:T(8,128)(2,1)} %param.20) | copy-start | bytes 49156
  29.9 14.4 %all-to-all-start = ((bf16[4,2,16384]{2,1,0:T(2,128)(2,1)}), bf16[4,2,16384]{2,1,0:T(2,128)(2,1)S(1)}, u32[]{:S(2)}, u32[]{:S(2)}) async-start(bf16[4,2,16384]{2,1,0:T(2,128)(2,1)} %reshape.178), calls=%async_computation | async-start | bytes 524288 | tf_op jit(solution)/shard_map/all_to_all | solution.py:70
  45.4 4.6 %copy-start.2 = (bf16[16,16,128]{2,1,0:T(8,128)(2,1)S(1)}, bf16[16,16,128]{2,1,0:T(8,128)(2,1)}, u32[]{:S(2)}) copy-start(bf16[16,16,128]{2,1,0:T(8,128)(2,1)} %param.17) | copy-start | bytes 196612
  45.4 4.6 %copy-start.6 = (bf16[66,128]{1,0:T(8,128)(2,1)S(1)}, bf16[66,128]{1,0:T(8,128)(2,1)}, u32[]{:S(2)}) copy-start(bf16[66,128]{1,0:T(8,128)(2,1)} %param.27) | copy-start | bytes 50692
  45.4 5.1 %copy-start.3 = (bf16[128,256]{1,0:T(8,128)(2,1)S(1)}, bf16[128,256]{1,0:T(8,128)(2,1)}, u32[]{:S(2)}) copy-start(bf16[128,256]{1,0:T(8,128)(2,1)} %param.23) | copy-start | bytes 196612
  45.4 5.3 %copy-start.4 = (bf16[128,256]{1,0:T(8,128)(2,1)S(1)}, bf16[128,256]{1,0:T(8,128)(2,1)}, u32[]{:S(2)}) copy-start(bf16[128,256]{1,0:T(8,128)(2,1)} %param.24) | copy-start | bytes 196612
  52.7 6.8 %all-to-all-start.2 = ((bf16[4,2,4096]{2,1,0:T(2,128)(2,1)}), bf16[4,2,4096]{2,1,0:T(2,128)(2,1)S(1)}, u32[]{:S(2)}, u32[]{:S(2)}) async-start(bf16[4,2,4096]{2,1,0:T(2,128)(2,1)} %reshape.182), calls=%async_computation.2 | async-start | bytes 131072 | tf_op jit(solution)/shard_map/all_to_all | solution.py:98
  59.5 19.3 %all-to-all-start.1 = ((bf16[4,2,4096]{2,1,0:T(2,128)(2,1)}), bf16[4,2,4096]{2,1,0:T(2,128)(2,1)S(1)}, u32[]{:S(2)}, u32[]{:S(2)}) async-start(bf16[4,2,4096]{2,1,0:T(2,128)(2,1)} %reshape.180), calls=%async_computation.1 | async-start | bytes 131072 | tf_op jit(solution)/shard_map/all_to_all | solution.py:97
  64.5 25.6 %copy-start.5 = (bf16[128,128]{1,0:T(8,128)(2,1)S(1)}, bf16[128,128]{1,0:T(8,128)(2,1)}, u32[]{:S(2)}) copy-start(bf16[128,128]{1,0:T(8,128)(2,1)} %param.26) | copy-start | bytes 98308
  64.5 25.8 %copy-start.10 = (bf16[128,128]{1,0:T(8,128)(2,1)S(1)}, bf16[128,128]{1,0:T(8,128)(2,1)}, u32[]{:S(2)}) copy-start(bf16[128,128]{1,0:T(8,128)(2,1)} %param.25) | copy-start | bytes 98308
  78.8 12.1 %copy-start.8 = (bf16[512,128]{1,0:T(8,128)(2,1)S(1)}, bf16[512,128]{1,0:T(8,128)(2,1)}, u32[]{:S(2)}) copy-start(bf16[512,128]{1,0:T(8,128)(2,1)} %param.29) | copy-start | bytes 393220
  78.8 12.1 %copy-start.9 = (bf16[128,512]{1,0:T(8,128)(2,1)S(1)}, bf16[128,512]{1,0:T(8,128)(2,1)}, u32[]{:S(2)}) copy-start(bf16[128,512]{1,0:T(8,128)(2,1)} %param.28) | copy-start | bytes 393220
where the time goes:
time: 93.4 us; the launch traced here: 92 us
  blocking collectives  43.3 us (46%)
  starting transfers between devices  14.6 us (16%)
  local copies, waits for them, and re-layouts  13.4 us (14%)
  matrix products  11.8 us (13%)
  other arithmetic  6.79 us (7%)
  waiting for transfers between devices  1.66 us (2%)
    all_gather x1, blocking collectives, per_device(): right_all = lax.all_gather(right_share, 'dap', axis=2, tiled=True)  21.1 us
    all_gather x1, blocking collectives, per_device(): lax.all_gather(right_split, 'dap', axis=1, tiled=True)  14.1 us
    all_to_all x1, blocking collectives, per_device(): lax.all_to_all(tri_sum, 'sub', split_axis=2, concat_axis=0, tiled=True)  8.07 us
    all_to_all x1, starting transfers between devices, per_device(): lax.all_to_all(right_all, 'sub', split_axis=2, concat_axis=0, tiled=True)  6.95 us
    unnamed x34, local copies, waits for them, and re-layouts  5.08 us
    dot_general x2, matrix products, outer_factor(): jnp.einsum('sic,ce->sei', normed, weight, preferred_element_type=jnp.floa...  4.41 us
    all_to_all x1, starting transfers between devices, per_device(): lax.all_to_all(left_tri, 'sub', split_axis=0, concat_axis=2, tiled=True)  4.12 us
    dot_general x1, matrix products, per_device(): jnp.einsum('icej,ced->ijd', outer, outer_proj, precision=highest)  3.77 us
  transfers between devices with their start and end apart: 3, of which 1 were waited for; matrix products, arithmetic and copies ran while one was open for 11% of the time, Pallas kernels for 0%

commit v1 on v0

v1 whole, which is shorter than its diff:
```python
import functools

import jax
import jax.numpy as jnp
from jax import lax
from jax.experimental import pallas as pl
from jax.experimental.pallas import tpu as pltpu
from jax.sharding import PartitionSpec as P

REL_CLIP = 32
LANES = 128
EPSILON = 1e-05
BF16 = jnp.bfloat16
F32 = jnp.float32
NT = (((1,), (1,)), ((), ()))


def layer_norm(values):
    average = jnp.mean(values, axis=-1, keepdims=True)
    centered = values - average
    spread = jnp.mean(centered * centered, axis=-1, keepdims=True)
    return centered * lax.rsqrt(spread + EPSILON)


def dot(left, right):
    return jnp.dot(left, right, preferred_element_type=F32)


def dot_nt(left, right):
    return lax.dot_general(left, right, NT, preferred_element_type=F32)


def iota(shape, dim):
    return lax.broadcasted_iota(jnp.int32, shape, dim)


def vmem():
    return pl.BlockSpec(memory_space=pltpu.VMEM)


def factor_kernel(x_ref, mask_ref, wl_ref, wr_ref, zl_ref, zr_ref, w_scr, yl_scr, yr_scr):
    seqs, rows, channels = x_ref.shape
    hidden = wl_ref.shape[1]
    rep = LANES // hidden
    residues = mask_ref.shape[1]
    start = lax.axis_index("dap") * rows

    @pl.when(pl.program_id(0) == 0)
    def _():
        wl, wr = wl_ref[...], wr_ref[...]
        w_scr[:, :LANES] = jnp.concatenate([wl] * rep, axis=1)
        w_scr[:, LANES : 2 * LANES] = jnp.concatenate([wr] * rep, axis=1)
        w_scr[:, 2 * LANES :] = jnp.ones((channels, LANES), BF16)

    x = x_ref[...].reshape(seqs * rows, channels)
    w = w_scr[...]
    sums = dot(jnp.ones((8, channels), BF16), w)[:1]
    y = dot(x, w)
    mean = y[:, 2 * LANES :] * (1.0 / channels)
    xf = x.astype(F32)
    square = jnp.zeros_like(mean)
    for part in range(channels // LANES):
        centered = xf[:, part * LANES : (part + 1) * LANES] - mean
        square = square + centered * centered
    ones = jnp.ones((LANES, LANES), BF16)
    scale = lax.rsqrt(dot(square.astype(BF16), ones) * (1.0 / channels) + EPSILON)
    yl_scr[...] = (y[:, :LANES] - mean * sums[:, :LANES]) * scale
    yr_scr[...] = (y[:, LANES : 2 * LANES] - mean * sums[:, LANES : 2 * LANES]) * scale
    width = rows * hidden
    spread = (iota((residues, width), 0) == start + iota((residues, width), 1) // hidden).astype(BF16)
    live = dot(mask_ref[...].astype(BF16), spread)
    block = iota((seqs, LANES), 1) // hidden
    for scr, out in ((yr_scr, zr_ref), (yl_scr, zl_ref)):
        for group in range(rows // rep):
            z = scr[pl.ds(group * rep, seqs, stride=rows), :]
            for k in range(1, rep):
                z = jnp.where(block == k, scr[pl.ds(group * rep + k, seqs, stride=rows), :], z)
            lanes = slice(group * LANES, (group + 1) * LANES)
            out[:, lanes] = (z * live[:, lanes]).astype(BF16)


def factors(alignment, alignment_mask, outer_left, outer_right):
    seqs, rows, channels = alignment.shape
    residues = alignment_mask.shape[1]
    hidden = outer_left.shape[1]
    step = seqs // 4
    width = rows * hidden
    out = jax.ShapeDtypeStruct((seqs, width), BF16)
    return pl.pallas_call(
        factor_kernel,
        out_shape=(out, out),
        grid=(seqs // step,),
        in_specs=[
            pl.BlockSpec((step, rows, channels), lambda s: (s, 0, 0)),
            pl.BlockSpec((step, residues), lambda s: (s, 0)),
            pl.BlockSpec((channels, hidden), lambda s: (0, 0)),
            pl.BlockSpec((channels, hidden), lambda s: (0, 0)),
        ],
        out_specs=[pl.BlockSpec((step, width), lambda s: (s, 0))] * 2,
        scratch_shapes=[
            pltpu.VMEM((channels, 3 * LANES), BF16),
            pltpu.VMEM((step * rows, LANES), F32),
            pltpu.VMEM((step * rows, LANES), F32),
        ],
        compiler_params=pltpu.CompilerParams(vmem_limit_bytes=24 << 20),
        cost_estimate=pl.CostEstimate(
            flops=2 * seqs * rows * channels * 512, bytes_accessed=4 << 20, transcendentals=0
        ),
    )(alignment, alignment_mask, outer_left, outer_right)


def prepare_kernel(
    zl_ref, mask_ref, pair_ref, live_ref, chain_ref, table_ref, proj_ref,
    zlt_ref, base_ref, inverse_ref, live_out_ref, proj_out_ref, pair_scr, table_scr,
):
    rows, cols, _ = pair_ref.shape
    pairs = rows * cols
    residues = mask_ref.shape[1]
    classes = table_ref.shape[0]
    row_start = lax.axis_index("dap") * rows
    col_start = lax.axis_index("sub") * cols
    zlt_ref[...] = zl_ref[...].T
    proj_out_ref[...] = proj_ref[...].reshape(proj_out_ref.shape).astype(BF16)
    which = iota((pairs, residues), 0)
    place = iota((pairs, residues), 1)
    pick_row = (place == row_start + which % rows).astype(BF16)
    pick_col = (place == col_start + which // rows).astype(BF16)
    mask = mask_ref[...].astype(BF16)
    both = (dot_nt(pick_row, mask) * dot_nt(pick_col, mask)).astype(BF16)
    counts = dot(both, jnp.ones((mask.shape[0], LANES), BF16))
    inverse_ref[...] = 1.0 / jnp.maximum(counts, 1.0)
    live = jnp.broadcast_to(live_ref[...].astype(F32), (LANES, residues)).astype(BF16)
    chain = jnp.broadcast_to(chain_ref[...].astype(F32), (LANES, residues)).astype(BF16)
    live_out_ref[...] = dot_nt(pick_row, live) * dot_nt(pick_col, live)
    same = dot_nt(pick_row, chain) == dot_nt(pick_col, chain)
    pair = iota((pairs, LANES), 0)
    offset = (row_start + pair % rows) - (col_start + pair // rows) + REL_CLIP
    bucket = jnp.where(same, jnp.clip(offset, 0, 2 * REL_CLIP), 2 * REL_CLIP + 1)
    table_scr[...] = jnp.zeros_like(table_scr)
    table_scr[pl.ds(0, classes), :] = table_ref[...].astype(F32)
    onehot = (bucket == iota((pairs, LANES), 1)).astype(BF16)
    relative = dot(onehot, table_scr[...].astype(BF16))
    pair_scr[...] = pair_ref[...].reshape(pairs, LANES).astype(F32)
    for col in range(cols):
        here = slice(col * rows, (col + 1) * rows)
        base_ref[here, :] = relative[here] + pair_scr[pl.ds(col, rows, stride=cols), :]


def prepare(zl, alignment_mask, pair_input, residue_mask, chain_index, table, proj):
    rows, cols, channels = pair_input.shape
    pairs = rows * cols
    shape = jax.ShapeDtypeStruct((pairs, channels), F32)
    depth = proj.shape[0] * proj.shape[1]
    return pl.pallas_call(
        prepare_kernel,
        out_shape=(
            jax.ShapeDtypeStruct(zl.shape[::-1], BF16),
            shape,
            shape,
            shape,
            jax.ShapeDtypeStruct((depth, channels), BF16),
        ),
        in_specs=[vmem()] * 7,
        out_specs=[vmem()] * 5,
        scratch_shapes=[pltpu.VMEM((pairs, channels), F32), pltpu.VMEM((LANES, channels), F32)],
        compiler_params=pltpu.CompilerParams(vmem_limit_bytes=24 << 20),
        cost_estimate=pl.CostEstimate(
            flops=2 * pairs * 256 * 1024, bytes_accessed=2 << 20, transcendentals=0
        ),
    )(zl, alignment_mask, pair_input, residue_mask[None, :], chain_index[None, :], table, proj)


def pair_kernel(ratio, hidden, zlt_ref, *refs):
    zr_refs, refs = refs[:ratio], refs[ratio:]
    (base_ref, inverse_ref, live_ref, proj_ref, tl_ref, tr_ref,
     left_ref, right_ref, one_ref, outer_scr, flat_scr, one_scr) = refs
    pairs, channels = base_ref.shape
    rows = zlt_ref.shape[0] // hidden
    rep = LANES // hidden
    me = lax.axis_index("dap")
    lane = iota((rows, LANES), 1)
    odd = (lane // hidden) % 2 == 1
    upper = lane // (2 * hidden) == 1
    half = 2 * hidden
    for step in range(ratio):
        block = lax.rem(me + step, ratio)
        outer = dot(zlt_ref[...], zr_refs[step][...])
        for group in range(rows // rep):
            outer_scr[group] = outer[:, group * LANES : (group + 1) * LANES]
        for group in range(rows // rep):
            for quad in range(hidden // rep):
                s0, s1, s2, s3 = (
                    outer_scr[group, pl.ds(quad * rep + k, rows, stride=hidden), :] for k in range(rep)
                )
                t0 = jnp.where(upper, pltpu.roll(s2, half, 1), s0)
                t1 = jnp.where(upper, pltpu.roll(s3, half, 1), s1)
                t2 = jnp.where(upper, s2, pltpu.roll(s0, half, 1))
                t3 = jnp.where(upper, s3, pltpu.roll(s1, half, 1))
                back = LANES - hidden
                found = (
                    jnp.where(odd, pltpu.roll(t1, hidden, 1), t0),
                    jnp.where(odd, t1, pltpu.roll(t0, back, 1)),
                    jnp.where(odd, pltpu.roll(t3, hidden, 1), t2),
                    jnp.where(odd, t3, pltpu.roll(t2, back, 1)),
                )
                for k in range(rep):
                    first = block * rows * rows + (group * rep + k) * rows
                    if ratio == 1:
                        first = (group * rep + k) * rows
                    else:
                        first = pl.multiple_of(first, rows)
                    flat_scr[pl.ds(first, rows), quad * LANES : (quad + 1) * LANES] = found[k].astype(BF16)
    outer_mean = dot(flat_scr[...], proj_ref[...]) * inverse_ref[...]
    one = (base_ref[...] + outer_mean).astype(BF16).astype(F32)
    one_scr[...] = one
    norm = layer_norm(one).astype(BF16)
    for weight, out in ((tl_ref, left_ref), (tr_ref, right_ref)):
        both = dot(norm, weight[...])
        out[...] = (jax.nn.sigmoid(both[:, :channels]) * both[:, channels:] * live_ref[...]).astype(BF16)
    cols = pairs // rows
    for row in range(rows):
        one_ref[row * cols : (row + 1) * cols, :] = one_scr[pl.ds(row, cols, stride=rows), :].astype(BF16)


def pair_update(hidden, zlt, zrs, base, inverse, live, proj, triangle_left, triangle_right):
    pairs, channels = base.shape
    ratio = len(zrs)
    shape = jax.ShapeDtypeStruct((pairs, channels), BF16)
    return pl.pallas_call(
        functools.partial(pair_kernel, ratio, hidden),
        out_shape=(shape, shape, shape),
        in_specs=[vmem()] * (7 + ratio),
        out_specs=[vmem()] * 3,
        scratch_shapes=[
            pltpu.VMEM((zrs[0].shape[1] // LANES, zlt.shape[0], LANES), F32),
            pltpu.VMEM((pairs, proj.shape[0]), BF16),
            pltpu.VMEM((pairs, channels), F32),
        ],
        compiler_params=pltpu.CompilerParams(vmem_limit_bytes=32 << 20),
        cost_estimate=pl.CostEstimate(
            flops=2 * pairs * 1024 * 512, bytes_accessed=2 << 20, transcendentals=pairs * 256
        ),
    )(zlt, *zrs, base, inverse, live, proj, triangle_left, triangle_right)


def triangle_kernel(subs, ratio, cols, *refs):
    lefts, refs = refs[:subs], refs[subs:]
    rights, refs = refs[: subs * ratio], refs[subs * ratio :]
    (one_ref, gate_ref, out_ref, up_ref, down_ref, result_ref, left_scr, right_scr, sum_scr) = refs
    pairs, channels = one_ref.shape
    rows = pairs // cols
    here, there = lax.axis_index("dap"), lax.axis_index("sub")
    for step in range(subs):
        left_scr[lax.rem(there + step, subs)] = lefts[step][...].astype(F32)
    for turn in range(ratio):
        block = lax.rem(here + turn, ratio)
        for step in range(subs):
            slot = block * subs + lax.rem(here // ratio + step, subs)
            right_scr[slot] = rights[turn * subs + step][...].astype(F32)
    for block in range(ratio):
        totals = tuple(jnp.zeros((rows, channels), F32) for _ in range(rows))
        for sub in range(subs):

            def body(k, totals, sub=sub, block=block):
                first = pl.multiple_of(k * rows, rows)
                right = right_scr[block * subs + sub, pl.ds(first, rows), :]
                return tuple(
                    totals[i] + left_scr[sub, pl.ds(first + i, 1), :] * right for i in range(rows)
                )

            totals = lax.fori_loop(0, cols, body, totals, unroll=4)
        for i in range(rows):
            sum_scr[i * cols + block * rows : i * cols + (block + 1) * rows, :] = totals[i]
    one = one_ref[...].astype(F32)
    norm = layer_norm(one).astype(BF16)
    gate = jax.nn.sigmoid(dot(norm, gate_ref[...]))
    hidden = layer_norm(sum_scr[...].astype(BF16).astype(F32)).astype(BF16)
    two = (one + gate * dot(hidden, out_ref[...])).astype(BF16).astype(F32)
    wide = jnp.maximum(dot(layer_norm(two).astype(BF16), up_ref[...]), 0.0).astype(BF16)
    result = (two + dot(wide, down_ref[...])).astype(BF16)
    result_ref[...] = result.reshape(result_ref.shape)


def triangle_update(lefts, rights, one, cols, gate, out, up, down):
    pairs, channels = one.shape
    rows = pairs // cols
    subs = len(lefts)
    ratio = len(rights) // subs
    return pl.pallas_call(
        functools.partial(triangle_kernel, subs, ratio, cols),
        out_shape=jax.ShapeDtypeStruct((rows, cols, channels), BF16),
        in_specs=[vmem()] * (subs + subs * ratio + 5),
        out_specs=vmem(),
        scratch_shapes=[
            pltpu.VMEM((subs, pairs, channels), F32),
            pltpu.VMEM((subs * ratio, pairs, channels), F32),
            pltpu.VMEM((pairs, channels), F32),
        ],
        compiler_params=pltpu.CompilerParams(vmem_limit_bytes=(16 << 20) if ratio == 1 else (50 << 20)),
        cost_estimate=pl.CostEstimate(
            flops=2 * pairs * channels * 2048, bytes_accessed=2 << 20, transcendentals=pairs * 128
        ),
    )(*lefts, *rights, one, gate, out, up, down)


def per_device(
    alignment,
    alignment_mask,
    pair_input,
    residue_mask,
    chain_index,
    outer_left,
    outer_right,
    outer_proj,
    triangle_left,
    triangle_right,
    triangle_gate,
    triangle_out,
    relative_table,
    transition_up,
    transition_down,
):
    daps, subs = lax.axis_size("dap"), lax.axis_size("sub")
    ratio = daps // subs
    cols = pair_input.shape[1]

    def fetch(values, source):
        perm = []
        for a in range(daps):
            for b in range(subs):
                dap, sub = source(a, b)
                perm.append((dap * subs + sub, a * subs + b))
        return lax.ppermute(values, ("dap", "sub"), perm)

    def owner(a, b, turn):
        return ratio * b + (a + turn) % ratio

    zl, zr = factors(alignment, alignment_mask, outer_left, outer_right)
    zrs = [
        fetch(zr, lambda a, b, turn=turn: (owner(a, b, turn), a // ratio)) for turn in range(ratio)
    ]
    zlt, base, inverse, live, proj = prepare(
        zl, alignment_mask, pair_input, residue_mask, chain_index, relative_table, outer_proj
    )
    left, right, one = pair_update(
        outer_left.shape[1], zlt, zrs, base, inverse, live, proj, triangle_left, triangle_right
    )
    rights = [
        fetch(right, lambda a, b, t=turn, m=step: (owner(a, b, t), (a // ratio + m) % subs))
        for turn in range(ratio)
        for step in range(subs)
    ]
    lefts = [left] + [
        fetch(left, lambda a, b, m=step: (a, (b + m) % subs)) for step in range(1, subs)
    ]
    return triangle_update(
        lefts, rights, one, cols, triangle_gate, triangle_out, transition_up, transition_down
    )


def solution(mesh):
    in_specs = (
        P("parts", "dap", None),
        P("parts", None),
        P(("parts", "dap"), "sub", None),
        P("parts"),
        P("parts"),
        P(),
        P(),
        P(),
        P(),
        P(),
        P(),
        P(),
        P(),
        P(),
        P(),
    )
    out_specs = P(("parts", "dap"), "sub", None)
    return jax.shard_map(
        per_device, mesh=mesh, in_specs=in_specs, out_specs=out_specs, check_vma=False
    )
```

time: 93.4 us -> 44.5 us (0.48)
  the two profiles are of different devices: /device:TPU:1 before, /device:TPU:16 now
where the time goes in v1:
time: 44.5 us; the launch traced here: 44.2 us
  waiting for transfers between devices  16.9 us (38%)
  starting transfers between devices  14.5 us (33%)
  Pallas kernels  8.19 us (18%)
  local copies, waits for them, and re-layouts  4.31 us (10%)
    ppermute x8, waiting for transfers between devices, fetch(): return lax.ppermute(values, ('dap', 'sub'), perm)  16.9 us
    ppermute x8, starting transfers between devices, fetch(): return lax.ppermute(values, ('dap', 'sub'), perm)  14.5 us
    unnamed x27, local copies, waits for them, and re-layouts  4.31 us
    pallas_call x1, Pallas kernels, factors(): pl.pallas_call(factor_kernel, out_shape=(out, out), grid=(seqs // step,),...  3.82 us
    pallas_call x1, Pallas kernels, triangle_update(): pl.pallas_call(functools.partial(triangle_kernel, subs, ratio, cols), out...  2.23 us
    pallas_call x1, Pallas kernels, pair_update(): pl.pallas_call(functools.partial(pair_kernel, ratio, hidden), out_shape=(...  1.6 us
  transfers between devices with their start and end apart: 8, of which 3 were waited for; matrix products, arithmetic and copies ran while one was open for 0% of the time, Pallas kernels for 1%

profile of v1, /device:TPU:16, one launch (start us, length us, event | category | flops | bytes accessed | tf_op | source)
XLA Modules:
  0.0 44.2 jit_solution(529637391163310021)
XLA Ops:
  0.0 0.8 %copy.17.wl_ref = bf16[256,32]{1,0:T(8,128)(2,1)S(1)} copy(bf16[256,32]{0,1:T(8,128)(2,1)} %param.20) | data formatting | bytes 32768 | tf_op args[5]
  0.8 0.8 %copy.18.wr_ref = bf16[256,32]{1,0:T(8,128)(2,1)S(1)} copy(bf16[256,32]{0,1:T(8,128)(2,1)} %param.21) | data formatting | bytes 32768 | tf_op args[6]
  1.7 0.0 copy-start
  1.7 0.0 copy-start.3
  1.7 0.0 copy-start.8
  1.7 0.0 copy-start.9
  1.7 0.0 copy-start.10
  1.7 1.0 %copy.16.mask_ref = s32[256,64]{1,0:T(8,128)S(1)} copy(s32[256,64]{0,1:T(8,128)} %param.16) | data formatting | bytes 131072 | tf_op args[1]
  2.7 0.0 copy-start.11
  2.7 1.6 %copy-done.11 = bf16[256,16,256]{2,1,0:T(8,128)(2,1)S(1)} copy-done((bf16[256,16,256]{2,1,0:T(8,128)(2,1)S(1)}, bf16[256,16,256]{2,1,0:T(8,128)(2,1)}, u32[]{:S(2)}) %copy-start.11) | copy-done | bytes 2097176
  4.3 0.0 copy-start.4
  4.3 0.0 copy-start.5
  4.3 3.8 %shard_map.145 = (bf16[256,512]{1,0:T(8,128)(2,1)S(1)}, bf16[256,512]{1,0:T(8,128)(2,1)S(1)}) custom-call(bf16[256,16,256]{2,1,0:T(8,128)(2,1)S(1)} %copy-done.11, s32[256,64]{1,0:T(8,128)S(1)} %copy.16.mask_ref, bf16[256,32]{1,0:T(8,128)(2,1)S(1)} %copy.17.wl_ref, bf16[256,32]{1,0:T(8,128)(2,1)S(1)} %copy.18.wr_ref), custom_call_target="tpu_custom_call" | custom-call | flops 1073741824 | bytes 4194304 | tf_op jit(solution)/shard_map/pallas_call | solution.py:89
  8.2 0.0 copy-start.1
  8.2 0.0 copy-start.2
  8.2 0.0 copy-start.6
  8.2 0.0 copy-start.7
  8.2 3.3 %collective-permute-start = (bf16[256,512]{1,0:T(8,128)(2,1)S(1)}, bf16[256,512]{1,0:T(8,128)(2,1)S(1)}, u32[]{:S(2)}, u32[]{:S(2)}) collective-permute-start(bf16[256,512]{1,0:T(8,128)(2,1)S(1)} %get-tuple-element.17), channel_id=1, source_target_pairs={{0,0},{4,1},{8,2},{12,3},{1,4},{5,5},{9,6},{13,7},{2,8},{6,9},{10,... | collective-permute-start | bytes 786440 | tf_op jit(solution)/shard_map/ppermute | solution.py:333
  11.5 0.0 copy-done
  11.5 0.0 copy-done.3
  11.5 0.0 copy-done.8
  11.5 0.0 copy-done.9
  11.6 0.0 copy-done.10
  11.6 0.5 %shard_map.146 = (bf16[512,256]{1,0:T(8,128)(2,1)S(1)}, f32[256,128]{1,0:T(8,128)S(1)}, f32[256,128]{1,0:T(8,128)S(1)}, f32[256,128]{1,0:T(8,128)S(1)}, bf16[1024,128]{1,0:T(8,128)(2,1)S(1)}) custom-call(bf16[256,512]{1,0:T(8,128)(2,1)S(1)} %get-tuple-element.15.zl_ref, s32[256,64]{1,0:T(8,128)S(1)} %copy.16.mask_ref, bf16[16,16,128]{2,1,0:T(8,128)(2,1)S(1)} %copy-done.3, ...), custom_call_target="tpu_custom_call" | custom-call | flops 134217728 | bytes 2097152 | tf_op jit(solution)/shard_map/pallas_call | solution.py:154
  12.1 11.2 %collective-permute-done.refs_0_ = bf16[256,512]{1,0:T(8,128)(2,1)S(1)} collective-permute-done((bf16[256,512]{1,0:T(8,128)(2,1)S(1)}, bf16[256,512]{1,0:T(8,128)(2,1)S(1)}, u32[]{:S(2)}, u32[]{:S(2)}) %collective-permute-start) | collective-permute-done | bytes 262176 | tf_op jit(solution)/shard_map/ppermute | solution.py:333
  23.3 0.0 copy-done.4
  23.4 0.0 copy-done.5
  23.4 1.6 %shard_map.147 = (bf16[256,128]{1,0:T(8,128)(2,1)S(1)}, bf16[256,128]{1,0:T(8,128)(2,1)S(1)}, bf16[256,128]{1,0:T(8,128)(2,1)S(1)}) custom-call(bf16[512,256]{1,0:T(8,128)(2,1)S(1)} %get-tuple-element.16.zlt_ref, bf16[256,512]{1,0:T(8,128)(2,1)S(1)} %collective-permute-done.refs_0_, f32[256,128]{1,0:T(8,128)S(1)} %get-tuple-element.18.refs_1_, ...), custom_call_target="tpu_custom_call" | custom-call | flops 268435456 | bytes 2097152 | tf_op jit(solution)/shard_map/pallas_call | solution.py:229
  25.0 1.5 %collective-permute-start.3 = (bf16[256,128]{1,0:T(8,128)(2,1)S(1)}, bf16[256,128]{1,0:T(8,128)(2,1)S(1)}, u32[]{:S(2)}, u32[]{:S(2)}) collective-permute-start(bf16[256,128]{1,0:T(8,128)(2,1)S(1)} %get-tuple-element.22.refs_0_), channel_id=1, source_target_pairs={{3,0},{0,1},{1,2},{2,3},{7,4},{4,5},{5,6},{6,7},{11,8},{8,9},{9,10... | collective-permute-start | bytes 196616 | tf_op jit(solution)/shard_map/ppermute | solution.py:333
  26.5 0.0 collective-permute-start.2
  26.5 1.4 %collective-permute-start.1 = (bf16[256,128]{1,0:T(8,128)(2,1)S(1)}, bf16[256,128]{1,0:T(8,128)(2,1)S(1)}, u32[]{:S(2)}, u32[]{:S(2)}) collective-permute-start(bf16[256,128]{1,0:T(8,128)(2,1)S(1)} %get-tuple-element.22.refs_0_), channel_id=1, source_target_pairs={{1,0},{2,1},{3,2},{0,3},{5,4},{6,5},{7,6},{4,7},{9,8},{10,9},{11,1... | collective-permute-start | bytes 196616 | tf_op jit(solution)/shard_map/ppermute | solution.py:333
  27.9 1.9 %collective-permute-start.7 = (bf16[256,128]{1,0:T(8,128)(2,1)S(1)}, bf16[256,128]{1,0:T(8,128)(2,1)S(1)}, u32[]{:S(2)}, u32[]{:S(2)}) collective-permute-start(bf16[256,128]{1,0:T(8,128)(2,1)S(1)} %get-tuple-element.23), channel_id=1, source_target_pairs={{3,0},{7,1},{11,2},{15,3},{0,4},{4,5},{8,6},{12,7},{1,8},{5,9},{9,... | collective-permute-start | bytes 196616 | tf_op jit(solution)/shard_map/ppermute | solution.py:333
  29.8 0.5 %collective-permute-start.6 = (bf16[256,128]{1,0:T(8,128)(2,1)S(1)}, bf16[256,128]{1,0:T(8,128)(2,1)S(1)}, u32[]{:S(2)}, u32[]{:S(2)}) collective-permute-start(bf16[256,128]{1,0:T(8,128)(2,1)S(1)} %get-tuple-element.23), channel_id=1, source_target_pairs={{2,0},{6,1},{10,2},{14,3},{3,4},{7,5},{11,6},{15,7},{0,8},{4,9},{8... | collective-permute-start | bytes 196616 | tf_op jit(solution)/shard_map/ppermute | solution.py:333
  30.4 0.0 collective-permute-done.3.refs_3_
  30.4 3.6 %collective-permute-start.5 = (bf16[256,128]{1,0:T(8,128)(2,1)S(1)}, bf16[256,128]{1,0:T(8,128)(2,1)S(1)}, u32[]{:S(2)}, u32[]{:S(2)}) collective-permute-start(bf16[256,128]{1,0:T(8,128)(2,1)S(1)} %get-tuple-element.23), channel_id=1, source_target_pairs={{1,0},{5,1},{9,2},{13,3},{2,4},{6,5},{10,6},{14,7},{3,8},{7,9},{11... | collective-permute-start | bytes 196616 | tf_op jit(solution)/shard_map/ppermute | solution.py:333
  34.0 0.0 collective-permute-done.2.refs_2_
  34.0 2.2 %collective-permute-start.4 = (bf16[256,128]{1,0:T(8,128)(2,1)S(1)}, bf16[256,128]{1,0:T(8,128)(2,1)S(1)}, u32[]{:S(2)}, u32[]{:S(2)}) collective-permute-start(bf16[256,128]{1,0:T(8,128)(2,1)S(1)} %get-tuple-element.23), channel_id=1, source_target_pairs={{0,0},{4,1},{8,2},{12,3},{1,4},{5,5},{9,6},{13,7},{2,8},{6,9},{10,... | collective-permute-start | bytes 196616 | tf_op jit(solution)/shard_map/ppermute | solution.py:333
  36.2 0.0 collective-permute-done.1.refs_1_
  36.2 0.0 collective-permute-done.7.refs_7_
  36.2 0.0 collective-permute-done.6.refs_6_
  36.2 0.6 %collective-permute-done.5.refs_5_ = bf16[256,128]{1,0:T(8,128)(2,1)S(1)} collective-permute-done((bf16[256,128]{1,0:T(8,128)(2,1)S(1)}, bf16[256,128]{1,0:T(8,128)(2,1)S(1)}, u32[]{:S(2)}, u32[]{:S(2)}) %collective-permute-start.5) | collective-permute-done | bytes 65568 | tf_op jit(solution)/shard_map/ppermute | solution.py:333
  36.8 5.1 %collective-permute-done.4.refs_4_ = bf16[256,128]{1,0:T(8,128)(2,1)S(1)} collective-permute-done((bf16[256,128]{1,0:T(8,128)(2,1)S(1)}, bf16[256,128]{1,0:T(8,128)(2,1)S(1)}, u32[]{:S(2)}, u32[]{:S(2)}) %collective-permute-start.4) | collective-permute-done | bytes 65568 | tf_op jit(solution)/shard_map/ppermute | solution.py:333
  41.9 0.0 copy-done.1
  41.9 0.0 copy-done.2
  41.9 0.0 copy-done.6
  41.9 0.0 copy-done.7
  42.0 2.2 %shard_map.148 = bf16[16,16,128]{2,1,0:T(8,128)(2,1)} custom-call(bf16[256,128]{1,0:T(8,128)(2,1)S(1)} %get-tuple-element.22.refs_0_, bf16[256,128]{1,0:T(8,128)(2,1)S(1)} %collective-permute-done.1.refs_1_, bf16[256,128]{1,0:T(8,128)(2,1)S(1)} %collective-permute-done.2.refs_2_, bf16[256,128]{1,0:T(8,128)(2,1)S(1)} %collective-permute-done.3.refs_3_, ...), custom_call_target="tpu_custom_call" | custom-call | flops 134217728 | bytes 2097152 | tf_op jit(solution)/shard_map/pallas_call | solution.py:289
Async XLA Ops:
  1.7 9.8 %copy-start = (f32[32,32,128]{2,1,0:T(8,128)S(1)}, f32[32,32,128]{2,1,0:T(8,128)}, u32[]{:S(2)}) copy-start(f32[32,32,128]{2,1,0:T(8,128)} %proj_ref.1) | copy-start | bytes 1572868
  1.7 9.8 %copy-start.3 = (bf16[16,16,128]{2,1,0:T(8,128)(2,1)S(1)}, bf16[16,16,128]{2,1,0:T(8,128)(2,1)}, u32[]{:S(2)}) copy-start(bf16[16,16,128]{2,1,0:T(8,128)(2,1)} %pair_ref.1) | copy-start | bytes 196612
  1.7 9.8 %copy-start.8 = (bf16[66,128]{1,0:T(8,128)(2,1)S(1)}, bf16[66,128]{1,0:T(8,128)(2,1)}, u32[]{:S(2)}) copy-start(bf16[66,128]{1,0:T(8,128)(2,1)} %table_ref.1) | copy-start | bytes 50692
  1.7 9.8 %copy-start.9 = (s32[64]{0:T(128)S(1)}, s32[64]{0:T(128)}, u32[]{:S(2)}) copy-start(s32[64]{0:T(128)} %param.18) | copy-start | bytes 772
  1.7 9.8 %copy-start.10 = (s32[64]{0:T(128)S(1)}, s32[64]{0:T(128)}, u32[]{:S(2)}) copy-start(s32[64]{0:T(128)} %param.19) | copy-start | bytes 772
  2.7 1.6 %copy-start.11 = (bf16[256,16,256]{2,1,0:T(8,128)(2,1)S(1)}, bf16[256,16,256]{2,1,0:T(8,128)(2,1)}, u32[]{:S(2)}) copy-start(bf16[256,16,256]{2,1,0:T(8,128)(2,1)} %x_ref.1) | copy-start | bytes 6291460
  4.3 19.0 %copy-start.4 = (bf16[128,256]{1,0:T(8,128)(2,1)S(1)}, bf16[128,256]{1,0:T(8,128)(2,1)}, u32[]{:S(2)}) copy-start(bf16[128,256]{1,0:T(8,128)(2,1)} %refs_5_.1) | copy-start | bytes 196612
  4.3 19.0 %copy-start.5 = (bf16[128,256]{1,0:T(8,128)(2,1)S(1)}, bf16[128,256]{1,0:T(8,128)(2,1)}, u32[]{:S(2)}) copy-start(bf16[128,256]{1,0:T(8,128)(2,1)} %refs_6_.1) | copy-start | bytes 196612
  8.2 33.8 %copy-start.1 = (bf16[128,512]{1,0:T(8,128)(2,1)S(1)}, bf16[128,512]{1,0:T(8,128)(2,1)}, u32[]{:S(2)}) copy-start(bf16[128,512]{1,0:T(8,128)(2,1)} %refs_11_.1) | copy-start | bytes 393220
  8.2 33.8 %copy-start.2 = (bf16[512,128]{1,0:T(8,128)(2,1)S(1)}, bf16[512,128]{1,0:T(8,128)(2,1)}, u32[]{:S(2)}) copy-start(bf16[512,128]{1,0:T(8,128)(2,1)} %refs_12_.1) | copy-start | bytes 393220
  8.2 33.8 %copy-start.6 = (bf16[128,128]{1,0:T(8,128)(2,1)S(1)}, bf16[128,128]{1,0:T(8,128)(2,1)}, u32[]{:S(2)}) copy-start(bf16[128,128]{1,0:T(8,128)(2,1)} %refs_9_.1) | copy-start | bytes 98308
  8.2 33.8 %copy-start.7 = (bf16[128,128]{1,0:T(8,128)(2,1)S(1)}, bf16[128,128]{1,0:T(8,128)(2,1)}, u32[]{:S(2)}) copy-start(bf16[128,128]{1,0:T(8,128)(2,1)} %refs_10_.1) | copy-start | bytes 98308
  8.2 15.1 %collective-permute-start = (bf16[256,512]{1,0:T(8,128)(2,1)S(1)}, bf16[256,512]{1,0:T(8,128)(2,1)S(1)}, u32[]{:S(2)}, u32[]{:S(2)}) collective-permute-start(bf16[256,512]{1,0:T(8,128)(2,1)S(1)} %get-tuple-element.17), channel_id=1, source_target_pairs={{0,0},{4,1},{8,2},{12,3},{1,4},{5,5},{9,6},{13,7},{2,8},{6,9},{10,... | collective-permute-start | bytes 786440 | tf_op jit(solution)/shard_map/ppermute | solution.py:333
  25.0 5.4 %collective-permute-start.3 = (bf16[256,128]{1,0:T(8,128)(2,1)S(1)}, bf16[256,128]{1,0:T(8,128)(2,1)S(1)}, u32[]{:S(2)}, u32[]{:S(2)}) collective-permute-start(bf16[256,128]{1,0:T(8,128)(2,1)S(1)} %get-tuple-element.22.refs_0_), channel_id=1, source_target_pairs={{3,0},{0,1},{1,2},{2,3},{7,4},{4,5},{5,6},{6,7},{11,8},{8,9},{9,10... | collective-permute-start | bytes 196616 | tf_op jit(solution)/shard_map/ppermute | solution.py:333
  26.5 7.5 %collective-permute-start.2 = (bf16[256,128]{1,0:T(8,128)(2,1)S(1)}, bf16[256,128]{1,0:T(8,128)(2,1)S(1)}, u32[]{:S(2)}, u32[]{:S(2)}) collective-permute-start(bf16[256,128]{1,0:T(8,128)(2,1)S(1)} %get-tuple-element.22.refs_0_), channel_id=1, source_target_pairs={{2,0},{3,1},{0,2},{1,3},{6,4},{7,5},{4,6},{5,7},{10,8},{11,9},{8,1... | collective-permute-start | bytes 196616 | tf_op jit(solution)/shard_map/ppermute | solution.py:333
  26.5 9.7 %collective-permute-start.1 = (bf16[256,128]{1,0:T(8,128)(2,1)S(1)}, bf16[256,128]{1,0:T(8,128)(2,1)S(1)}, u32[]{:S(2)}, u32[]{:S(2)}) collective-permute-start(bf16[256,128]{1,0:T(8,128)(2,1)S(1)} %get-tuple-element.22.refs_0_), channel_id=1, source_target_pairs={{1,0},{2,1},{3,2},{0,3},{5,4},{6,5},{7,6},{4,7},{9,8},{10,9},{11,1... | collective-permute-start | bytes 196616 | tf_op jit(solution)/shard_map/ppermute | solution.py:333
  27.9 8.3 %collective-permute-start.7 = (bf16[256,128]{1,0:T(8,128)(2,1)S(1)}, bf16[256,128]{1,0:T(8,128)(2,1)S(1)}, u32[]{:S(2)}, u32[]{:S(2)}) collective-permute-start(bf16[256,128]{1,0:T(8,128)(2,1)S(1)} %get-tuple-element.23), channel_id=1, source_target_pairs={{3,0},{7,1},{11,2},{15,3},{0,4},{4,5},{8,6},{12,7},{1,8},{5,9},{9,... | collective-permute-start | bytes 196616 | tf_op jit(solution)/shard_map/ppermute | solution.py:333
  29.8 6.4 %collective-permute-start.6 = (bf16[256,128]{1,0:T(8,128)(2,1)S(1)}, bf16[256,128]{1,0:T(8,128)(2,1)S(1)}, u32[]{:S(2)}, u32[]{:S(2)}) collective-permute-start(bf16[256,128]{1,0:T(8,128)(2,1)S(1)} %get-tuple-element.23), channel_id=1, source_target_pairs={{2,0},{6,1},{10,2},{14,3},{3,4},{7,5},{11,6},{15,7},{0,8},{4,9},{8... | collective-permute-start | bytes 196616 | tf_op jit(solution)/shard_map/ppermute | solution.py:333
  30.4 6.5 %collective-permute-start.5 = (bf16[256,128]{1,0:T(8,128)(2,1)S(1)}, bf16[256,128]{1,0:T(8,128)(2,1)S(1)}, u32[]{:S(2)}, u32[]{:S(2)}) collective-permute-start(bf16[256,128]{1,0:T(8,128)(2,1)S(1)} %get-tuple-element.23), channel_id=1, source_target_pairs={{1,0},{5,1},{9,2},{13,3},{2,4},{6,5},{10,6},{14,7},{3,8},{7,9},{11... | collective-permute-start | bytes 196616 | tf_op jit(solution)/shard_map/ppermute | solution.py:333
  34.0 7.9 %collective-permute-start.4 = (bf16[256,128]{1,0:T(8,128)(2,1)S(1)}, bf16[256,128]{1,0:T(8,128)(2,1)S(1)}, u32[]{:S(2)}, u32[]{:S(2)}) collective-permute-start(bf16[256,128]{1,0:T(8,128)(2,1)S(1)} %get-tuple-element.23), channel_id=1, source_target_pairs={{0,0},{4,1},{8,2},{12,3},{1,4},{5,5},{9,6},{13,7},{2,8},{6,9},{10,... | collective-permute-start | bytes 196616 | tf_op jit(solution)/shard_map/ppermute | solution.py:333

commit v2 on v1

--- a/solution.py
+++ b/solution.py
@@ -13,6 +13,7 @@
 BF16 = jnp.bfloat16
 F32 = jnp.float32
 NT = (((1,), (1,)), ((), ()))
+TN = (((0,), (0,)), ((), ()))
 
 
 def layer_norm(values):
@@ -30,6 +31,10 @@
     return lax.dot_general(left, right, NT, preferred_element_type=F32)
 
 
+def dot_tn(left, right):
+    return lax.dot_general(left, right, TN, preferred_element_type=F32)
+
+
 def iota(shape, dim):
     return lax.broadcasted_iota(jnp.int32, shape, dim)
 
@@ -38,24 +43,28 @@
     return pl.BlockSpec(memory_space=pltpu.VMEM)
 
 
-def factor_kernel(x_ref, mask_ref, wl_ref, wr_ref, zl_ref, zr_ref, w_scr, yl_scr, yr_scr):
+def factor_kernel(x_ref, mask_ref, wl_ref, wr_ref, zl_ref, zr_ref, w_scr, live_scr, yl_scr, yr_scr):
     seqs, rows, channels = x_ref.shape
-    hidden = wl_ref.shape[1]
+    hidden = wl_ref.shape[0]
     rep = LANES // hidden
-    residues = mask_ref.shape[1]
-    start = lax.axis_index("dap") * rows
-
-    @pl.when(pl.program_id(0) == 0)
+    residues = mask_ref.shape[0]
+    width = rows * hidden
+    step = pl.program_id(0)
+
+    @pl.when(step == 0)
     def _():
-        wl, wr = wl_ref[...], wr_ref[...]
-        w_scr[:, :LANES] = jnp.concatenate([wl] * rep, axis=1)
-        w_scr[:, LANES : 2 * LANES] = jnp.concatenate([wr] * rep, axis=1)
-        w_scr[:, 2 * LANES :] = jnp.ones((channels, LANES), BF16)
+        for k in range(rep):
+            w_scr[k * hidden : (k + 1) * hidden, :] = wl_ref[...]
+            w_scr[LANES + k * hidden : LANES + (k + 1) * hidden, :] = wr_ref[...]
+        w_scr[2 * LANES :, :] = jnp.ones((LANES, channels), BF16)
+        start = lax.axis_index("dap") * rows
+        spread = iota((residues, width), 0) == start + iota((residues, width), 1) // hidden
+        live_scr[...] = dot_tn(mask_ref[...].astype(BF16), spread.astype(BF16))
 
     x = x_ref[...].reshape(seqs * rows, channels)
     w = w_scr[...]
-    sums = dot(jnp.ones((8, channels), BF16), w)[:1]
-    y = dot(x, w)
+    sums = dot_nt(jnp.ones((8, channels), BF16), w)[:1]
+    y = dot_nt(x, w)
     mean = y[:, 2 * LANES :] * (1.0 / channels)
     xf = x.astype(F32)
     square = jnp.zeros_like(mean)
@@ -66,23 +75,22 @@
     scale = lax.rsqrt(dot(square.astype(BF16), ones) * (1.0 / channels) + EPSILON)
     yl_scr[...] = (y[:, :LANES] - mean * sums[:, :LANES]) * scale
     yr_scr[...] = (y[:, LANES : 2 * LANES] - mean * sums[:, LANES : 2 * LANES]) * scale
-    width = rows * hidden
-    spread = (iota((residues, width), 0) == start + iota((residues, width), 1) // hidden).astype(BF16)
-    live = dot(mask_ref[...].astype(BF16), spread)
     block = iota((seqs, LANES), 1) // hidden
-    for scr, out in ((yr_scr, zr_ref), (yl_scr, zl_ref)):
-        for group in range(rows // rep):
+    here = pl.ds(pl.multiple_of(step * seqs, seqs), seqs)
+    for group in range(rows // rep):
+        lanes = slice(group * LANES, (group + 1) * LANES)
+        live = live_scr[here, lanes]
+        for scr, out in ((yr_scr, zr_ref), (yl_scr, zl_ref)):
             z = scr[pl.ds(group * rep, seqs, stride=rows), :]
             for k in range(1, rep):
                 z = jnp.where(block == k, scr[pl.ds(group * rep + k, seqs, stride=rows), :], z)
-            lanes = slice(group * LANES, (group + 1) * LANES)
-            out[:, lanes] = (z * live[:, lanes]).astype(BF16)
-
-
-def factors(alignment, alignment_mask, outer_left, outer_right):
+            out[:, lanes] = (z * live).astype(BF16)
+
+
+def factors(alignment, mask, outer_left, outer_right):
     seqs, rows, channels = alignment.shape
-    residues = alignment_mask.shape[1]
-    hidden = outer_left.shape[1]
+    residues = mask.shape[0]
+    hidden = outer_left.shape[0]
     step = seqs // 4
     width = rows * hidden
     out = jax.ShapeDtypeStruct((seqs, width), BF16)
@@ -92,21 +100,22 @@
         grid=(seqs // step,),
         in_specs=[
             pl.BlockSpec((step, rows, channels), lambda s: (s, 0, 0)),
-            pl.BlockSpec((step, residues), lambda s: (s, 0)),
-            pl.BlockSpec((channels, hidden), lambda s: (0, 0)),
-            pl.BlockSpec((channels, hidden), lambda s: (0, 0)),
+            pl.BlockSpec((residues, seqs), lambda s: (0, 0)),
+            pl.BlockSpec((hidden, channels), lambda s: (0, 0)),
+            pl.BlockSpec((hidden, channels), lambda s: (0, 0)),
         ],
         out_specs=[pl.BlockSpec((step, width), lambda s: (s, 0))] * 2,
         scratch_shapes=[
-            pltpu.VMEM((channels, 3 * LANES), BF16),
+            pltpu.VMEM((3 * LANES, channels), BF16),
+            pltpu.VMEM((seqs, width), F32),
             pltpu.VMEM((step * rows, LANES), F32),
             pltpu.VMEM((step * rows, LANES), F32),
         ],
-        compiler_params=pltpu.CompilerParams(vmem_limit_bytes=24 << 20),
+        compiler_params=pltpu.CompilerParams(vmem_limit_bytes=119 << 19),
         cost_estimate=pl.CostEstimate(
             flops=2 * seqs * rows * channels * 512, bytes_accessed=4 << 20, transcendentals=0
         ),
-    )(alignment, alignment_mask, outer_left, outer_right)
+    )(alignment, mask, outer_left, outer_right)
 
 
 def prepare_kernel(
@@ -115,7 +124,7 @@
 ):
     rows, cols, _ = pair_ref.shape
     pairs = rows * cols
-    residues = mask_ref.shape[1]
+    residues = mask_ref.shape[0]
     classes = table_ref.shape[0]
     row_start = lax.axis_index("dap") * rows
     col_start = lax.axis_index("sub") * cols
@@ -126,8 +135,8 @@
     pick_row = (place == row_start + which % rows).astype(BF16)
     pick_col = (place == col_start + which // rows).astype(BF16)
     mask = mask_ref[...].astype(BF16)
-    both = (dot_nt(pick_row, mask) * dot_nt(pick_col, mask)).astype(BF16)
-    counts = dot(both, jnp.ones((mask.shape[0], LANES), BF16))
+    both = (dot(pick_row, mask) * dot(pick_col, mask)).astype(BF16)
+    counts = dot(both, jnp.ones((mask.shape[1], LANES), BF16))
     inverse_ref[...] = 1.0 / jnp.maximum(counts, 1.0)
     live = jnp.broadcast_to(live_ref[...].astype(F32), (LANES, residues)).astype(BF16)
     chain = jnp.broadcast_to(chain_ref[...].astype(F32), (LANES, residues)).astype(BF16)
@@ -146,7 +155,7 @@
         base_ref[here, :] = relative[here] + pair_scr[pl.ds(col, rows, stride=cols), :]
 
 
-def prepare(zl, alignment_mask, pair_input, residue_mask, chain_index, table, proj):
+def prepare(zl, mask, pair_input, residue_mask, chain_index, table, proj):
     rows, cols, channels = pair_input.shape
     pairs = rows * cols
     shape = jax.ShapeDtypeStruct((pairs, channels), F32)
@@ -167,7 +176,7 @@
         cost_estimate=pl.CostEstimate(
             flops=2 * pairs * 256 * 1024, bytes_accessed=2 << 20, transcendentals=0
         ),
-    )(zl, alignment_mask, pair_input, residue_mask[None, :], chain_index[None, :], table, proj)
+    )(zl, mask, pair_input, residue_mask[None, :], chain_index[None, :], table, proj)
 
 
 def pair_kernel(ratio, hidden, zlt_ref, *refs):
@@ -335,12 +344,18 @@
     def owner(a, b, turn):
         return ratio * b + (a + turn) % ratio
 
-    zl, zr = factors(alignment, alignment_mask, outer_left, outer_right)
+    def spread(sub):
+        half = subs // 2
+        return (sub % half) * 2 + sub // half
+
+    mask = alignment_mask.T
+    zl, zr = factors(alignment, mask, outer_left.T, outer_right.T)
     zrs = [
-        fetch(zr, lambda a, b, turn=turn: (owner(a, b, turn), a // ratio)) for turn in range(ratio)
+        fetch(zr, lambda a, b, turn=turn: (owner(a, b, turn), spread(a // ratio)))
+        for turn in range(ratio)
     ]
     zlt, base, inverse, live, proj = prepare(
-        zl, alignment_mask, pair_input, residue_mask, chain_index, relative_table, outer_proj
+        zl, mask, pair_input, residue_mask, chain_index, relative_table, outer_proj
     )
     left, right, one = pair_update(
         outer_left.shape[1], zlt, zrs, base, inverse, live, proj, triangle_left, triangle_right

time: 44.5 us -> 39.9 us (0.90)
  the two profiles are of different devices: /device:TPU:16 before, /device:TPU:7 now
where the time goes in v2:
time: 39.9 us; the launch traced here: 39.6 us
  starting transfers between devices  16 us (40%)
  waiting for transfers between devices  12 us (30%)
  Pallas kernels  10.4 us (26%)
  local copies, waits for them, and re-layouts  0.99 us (2%)
    ppermute x8, starting transfers between devices, fetch(): return lax.ppermute(values, ('dap', 'sub'), perm)  16 us
    ppermute x8, waiting for transfers between devices, fetch(): return lax.ppermute(values, ('dap', 'sub'), perm)  12 us
    pallas_call x1, Pallas kernels, factors(): pl.pallas_call(factor_kernel, out_shape=(out, out), grid=(seqs // step,),...  6.1 us
    pallas_call x1, Pallas kernels, triangle_update(): pl.pallas_call(functools.partial(triangle_kernel, subs, ratio, cols), out...  2.23 us
    pallas_call x1, Pallas kernels, pair_update(): pl.pallas_call(functools.partial(pair_kernel, ratio, hidden), out_shape=(...  1.6 us
    unnamed x26, local copies, waits for them, and re-layouts  0.99 us
  transfers between devices with their start and end apart: 8, of which 3 were waited for; matrix products, arithmetic and copies ran while one was open for 0% of the time, Pallas kernels for 1%

profile of v2, /device:TPU:7, one launch (start us, length us, event | category | flops | bytes accessed | tf_op | source)
XLA Modules:
  0.0 39.6 jit_solution(858329758954608069)
XLA Ops:
  0.0 0.0 copy-start.4
  0.0 0.0 copy-start.10
  0.0 0.0 copy-start
  0.0 0.0 copy-start.12
  0.0 0.0 copy-start.11
  0.0 0.0 copy-start.5
  0.0 0.0 copy-start.6
  0.0 0.0 copy-start.7
  0.1 0.0 copy-start.2
  0.1 0.0 copy-start.3
  0.1 0.0 copy-start.8
  0.1 0.0 copy-start.9
  0.1 6.1 %shard_map.145 = (bf16[256,512]{1,0:T(8,128)(2,1)}, bf16[256,512]{1,0:T(8,128)(2,1)}) custom-call(bf16[256,16,256]{2,1,0:T(8,128)(2,1)} %x_ref.1, s32[64,256]{1,0:T(8,128)} %bitcast.5, bf16[32,256]{1,0:T(8,128)(2,1)} %bitcast.9, bf16[32,256]{1,0:T(8,128)(2,1)} %bitcast.10), custom_call_target="tpu_custom_call" | custom-call | flops 1073741824 | bytes 4194304 | tf_op jit(solution)/shard_map/pallas_call | solution.py:97
  6.2 5.8 %collective-permute-start = (bf16[256,512]{1,0:T(8,128)(2,1)}, bf16[256,512]{1,0:T(8,128)(2,1)S(1)}, u32[]{:S(2)}, u32[]{:S(2)}) collective-permute-start(bf16[256,512]{1,0:T(8,128)(2,1)} %get-tuple-element.17), channel_id=1, source_target_pairs={{0,0},{4,1},{8,2},{12,3},{2,4},{6,5},{10,6},{14,7},{1,8},{5,9},{9,... | collective-permute-start | bytes 786440 | tf_op jit(solution)/shard_map/ppermute | solution.py:342
  12.0 0.0 copy-done.4
  12.0 0.0 copy-done.10
  12.0 0.0 copy-done
  12.0 0.0 copy-done.12
  12.0 0.0 copy-done.11
  12.0 0.0 copy-done.5
  12.0 0.0 copy-start.1
  12.0 0.9 %copy-done.1 = bf16[256,512]{1,0:T(8,128)(2,1)S(1)} copy-done((bf16[256,512]{1,0:T(8,128)(2,1)S(1)}, bf16[256,512]{1,0:T(8,128)(2,1)}, u32[]{:S(2)}) %copy-start.1) | copy-done | bytes 262168
  13.0 0.5 %shard_map.146 = (bf16[512,256]{1,0:T(8,128)(2,1)S(1)}, f32[256,128]{1,0:T(8,128)S(1)}, f32[256,128]{1,0:T(8,128)S(1)}, f32[256,128]{1,0:T(8,128)S(1)}, bf16[1024,128]{1,0:T(8,128)(2,1)S(1)}) custom-call(bf16[256,512]{1,0:T(8,128)(2,1)S(1)} %copy-done.1, s32[64,256]{1,0:T(8,128)S(1)} %bitcast.6, bf16[16,16,128]{2,1,0:T(8,128)(2,1)S(1)} %copy-done.5, ...), custom_call_target="tpu_custom_call" | custom-call | flops 134217728 | bytes 2097152 | tf_op jit(solution)/shard_map/pallas_call | solution.py:163
  13.5 5.8 %collective-permute-done.refs_0_ = bf16[256,512]{1,0:T(8,128)(2,1)S(1)} collective-permute-done((bf16[256,512]{1,0:T(8,128)(2,1)}, bf16[256,512]{1,0:T(8,128)(2,1)S(1)}, u32[]{:S(2)}, u32[]{:S(2)}) %collective-permute-start) | collective-permute-done | bytes 262176 | tf_op jit(solution)/shard_map/ppermute | solution.py:342
  19.3 0.0 copy-done.6
  19.3 0.0 copy-done.7
  19.3 1.6 %shard_map.147 = (bf16[256,128]{1,0:T(8,128)(2,1)S(1)}, bf16[256,128]{1,0:T(8,128)(2,1)S(1)}, bf16[256,128]{1,0:T(8,128)(2,1)S(1)}) custom-call(bf16[512,256]{1,0:T(8,128)(2,1)S(1)} %get-tuple-element.16.zlt_ref, bf16[256,512]{1,0:T(8,128)(2,1)S(1)} %collective-permute-done.refs_0_, f32[256,128]{1,0:T(8,128)S(1)} %get-tuple-element.18.refs_1_, ...), custom_call_target="tpu_custom_call" | custom-call | flops 268435456 | bytes 2097152 | tf_op jit(solution)/shard_map/pallas_call | solution.py:238
  20.9 0.1 collective-permute-start.3
  21.0 2.1 %collective-permute-start.2 = (bf16[256,128]{1,0:T(8,128)(2,1)S(1)}, bf16[256,128]{1,0:T(8,128)(2,1)S(1)}, u32[]{:S(2)}, u32[]{:S(2)}) collective-permute-start(bf16[256,128]{1,0:T(8,128)(2,1)S(1)} %get-tuple-element.22.refs_0_), channel_id=1, source_target_pairs={{2,0},{3,1},{0,2},{1,3},{6,4},{7,5},{4,6},{5,7},{10,8},{11,9},{8,1... | collective-permute-start | bytes 196616 | tf_op jit(solution)/shard_map/ppermute | solution.py:342
  23.1 0.0 collective-permute-start.1
  23.1 1.7 %collective-permute-start.7 = (bf16[256,128]{1,0:T(8,128)(2,1)S(1)}, bf16[256,128]{1,0:T(8,128)(2,1)S(1)}, u32[]{:S(2)}, u32[]{:S(2)}) collective-permute-start(bf16[256,128]{1,0:T(8,128)(2,1)S(1)} %get-tuple-element.23), channel_id=1, source_target_pairs={{3,0},{7,1},{11,2},{15,3},{0,4},{4,5},{8,6},{12,7},{1,8},{5,9},{9,... | collective-permute-start | bytes 196616 | tf_op jit(solution)/shard_map/ppermute | solution.py:342
  24.8 0.0 collective-permute-start.6
  24.8 0.0 collective-permute-done.3.refs_3_
  24.8 4.3 %collective-permute-start.5 = (bf16[256,128]{1,0:T(8,128)(2,1)S(1)}, bf16[256,128]{1,0:T(8,128)(2,1)S(1)}, u32[]{:S(2)}, u32[]{:S(2)}) collective-permute-start(bf16[256,128]{1,0:T(8,128)(2,1)S(1)} %get-tuple-element.23), channel_id=1, source_target_pairs={{1,0},{5,1},{9,2},{13,3},{2,4},{6,5},{10,6},{14,7},{3,8},{7,9},{11... | collective-permute-start | bytes 196616 | tf_op jit(solution)/shard_map/ppermute | solution.py:342
  29.1 0.0 collective-permute-done.2.refs_2_
  29.1 2.1 %collective-permute-start.4 = (bf16[256,128]{1,0:T(8,128)(2,1)S(1)}, bf16[256,128]{1,0:T(8,128)(2,1)S(1)}, u32[]{:S(2)}, u32[]{:S(2)}) collective-permute-start(bf16[256,128]{1,0:T(8,128)(2,1)S(1)} %get-tuple-element.23), channel_id=1, source_target_pairs={{0,0},{4,1},{8,2},{12,3},{1,4},{5,5},{9,6},{13,7},{2,8},{6,9},{10,... | collective-permute-start | bytes 196616 | tf_op jit(solution)/shard_map/ppermute | solution.py:342
  31.2 0.0 collective-permute-done.1.refs_1_
  31.2 0.0 collective-permute-done.7.refs_7_
  31.2 0.0 collective-permute-done.6.refs_6_
  31.2 0.1 collective-permute-done.5.refs_5_
  31.3 6.1 %collective-permute-done.4.refs_4_ = bf16[256,128]{1,0:T(8,128)(2,1)S(1)} collective-permute-done((bf16[256,128]{1,0:T(8,128)(2,1)S(1)}, bf16[256,128]{1,0:T(8,128)(2,1)S(1)}, u32[]{:S(2)}, u32[]{:S(2)}) %collective-permute-start.4) | collective-permute-done | bytes 65568 | tf_op jit(solution)/shard_map/ppermute | solution.py:342
  37.4 0.0 copy-done.2
  37.4 0.0 copy-done.3
  37.4 0.0 copy-done.8
  37.4 0.0 copy-done.9
  37.4 2.2 %shard_map.148 = bf16[16,16,128]{2,1,0:T(8,128)(2,1)} custom-call(bf16[256,128]{1,0:T(8,128)(2,1)S(1)} %get-tuple-element.22.refs_0_, bf16[256,128]{1,0:T(8,128)(2,1)S(1)} %collective-permute-done.1.refs_1_, bf16[256,128]{1,0:T(8,128)(2,1)S(1)} %collective-permute-done.2.refs_2_, bf16[256,128]{1,0:T(8,128)(2,1)S(1)} %collective-permute-done.3.refs_3_, ...), custom_call_target="tpu_custom_call" | custom-call | flops 134217728 | bytes 2097152 | tf_op jit(solution)/shard_map/pallas_call | solution.py:298
Async XLA Ops:
  0.0 12.0 %copy-start.4 = (s32[256,64]{0,1:T(8,128)S(1)}, s32[256,64]{0,1:T(8,128)}, u32[]{:S(2)}) copy-start(s32[256,64]{0,1:T(8,128)} %param.16) | copy-start | bytes 196612
  0.0 12.0 %copy-start.10 = (bf16[66,128]{1,0:T(8,128)(2,1)S(1)}, bf16[66,128]{1,0:T(8,128)(2,1)}, u32[]{:S(2)}) copy-start(bf16[66,128]{1,0:T(8,128)(2,1)} %table_ref.1) | copy-start | bytes 50692
  0.0 12.0 %copy-start = (f32[32,32,128]{2,1,0:T(8,128)S(1)}, f32[32,32,128]{2,1,0:T(8,128)}, u32[]{:S(2)}) copy-start(f32[32,32,128]{2,1,0:T(8,128)} %proj_ref.1) | copy-start | bytes 1572868
  0.0 12.0 %copy-start.12 = (s32[64]{0:T(128)S(1)}, s32[64]{0:T(128)}, u32[]{:S(2)}) copy-start(s32[64]{0:T(128)} %param.19) | copy-start | bytes 772
  0.0 12.0 %copy-start.11 = (s32[64]{0:T(128)S(1)}, s32[64]{0:T(128)}, u32[]{:S(2)}) copy-start(s32[64]{0:T(128)} %param.18) | copy-start | bytes 772
  0.0 12.0 %copy-start.5 = (bf16[16,16,128]{2,1,0:T(8,128)(2,1)S(1)}, bf16[16,16,128]{2,1,0:T(8,128)(2,1)}, u32[]{:S(2)}) copy-start(bf16[16,16,128]{2,1,0:T(8,128)(2,1)} %pair_ref.1) | copy-start | bytes 196612
  0.0 19.3 %copy-start.6 = (bf16[128,256]{1,0:T(8,128)(2,1)S(1)}, bf16[128,256]{1,0:T(8,128)(2,1)}, u32[]{:S(2)}) copy-start(bf16[128,256]{1,0:T(8,128)(2,1)} %refs_5_.1) | copy-start | bytes 196612
  0.0 19.3 %copy-start.7 = (bf16[128,256]{1,0:T(8,128)(2,1)S(1)}, bf16[128,256]{1,0:T(8,128)(2,1)}, u32[]{:S(2)}) copy-start(bf16[128,256]{1,0:T(8,128)(2,1)} %refs_6_.1) | copy-start | bytes 196612
  0.1 37.3 %copy-start.2 = (bf16[128,512]{1,0:T(8,128)(2,1)S(1)}, bf16[128,512]{1,0:T(8,128)(2,1)}, u32[]{:S(2)}) copy-start(bf16[128,512]{1,0:T(8,128)(2,1)} %refs_11_.1) | copy-start | bytes 393220
  0.1 37.3 %copy-start.3 = (bf16[512,128]{1,0:T(8,128)(2,1)S(1)}, bf16[512,128]{1,0:T(8,128)(2,1)}, u32[]{:S(2)}) copy-start(bf16[512,128]{1,0:T(8,128)(2,1)} %refs_12_.1) | copy-start | bytes 393220
  0.1 37.3 %copy-start.8 = (bf16[128,128]{1,0:T(8,128)(2,1)S(1)}, bf16[128,128]{1,0:T(8,128)(2,1)}, u32[]{:S(2)}) copy-start(bf16[128,128]{1,0:T(8,128)(2,1)} %refs_9_.1) | copy-start | bytes 98308
  0.1 37.3 %copy-start.9 = (bf16[128,128]{1,0:T(8,128)(2,1)S(1)}, bf16[128,128]{1,0:T(8,128)(2,1)}, u32[]{:S(2)}) copy-start(bf16[128,128]{1,0:T(8,128)(2,1)} %refs_10_.1) | copy-start | bytes 98308
  6.2 13.1 %collective-permute-start = (bf16[256,512]{1,0:T(8,128)(2,1)}, bf16[256,512]{1,0:T(8,128)(2,1)S(1)}, u32[]{:S(2)}, u32[]{:S(2)}) collective-permute-start(bf16[256,512]{1,0:T(8,128)(2,1)} %get-tuple-element.17), channel_id=1, source_target_pairs={{0,0},{4,1},{8,2},{12,3},{2,4},{6,5},{10,6},{14,7},{1,8},{5,9},{9,... | collective-permute-start | bytes 786440 | tf_op jit(solution)/shard_map/ppermute | solution.py:342
  12.0 1.0 %copy-start.1 = (bf16[256,512]{1,0:T(8,128)(2,1)S(1)}, bf16[256,512]{1,0:T(8,128)(2,1)}, u32[]{:S(2)}) copy-start(bf16[256,512]{1,0:T(8,128)(2,1)} %get-tuple-element.15.zl_ref) | copy-start | bytes 786436
  20.9 3.9 %collective-permute-start.3 = (bf16[256,128]{1,0:T(8,128)(2,1)S(1)}, bf16[256,128]{1,0:T(8,128)(2,1)S(1)}, u32[]{:S(2)}, u32[]{:S(2)}) collective-permute-start(bf16[256,128]{1,0:T(8,128)(2,1)S(1)} %get-tuple-element.22.refs_0_), channel_id=1, source_target_pairs={{3,0},{0,1},{1,2},{2,3},{7,4},{4,5},{5,6},{6,7},{11,8},{8,9},{9,10... | collective-permute-start | bytes 196616 | tf_op jit(solution)/shard_map/ppermute | solution.py:342
  21.0 8.1 %collective-permute-start.2 = (bf16[256,128]{1,0:T(8,128)(2,1)S(1)}, bf16[256,128]{1,0:T(8,128)(2,1)S(1)}, u32[]{:S(2)}, u32[]{:S(2)}) collective-permute-start(bf16[256,128]{1,0:T(8,128)(2,1)S(1)} %get-tuple-element.22.refs_0_), channel_id=1, source_target_pairs={{2,0},{3,1},{0,2},{1,3},{6,4},{7,5},{4,6},{5,7},{10,8},{11,9},{8,1... | collective-permute-start | bytes 196616 | tf_op jit(solution)/shard_map/ppermute | solution.py:342
  23.1 8.1 %collective-permute-start.1 = (bf16[256,128]{1,0:T(8,128)(2,1)S(1)}, bf16[256,128]{1,0:T(8,128)(2,1)S(1)}, u32[]{:S(2)}, u32[]{:S(2)}) collective-permute-start(bf16[256,128]{1,0:T(8,128)(2,1)S(1)} %get-tuple-element.22.refs_0_), channel_id=1, source_target_pairs={{1,0},{2,1},{3,2},{0,3},{5,4},{6,5},{7,6},{4,7},{9,8},{10,9},{11,1... | collective-permute-start | bytes 196616 | tf_op jit(solution)/shard_map/ppermute | solution.py:342
  23.1 8.1 %collective-permute-start.7 = (bf16[256,128]{1,0:T(8,128)(2,1)S(1)}, bf16[256,128]{1,0:T(8,128)(2,1)S(1)}, u32[]{:S(2)}, u32[]{:S(2)}) collective-permute-start(bf16[256,128]{1,0:T(8,128)(2,1)S(1)} %get-tuple-element.23), channel_id=1, source_target_pairs={{3,0},{7,1},{11,2},{15,3},{0,4},{4,5},{8,6},{12,7},{1,8},{5,9},{9,... | collective-permute-start | bytes 196616 | tf_op jit(solution)/shard_map/ppermute | solution.py:342
  24.8 6.4 %collective-permute-start.6 = (bf16[256,128]{1,0:T(8,128)(2,1)S(1)}, bf16[256,128]{1,0:T(8,128)(2,1)S(1)}, u32[]{:S(2)}, u32[]{:S(2)}) collective-permute-start(bf16[256,128]{1,0:T(8,128)(2,1)S(1)} %get-tuple-element.23), channel_id=1, source_target_pairs={{2,0},{6,1},{10,2},{14,3},{3,4},{7,5},{11,6},{15,7},{0,8},{4,9},{8... | collective-permute-start | bytes 196616 | tf_op jit(solution)/shard_map/ppermute | solution.py:342
  24.8 6.4 %collective-permute-start.5 = (bf16[256,128]{1,0:T(8,128)(2,1)S(1)}, bf16[256,128]{1,0:T(8,128)(2,1)S(1)}, u32[]{:S(2)}, u32[]{:S(2)}) collective-permute-start(bf16[256,128]{1,0:T(8,128)(2,1)S(1)} %get-tuple-element.23), channel_id=1, source_target_pairs={{1,0},{5,1},{9,2},{13,3},{2,4},{6,5},{10,6},{14,7},{3,8},{7,9},{11... | collective-permute-start | bytes 196616 | tf_op jit(solution)/shard_map/ppermute | solution.py:342
  29.1 8.3 %collective-permute-start.4 = (bf16[256,128]{1,0:T(8,128)(2,1)S(1)}, bf16[256,128]{1,0:T(8,128)(2,1)S(1)}, u32[]{:S(2)}, u32[]{:S(2)}) collective-permute-start(bf16[256,128]{1,0:T(8,128)(2,1)S(1)} %get-tuple-element.23), channel_id=1, source_target_pairs={{0,0},{4,1},{8,2},{12,3},{1,4},{5,5},{9,6},{13,7},{2,8},{6,9},{10,... | collective-permute-start | bytes 196616 | tf_op jit(solution)/shard_map/ppermute | solution.py:342

commit v3 on v2

--- a/solution.py
+++ b/solution.py
@@ -9,6 +9,7 @@
 
 REL_CLIP = 32
 LANES = 128
+PIECE = 16
 EPSILON = 1e-05
 BF16 = jnp.bfloat16
 F32 = jnp.float32
@@ -43,10 +44,11 @@
     return pl.BlockSpec(memory_space=pltpu.VMEM)
 
 
-def factor_kernel(x_ref, mask_ref, wl_ref, wr_ref, zl_ref, zr_ref, w_scr, live_scr, yl_scr, yr_scr):
+def factor_kernel(x_ref, mask_ref, wl_ref, wr_ref, zl_ref, zr_ref, w_scr, live_scr, gather_scr):
     seqs, rows, channels = x_ref.shape
     hidden = wl_ref.shape[0]
     rep = LANES // hidden
+    groups = rows // rep
     residues = mask_ref.shape[0]
     width = rows * hidden
     step = pl.program_id(0)
@@ -60,31 +62,37 @@
         start = lax.axis_index("dap") * rows
         spread = iota((residues, width), 0) == start + iota((residues, width), 1) // hidden
         live_scr[...] = dot_tn(mask_ref[...].astype(BF16), spread.astype(BF16))
-
-    x = x_ref[...].reshape(seqs * rows, channels)
+        to, at = iota(gather_scr.shape, 0), iota(gather_scr.shape, 1)
+        same = (to % PIECE == at // rows) & (to // PIECE == (at % rows) // rep)
+        gather_scr[...] = same.astype(BF16)
+
     w = w_scr[...]
     sums = dot_nt(jnp.ones((8, channels), BF16), w)[:1]
-    y = dot_nt(x, w)
-    mean = y[:, 2 * LANES :] * (1.0 / channels)
-    xf = x.astype(F32)
-    square = jnp.zeros_like(mean)
-    for part in range(channels // LANES):
-        centered = xf[:, part * LANES : (part + 1) * LANES] - mean
-        square = square + centered * centered
     ones = jnp.ones((LANES, LANES), BF16)
-    scale = lax.rsqrt(dot(square.astype(BF16), ones) * (1.0 / channels) + EPSILON)
-    yl_scr[...] = (y[:, :LANES] - mean * sums[:, :LANES]) * scale
-    yr_scr[...] = (y[:, LANES : 2 * LANES] - mean * sums[:, LANES : 2 * LANES]) * scale
-    block = iota((seqs, LANES), 1) // hidden
-    here = pl.ds(pl.multiple_of(step * seqs, seqs), seqs)
-    for group in range(rows // rep):
-        lanes = slice(group * LANES, (group + 1) * LANES)
-        live = live_scr[here, lanes]
-        for scr, out in ((yr_scr, zr_ref), (yl_scr, zl_ref)):
-            z = scr[pl.ds(group * rep, seqs, stride=rows), :]
-            for k in range(1, rep):
-                z = jnp.where(block == k, scr[pl.ds(group * rep + k, seqs, stride=rows), :], z)
-            out[:, lanes] = (z * live).astype(BF16)
+    piece_rows = PIECE * rows
+    own = iota((piece_rows, LANES), 1) // hidden == iota((piece_rows, LANES), 0) % rep
+    own = own.astype(F32)
+    for piece in range(seqs // PIECE):
+        x = x_ref[piece * PIECE : (piece + 1) * PIECE].reshape(piece_rows, channels)
+        y = dot_nt(x, w)
+        mean = y[:, 2 * LANES :] * (1.0 / channels)
+        xf = x.astype(F32)
+        square = jnp.zeros_like(mean)
+        for part in range(channels // LANES):
+            centered = xf[:, part * LANES : (part + 1) * LANES] - mean
+            square = square + centered * centered
+        scale = lax.rsqrt(dot(square.astype(BF16), ones) * (1.0 / channels) + EPSILON) * own
+        left = ((y[:, :LANES] - mean * sums[:, :LANES]) * scale).astype(BF16)
+        right = ((y[:, LANES : 2 * LANES] - mean * sums[:, LANES : 2 * LANES]) * scale).astype(BF16)
+        z = dot(gather_scr[...], jnp.concatenate([left, right], axis=1))
+        here = slice(piece * PIECE, (piece + 1) * PIECE)
+        whole = pl.ds(pl.multiple_of(step * seqs + piece * PIECE, PIECE), PIECE)
+        for group in range(groups):
+            lanes = slice(group * LANES, (group + 1) * LANES)
+            both = z[group * PIECE : (group + 1) * PIECE]
+            live = live_scr[whole, lanes]
+            zl_ref[here, lanes] = (both[:, :LANES] * live).astype(BF16)
+            zr_ref[here, lanes] = (both[:, LANES:] * live).astype(BF16)
 
 
 def factors(alignment, mask, outer_left, outer_right):
@@ -108,8 +116,7 @@
         scratch_shapes=[
             pltpu.VMEM((3 * LANES, channels), BF16),
             pltpu.VMEM((seqs, width), F32),
-            pltpu.VMEM((step * rows, LANES), F32),
-            pltpu.VMEM((step * rows, LANES), F32),
+            pltpu.VMEM((rows * hidden // LANES * PIECE, PIECE * rows), BF16),
         ],
         compiler_params=pltpu.CompilerParams(vmem_limit_bytes=119 << 19),
         cost_estimate=pl.CostEstimate(
@@ -182,7 +189,7 @@
 def pair_kernel(ratio, hidden, zlt_ref, *refs):
     zr_refs, refs = refs[:ratio], refs[ratio:]
     (base_ref, inverse_ref, live_ref, proj_ref, tl_ref, tr_ref,
-     left_ref, right_ref, one_ref, outer_scr, flat_scr, one_scr) = refs
+     both_ref, one_ref, outer_scr, flat_scr, one_scr) = refs
     pairs, channels = base_ref.shape
     rows = zlt_ref.shape[0] // hidden
     rep = LANES // hidden
@@ -223,9 +230,10 @@
     one = (base_ref[...] + outer_mean).astype(BF16).astype(F32)
     one_scr[...] = one
     norm = layer_norm(one).astype(BF16)
-    for weight, out in ((tl_ref, left_ref), (tr_ref, right_ref)):
+    for side, weight in enumerate((tl_ref, tr_ref)):
         both = dot(norm, weight[...])
-        out[...] = (jax.nn.sigmoid(both[:, :channels]) * both[:, channels:] * live_ref[...]).astype(BF16)
+        factor = jax.nn.sigmoid(both[:, :channels]) * both[:, channels:] * live_ref[...]
+        both_ref[side] = factor.astype(BF16)
     cols = pairs // rows
     for row in range(rows):
         one_ref[row * cols : (row + 1) * cols, :] = one_scr[pl.ds(row, cols, stride=rows), :].astype(BF16)
@@ -237,9 +245,9 @@
     shape = jax.ShapeDtypeStruct((pairs, channels), BF16)
     return pl.pallas_call(
         functools.partial(pair_kernel, ratio, hidden),
-        out_shape=(shape, shape, shape),
+        out_shape=(jax.ShapeDtypeStruct((2, pairs, channels), BF16), shape),
         in_specs=[vmem()] * (7 + ratio),
-        out_specs=[vmem()] * 3,
+        out_specs=[vmem()] * 2,
         scratch_shapes=[
             pltpu.VMEM((zrs[0].shape[1] // LANES, zlt.shape[0], LANES), F32),
             pltpu.VMEM((pairs, proj.shape[0]), BF16),
@@ -252,20 +260,28 @@
     )(zlt, *zrs, base, inverse, live, proj, triangle_left, triangle_right)
 
 
+def other(sub):
+    return sub + 1 - 2 * (sub % 2)
+
+
 def triangle_kernel(subs, ratio, cols, *refs):
-    lefts, refs = refs[:subs], refs[subs:]
-    rights, refs = refs[: subs * ratio], refs[subs * ratio :]
+    twos = subs // 2
+    lefts, refs = refs[:twos], refs[twos:]
+    rights, refs = refs[: twos * ratio], refs[twos * ratio :]
     (one_ref, gate_ref, out_ref, up_ref, down_ref, result_ref, left_scr, right_scr, sum_scr) = refs
     pairs, channels = one_ref.shape
     rows = pairs // cols
     here, there = lax.axis_index("dap"), lax.axis_index("sub")
-    for step in range(subs):
-        left_scr[lax.rem(there + step, subs)] = lefts[step][...].astype(F32)
+    for step in range(twos):
+        sub = lax.rem(there + 2 * step, subs)
+        left_scr[sub] = lefts[step][0].astype(F32)
+        left_scr[other(sub)] = lefts[step][1].astype(F32)
     for turn in range(ratio):
         block = lax.rem(here + turn, ratio)
-        for step in range(subs):
-            slot = block * subs + lax.rem(here // ratio + step, subs)
-            right_scr[slot] = rights[turn * subs + step][...].astype(F32)
+        for step in range(twos):
+            sub = lax.rem(here // ratio + 2 * step, subs)
+            right_scr[block * subs + sub] = rights[turn * twos + step][0].astype(F32)
+            right_scr[block * subs + other(sub)] = rights[turn * twos + step][1].astype(F32)
     for block in range(ratio):
         totals = tuple(jnp.zeros((rows, channels), F32) for _ in range(rows))
         for sub in range(subs):
@@ -293,12 +309,12 @@
 def triangle_update(lefts, rights, one, cols, gate, out, up, down):
     pairs, channels = one.shape
     rows = pairs // cols
-    subs = len(lefts)
-    ratio = len(rights) // subs
+    subs = 2 * len(lefts)
+    ratio = len(rights) // len(lefts)
     return pl.pallas_call(
         functools.partial(triangle_kernel, subs, ratio, cols),
         out_shape=jax.ShapeDtypeStruct((rows, cols, channels), BF16),
-        in_specs=[vmem()] * (subs + subs * ratio + 5),
+        in_specs=[vmem()] * (len(lefts) + len(rights) + 5),
         out_specs=vmem(),
         scratch_shapes=[
             pltpu.VMEM((subs, pairs, channels), F32),
@@ -344,29 +360,33 @@
     def owner(a, b, turn):
         return ratio * b + (a + turn) % ratio
 
-    def spread(sub):
-        half = subs // 2
-        return (sub % half) * 2 + sub // half
+    def sender(a, b):
+        if (daps, subs) == (4, 4):
+            return ((0, 2, 1, 3), (2, 1, 3, 0), (3, 1, 2, 0), (1, 2, 0, 3))[b][a]
+        return a // ratio
 
     mask = alignment_mask.T
     zl, zr = factors(alignment, mask, outer_left.T, outer_right.T)
     zrs = [
-        fetch(zr, lambda a, b, turn=turn: (owner(a, b, turn), spread(a // ratio)))
+        fetch(zr, lambda a, b, turn=turn: (owner(a, b, turn), sender(a, b)))
         for turn in range(ratio)
     ]
     zlt, base, inverse, live, proj = prepare(
         zl, mask, pair_input, residue_mask, chain_index, relative_table, outer_proj
     )
-    left, right, one = pair_update(
+    own, one = pair_update(
         outer_left.shape[1], zlt, zrs, base, inverse, live, proj, triangle_left, triangle_right
     )
+    near = fetch(own, lambda a, b: (a, other(b)))
+    left = jnp.stack([own[0], near[0]])
+    right = jnp.stack([own[1], near[1]])
     rights = [
-        fetch(right, lambda a, b, t=turn, m=step: (owner(a, b, t), (a // ratio + m) % subs))
+        fetch(right, lambda a, b, t=turn, m=step: (owner(a, b, t), (a // ratio + 2 * m) % subs))
         for turn in range(ratio)
-        for step in range(subs)
+        for step in range(subs // 2)
     ]
     lefts = [left] + [
-        fetch(left, lambda a, b, m=step: (a, (b + m) % subs)) for step in range(1, subs)
+        fetch(left, lambda a, b, m=step: (a, (b + 2 * m) % subs)) for step in range(1, subs // 2)
     ]
     return triangle_update(
         lefts, rights, one, cols, triangle_gate, triangle_out, transition_up, transition_down

time: 39.9 us -> 41.6 us (1.043)
  the two profiles are of different devices: /device:TPU:7 before, /device:TPU:1 now
where the time goes in v3:
time: 41.6 us; the launch traced here: 41.4 us
  starting transfers between devices  14.9 us (36%)
  Pallas kernels  13 us (31%)
  waiting for transfers between devices  12.3 us (30%)
  local copies, waits for them, and re-layouts  1.01 us (2%)
    ppermute x5, starting transfers between devices, fetch(): return lax.ppermute(values, ('dap', 'sub'), perm)  14.9 us
    ppermute x5, waiting for transfers between devices, fetch(): return lax.ppermute(values, ('dap', 'sub'), perm)  12.3 us
    pallas_call x1, Pallas kernels, factors(): pl.pallas_call(factor_kernel, out_shape=(out, out), grid=(seqs // step,),...  8.64 us
    pallas_call x1, Pallas kernels, triangle_update(): pl.pallas_call(functools.partial(triangle_kernel, subs, ratio, cols), out...  2.23 us
    pallas_call x1, Pallas kernels, pair_update(): pl.pallas_call(functools.partial(pair_kernel, ratio, hidden), out_shape=(...  1.6 us
    unnamed x26, local copies, waits for them, and re-layouts  0.99 us
  transfers between devices with their start and end apart: 5, of which 3 were waited for; matrix products, arithmetic and copies ran while one was open for 0% of the time, Pallas kernels for 1%

profile of v3, /device:TPU:1, one launch (start us, length us, event | category | flops | bytes accessed | tf_op | source)
XLA Modules:
  0.0 41.4 jit_solution(9599967134037453947)
XLA Ops:
  0.0 0.0 copy-start.4
  0.0 0.0 copy-start.10
  0.0 0.0 copy-start
  0.0 0.0 copy-start.12
  0.0 0.0 copy-start.11
  0.0 0.0 copy-start.5
  0.0 0.0 copy-start.6
  0.0 0.0 copy-start.7
  0.1 0.0 copy-start.2
  0.1 0.0 copy-start.3
  0.1 0.0 copy-start.8
  0.1 0.0 copy-start.9
  0.1 8.6 %shard_map.145 = (bf16[256,512]{1,0:T(8,128)(2,1)}, bf16[256,512]{1,0:T(8,128)(2,1)}) custom-call(bf16[256,16,256]{2,1,0:T(8,128)(2,1)} %x_ref.1, s32[64,256]{1,0:T(8,128)} %bitcast.5, bf16[32,256]{1,0:T(8,128)(2,1)} %bitcast.9, bf16[32,256]{1,0:T(8,128)(2,1)} %bitcast.10), custom_call_target="tpu_custom_call" | custom-call | flops 1073741824 | bytes 4194304 | tf_op jit(solution)/shard_map/pallas_call | solution.py:105
  8.7 5.6 %collective-permute-start = (bf16[256,512]{1,0:T(8,128)(2,1)}, bf16[256,512]{1,0:T(8,128)(2,1)S(1)}, u32[]{:S(2)}, u32[]{:S(2)}) collective-permute-start(bf16[256,512]{1,0:T(8,128)(2,1)} %get-tuple-element.16), channel_id=1, source_target_pairs={{0,0},{6,1},{11,2},{13,3},{2,4},{5,5},{9,6},{14,7},{1,8},{7,9},{10... | collective-permute-start | bytes 786440 | tf_op jit(solution)/shard_map/ppermute | solution.py:358
  14.3 0.0 copy-done.4
  14.4 0.0 copy-done.10
  14.4 0.0 copy-done
  14.4 0.0 copy-done.12
  14.4 0.0 copy-done.11
  14.4 0.0 copy-done.5
  14.4 0.0 copy-start.1
  14.4 0.9 %copy-done.1 = bf16[256,512]{1,0:T(8,128)(2,1)S(1)} copy-done((bf16[256,512]{1,0:T(8,128)(2,1)S(1)}, bf16[256,512]{1,0:T(8,128)(2,1)}, u32[]{:S(2)}) %copy-start.1) | copy-done | bytes 262168
  15.4 0.5 %shard_map.146 = (bf16[512,256]{1,0:T(8,128)(2,1)S(1)}, f32[256,128]{1,0:T(8,128)S(1)}, f32[256,128]{1,0:T(8,128)S(1)}, f32[256,128]{1,0:T(8,128)S(1)}, bf16[1024,128]{1,0:T(8,128)(2,1)S(1)}) custom-call(bf16[256,512]{1,0:T(8,128)(2,1)S(1)} %copy-done.1, s32[64,256]{1,0:T(8,128)S(1)} %bitcast.6, bf16[16,16,128]{2,1,0:T(8,128)(2,1)S(1)} %copy-done.5, ...), custom_call_target="tpu_custom_call" | custom-call | flops 134217728 | bytes 2097152 | tf_op jit(solution)/shard_map/pallas_call | solution.py:170
  15.9 4.0 %collective-permute-done.refs_0_ = bf16[256,512]{1,0:T(8,128)(2,1)S(1)} collective-permute-done((bf16[256,512]{1,0:T(8,128)(2,1)}, bf16[256,512]{1,0:T(8,128)(2,1)S(1)}, u32[]{:S(2)}, u32[]{:S(2)}) %collective-permute-start) | collective-permute-done | bytes 262176 | tf_op jit(solution)/shard_map/ppermute | solution.py:358
  19.8 0.0 copy-done.6
  19.8 0.0 copy-done.7
  19.8 1.6 %shard_map.147 = (bf16[2,256,128]{2,1,0:T(8,128)(2,1)S(1)}, bf16[256,128]{1,0:T(8,128)(2,1)S(1)}) custom-call(bf16[512,256]{1,0:T(8,128)(2,1)S(1)} %get-tuple-element.15.zlt_ref, bf16[256,512]{1,0:T(8,128)(2,1)S(1)} %collective-permute-done.refs_0_, f32[256,128]{1,0:T(8,128)S(1)} %get-tuple-element.17.refs_1_, f32[256,128]{1,0:T(8,128)S(1)} %get-tuple-element.18.refs_2_, ...), custom_call_target="tpu_custom_call" | custom-call | flops 268435456 | bytes 2097152 | tf_op jit(solution)/shard_map/pallas_call | solution.py:246
  21.5 0.1 collective-permute-start.1
  21.6 1.3 %collective-permute-done.1 = bf16[2,256,128]{2,1,0:T(8,128)(2,1)S(1)} collective-permute-done((bf16[2,256,128]{2,1,0:T(8,128)(2,1)S(1)}, bf16[2,256,128]{2,1,0:T(8,128)(2,1)S(1)}, u32[]{:S(2)}, u32[]{:S(2)}) %collective-permute-start.1) | collective-permute-done | bytes 131104 | tf_op jit(solution)/shard_map/ppermute | solution.py:358
  22.9 3.1 %collective-permute-start.2 = (bf16[2,256,128]{2,1,0:T(8,128)(2,1)S(1)}, bf16[2,256,128]{2,1,0:T(8,128)(2,1)S(1)}, u32[]{:S(2)}, u32[]{:S(2)}) collective-permute-start(bf16[2,256,128]{2,1,0:T(8,128)(2,1)S(1)} %pad_maximum_fusion.refs_0_), channel_id=1, source_target_pairs={{2,0},{3,1},{0,2},{1,3},{6,4},{7,5},{4,6},{5,7},{10,8},{11,9},{8,1... | collective-permute-start | bytes 393224 | tf_op jit(solution)/shard_map/ppermute | solution.py:358
  26.0 4.3 %collective-permute-start.4 = (bf16[2,256,128]{2,1,0:T(8,128)(2,1)S(1)}, bf16[2,256,128]{2,1,0:T(8,128)(2,1)S(1)}, u32[]{:S(2)}, u32[]{:S(2)}) collective-permute-start(bf16[2,256,128]{2,1,0:T(8,128)(2,1)S(1)} %pad_maximum_fusion.1), channel_id=1, source_target_pairs={{2,0},{6,1},{10,2},{14,3},{3,4},{7,5},{11,6},{15,7},{0,8},{4,9},{8... | collective-permute-start | bytes 393224 | tf_op jit(solution)/shard_map/ppermute | solution.py:358
  30.3 1.9 %collective-permute-start.3 = (bf16[2,256,128]{2,1,0:T(8,128)(2,1)S(1)}, bf16[2,256,128]{2,1,0:T(8,128)(2,1)S(1)}, u32[]{:S(2)}, u32[]{:S(2)}) collective-permute-start(bf16[2,256,128]{2,1,0:T(8,128)(2,1)S(1)} %pad_maximum_fusion.1), channel_id=1, source_target_pairs={{0,0},{4,1},{8,2},{12,3},{1,4},{5,5},{9,6},{13,7},{2,8},{6,9},{10,... | collective-permute-start | bytes 393224 | tf_op jit(solution)/shard_map/ppermute | solution.py:358
  32.2 0.0 collective-permute-done.2.refs_1_
  32.2 0.0 collective-permute-done.4.refs_3_
  32.2 6.9 %collective-permute-done.3.refs_2_ = bf16[2,256,128]{2,1,0:T(8,128)(2,1)S(1)} collective-permute-done((bf16[2,256,128]{2,1,0:T(8,128)(2,1)S(1)}, bf16[2,256,128]{2,1,0:T(8,128)(2,1)S(1)}, u32[]{:S(2)}, u32[]{:S(2)}) %collective-permute-start.3) | collective-permute-done | bytes 131104 | tf_op jit(solution)/shard_map/ppermute | solution.py:358
  39.2 0.0 copy-done.2
  39.2 0.0 copy-done.3
  39.2 0.0 copy-done.8
  39.2 0.0 copy-done.9
  39.2 2.2 %shard_map.148 = bf16[16,16,128]{2,1,0:T(8,128)(2,1)} custom-call(bf16[2,256,128]{2,1,0:T(8,128)(2,1)S(1)} %pad_maximum_fusion.refs_0_, bf16[2,256,128]{2,1,0:T(8,128)(2,1)S(1)} %collective-permute-done.2.refs_1_, bf16[2,256,128]{2,1,0:T(8,128)(2,1)S(1)} %collective-permute-done.3.refs_2_, bf16[2,256,128]{2,1,0:T(8,128)(2,1)S(1)} %collective-permute-done.4.refs_3_, ...), custom_call_target="tpu_custom_call" | custom-call | flops 134217728 | bytes 2097152 | tf_op jit(solution)/shard_map/pallas_call | solution.py:314
  (4 shorter events, 0.1 us)
Async XLA Ops:
  0.0 14.3 %copy-start.4 = (s32[256,64]{0,1:T(8,128)S(1)}, s32[256,64]{0,1:T(8,128)}, u32[]{:S(2)}) copy-start(s32[256,64]{0,1:T(8,128)} %param.16) | copy-start | bytes 196612
  0.0 14.4 %copy-start.10 = (bf16[66,128]{1,0:T(8,128)(2,1)S(1)}, bf16[66,128]{1,0:T(8,128)(2,1)}, u32[]{:S(2)}) copy-start(bf16[66,128]{1,0:T(8,128)(2,1)} %table_ref.1) | copy-start | bytes 50692
  0.0 14.4 %copy-start = (f32[32,32,128]{2,1,0:T(8,128)S(1)}, f32[32,32,128]{2,1,0:T(8,128)}, u32[]{:S(2)}) copy-start(f32[32,32,128]{2,1,0:T(8,128)} %proj_ref.1) | copy-start | bytes 1572868
  0.0 14.4 %copy-start.12 = (s32[64]{0:T(128)S(1)}, s32[64]{0:T(128)}, u32[]{:S(2)}) copy-start(s32[64]{0:T(128)} %param.19) | copy-start | bytes 772
  0.0 14.4 %copy-start.11 = (s32[64]{0:T(128)S(1)}, s32[64]{0:T(128)}, u32[]{:S(2)}) copy-start(s32[64]{0:T(128)} %param.18) | copy-start | bytes 772
  0.0 14.4 %copy-start.5 = (bf16[16,16,128]{2,1,0:T(8,128)(2,1)S(1)}, bf16[16,16,128]{2,1,0:T(8,128)(2,1)}, u32[]{:S(2)}) copy-start(bf16[16,16,128]{2,1,0:T(8,128)(2,1)} %pair_ref.1) | copy-start | bytes 196612
  0.0 19.8 %copy-start.6 = (bf16[128,256]{1,0:T(8,128)(2,1)S(1)}, bf16[128,256]{1,0:T(8,128)(2,1)}, u32[]{:S(2)}) copy-start(bf16[128,256]{1,0:T(8,128)(2,1)} %refs_5_.2) | copy-start | bytes 196612
  0.0 19.8 %copy-start.7 = (bf16[128,256]{1,0:T(8,128)(2,1)S(1)}, bf16[128,256]{1,0:T(8,128)(2,1)}, u32[]{:S(2)}) copy-start(bf16[128,256]{1,0:T(8,128)(2,1)} %refs_6_.2) | copy-start | bytes 196612
  0.1 39.1 %copy-start.2 = (bf16[128,512]{1,0:T(8,128)(2,1)S(1)}, bf16[128,512]{1,0:T(8,128)(2,1)}, u32[]{:S(2)}) copy-start(bf16[128,512]{1,0:T(8,128)(2,1)} %refs_7_.1) | copy-start | bytes 393220
  0.1 39.1 %copy-start.3 = (bf16[512,128]{1,0:T(8,128)(2,1)S(1)}, bf16[512,128]{1,0:T(8,128)(2,1)}, u32[]{:S(2)}) copy-start(bf16[512,128]{1,0:T(8,128)(2,1)} %refs_8_.1) | copy-start | bytes 393220
  0.1 39.1 %copy-start.8 = (bf16[128,128]{1,0:T(8,128)(2,1)S(1)}, bf16[128,128]{1,0:T(8,128)(2,1)}, u32[]{:S(2)}) copy-start(bf16[128,128]{1,0:T(8,128)(2,1)} %refs_5_.3) | copy-start | bytes 98308
  0.1 39.1 %copy-start.9 = (bf16[128,128]{1,0:T(8,128)(2,1)S(1)}, bf16[128,128]{1,0:T(8,128)(2,1)}, u32[]{:S(2)}) copy-start(bf16[128,128]{1,0:T(8,128)(2,1)} %refs_6_.3) | copy-start | bytes 98308
  8.7 11.1 %collective-permute-start = (bf16[256,512]{1,0:T(8,128)(2,1)}, bf16[256,512]{1,0:T(8,128)(2,1)S(1)}, u32[]{:S(2)}, u32[]{:S(2)}) collective-permute-start(bf16[256,512]{1,0:T(8,128)(2,1)} %get-tuple-element.16), channel_id=1, source_target_pairs={{0,0},{6,1},{11,2},{13,3},{2,4},{5,5},{9,6},{14,7},{1,8},{7,9},{10... | collective-permute-start | bytes 786440 | tf_op jit(solution)/shard_map/ppermute | solution.py:358
  14.4 1.0 %copy-start.1 = (bf16[256,512]{1,0:T(8,128)(2,1)S(1)}, bf16[256,512]{1,0:T(8,128)(2,1)}, u32[]{:S(2)}) copy-start(bf16[256,512]{1,0:T(8,128)(2,1)} %get-tuple-element.14.zl_ref) | copy-start | bytes 786436
  21.5 1.4 %collective-permute-start.1 = (bf16[2,256,128]{2,1,0:T(8,128)(2,1)S(1)}, bf16[2,256,128]{2,1,0:T(8,128)(2,1)S(1)}, u32[]{:S(2)}, u32[]{:S(2)}) collective-permute-start(bf16[2,256,128]{2,1,0:T(8,128)(2,1)S(1)} %get-tuple-element.21), channel_id=1, source_target_pairs={{1,0},{0,1},{3,2},{2,3},{5,4},{4,5},{7,6},{6,7},{9,8},{8,9},{11,10... | collective-permute-start | bytes 393224 | tf_op jit(solution)/shard_map/ppermute | solution.py:358
  22.9 9.3 %collective-permute-start.2 = (bf16[2,256,128]{2,1,0:T(8,128)(2,1)S(1)}, bf16[2,256,128]{2,1,0:T(8,128)(2,1)S(1)}, u32[]{:S(2)}, u32[]{:S(2)}) collective-permute-start(bf16[2,256,128]{2,1,0:T(8,128)(2,1)S(1)} %pad_maximum_fusion.refs_0_), channel_id=1, source_target_pairs={{2,0},{3,1},{0,2},{1,3},{6,4},{7,5},{4,6},{5,7},{10,8},{11,9},{8,1... | collective-permute-start | bytes 393224 | tf_op jit(solution)/shard_map/ppermute | solution.py:358
  26.0 6.2 %collective-permute-start.4 = (bf16[2,256,128]{2,1,0:T(8,128)(2,1)S(1)}, bf16[2,256,128]{2,1,0:T(8,128)(2,1)S(1)}, u32[]{:S(2)}, u32[]{:S(2)}) collective-permute-start(bf16[2,256,128]{2,1,0:T(8,128)(2,1)S(1)} %pad_maximum_fusion.1), channel_id=1, source_target_pairs={{2,0},{6,1},{10,2},{14,3},{3,4},{7,5},{11,6},{15,7},{0,8},{4,9},{8... | collective-permute-start | bytes 393224 | tf_op jit(solution)/shard_map/ppermute | solution.py:358
  30.3 8.9 %collective-permute-start.3 = (bf16[2,256,128]{2,1,0:T(8,128)(2,1)S(1)}, bf16[2,256,128]{2,1,0:T(8,128)(2,1)S(1)}, u32[]{:S(2)}, u32[]{:S(2)}) collective-permute-start(bf16[2,256,128]{2,1,0:T(8,128)(2,1)S(1)} %pad_maximum_fusion.1), channel_id=1, source_target_pairs={{0,0},{4,1},{8,2},{12,3},{1,4},{5,5},{9,6},{13,7},{2,8},{6,9},{10,... | collective-permute-start | bytes 393224 | tf_op jit(solution)/shard_map/ppermute | solution.py:358

commit v4 on v3

--- a/solution.py
+++ b/solution.py
@@ -55,10 +55,9 @@
 
     @pl.when(step == 0)
     def _():
-        for k in range(rep):
-            w_scr[k * hidden : (k + 1) * hidden, :] = wl_ref[...]
-            w_scr[LANES + k * hidden : LANES + (k + 1) * hidden, :] = wr_ref[...]
-        w_scr[2 * LANES :, :] = jnp.ones((LANES, channels), BF16)
+        turned = jnp.concatenate([wl_ref[...]] * rep + [wr_ref[...]] * rep, axis=0)
+        w_scr[:, : 2 * LANES] = turned.T
+        w_scr[:, 2 * LANES :] = jnp.ones((channels, LANES), BF16)
         start = lax.axis_index("dap") * rows
         spread = iota((residues, width), 0) == start + iota((residues, width), 1) // hidden
         live_scr[...] = dot_tn(mask_ref[...].astype(BF16), spread.astype(BF16))
@@ -67,14 +66,14 @@
         gather_scr[...] = same.astype(BF16)
 
     w = w_scr[...]
-    sums = dot_nt(jnp.ones((8, channels), BF16), w)[:1]
+    sums = dot(jnp.ones((8, channels), BF16), w)[:1]
     ones = jnp.ones((LANES, LANES), BF16)
     piece_rows = PIECE * rows
     own = iota((piece_rows, LANES), 1) // hidden == iota((piece_rows, LANES), 0) % rep
     own = own.astype(F32)
     for piece in range(seqs // PIECE):
         x = x_ref[piece * PIECE : (piece + 1) * PIECE].reshape(piece_rows, channels)
-        y = dot_nt(x, w)
+        y = dot(x, w)
         mean = y[:, 2 * LANES :] * (1.0 / channels)
         xf = x.astype(F32)
         square = jnp.zeros_like(mean)
@@ -114,7 +113,7 @@
         ],
         out_specs=[pl.BlockSpec((step, width), lambda s: (s, 0))] * 2,
         scratch_shapes=[
-            pltpu.VMEM((3 * LANES, channels), BF16),
+            pltpu.VMEM((channels, 3 * LANES), BF16),
             pltpu.VMEM((seqs, width), F32),
             pltpu.VMEM((rows * hidden // LANES * PIECE, PIECE * rows), BF16),
         ],
@@ -264,14 +263,34 @@
     return sub + 1 - 2 * (sub % 2)
 
 
+SENDERS = ((0, 2, 1, 3), (2, 1, 3, 0), (3, 1, 2, 0), (1, 2, 0, 3))
+
+
+def sender(a, b, subs, ratio):
+    if (subs, ratio) == (4, 1):
+        return SENDERS[b][a]
+    return a // ratio
+
+
+def sender_index(a, b, subs, ratio):
+    if (subs, ratio) != (4, 1):
+        return a // ratio
+    found = 0
+    for col, places in enumerate(SENDERS):
+        for row, place in enumerate(places):
+            found = jnp.where((a == row) & (b == col), place, found)
+    return found
+
+
 def triangle_kernel(subs, ratio, cols, *refs):
     twos = subs // 2
+    rights, refs = refs[: twos * ratio], refs[twos * ratio :]
     lefts, refs = refs[:twos], refs[twos:]
-    rights, refs = refs[: twos * ratio], refs[twos * ratio :]
     (one_ref, gate_ref, out_ref, up_ref, down_ref, result_ref, left_scr, right_scr, sum_scr) = refs
     pairs, channels = one_ref.shape
     rows = pairs // cols
     here, there = lax.axis_index("dap"), lax.axis_index("sub")
+    first_sub = sender_index(here, there, subs, ratio)
     for step in range(twos):
         sub = lax.rem(there + 2 * step, subs)
         left_scr[sub] = lefts[step][0].astype(F32)
@@ -279,7 +298,7 @@
     for turn in range(ratio):
         block = lax.rem(here + turn, ratio)
         for step in range(twos):
-            sub = lax.rem(here // ratio + 2 * step, subs)
+            sub = lax.rem(first_sub + 2 * step, subs)
             right_scr[block * subs + sub] = rights[turn * twos + step][0].astype(F32)
             right_scr[block * subs + other(sub)] = rights[turn * twos + step][1].astype(F32)
     for block in range(ratio):
@@ -325,7 +344,7 @@
         cost_estimate=pl.CostEstimate(
             flops=2 * pairs * channels * 2048, bytes_accessed=2 << 20, transcendentals=pairs * 128
         ),
-    )(*lefts, *rights, one, gate, out, up, down)
+    )(*rights, *lefts, one, gate, out, up, down)
 
 
 def per_device(
@@ -360,15 +379,10 @@
     def owner(a, b, turn):
         return ratio * b + (a + turn) % ratio
 
-    def sender(a, b):
-        if (daps, subs) == (4, 4):
-            return ((0, 2, 1, 3), (2, 1, 3, 0), (3, 1, 2, 0), (1, 2, 0, 3))[b][a]
-        return a // ratio
-
     mask = alignment_mask.T
     zl, zr = factors(alignment, mask, outer_left.T, outer_right.T)
     zrs = [
-        fetch(zr, lambda a, b, turn=turn: (owner(a, b, turn), sender(a, b)))
+        fetch(zr, lambda a, b, turn=turn: (owner(a, b, turn), sender(a, b, subs, ratio)))
         for turn in range(ratio)
     ]
     zlt, base, inverse, live, proj = prepare(
@@ -381,7 +395,12 @@
     left = jnp.stack([own[0], near[0]])
     right = jnp.stack([own[1], near[1]])
     rights = [
-        fetch(right, lambda a, b, t=turn, m=step: (owner(a, b, t), (a // ratio + 2 * m) % subs))
+        fetch(
+            right,
+            lambda a, b, t=turn, m=step: (
+                owner(a, b, t), (sender(a, b, subs, ratio) + 2 * m) % subs
+            ),
+        )
         for turn in range(ratio)
         for step in range(subs // 2)
     ]

time: 41.6 us -> 38.2 us (0.918)
  waiting for transfers between devices: 12.3 us -> 9.03 us
    ppermute x5, waiting for transfers between devices: 12.3 us -> 9.03 us  [fetch(): return lax.ppermute(values, ('dap', 'sub'), perm)]
    pallas_call x1, Pallas kernels: 8.64 us -> 8.22 us  [factors(): pl.pallas_call(factor_kernel, out_shape=(out, out), grid=(seqs // step,),...]
  transfers between devices with their start and end apart: 5 -> 5, of which waited for: 3 -> 4; matrix products, arithmetic and copies ran while one was open for 0% -> 0% of each run, Pallas kernels for 1% -> 1%
where the time goes in v4:
time: 38.2 us; the launch traced here: 38 us
  starting transfers between devices  15.1 us (40%)
  Pallas kernels  12.6 us (33%)
  waiting for transfers between devices  9.03 us (24%)
  local copies, waits for them, and re-layouts  1.01 us (3%)
    ppermute x5, starting transfers between devices, fetch(): return lax.ppermute(values, ('dap', 'sub'), perm)  15.1 us
    ppermute x5, waiting for transfers between devices, fetch(): return lax.ppermute(values, ('dap', 'sub'), perm)  9.03 us
    pallas_call x1, Pallas kernels, factors(): pl.pallas_call(factor_kernel, out_shape=(out, out), grid=(seqs // step,),...  8.22 us
    pallas_call x1, Pallas kernels, triangle_update(): pl.pallas_call(functools.partial(triangle_kernel, subs, ratio, cols), out...  2.23 us
    pallas_call x1, Pallas kernels, pair_update(): pl.pallas_call(functools.partial(pair_kernel, ratio, hidden), out_shape=(...  1.61 us
    unnamed x26, local copies, waits for them, and re-layouts  0.99 us
  transfers between devices with their start and end apart: 5, of which 4 were waited for; matrix products, arithmetic and copies ran while one was open for 0% of the time, Pallas kernels for 1%

profile of v4, /device:TPU:1, one launch (start us, length us, event | category | flops | bytes accessed | tf_op | source)
XLA Modules:
  0.0 38.0 jit_solution(11455056551949987223)
XLA Ops:
  0.0 0.0 copy-start.4
  0.0 0.0 copy-start.10
  0.0 0.0 copy-start
  0.0 0.0 copy-start.12
  0.0 0.0 copy-start.11
  0.0 0.0 copy-start.5
  0.0 0.0 copy-start.6
  0.0 0.0 copy-start.7
  0.1 0.0 copy-start.2
  0.1 0.0 copy-start.3
  0.1 0.0 copy-start.8
  0.1 0.0 copy-start.9
  0.1 8.2 %shard_map.145 = (bf16[256,512]{1,0:T(8,128)(2,1)}, bf16[256,512]{1,0:T(8,128)(2,1)}) custom-call(bf16[256,16,256]{2,1,0:T(8,128)(2,1)} %x_ref.1, s32[64,256]{1,0:T(8,128)} %bitcast.5, bf16[32,256]{1,0:T(8,128)(2,1)} %bitcast.9, bf16[32,256]{1,0:T(8,128)(2,1)} %bitcast.10), custom_call_target="tpu_custom_call" | custom-call | flops 1073741824 | bytes 4194304 | tf_op jit(solution)/shard_map/pallas_call | solution.py:104
  8.3 5.6 %collective-permute-start = (bf16[256,512]{1,0:T(8,128)(2,1)}, bf16[256,512]{1,0:T(8,128)(2,1)S(1)}, u32[]{:S(2)}, u32[]{:S(2)}) collective-permute-start(bf16[256,512]{1,0:T(8,128)(2,1)} %get-tuple-element.16), channel_id=1, source_target_pairs={{0,0},{6,1},{11,2},{13,3},{2,4},{5,5},{9,6},{14,7},{1,8},{7,9},{10... | collective-permute-start | bytes 786440 | tf_op jit(solution)/shard_map/ppermute | solution.py:377
  13.9 0.0 copy-done.4
  13.9 0.0 copy-done.10
  13.9 0.0 copy-done
  14.0 0.0 copy-done.12
  14.0 0.0 copy-done.11
  14.0 0.0 copy-done.5
  14.0 0.0 copy-start.1
  14.0 0.9 %copy-done.1 = bf16[256,512]{1,0:T(8,128)(2,1)S(1)} copy-done((bf16[256,512]{1,0:T(8,128)(2,1)S(1)}, bf16[256,512]{1,0:T(8,128)(2,1)}, u32[]{:S(2)}) %copy-start.1) | copy-done | bytes 262168
  14.9 0.5 %shard_map.146 = (bf16[512,256]{1,0:T(8,128)(2,1)S(1)}, f32[256,128]{1,0:T(8,128)S(1)}, f32[256,128]{1,0:T(8,128)S(1)}, f32[256,128]{1,0:T(8,128)S(1)}, bf16[1024,128]{1,0:T(8,128)(2,1)S(1)}) custom-call(bf16[256,512]{1,0:T(8,128)(2,1)S(1)} %copy-done.1, s32[64,256]{1,0:T(8,128)S(1)} %bitcast.6, bf16[16,16,128]{2,1,0:T(8,128)(2,1)S(1)} %copy-done.5, ...), custom_call_target="tpu_custom_call" | custom-call | flops 134217728 | bytes 2097152 | tf_op jit(solution)/shard_map/pallas_call | solution.py:169
  15.5 4.0 %collective-permute-done.refs_0_ = bf16[256,512]{1,0:T(8,128)(2,1)S(1)} collective-permute-done((bf16[256,512]{1,0:T(8,128)(2,1)}, bf16[256,512]{1,0:T(8,128)(2,1)S(1)}, u32[]{:S(2)}, u32[]{:S(2)}) %collective-permute-start) | collective-permute-done | bytes 262176 | tf_op jit(solution)/shard_map/ppermute | solution.py:377
  19.4 0.0 copy-done.6
  19.4 0.0 copy-done.7
  19.4 1.6 %shard_map.147 = (bf16[2,256,128]{2,1,0:T(8,128)(2,1)S(1)}, bf16[256,128]{1,0:T(8,128)(2,1)S(1)}) custom-call(bf16[512,256]{1,0:T(8,128)(2,1)S(1)} %get-tuple-element.15.zlt_ref, bf16[256,512]{1,0:T(8,128)(2,1)S(1)} %collective-permute-done.refs_0_, f32[256,128]{1,0:T(8,128)S(1)} %get-tuple-element.17.refs_1_, f32[256,128]{1,0:T(8,128)S(1)} %get-tuple-element.18.refs_2_, ...), custom_call_target="tpu_custom_call" | custom-call | flops 268435456 | bytes 2097152 | tf_op jit(solution)/shard_map/pallas_call | solution.py:245
  21.0 0.1 collective-permute-start.1
  21.1 1.3 %collective-permute-done.1 = bf16[2,256,128]{2,1,0:T(8,128)(2,1)S(1)} collective-permute-done((bf16[2,256,128]{2,1,0:T(8,128)(2,1)S(1)}, bf16[2,256,128]{2,1,0:T(8,128)(2,1)S(1)}, u32[]{:S(2)}, u32[]{:S(2)}) %collective-permute-start.1) | collective-permute-done | bytes 131104 | tf_op jit(solution)/shard_map/ppermute | solution.py:377
  22.5 5.6 %collective-permute-start.3 = (bf16[2,256,128]{2,1,0:T(8,128)(2,1)S(1)}, bf16[2,256,128]{2,1,0:T(8,128)(2,1)S(1)}, u32[]{:S(2)}, u32[]{:S(2)}) collective-permute-start(bf16[2,256,128]{2,1,0:T(8,128)(2,1)S(1)} %pad_maximum_fusion), channel_id=1, source_target_pairs={{2,0},{4,1},{9,2},{15,3},{0,4},{7,5},{11,6},{12,7},{3,8},{5,9},{8,... | collective-permute-start | bytes 393224 | tf_op jit(solution)/shard_map/ppermute | solution.py:377
  28.1 1.9 %collective-permute-start.2 = (bf16[2,256,128]{2,1,0:T(8,128)(2,1)S(1)}, bf16[2,256,128]{2,1,0:T(8,128)(2,1)S(1)}, u32[]{:S(2)}, u32[]{:S(2)}) collective-permute-start(bf16[2,256,128]{2,1,0:T(8,128)(2,1)S(1)} %pad_maximum_fusion), channel_id=1, source_target_pairs={{0,0},{6,1},{11,2},{13,3},{2,4},{5,5},{9,6},{14,7},{1,8},{7,9},{10... | collective-permute-start | bytes 393224 | tf_op jit(solution)/shard_map/ppermute | solution.py:377
  30.1 1.9 %collective-permute-start.4 = (bf16[2,256,128]{2,1,0:T(8,128)(2,1)S(1)}, bf16[2,256,128]{2,1,0:T(8,128)(2,1)S(1)}, u32[]{:S(2)}, u32[]{:S(2)}) collective-permute-start(bf16[2,256,128]{2,1,0:T(8,128)(2,1)S(1)} %pad_maximum_fusion.1.refs_2_), channel_id=1, source_target_pairs={{2,0},{3,1},{0,2},{1,3},{6,4},{7,5},{4,6},{5,7},{10,8},{11,9},{8,1... | collective-permute-start | bytes 393224 | tf_op jit(solution)/shard_map/ppermute | solution.py:377
  32.0 0.0 collective-permute-done.3.refs_1_
  32.0 3.6 %collective-permute-done.2.refs_0_ = bf16[2,256,128]{2,1,0:T(8,128)(2,1)S(1)} collective-permute-done((bf16[2,256,128]{2,1,0:T(8,128)(2,1)S(1)}, bf16[2,256,128]{2,1,0:T(8,128)(2,1)S(1)}, u32[]{:S(2)}, u32[]{:S(2)}) %collective-permute-start.2) | collective-permute-done | bytes 131104 | tf_op jit(solution)/shard_map/ppermute | solution.py:377
  35.5 0.2 collective-permute-done.4.refs_3_
  35.7 0.0 copy-done.2
  35.7 0.0 copy-done.3
  35.7 0.0 copy-done.8
  35.7 0.0 copy-done.9
  35.7 2.2 %shard_map.148 = bf16[16,16,128]{2,1,0:T(8,128)(2,1)} custom-call(bf16[2,256,128]{2,1,0:T(8,128)(2,1)S(1)} %collective-permute-done.2.refs_0_, bf16[2,256,128]{2,1,0:T(8,128)(2,1)S(1)} %collective-permute-done.3.refs_1_, bf16[2,256,128]{2,1,0:T(8,128)(2,1)S(1)} %pad_maximum_fusion.1.refs_2_, bf16[2,256,128]{2,1,0:T(8,128)(2,1)S(1)} %collective-permute-done.4.refs_3_, ...), custom_call_target="tpu_custom_call" | custom-call | flops 134217728 | bytes 2097152 | tf_op jit(solution)/shard_map/pallas_call | solution.py:333
  (4 shorter events, 0.1 us)
Async XLA Ops:
  0.0 13.9 %copy-start.4 = (s32[256,64]{0,1:T(8,128)S(1)}, s32[256,64]{0,1:T(8,128)}, u32[]{:S(2)}) copy-start(s32[256,64]{0,1:T(8,128)} %param.16) | copy-start | bytes 196612
  0.0 13.9 %copy-start.10 = (bf16[66,128]{1,0:T(8,128)(2,1)S(1)}, bf16[66,128]{1,0:T(8,128)(2,1)}, u32[]{:S(2)}) copy-start(bf16[66,128]{1,0:T(8,128)(2,1)} %table_ref.1) | copy-start | bytes 50692
  0.0 13.9 %copy-start = (f32[32,32,128]{2,1,0:T(8,128)S(1)}, f32[32,32,128]{2,1,0:T(8,128)}, u32[]{:S(2)}) copy-start(f32[32,32,128]{2,1,0:T(8,128)} %proj_ref.1) | copy-start | bytes 1572868
  0.0 14.0 %copy-start.12 = (s32[64]{0:T(128)S(1)}, s32[64]{0:T(128)}, u32[]{:S(2)}) copy-start(s32[64]{0:T(128)} %param.19) | copy-start | bytes 772
  0.0 14.0 %copy-start.11 = (s32[64]{0:T(128)S(1)}, s32[64]{0:T(128)}, u32[]{:S(2)}) copy-start(s32[64]{0:T(128)} %param.18) | copy-start | bytes 772
  0.0 14.0 %copy-start.5 = (bf16[16,16,128]{2,1,0:T(8,128)(2,1)S(1)}, bf16[16,16,128]{2,1,0:T(8,128)(2,1)}, u32[]{:S(2)}) copy-start(bf16[16,16,128]{2,1,0:T(8,128)(2,1)} %pair_ref.1) | copy-start | bytes 196612
  0.0 19.4 %copy-start.6 = (bf16[128,256]{1,0:T(8,128)(2,1)S(1)}, bf16[128,256]{1,0:T(8,128)(2,1)}, u32[]{:S(2)}) copy-start(bf16[128,256]{1,0:T(8,128)(2,1)} %refs_5_.2) | copy-start | bytes 196612
  0.0 19.4 %copy-start.7 = (bf16[128,256]{1,0:T(8,128)(2,1)S(1)}, bf16[128,256]{1,0:T(8,128)(2,1)}, u32[]{:S(2)}) copy-start(bf16[128,256]{1,0:T(8,128)(2,1)} %refs_6_.2) | copy-start | bytes 196612
  0.1 35.7 %copy-start.2 = (bf16[128,512]{1,0:T(8,128)(2,1)S(1)}, bf16[128,512]{1,0:T(8,128)(2,1)}, u32[]{:S(2)}) copy-start(bf16[128,512]{1,0:T(8,128)(2,1)} %refs_7_.1) | copy-start | bytes 393220
  0.1 35.7 %copy-start.3 = (bf16[512,128]{1,0:T(8,128)(2,1)S(1)}, bf16[512,128]{1,0:T(8,128)(2,1)}, u32[]{:S(2)}) copy-start(bf16[512,128]{1,0:T(8,128)(2,1)} %refs_8_.1) | copy-start | bytes 393220
  0.1 35.6 %copy-start.8 = (bf16[128,128]{1,0:T(8,128)(2,1)S(1)}, bf16[128,128]{1,0:T(8,128)(2,1)}, u32[]{:S(2)}) copy-start(bf16[128,128]{1,0:T(8,128)(2,1)} %refs_5_.3) | copy-start | bytes 98308
  0.1 35.6 %copy-start.9 = (bf16[128,128]{1,0:T(8,128)(2,1)S(1)}, bf16[128,128]{1,0:T(8,128)(2,1)}, u32[]{:S(2)}) copy-start(bf16[128,128]{1,0:T(8,128)(2,1)} %refs_6_.3) | copy-start | bytes 98308
  8.3 11.1 %collective-permute-start = (bf16[256,512]{1,0:T(8,128)(2,1)}, bf16[256,512]{1,0:T(8,128)(2,1)S(1)}, u32[]{:S(2)}, u32[]{:S(2)}) collective-permute-start(bf16[256,512]{1,0:T(8,128)(2,1)} %get-tuple-element.16), channel_id=1, source_target_pairs={{0,0},{6,1},{11,2},{13,3},{2,4},{5,5},{9,6},{14,7},{1,8},{7,9},{10... | collective-permute-start | bytes 786440 | tf_op jit(solution)/shard_map/ppermute | solution.py:377
  14.0 1.0 %copy-start.1 = (bf16[256,512]{1,0:T(8,128)(2,1)S(1)}, bf16[256,512]{1,0:T(8,128)(2,1)}, u32[]{:S(2)}) copy-start(bf16[256,512]{1,0:T(8,128)(2,1)} %get-tuple-element.14.zl_ref) | copy-start | bytes 786436
  21.0 1.4 %collective-permute-start.1 = (bf16[2,256,128]{2,1,0:T(8,128)(2,1)S(1)}, bf16[2,256,128]{2,1,0:T(8,128)(2,1)S(1)}, u32[]{:S(2)}, u32[]{:S(2)}) collective-permute-start(bf16[2,256,128]{2,1,0:T(8,128)(2,1)S(1)} %get-tuple-element.21), channel_id=1, source_target_pairs={{1,0},{0,1},{3,2},{2,3},{5,4},{4,5},{7,6},{6,7},{9,8},{8,9},{11,10... | collective-permute-start | bytes 393224 | tf_op jit(solution)/shard_map/ppermute | solution.py:377
  22.5 9.5 %collective-permute-start.3 = (bf16[2,256,128]{2,1,0:T(8,128)(2,1)S(1)}, bf16[2,256,128]{2,1,0:T(8,128)(2,1)S(1)}, u32[]{:S(2)}, u32[]{:S(2)}) collective-permute-start(bf16[2,256,128]{2,1,0:T(8,128)(2,1)S(1)} %pad_maximum_fusion), channel_id=1, source_target_pairs={{2,0},{4,1},{9,2},{15,3},{0,4},{7,5},{11,6},{12,7},{3,8},{5,9},{8,... | collective-permute-start | bytes 393224 | tf_op jit(solution)/shard_map/ppermute | solution.py:377
  28.1 7.4 %collective-permute-start.2 = (bf16[2,256,128]{2,1,0:T(8,128)(2,1)S(1)}, bf16[2,256,128]{2,1,0:T(8,128)(2,1)S(1)}, u32[]{:S(2)}, u32[]{:S(2)}) collective-permute-start(bf16[2,256,128]{2,1,0:T(8,128)(2,1)S(1)} %pad_maximum_fusion), channel_id=1, source_target_pairs={{0,0},{6,1},{11,2},{13,3},{2,4},{5,5},{9,6},{14,7},{1,8},{7,9},{10... | collective-permute-start | bytes 393224 | tf_op jit(solution)/shard_map/ppermute | solution.py:377
  30.1 5.7 %collective-permute-start.4 = (bf16[2,256,128]{2,1,0:T(8,128)(2,1)S(1)}, bf16[2,256,128]{2,1,0:T(8,128)(2,1)S(1)}, u32[]{:S(2)}, u32[]{:S(2)}) collective-permute-start(bf16[2,256,128]{2,1,0:T(8,128)(2,1)S(1)} %pad_maximum_fusion.1.refs_2_), channel_id=1, source_target_pairs={{2,0},{3,1},{0,2},{1,3},{6,4},{7,5},{4,6},{5,7},{10,8},{11,9},{8,1... | collective-permute-start | bytes 393224 | tf_op jit(solution)/shard_map/ppermute | solution.py:377

commit v5 on v4

--- a/solution.py
+++ b/solution.py
@@ -44,9 +44,9 @@
     return pl.BlockSpec(memory_space=pltpu.VMEM)
 
 
-def factor_kernel(x_ref, mask_ref, wl_ref, wr_ref, zl_ref, zr_ref, w_scr, live_scr, gather_scr):
+def factor_kernel(x_ref, mask_ref, weight_ref, z_ref, w_scr, live_scr, gather_scr, y_scr):
     seqs, rows, channels = x_ref.shape
-    hidden = wl_ref.shape[0]
+    hidden = weight_ref.shape[0]
     rep = LANES // hidden
     groups = rows // rep
     residues = mask_ref.shape[0]
@@ -55,9 +55,8 @@
 
     @pl.when(step == 0)
     def _():
-        turned = jnp.concatenate([wl_ref[...]] * rep + [wr_ref[...]] * rep, axis=0)
-        w_scr[:, : 2 * LANES] = turned.T
-        w_scr[:, 2 * LANES :] = jnp.ones((channels, LANES), BF16)
+        w_scr[:, :LANES] = jnp.concatenate([weight_ref[...]] * rep, axis=0).T
+        w_scr[:, LANES:] = jnp.ones((channels, LANES), BF16)
         start = lax.axis_index("dap") * rows
         spread = iota((residues, width), 0) == start + iota((residues, width), 1) // hidden
         live_scr[...] = dot_tn(mask_ref[...].astype(BF16), spread.astype(BF16))
@@ -66,62 +65,56 @@
         gather_scr[...] = same.astype(BF16)
 
     w = w_scr[...]
-    sums = dot(jnp.ones((8, channels), BF16), w)[:1]
-    ones = jnp.ones((LANES, LANES), BF16)
-    piece_rows = PIECE * rows
-    own = iota((piece_rows, LANES), 1) // hidden == iota((piece_rows, LANES), 0) % rep
-    own = own.astype(F32)
+    sums = dot(jnp.ones((8, channels), BF16), w)[:1, :LANES]
+    x = x_ref[...].reshape(seqs * rows, channels)
+    y = dot(x, w)
+    mean = y[:, LANES:] * (1.0 / channels)
+    xf = x.astype(F32)
+    square = jnp.zeros_like(mean)
+    for part in range(channels // LANES):
+        centered = xf[:, part * LANES : (part + 1) * LANES] - mean
+        square = square + centered * centered
+    spread = dot(square.astype(BF16), jnp.ones((LANES, LANES), BF16))
+    own = (iota(mean.shape, 1) // hidden == iota(mean.shape, 0) % rep).astype(F32)
+    scale = lax.rsqrt(spread * (1.0 / channels) + EPSILON) * own
+    y_scr[...] = ((y[:, :LANES] - mean * sums) * scale).astype(BF16)
     for piece in range(seqs // PIECE):
-        x = x_ref[piece * PIECE : (piece + 1) * PIECE].reshape(piece_rows, channels)
-        y = dot(x, w)
-        mean = y[:, 2 * LANES :] * (1.0 / channels)
-        xf = x.astype(F32)
-        square = jnp.zeros_like(mean)
-        for part in range(channels // LANES):
-            centered = xf[:, part * LANES : (part + 1) * LANES] - mean
-            square = square + centered * centered
-        scale = lax.rsqrt(dot(square.astype(BF16), ones) * (1.0 / channels) + EPSILON) * own
-        left = ((y[:, :LANES] - mean * sums[:, :LANES]) * scale).astype(BF16)
-        right = ((y[:, LANES : 2 * LANES] - mean * sums[:, LANES : 2 * LANES]) * scale).astype(BF16)
-        z = dot(gather_scr[...], jnp.concatenate([left, right], axis=1))
+        z = dot(gather_scr[...], y_scr[piece * PIECE * rows : (piece + 1) * PIECE * rows, :])
         here = slice(piece * PIECE, (piece + 1) * PIECE)
         whole = pl.ds(pl.multiple_of(step * seqs + piece * PIECE, PIECE), PIECE)
         for group in range(groups):
             lanes = slice(group * LANES, (group + 1) * LANES)
-            both = z[group * PIECE : (group + 1) * PIECE]
-            live = live_scr[whole, lanes]
-            zl_ref[here, lanes] = (both[:, :LANES] * live).astype(BF16)
-            zr_ref[here, lanes] = (both[:, LANES:] * live).astype(BF16)
-
-
-def factors(alignment, mask, outer_left, outer_right):
+            part = z[group * PIECE : (group + 1) * PIECE]
+            z_ref[here, lanes] = (part * live_scr[whole, lanes]).astype(BF16)
+
+
+def factor(alignment, mask, weight):
     seqs, rows, channels = alignment.shape
     residues = mask.shape[0]
-    hidden = outer_left.shape[0]
+    hidden = weight.shape[0]
     step = seqs // 4
     width = rows * hidden
-    out = jax.ShapeDtypeStruct((seqs, width), BF16)
     return pl.pallas_call(
         factor_kernel,
-        out_shape=(out, out),
+        out_shape=jax.ShapeDtypeStruct((seqs, width), BF16),
         grid=(seqs // step,),
         in_specs=[
             pl.BlockSpec((step, rows, channels), lambda s: (s, 0, 0)),
             pl.BlockSpec((residues, seqs), lambda s: (0, 0)),
             pl.BlockSpec((hidden, channels), lambda s: (0, 0)),
-            pl.BlockSpec((hidden, channels), lambda s: (0, 0)),
         ],
-        out_specs=[pl.BlockSpec((step, width), lambda s: (s, 0))] * 2,
+        out_specs=pl.BlockSpec((step, width), lambda s: (s, 0)),
         scratch_shapes=[
-            pltpu.VMEM((channels, 3 * LANES), BF16),
+            pltpu.VMEM((channels, 2 * LANES), BF16),
             pltpu.VMEM((seqs, width), F32),
             pltpu.VMEM((rows * hidden // LANES * PIECE, PIECE * rows), BF16),
+            pltpu.VMEM((step * rows, LANES), BF16),
         ],
         compiler_params=pltpu.CompilerParams(vmem_limit_bytes=119 << 19),
         cost_estimate=pl.CostEstimate(
             flops=2 * seqs * rows * channels * 512, bytes_accessed=4 << 20, transcendentals=0
         ),
-    )(alignment, mask, outer_left, outer_right)
+    )(alignment, mask, weight)
 
 
 def prepare_kernel(
@@ -263,6 +256,23 @@
     return sub + 1 - 2 * (sub % 2)
 
 
+def gate_kernel(one_ref, weight_ref, gate_ref):
+    norm = layer_norm(one_ref[...].astype(F32)).astype(BF16)
+    gate_ref[...] = jax.nn.sigmoid(dot(norm, weight_ref[...]))
+
+
+def output_gate(one, weight):
+    return pl.pallas_call(
+        gate_kernel,
+        out_shape=jax.ShapeDtypeStruct(one.shape, F32),
+        in_specs=[vmem()] * 2,
+        out_specs=vmem(),
+        cost_estimate=pl.CostEstimate(
+            flops=2 * one.size * LANES, bytes_accessed=1 << 18, transcendentals=one.size
+        ),
+    )(one, weight)
+
+
 SENDERS = ((0, 2, 1, 3), (2, 1, 3, 0), (3, 1, 2, 0), (1, 2, 0, 3))
 
 
@@ -284,8 +294,8 @@
 
 def triangle_kernel(subs, ratio, cols, *refs):
     twos = subs // 2
+    lefts, refs = refs[:twos], refs[twos:]
     rights, refs = refs[: twos * ratio], refs[twos * ratio :]
-    lefts, refs = refs[:twos], refs[twos:]
     (one_ref, gate_ref, out_ref, up_ref, down_ref, result_ref, left_scr, right_scr, sum_scr) = refs
     pairs, channels = one_ref.shape
     rows = pairs // cols
@@ -316,10 +326,8 @@
         for i in range(rows):
             sum_scr[i * cols + block * rows : i * cols + (block + 1) * rows, :] = totals[i]
     one = one_ref[...].astype(F32)
-    norm = layer_norm(one).astype(BF16)
-    gate = jax.nn.sigmoid(dot(norm, gate_ref[...]))
     hidden = layer_norm(sum_scr[...].astype(BF16).astype(F32)).astype(BF16)
-    two = (one + gate * dot(hidden, out_ref[...])).astype(BF16).astype(F32)
+    two = (one + gate_ref[...] * dot(hidden, out_ref[...])).astype(BF16).astype(F32)
     wide = jnp.maximum(dot(layer_norm(two).astype(BF16), up_ref[...]), 0.0).astype(BF16)
     result = (two + dot(wide, down_ref[...])).astype(BF16)
     result_ref[...] = result.reshape(result_ref.shape)
@@ -344,7 +352,7 @@
         cost_estimate=pl.CostEstimate(
             flops=2 * pairs * channels * 2048, bytes_accessed=2 << 20, transcendentals=pairs * 128
         ),
-    )(*rights, *lefts, one, gate, out, up, down)
+    )(*lefts, *rights, one, gate, out, up, down)
 
 
 def per_device(
@@ -380,11 +388,12 @@
         return ratio * b + (a + turn) % ratio
 
     mask = alignment_mask.T
-    zl, zr = factors(alignment, mask, outer_left.T, outer_right.T)
+    zr = factor(alignment, mask, outer_right.T)
     zrs = [
         fetch(zr, lambda a, b, turn=turn: (owner(a, b, turn), sender(a, b, subs, ratio)))
         for turn in range(ratio)
     ]
+    zl = factor(alignment, mask, outer_left.T)
     zlt, base, inverse, live, proj = prepare(
         zl, mask, pair_input, residue_mask, chain_index, relative_table, outer_proj
     )
@@ -407,8 +416,9 @@
     lefts = [left] + [
         fetch(left, lambda a, b, m=step: (a, (b + 2 * m) % subs)) for step in range(1, subs // 2)
     ]
+    gate = output_gate(one, triangle_gate)
     return triangle_update(
-        lefts, rights, one, cols, triangle_gate, triangle_out, transition_up, transition_down
+        lefts, rights, one, cols, gate, triangle_out, transition_up, transition_down
     )
 
 

time: 38.2 us -> 39.1 us (1.024)
  Pallas kernels: 12.6 us -> 16.8 us
  waiting for transfers between devices: 9.03 us -> 5.26 us
  local copies, waits for them, and re-layouts: 1.01 us -> 2.77 us
  starting transfers between devices: 15.1 us -> 13.6 us
    pallas_call x1 -> x3, Pallas kernels: 8.22 us -> 12.5 us  [the longest x2 10.7 us: factor(): pl.pallas_call(factor_kernel, out_shape=jax.ShapeDtypeStruct((seqs, width...]
    ppermute x5, waiting for transfers between devices: 9.03 us -> 5.26 us  [fetch(): return lax.ppermute(values, ('dap', 'sub'), perm)]
    unnamed x26 -> x30, local copies, waits for them, and re-layouts: 0.99 us -> 2.75 us
    ppermute x5, starting transfers between devices: 15.1 us -> 13.6 us  [fetch(): return lax.ppermute(values, ('dap', 'sub'), perm)]
  transfers between devices with their start and end apart: 5 -> 5, of which waited for: 4 -> 2; matrix products, arithmetic and copies ran while one was open for 0% -> 0% of each run, Pallas kernels for 1% -> 20%
where the time goes in v5:
time: 39.1 us; the launch traced here: 38.7 us
  Pallas kernels  16.8 us (43%)
  starting transfers between devices  13.6 us (35%)
  waiting for transfers between devices  5.26 us (13%)
  local copies, waits for them, and re-layouts  2.77 us (7%)
    ppermute x5, starting transfers between devices, fetch(): return lax.ppermute(values, ('dap', 'sub'), perm)  13.6 us
    pallas_call x2, Pallas kernels, factor(): pl.pallas_call(factor_kernel, out_shape=jax.ShapeDtypeStruct((seqs, width...  10.7 us
    ppermute x5, waiting for transfers between devices, fetch(): return lax.ppermute(values, ('dap', 'sub'), perm)  5.26 us
    unnamed x30, local copies, waits for them, and re-layouts  2.75 us
    pallas_call x1, Pallas kernels, triangle_update(): pl.pallas_call(functools.partial(triangle_kernel, subs, ratio, cols), out...  2.2 us
    pallas_call x1, Pallas kernels, output_gate(): pl.pallas_call(gate_kernel, out_shape=jax.ShapeDtypeStruct(one.shape, F32...  1.82 us
    pallas_call x1, Pallas kernels, pair_update(): pl.pallas_call(functools.partial(pair_kernel, ratio, hidden), out_shape=(...  1.61 us
  transfers between devices with their start and end apart: 5, of which 2 were waited for; matrix products, arithmetic and copies ran while one was open for 0% of the time, Pallas kernels for 20%

profile of v5, /device:TPU:1, one launch (start us, length us, event | category | flops | bytes accessed | tf_op | source)
XLA Modules:
  0.0 38.7 jit_solution(6162476189053820523)
XLA Ops:
  0.0 5.3 %shard_map.147 = bf16[256,512]{1,0:T(8,128)(2,1)} custom-call(bf16[256,16,256]{2,1,0:T(8,128)(2,1)} %x_ref.3, s32[64,256]{1,0:T(8,128)} %bitcast.5, bf16[32,256]{1,0:T(8,128)(2,1)} %bitcast.10), custom_call_target="tpu_custom_call" | custom-call | flops 1073741824 | bytes 4194304 | tf_op jit(solution)/shard_map/pallas_call | solution.py:97
  5.3 0.0 copy-start.1
  5.3 0.0 copy-start.7
  5.3 0.0 copy-start.8
  5.3 0.0 copy-start.12
  5.3 0.0 copy-start.13
  5.3 0.0 copy-start.14
  5.3 5.7 %collective-permute-start = (bf16[256,512]{1,0:T(8,128)(2,1)}, bf16[256,512]{1,0:T(8,128)(2,1)S(1)}, u32[]{:S(2)}, u32[]{:S(2)}) collective-permute-start(bf16[256,512]{1,0:T(8,128)(2,1)} %shard_map.147), channel_id=1, source_target_pairs={{0,0},{6,1},{11,2},{13,3},{2,4},{5,5},{9,6},{14,7},{1,8},{7,9},{10... | collective-permute-start | bytes 786440 | tf_op jit(solution)/shard_map/ppermute | solution.py:385
  11.1 0.0 copy-start.9
  11.1 0.0 copy-start.10
  11.1 0.0 copy-start.5
  11.1 0.0 copy-start.6
  11.1 0.0 copy-start.11
  11.1 5.4 %shard_map.145.zl_ref = bf16[256,512]{1,0:T(8,128)(2,1)} custom-call(bf16[256,16,256]{2,1,0:T(8,128)(2,1)} %x_ref.3, s32[64,256]{1,0:T(8,128)} %bitcast.6, bf16[32,256]{1,0:T(8,128)(2,1)} %bitcast.11), custom_call_target="tpu_custom_call" | custom-call | flops 1073741824 | bytes 4194304 | tf_op jit(solution)/shard_map/pallas_call | solution.py:97
  16.6 0.0 copy-done.1
  16.6 0.0 copy-done.7
  16.6 0.0 copy-done.8
  16.6 0.0 copy-done.12
  16.6 0.0 copy-done.13
  16.6 0.0 copy-done.14
  16.6 0.0 copy-start.2
  16.6 0.9 %copy-done.2 = bf16[256,512]{1,0:T(8,128)(2,1)S(1)} copy-done((bf16[256,512]{1,0:T(8,128)(2,1)S(1)}, bf16[256,512]{1,0:T(8,128)(2,1)}, u32[]{:S(2)}) %copy-start.2) | copy-done | bytes 262168
  17.5 0.5 %shard_map.146 = (bf16[512,256]{1,0:T(8,128)(2,1)S(1)}, f32[256,128]{1,0:T(8,128)S(1)}, f32[256,128]{1,0:T(8,128)S(1)}, f32[256,128]{1,0:T(8,128)S(1)}, bf16[1024,128]{1,0:T(8,128)(2,1)S(1)}) custom-call(bf16[256,512]{1,0:T(8,128)(2,1)S(1)} %copy-done.2, s32[64,256]{1,0:T(8,128)S(1)} %bitcast.7, bf16[16,16,128]{2,1,0:T(8,128)(2,1)S(1)} %copy-done.8, ...), custom_call_target="tpu_custom_call" | custom-call | flops 134217728 | bytes 2097152 | tf_op jit(solution)/shard_map/pallas_call | solution.py:162
  18.1 0.0 collective-permute-done.refs_0_
  18.1 0.0 copy-done.9
  18.1 0.0 copy-done.10
  18.1 1.6 %shard_map.148 = (bf16[2,256,128]{2,1,0:T(8,128)(2,1)S(1)}, bf16[256,128]{1,0:T(8,128)(2,1)S(1)}) custom-call(bf16[512,256]{1,0:T(8,128)(2,1)S(1)} %get-tuple-element.12.zlt_ref, bf16[256,512]{1,0:T(8,128)(2,1)S(1)} %collective-permute-done.refs_0_, f32[256,128]{1,0:T(8,128)S(1)} %get-tuple-element.13.refs_1_, f32[256,128]{1,0:T(8,128)S(1)} %get-tuple-element.14.refs_2_, ...), custom_call_target="tpu_custom_call" | custom-call | flops 268435456 | bytes 2097152 | tf_op jit(solution)/shard_map/pallas_call | solution.py:238
  19.7 0.0 copy-start.3
  19.7 0.1 collective-permute-start.1
  19.8 1.3 %collective-permute-done.1 = bf16[2,256,128]{2,1,0:T(8,128)(2,1)S(1)} collective-permute-done((bf16[2,256,128]{2,1,0:T(8,128)(2,1)S(1)}, bf16[2,256,128]{2,1,0:T(8,128)(2,1)S(1)}, u32[]{:S(2)}, u32[]{:S(2)}) %collective-permute-start.1) | collective-permute-done | bytes 131104 | tf_op jit(solution)/shard_map/ppermute | solution.py:385
  21.1 0.0 copy-done.3
  21.2 2.3 %collective-permute-start.2 = (bf16[2,256,128]{2,1,0:T(8,128)(2,1)S(1)}, bf16[2,256,128]{2,1,0:T(8,128)(2,1)S(1)}, u32[]{:S(2)}, u32[]{:S(2)}) collective-permute-start(bf16[2,256,128]{2,1,0:T(8,128)(2,1)S(1)} %pad_maximum_fusion.refs_0_), channel_id=1, source_target_pairs={{2,0},{3,1},{0,2},{1,3},{6,4},{7,5},{4,6},{5,7},{10,8},{11,9},{8,1... | collective-permute-start | bytes 393224 | tf_op jit(solution)/shard_map/ppermute | solution.py:385
  23.5 3.6 %collective-permute-start.4 = (bf16[2,256,128]{2,1,0:T(8,128)(2,1)S(1)}, bf16[2,256,128]{2,1,0:T(8,128)(2,1)S(1)}, u32[]{:S(2)}, u32[]{:S(2)}) collective-permute-start(bf16[2,256,128]{2,1,0:T(8,128)(2,1)S(1)} %pad_maximum_fusion.1), channel_id=1, source_target_pairs={{2,0},{4,1},{9,2},{15,3},{0,4},{7,5},{11,6},{12,7},{3,8},{5,9},{8,... | collective-permute-start | bytes 393224 | tf_op jit(solution)/shard_map/ppermute | solution.py:385
  27.0 1.9 %collective-permute-start.3 = (bf16[2,256,128]{2,1,0:T(8,128)(2,1)S(1)}, bf16[2,256,128]{2,1,0:T(8,128)(2,1)S(1)}, u32[]{:S(2)}, u32[]{:S(2)}) collective-permute-start(bf16[2,256,128]{2,1,0:T(8,128)(2,1)S(1)} %pad_maximum_fusion.1), channel_id=1, source_target_pairs={{0,0},{6,1},{11,2},{13,3},{2,4},{5,5},{9,6},{14,7},{1,8},{7,9},{10... | collective-permute-start | bytes 393224 | tf_op jit(solution)/shard_map/ppermute | solution.py:385
  29.0 1.8 %shard_map.149.refs_5_ = f32[256,128]{1,0:T(8,128)} custom-call(bf16[256,128]{1,0:T(8,128)(2,1)} %copy-done.3, bf16[128,128]{1,0:T(8,128)(2,1)} %weight_ref.1), custom_call_target="tpu_custom_call" | custom-call | flops 8388608 | bytes 262144 | tf_op jit(solution)/shard_map/pallas_call | solution.py:265
  30.8 0.0 collective-permute-done.2.refs_1_
  30.8 0.0 collective-permute-done.4.refs_3_
  30.8 3.9 %collective-permute-done.3.refs_2_ = bf16[2,256,128]{2,1,0:T(8,128)(2,1)S(1)} collective-permute-done((bf16[2,256,128]{2,1,0:T(8,128)(2,1)S(1)}, bf16[2,256,128]{2,1,0:T(8,128)(2,1)S(1)}, u32[]{:S(2)}, u32[]{:S(2)}) %collective-permute-start.3) | collective-permute-done | bytes 131104 | tf_op jit(solution)/shard_map/ppermute | solution.py:385
  34.7 0.0 copy-done.5
  34.7 0.0 copy-done.6
  34.7 0.0 copy-done.11
  34.7 0.0 copy-start
  34.7 0.9 %copy-done = f32[256,128]{1,0:T(8,128)S(1)} copy-done((f32[256,128]{1,0:T(8,128)S(1)}, f32[256,128]{1,0:T(8,128)}, u32[]{:S(2)}) %copy-start) | copy-done | bytes 131096
  35.6 0.0 copy-start.4
  35.6 0.8 %copy-done.4 = bf16[256,128]{1,0:T(8,128)(2,1)S(1)} copy-done((bf16[256,128]{1,0:T(8,128)(2,1)S(1)}, bf16[256,128]{1,0:T(8,128)(2,1)}, u32[]{:S(2)}) %copy-start.4) | copy-done | bytes 65560
  36.5 2.2 %shard_map.150 = bf16[16,16,128]{2,1,0:T(8,128)(2,1)} custom-call(bf16[2,256,128]{2,1,0:T(8,128)(2,1)S(1)} %pad_maximum_fusion.refs_0_, bf16[2,256,128]{2,1,0:T(8,128)(2,1)S(1)} %collective-permute-done.2.refs_1_, bf16[2,256,128]{2,1,0:T(8,128)(2,1)S(1)} %collective-permute-done.3.refs_2_, bf16[2,256,128]{2,1,0:T(8,128)(2,1)S(1)} %collective-permute-done.4.refs_3_, ...), custom_call_target="tpu_custom_call" | custom-call | flops 134217728 | bytes 2097152 | tf_op jit(solution)/shard_map/pallas_call | solution.py:341
  (4 shorter events, 0.1 us)
Async XLA Ops:
  5.3 11.3 %copy-start.1 = (f32[32,32,128]{2,1,0:T(8,128)S(1)}, f32[32,32,128]{2,1,0:T(8,128)}, u32[]{:S(2)}) copy-start(f32[32,32,128]{2,1,0:T(8,128)} %proj_ref.1) | copy-start | bytes 1572868
  5.3 11.3 %copy-start.7 = (s32[256,64]{0,1:T(8,128)S(1)}, s32[256,64]{0,1:T(8,128)}, u32[]{:S(2)}) copy-start(s32[256,64]{0,1:T(8,128)} %param.16) | copy-start | bytes 196612
  5.3 11.3 %copy-start.8 = (bf16[16,16,128]{2,1,0:T(8,128)(2,1)S(1)}, bf16[16,16,128]{2,1,0:T(8,128)(2,1)}, u32[]{:S(2)}) copy-start(bf16[16,16,128]{2,1,0:T(8,128)(2,1)} %pair_ref.1) | copy-start | bytes 196612
  5.3 11.3 %copy-start.12 = (bf16[66,128]{1,0:T(8,128)(2,1)S(1)}, bf16[66,128]{1,0:T(8,128)(2,1)}, u32[]{:S(2)}) copy-start(bf16[66,128]{1,0:T(8,128)(2,1)} %table_ref.1) | copy-start | bytes 50692
  5.3 11.3 %copy-start.13 = (s32[64]{0:T(128)S(1)}, s32[64]{0:T(128)}, u32[]{:S(2)}) copy-start(s32[64]{0:T(128)} %param.18) | copy-start | bytes 772
  5.3 11.3 %copy-start.14 = (s32[64]{0:T(128)S(1)}, s32[64]{0:T(128)}, u32[]{:S(2)}) copy-start(s32[64]{0:T(128)} %param.19) | copy-start | bytes 772
  5.3 12.7 %collective-permute-start = (bf16[256,512]{1,0:T(8,128)(2,1)}, bf16[256,512]{1,0:T(8,128)(2,1)S(1)}, u32[]{:S(2)}, u32[]{:S(2)}) collective-permute-start(bf16[256,512]{1,0:T(8,128)(2,1)} %shard_map.147), channel_id=1, source_target_pairs={{0,0},{6,1},{11,2},{13,3},{2,4},{5,5},{9,6},{14,7},{1,8},{7,9},{10... | collective-permute-start | bytes 786440 | tf_op jit(solution)/shard_map/ppermute | solution.py:385
  11.1 7.0 %copy-start.9 = (bf16[128,256]{1,0:T(8,128)(2,1)S(1)}, bf16[128,256]{1,0:T(8,128)(2,1)}, u32[]{:S(2)}) copy-start(bf16[128,256]{1,0:T(8,128)(2,1)} %refs_5_.1) | copy-start | bytes 196612
  11.1 7.0 %copy-start.10 = (bf16[128,256]{1,0:T(8,128)(2,1)S(1)}, bf16[128,256]{1,0:T(8,128)(2,1)}, u32[]{:S(2)}) copy-start(bf16[128,256]{1,0:T(8,128)(2,1)} %refs_6_.2) | copy-start | bytes 196612
  11.1 23.6 %copy-start.5 = (bf16[128,512]{1,0:T(8,128)(2,1)S(1)}, bf16[128,512]{1,0:T(8,128)(2,1)}, u32[]{:S(2)}) copy-start(bf16[128,512]{1,0:T(8,128)(2,1)} %refs_7_.1) | copy-start | bytes 393220
  11.1 23.6 %copy-start.6 = (bf16[512,128]{1,0:T(8,128)(2,1)S(1)}, bf16[512,128]{1,0:T(8,128)(2,1)}, u32[]{:S(2)}) copy-start(bf16[512,128]{1,0:T(8,128)(2,1)} %refs_8_.1) | copy-start | bytes 393220
  11.1 23.6 %copy-start.11 = (bf16[128,128]{1,0:T(8,128)(2,1)S(1)}, bf16[128,128]{1,0:T(8,128)(2,1)}, u32[]{:S(2)}) copy-start(bf16[128,128]{1,0:T(8,128)(2,1)} %refs_6_.3) | copy-start | bytes 98308
  16.6 1.0 %copy-start.2 = (bf16[256,512]{1,0:T(8,128)(2,1)S(1)}, bf16[256,512]{1,0:T(8,128)(2,1)}, u32[]{:S(2)}) copy-start(bf16[256,512]{1,0:T(8,128)(2,1)} %shard_map.145.zl_ref) | copy-start | bytes 786436
  19.7 1.4 %copy-start.3 = (bf16[256,128]{1,0:T(8,128)(2,1)}, bf16[256,128]{1,0:T(8,128)(2,1)S(1)}, u32[]{:S(2)}) copy-start(bf16[256,128]{1,0:T(8,128)(2,1)S(1)} %get-tuple-element.18.one_ref.refs_4_) | copy-start | bytes 196612
  19.7 1.4 %collective-permute-start.1 = (bf16[2,256,128]{2,1,0:T(8,128)(2,1)S(1)}, bf16[2,256,128]{2,1,0:T(8,128)(2,1)S(1)}, u32[]{:S(2)}, u32[]{:S(2)}) collective-permute-start(bf16[2,256,128]{2,1,0:T(8,128)(2,1)S(1)} %get-tuple-element.17), channel_id=1, source_target_pairs={{1,0},{0,1},{3,2},{2,3},{5,4},{4,5},{7,6},{6,7},{9,8},{8,9},{11,10... | collective-permute-start | bytes 393224 | tf_op jit(solution)/shard_map/ppermute | solution.py:385
  21.2 9.6 %collective-permute-start.2 = (bf16[2,256,128]{2,1,0:T(8,128)(2,1)S(1)}, bf16[2,256,128]{2,1,0:T(8,128)(2,1)S(1)}, u32[]{:S(2)}, u32[]{:S(2)}) collective-permute-start(bf16[2,256,128]{2,1,0:T(8,128)(2,1)S(1)} %pad_maximum_fusion.refs_0_), channel_id=1, source_target_pairs={{2,0},{3,1},{0,2},{1,3},{6,4},{7,5},{4,6},{5,7},{10,8},{11,9},{8,1... | collective-permute-start | bytes 393224 | tf_op jit(solution)/shard_map/ppermute | solution.py:385
  23.5 7.3 %collective-permute-start.4 = (bf16[2,256,128]{2,1,0:T(8,128)(2,1)S(1)}, bf16[2,256,128]{2,1,0:T(8,128)(2,1)S(1)}, u32[]{:S(2)}, u32[]{:S(2)}) collective-permute-start(bf16[2,256,128]{2,1,0:T(8,128)(2,1)S(1)} %pad_maximum_fusion.1), channel_id=1, source_target_pairs={{2,0},{4,1},{9,2},{15,3},{0,4},{7,5},{11,6},{12,7},{3,8},{5,9},{8,... | collective-permute-start | bytes 393224 | tf_op jit(solution)/shard_map/ppermute | solution.py:385
  27.0 7.7 %collective-permute-start.3 = (bf16[2,256,128]{2,1,0:T(8,128)(2,1)S(1)}, bf16[2,256,128]{2,1,0:T(8,128)(2,1)S(1)}, u32[]{:S(2)}, u32[]{:S(2)}) collective-permute-start(bf16[2,256,128]{2,1,0:T(8,128)(2,1)S(1)} %pad_maximum_fusion.1), channel_id=1, source_target_pairs={{0,0},{6,1},{11,2},{13,3},{2,4},{5,5},{9,6},{14,7},{1,8},{7,9},{10... | collective-permute-start | bytes 393224 | tf_op jit(solution)/shard_map/ppermute | solution.py:385
  34.7 0.9 %copy-start = (f32[256,128]{1,0:T(8,128)S(1)}, f32[256,128]{1,0:T(8,128)}, u32[]{:S(2)}) copy-start(f32[256,128]{1,0:T(8,128)} %shard_map.149.refs_5_) | copy-start | bytes 393220
  35.6 0.8 %copy-start.4 = (bf16[256,128]{1,0:T(8,128)(2,1)S(1)}, bf16[256,128]{1,0:T(8,128)(2,1)}, u32[]{:S(2)}) copy-start(bf16[256,128]{1,0:T(8,128)(2,1)} %copy-done.3) | copy-start | bytes 196612

commit v6 on v5

--- a/solution.py
+++ b/solution.py
@@ -10,6 +10,7 @@
 REL_CLIP = 32
 LANES = 128
 PIECE = 16
+STEPS = 4
 EPSILON = 1e-05
 BF16 = jnp.bfloat16
 F32 = jnp.float32
@@ -44,71 +45,74 @@
     return pl.BlockSpec(memory_space=pltpu.VMEM)
 
 
-def factor_kernel(x_ref, mask_ref, weight_ref, z_ref, w_scr, live_scr, gather_scr, y_scr):
-    seqs, rows, channels = x_ref.shape
+def over(index, size):
+    return lax.shift_right_logical(index, size.bit_length() - 1)
+
+
+def within(index, size):
+    return lax.bitwise_and(index, size - 1)
+
+
+def factor_kernel(x_any, mask_ref, weight_ref, z_ref, x_scr, y_scr, sems):
+    seqs, rows, channels = x_scr.shape
     hidden = weight_ref.shape[0]
     rep = LANES // hidden
     groups = rows // rep
     residues = mask_ref.shape[0]
     width = rows * hidden
-    step = pl.program_id(0)
-
-    @pl.when(step == 0)
-    def _():
-        w_scr[:, :LANES] = jnp.concatenate([weight_ref[...]] * rep, axis=0).T
-        w_scr[:, LANES:] = jnp.ones((channels, LANES), BF16)
-        start = lax.axis_index("dap") * rows
-        spread = iota((residues, width), 0) == start + iota((residues, width), 1) // hidden
-        live_scr[...] = dot_tn(mask_ref[...].astype(BF16), spread.astype(BF16))
-        to, at = iota(gather_scr.shape, 0), iota(gather_scr.shape, 1)
-        same = (to % PIECE == at // rows) & (to // PIECE == (at % rows) // rep)
-        gather_scr[...] = same.astype(BF16)
-
-    w = w_scr[...]
+    step = seqs // STEPS
+    copies = []
+    for turn in range(STEPS):
+        part = pl.ds(turn * step, step)
+        copies.append(pltpu.make_async_copy(x_any.at[part], x_scr.at[part], sems.at[turn]))
+        copies[-1].start()
+    weight = jnp.concatenate([weight_ref[...]] * rep, axis=0).T
+    w = jnp.concatenate([weight, jnp.ones((channels, LANES), BF16)], axis=1)
     sums = dot(jnp.ones((8, channels), BF16), w)[:1, :LANES]
-    x = x_ref[...].reshape(seqs * rows, channels)
-    y = dot(x, w)
-    mean = y[:, LANES:] * (1.0 / channels)
-    xf = x.astype(F32)
-    square = jnp.zeros_like(mean)
-    for part in range(channels // LANES):
-        centered = xf[:, part * LANES : (part + 1) * LANES] - mean
-        square = square + centered * centered
-    spread = dot(square.astype(BF16), jnp.ones((LANES, LANES), BF16))
-    own = (iota(mean.shape, 1) // hidden == iota(mean.shape, 0) % rep).astype(F32)
-    scale = lax.rsqrt(spread * (1.0 / channels) + EPSILON) * own
-    y_scr[...] = ((y[:, :LANES] - mean * sums) * scale).astype(BF16)
-    for piece in range(seqs // PIECE):
-        z = dot(gather_scr[...], y_scr[piece * PIECE * rows : (piece + 1) * PIECE * rows, :])
-        here = slice(piece * PIECE, (piece + 1) * PIECE)
-        whole = pl.ds(pl.multiple_of(step * seqs + piece * PIECE, PIECE), PIECE)
-        for group in range(groups):
-            lanes = slice(group * LANES, (group + 1) * LANES)
-            part = z[group * PIECE : (group + 1) * PIECE]
-            z_ref[here, lanes] = (part * live_scr[whole, lanes]).astype(BF16)
+    start = lax.axis_index("dap") * rows
+    spread = iota((residues, width), 0) == start + over(iota((residues, width), 1), hidden)
+    live = dot_tn(mask_ref[...].astype(BF16), spread.astype(BF16))
+    to, at = iota((groups * PIECE, PIECE * rows), 0), iota((groups * PIECE, PIECE * rows), 1)
+    gather = within(to, PIECE) == over(at, rows)
+    gather = (gather & (over(to, PIECE) == over(within(at, rows), rep))).astype(BF16)
+    own = over(iota((8, LANES), 1), hidden) == within(iota((8, LANES), 0), rep)
+    own = own.astype(F32)
+    ones = jnp.ones((LANES, LANES), BF16)
+    for turn in range(STEPS):
+        copies[turn].wait()
+        x = x_scr[turn * step : (turn + 1) * step].reshape(step * rows, channels)
+        y = dot(x, w)
+        mean = y[:, LANES:] * (1.0 / channels)
+        xf = x.astype(F32)
+        square = jnp.zeros_like(mean)
+        for part in range(channels // LANES):
+            centered = xf[:, part * LANES : (part + 1) * LANES] - mean
+            square = square + centered * centered
+        spread = dot(square.astype(BF16), ones)
+        scale = lax.rsqrt(spread * (1.0 / channels) + EPSILON).reshape(-1, 8, LANES) * own[None]
+        scaled = (y[:, :LANES] - mean * sums) * scale.reshape(mean.shape)
+        y_scr[turn * step * rows : (turn + 1) * step * rows, :] = scaled.astype(BF16)
+        for piece in range(turn * step // PIECE, (turn + 1) * step // PIECE):
+            z = dot(gather, y_scr[piece * PIECE * rows : (piece + 1) * PIECE * rows, :])
+            here = slice(piece * PIECE, (piece + 1) * PIECE)
+            for group in range(groups):
+                lanes = slice(group * LANES, (group + 1) * LANES)
+                part = z[group * PIECE : (group + 1) * PIECE]
+                z_ref[here, lanes] = (part * live[here, lanes]).astype(BF16)
 
 
 def factor(alignment, mask, weight):
     seqs, rows, channels = alignment.shape
-    residues = mask.shape[0]
     hidden = weight.shape[0]
-    step = seqs // 4
-    width = rows * hidden
     return pl.pallas_call(
         factor_kernel,
-        out_shape=jax.ShapeDtypeStruct((seqs, width), BF16),
-        grid=(seqs // step,),
-        in_specs=[
-            pl.BlockSpec((step, rows, channels), lambda s: (s, 0, 0)),
-            pl.BlockSpec((residues, seqs), lambda s: (0, 0)),
-            pl.BlockSpec((hidden, channels), lambda s: (0, 0)),
-        ],
-        out_specs=pl.BlockSpec((step, width), lambda s: (s, 0)),
+        out_shape=jax.ShapeDtypeStruct((seqs, rows * hidden), BF16),
+        in_specs=[pl.BlockSpec(memory_space=pl.ANY), vmem(), vmem()],
+        out_specs=vmem(),
         scratch_shapes=[
-            pltpu.VMEM((channels, 2 * LANES), BF16),
-            pltpu.VMEM((seqs, width), F32),
-            pltpu.VMEM((rows * hidden // LANES * PIECE, PIECE * rows), BF16),
-            pltpu.VMEM((step * rows, LANES), BF16),
+            pltpu.VMEM(alignment.shape, BF16),
+            pltpu.VMEM((seqs * rows, LANES), BF16),
+            pltpu.SemaphoreType.DMA((STEPS,)),
         ],
         compiler_params=pltpu.CompilerParams(vmem_limit_bytes=119 << 19),
         cost_estimate=pl.CostEstimate(
@@ -131,8 +135,8 @@
     proj_out_ref[...] = proj_ref[...].reshape(proj_out_ref.shape).astype(BF16)
     which = iota((pairs, residues), 0)
     place = iota((pairs, residues), 1)
-    pick_row = (place == row_start + which % rows).astype(BF16)
-    pick_col = (place == col_start + which // rows).astype(BF16)
+    pick_row = (place == row_start + within(which, rows)).astype(BF16)
+    pick_col = (place == col_start + over(which, rows)).astype(BF16)
     mask = mask_ref[...].astype(BF16)
     both = (dot(pick_row, mask) * dot(pick_col, mask)).astype(BF16)
     counts = dot(both, jnp.ones((mask.shape[1], LANES), BF16))
@@ -142,7 +146,7 @@
     live_out_ref[...] = dot_nt(pick_row, live) * dot_nt(pick_col, live)
     same = dot_nt(pick_row, chain) == dot_nt(pick_col, chain)
     pair = iota((pairs, LANES), 0)
-    offset = (row_start + pair % rows) - (col_start + pair // rows) + REL_CLIP
+    offset = (row_start + within(pair, rows)) - (col_start + over(pair, rows)) + REL_CLIP
     bucket = jnp.where(same, jnp.clip(offset, 0, 2 * REL_CLIP), 2 * REL_CLIP + 1)
     table_scr[...] = jnp.zeros_like(table_scr)
     table_scr[pl.ds(0, classes), :] = table_ref[...].astype(F32)
@@ -267,6 +271,7 @@
         out_shape=jax.ShapeDtypeStruct(one.shape, F32),
         in_specs=[vmem()] * 2,
         out_specs=vmem(),
+        compiler_params=pltpu.CompilerParams(vmem_limit_bytes=4 << 20),
         cost_estimate=pl.CostEstimate(
             flops=2 * one.size * LANES, bytes_accessed=1 << 18, transcendentals=one.size
         ),

time: 39.1 us -> 37.5 us (0.959)
  local copies, waits for them, and re-layouts: 2.77 us -> 1.04 us
  waiting for transfers between devices: 5.26 us -> 6.86 us
  Pallas kernels: 16.8 us -> 15.7 us
    unnamed x30 -> x26, local copies, waits for them, and re-layouts: 2.75 us -> 1.02 us
    ppermute x5, waiting for transfers between devices: 5.26 us -> 6.86 us  [fetch(): return lax.ppermute(values, ('dap', 'sub'), perm)]
    pallas_call x1, Pallas kernels: 1.82 us -> 0.32 us  [output_gate(): pl.pallas_call(gate_kernel, out_shape=jax.ShapeDtypeStruct(one.shape, F32...]
  transfers between devices with their start and end apart: 5 -> 5, of which waited for: 2 -> 3; matrix products, arithmetic and copies ran while one was open for 0% -> 0% of each run, Pallas kernels for 20% -> 17%
where the time goes in v6:
time: 37.5 us; the launch traced here: 37.3 us
  Pallas kernels  15.7 us (42%)
  starting transfers between devices  13.4 us (36%)
  waiting for transfers between devices  6.86 us (18%)
  local copies, waits for them, and re-layouts  1.04 us (3%)
    ppermute x5, starting transfers between devices, fetch(): return lax.ppermute(values, ('dap', 'sub'), perm)  13.4 us
    pallas_call x2, Pallas kernels, factor(): pl.pallas_call(factor_kernel, out_shape=jax.ShapeDtypeStruct((seqs, rows...  11 us
    ppermute x5, waiting for transfers between devices, fetch(): return lax.ppermute(values, ('dap', 'sub'), perm)  6.86 us
    pallas_call x1, Pallas kernels, triangle_update(): pl.pallas_call(functools.partial(triangle_kernel, subs, ratio, cols), out...  2.21 us
    pallas_call x1, Pallas kernels, pair_update(): pl.pallas_call(functools.partial(pair_kernel, ratio, hidden), out_shape=(...  1.61 us
    unnamed x26, local copies, waits for them, and re-layouts  1.02 us
  transfers between devices with their start and end apart: 5, of which 3 were waited for; matrix products, arithmetic and copies ran while one was open for 0% of the time, Pallas kernels for 17%

profile of v6, /device:TPU:1, one launch (start us, length us, event | category | flops | bytes accessed | tf_op | source)
XLA Modules:
  0.0 37.3 jit_solution(8705733021369665077)
XLA Ops:
  0.0 5.5 %shard_map.147 = bf16[256,512]{1,0:T(8,128)(2,1)} custom-call(bf16[256,16,256]{2,1,0:T(8,128)(2,1)} %x_any.3, s32[64,256]{1,0:T(8,128)} %bitcast.5, bf16[32,256]{1,0:T(8,128)(2,1)} %bitcast.10), custom_call_target="tpu_custom_call" | custom-call | flops 1073741824 | bytes 4194304 | tf_op jit(solution)/shard_map/pallas_call | solution.py:107
  5.5 0.0 copy-start
  5.5 0.0 copy-start.4
  5.5 0.0 copy-start.5
  5.5 0.0 copy-start.10
  5.5 0.0 copy-start.11
  5.5 0.0 copy-start.12
  5.6 5.7 %collective-permute-start = (bf16[256,512]{1,0:T(8,128)(2,1)}, bf16[256,512]{1,0:T(8,128)(2,1)S(1)}, u32[]{:S(2)}, u32[]{:S(2)}) collective-permute-start(bf16[256,512]{1,0:T(8,128)(2,1)} %shard_map.147), channel_id=1, source_target_pairs={{0,0},{6,1},{11,2},{13,3},{2,4},{5,5},{9,6},{14,7},{1,8},{7,9},{10... | collective-permute-start | bytes 786440 | tf_op jit(solution)/shard_map/ppermute | solution.py:390
  11.3 0.0 copy-start.6
  11.3 0.0 copy-start.7
  11.3 0.0 copy-start.8
  11.3 0.0 copy-start.2
  11.4 0.0 copy-start.3
  11.4 0.0 copy-start.9
  11.4 5.6 %shard_map.145.zl_ref = bf16[256,512]{1,0:T(8,128)(2,1)} custom-call(bf16[256,16,256]{2,1,0:T(8,128)(2,1)} %x_any.3, s32[64,256]{1,0:T(8,128)} %bitcast.6, bf16[32,256]{1,0:T(8,128)(2,1)} %bitcast.11), custom_call_target="tpu_custom_call" | custom-call | flops 1073741824 | bytes 4194304 | tf_op jit(solution)/shard_map/pallas_call | solution.py:107
  16.9 0.0 copy-done
  17.0 0.0 copy-done.4
  17.0 0.0 copy-done.5
  17.0 0.0 copy-done.10
  17.0 0.0 copy-done.11
  17.0 0.0 copy-done.12
  17.0 0.0 copy-start.1
  17.0 0.9 %copy-done.1 = bf16[256,512]{1,0:T(8,128)(2,1)S(1)} copy-done((bf16[256,512]{1,0:T(8,128)(2,1)S(1)}, bf16[256,512]{1,0:T(8,128)(2,1)}, u32[]{:S(2)}) %copy-start.1) | copy-done | bytes 262168
  18.0 0.5 %shard_map.146 = (bf16[512,256]{1,0:T(8,128)(2,1)S(1)}, f32[256,128]{1,0:T(8,128)S(1)}, f32[256,128]{1,0:T(8,128)S(1)}, f32[256,128]{1,0:T(8,128)S(1)}, bf16[1024,128]{1,0:T(8,128)(2,1)S(1)}) custom-call(bf16[256,512]{1,0:T(8,128)(2,1)S(1)} %copy-done.1, s32[64,256]{1,0:T(8,128)S(1)} %bitcast.7, bf16[16,16,128]{2,1,0:T(8,128)(2,1)S(1)} %copy-done.5, ...), custom_call_target="tpu_custom_call" | custom-call | flops 134217728 | bytes 2097152 | tf_op jit(solution)/shard_map/pallas_call | solution.py:166
  18.5 0.0 collective-permute-done.refs_0_
  18.5 0.0 copy-done.6
  18.5 0.0 copy-done.7
  18.5 1.6 %shard_map.148 = (bf16[2,256,128]{2,1,0:T(8,128)(2,1)S(1)}, bf16[256,128]{1,0:T(8,128)(2,1)S(1)}) custom-call(bf16[512,256]{1,0:T(8,128)(2,1)S(1)} %get-tuple-element.12.zlt_ref, bf16[256,512]{1,0:T(8,128)(2,1)S(1)} %collective-permute-done.refs_0_, f32[256,128]{1,0:T(8,128)S(1)} %get-tuple-element.13.refs_1_, f32[256,128]{1,0:T(8,128)S(1)} %get-tuple-element.14.refs_2_, ...), custom_call_target="tpu_custom_call" | custom-call | flops 268435456 | bytes 2097152 | tf_op jit(solution)/shard_map/pallas_call | solution.py:242
  20.1 0.1 collective-permute-start.1
  20.2 1.3 %collective-permute-done.1 = bf16[2,256,128]{2,1,0:T(8,128)(2,1)S(1)} collective-permute-done((bf16[2,256,128]{2,1,0:T(8,128)(2,1)S(1)}, bf16[2,256,128]{2,1,0:T(8,128)(2,1)S(1)}, u32[]{:S(2)}, u32[]{:S(2)}) %collective-permute-start.1) | collective-permute-done | bytes 131104 | tf_op jit(solution)/shard_map/ppermute | solution.py:390
  21.6 2.3 %collective-permute-start.2 = (bf16[2,256,128]{2,1,0:T(8,128)(2,1)S(1)}, bf16[2,256,128]{2,1,0:T(8,128)(2,1)S(1)}, u32[]{:S(2)}, u32[]{:S(2)}) collective-permute-start(bf16[2,256,128]{2,1,0:T(8,128)(2,1)S(1)} %pad_maximum_fusion.refs_0_), channel_id=1, source_target_pairs={{2,0},{3,1},{0,2},{1,3},{6,4},{7,5},{4,6},{5,7},{10,8},{11,9},{8,1... | collective-permute-start | bytes 393224 | tf_op jit(solution)/shard_map/ppermute | solution.py:390
  23.8 3.4 %collective-permute-start.4 = (bf16[2,256,128]{2,1,0:T(8,128)(2,1)S(1)}, bf16[2,256,128]{2,1,0:T(8,128)(2,1)S(1)}, u32[]{:S(2)}, u32[]{:S(2)}) collective-permute-start(bf16[2,256,128]{2,1,0:T(8,128)(2,1)S(1)} %pad_maximum_fusion.1), channel_id=1, source_target_pairs={{2,0},{4,1},{9,2},{15,3},{0,4},{7,5},{11,6},{12,7},{3,8},{5,9},{8,... | collective-permute-start | bytes 393224 | tf_op jit(solution)/shard_map/ppermute | solution.py:390
  27.2 1.9 %collective-permute-start.3 = (bf16[2,256,128]{2,1,0:T(8,128)(2,1)S(1)}, bf16[2,256,128]{2,1,0:T(8,128)(2,1)S(1)}, u32[]{:S(2)}, u32[]{:S(2)}) collective-permute-start(bf16[2,256,128]{2,1,0:T(8,128)(2,1)S(1)} %pad_maximum_fusion.1), channel_id=1, source_target_pairs={{0,0},{6,1},{11,2},{13,3},{2,4},{5,5},{9,6},{14,7},{1,8},{7,9},{10... | collective-permute-start | bytes 393224 | tf_op jit(solution)/shard_map/ppermute | solution.py:390
  29.1 0.0 copy-done.8
  29.2 0.3 shard_map.149.refs_5_
  29.5 0.0 collective-permute-done.2.refs_1_
  29.5 0.2 collective-permute-done.4.refs_3_
  29.7 5.3 %collective-permute-done.3.refs_2_ = bf16[2,256,128]{2,1,0:T(8,128)(2,1)S(1)} collective-permute-done((bf16[2,256,128]{2,1,0:T(8,128)(2,1)S(1)}, bf16[2,256,128]{2,1,0:T(8,128)(2,1)S(1)}, u32[]{:S(2)}, u32[]{:S(2)}) %collective-permute-start.3) | collective-permute-done | bytes 131104 | tf_op jit(solution)/shard_map/ppermute | solution.py:390
  35.0 0.0 copy-done.2
  35.0 0.0 copy-done.3
  35.0 0.0 copy-done.9
  35.0 2.2 %shard_map.150 = bf16[16,16,128]{2,1,0:T(8,128)(2,1)} custom-call(bf16[2,256,128]{2,1,0:T(8,128)(2,1)S(1)} %pad_maximum_fusion.refs_0_, bf16[2,256,128]{2,1,0:T(8,128)(2,1)S(1)} %collective-permute-done.2.refs_1_, bf16[2,256,128]{2,1,0:T(8,128)(2,1)S(1)} %collective-permute-done.3.refs_2_, bf16[2,256,128]{2,1,0:T(8,128)(2,1)S(1)} %collective-permute-done.4.refs_3_, ...), custom_call_target="tpu_custom_call" | custom-call | flops 134217728 | bytes 2097152 | tf_op jit(solution)/shard_map/pallas_call | solution.py:346
  (4 shorter events, 0.1 us)
Async XLA Ops:
  5.5 11.5 %copy-start = (f32[32,32,128]{2,1,0:T(8,128)S(1)}, f32[32,32,128]{2,1,0:T(8,128)}, u32[]{:S(2)}) copy-start(f32[32,32,128]{2,1,0:T(8,128)} %proj_ref.1) | copy-start | bytes 1572868
  5.5 11.5 %copy-start.4 = (s32[256,64]{0,1:T(8,128)S(1)}, s32[256,64]{0,1:T(8,128)}, u32[]{:S(2)}) copy-start(s32[256,64]{0,1:T(8,128)} %param.16) | copy-start | bytes 196612
  5.5 11.5 %copy-start.5 = (bf16[16,16,128]{2,1,0:T(8,128)(2,1)S(1)}, bf16[16,16,128]{2,1,0:T(8,128)(2,1)}, u32[]{:S(2)}) copy-start(bf16[16,16,128]{2,1,0:T(8,128)(2,1)} %pair_ref.1) | copy-start | bytes 196612
  5.5 11.5 %copy-start.10 = (bf16[66,128]{1,0:T(8,128)(2,1)S(1)}, bf16[66,128]{1,0:T(8,128)(2,1)}, u32[]{:S(2)}) copy-start(bf16[66,128]{1,0:T(8,128)(2,1)} %table_ref.1) | copy-start | bytes 50692
  5.5 11.5 %copy-start.11 = (s32[64]{0:T(128)S(1)}, s32[64]{0:T(128)}, u32[]{:S(2)}) copy-start(s32[64]{0:T(128)} %param.18) | copy-start | bytes 772
  5.5 11.5 %copy-start.12 = (s32[64]{0:T(128)S(1)}, s32[64]{0:T(128)}, u32[]{:S(2)}) copy-start(s32[64]{0:T(128)} %param.19) | copy-start | bytes 772
  5.6 12.9 %collective-permute-start = (bf16[256,512]{1,0:T(8,128)(2,1)}, bf16[256,512]{1,0:T(8,128)(2,1)S(1)}, u32[]{:S(2)}, u32[]{:S(2)}) collective-permute-start(bf16[256,512]{1,0:T(8,128)(2,1)} %shard_map.147), channel_id=1, source_target_pairs={{0,0},{6,1},{11,2},{13,3},{2,4},{5,5},{9,6},{14,7},{1,8},{7,9},{10... | collective-permute-start | bytes 786440 | tf_op jit(solution)/shard_map/ppermute | solution.py:390
  11.3 7.2 %copy-start.6 = (bf16[128,256]{1,0:T(8,128)(2,1)S(1)}, bf16[128,256]{1,0:T(8,128)(2,1)}, u32[]{:S(2)}) copy-start(bf16[128,256]{1,0:T(8,128)(2,1)} %refs_5_.1) | copy-start | bytes 196612
  11.3 7.2 %copy-start.7 = (bf16[128,256]{1,0:T(8,128)(2,1)S(1)}, bf16[128,256]{1,0:T(8,128)(2,1)}, u32[]{:S(2)}) copy-start(bf16[128,256]{1,0:T(8,128)(2,1)} %refs_6_.2) | copy-start | bytes 196612
  11.3 17.8 %copy-start.8 = (bf16[128,128]{1,0:T(8,128)(2,1)S(1)}, bf16[128,128]{1,0:T(8,128)(2,1)}, u32[]{:S(2)}) copy-start(bf16[128,128]{1,0:T(8,128)(2,1)} %weight_ref.1) | copy-start | bytes 98308
  11.3 23.7 %copy-start.2 = (bf16[128,512]{1,0:T(8,128)(2,1)S(1)}, bf16[128,512]{1,0:T(8,128)(2,1)}, u32[]{:S(2)}) copy-start(bf16[128,512]{1,0:T(8,128)(2,1)} %refs_7_.1) | copy-start | bytes 393220
  11.4 23.7 %copy-start.3 = (bf16[512,128]{1,0:T(8,128)(2,1)S(1)}, bf16[512,128]{1,0:T(8,128)(2,1)}, u32[]{:S(2)}) copy-start(bf16[512,128]{1,0:T(8,128)(2,1)} %refs_8_.1) | copy-start | bytes 393220
  11.4 23.7 %copy-start.9 = (bf16[128,128]{1,0:T(8,128)(2,1)S(1)}, bf16[128,128]{1,0:T(8,128)(2,1)}, u32[]{:S(2)}) copy-start(bf16[128,128]{1,0:T(8,128)(2,1)} %refs_6_.3) | copy-start | bytes 98308
  17.0 1.0 %copy-start.1 = (bf16[256,512]{1,0:T(8,128)(2,1)S(1)}, bf16[256,512]{1,0:T(8,128)(2,1)}, u32[]{:S(2)}) copy-start(bf16[256,512]{1,0:T(8,128)(2,1)} %shard_map.145.zl_ref) | copy-start | bytes 786436
  20.1 1.4 %collective-permute-start.1 = (bf16[2,256,128]{2,1,0:T(8,128)(2,1)S(1)}, bf16[2,256,128]{2,1,0:T(8,128)(2,1)S(1)}, u32[]{:S(2)}, u32[]{:S(2)}) collective-permute-start(bf16[2,256,128]{2,1,0:T(8,128)(2,1)S(1)} %get-tuple-element.17), channel_id=1, source_target_pairs={{1,0},{0,1},{3,2},{2,3},{5,4},{4,5},{7,6},{6,7},{9,8},{8,9},{11,10... | collective-permute-start | bytes 393224 | tf_op jit(solution)/shard_map/ppermute | solution.py:390
  21.6 7.9 %collective-permute-start.2 = (bf16[2,256,128]{2,1,0:T(8,128)(2,1)S(1)}, bf16[2,256,128]{2,1,0:T(8,128)(2,1)S(1)}, u32[]{:S(2)}, u32[]{:S(2)}) collective-permute-start(bf16[2,256,128]{2,1,0:T(8,128)(2,1)S(1)} %pad_maximum_fusion.refs_0_), channel_id=1, source_target_pairs={{2,0},{3,1},{0,2},{1,3},{6,4},{7,5},{4,6},{5,7},{10,8},{11,9},{8,1... | collective-permute-start | bytes 393224 | tf_op jit(solution)/shard_map/ppermute | solution.py:390
  23.8 5.9 %collective-permute-start.4 = (bf16[2,256,128]{2,1,0:T(8,128)(2,1)S(1)}, bf16[2,256,128]{2,1,0:T(8,128)(2,1)S(1)}, u32[]{:S(2)}, u32[]{:S(2)}) collective-permute-start(bf16[2,256,128]{2,1,0:T(8,128)(2,1)S(1)} %pad_maximum_fusion.1), channel_id=1, source_target_pairs={{2,0},{4,1},{9,2},{15,3},{0,4},{7,5},{11,6},{12,7},{3,8},{5,9},{8,... | collective-permute-start | bytes 393224 | tf_op jit(solution)/shard_map/ppermute | solution.py:390
  27.2 7.8 %collective-permute-start.3 = (bf16[2,256,128]{2,1,0:T(8,128)(2,1)S(1)}, bf16[2,256,128]{2,1,0:T(8,128)(2,1)S(1)}, u32[]{:S(2)}, u32[]{:S(2)}) collective-permute-start(bf16[2,256,128]{2,1,0:T(8,128)(2,1)S(1)} %pad_maximum_fusion.1), channel_id=1, source_target_pairs={{0,0},{6,1},{11,2},{13,3},{2,4},{5,5},{9,6},{14,7},{1,8},{7,9},{10... | collective-permute-start | bytes 393224 | tf_op jit(solution)/shard_map/ppermute | solution.py:390

commit v7 on v6

--- a/solution.py
+++ b/solution.py
@@ -54,8 +54,8 @@
 
 
 def factor_kernel(x_any, mask_ref, weight_ref, z_ref, x_scr, y_scr, sems):
-    seqs, rows, channels = x_scr.shape
-    hidden = weight_ref.shape[0]
+    halves, seqs, rows, _ = x_scr.shape
+    hidden, channels = weight_ref.shape
     rep = LANES // hidden
     groups = rows // rep
     residues = mask_ref.shape[0]
@@ -64,8 +64,10 @@
     copies = []
     for turn in range(STEPS):
         part = pl.ds(turn * step, step)
-        copies.append(pltpu.make_async_copy(x_any.at[part], x_scr.at[part], sems.at[turn]))
-        copies[-1].start()
+        for half in range(halves):
+            source = x_any.at[part, :, pl.ds(half * LANES, LANES)]
+            copies.append(pltpu.make_async_copy(source, x_scr.at[half, part], sems.at[turn, half]))
+            copies[-1].start()
     weight = jnp.concatenate([weight_ref[...]] * rep, axis=0).T
     w = jnp.concatenate([weight, jnp.ones((channels, LANES), BF16)], axis=1)
     sums = dot(jnp.ones((8, channels), BF16), w)[:1, :LANES]
@@ -79,14 +81,15 @@
     own = own.astype(F32)
     ones = jnp.ones((LANES, LANES), BF16)
     for turn in range(STEPS):
-        copies[turn].wait()
-        x = x_scr[turn * step : (turn + 1) * step].reshape(step * rows, channels)
-        y = dot(x, w)
+        x = []
+        for half in range(halves):
+            copies[turn * halves + half].wait()
+            x.append(x_scr[half, turn * step : (turn + 1) * step].reshape(step * rows, LANES))
+        y = dot(jnp.concatenate(x, axis=1), w)
         mean = y[:, LANES:] * (1.0 / channels)
-        xf = x.astype(F32)
         square = jnp.zeros_like(mean)
-        for part in range(channels // LANES):
-            centered = xf[:, part * LANES : (part + 1) * LANES] - mean
+        for half in range(halves):
+            centered = x[half].astype(F32) - mean
             square = square + centered * centered
         spread = dot(square.astype(BF16), ones)
         scale = lax.rsqrt(spread * (1.0 / channels) + EPSILON).reshape(-1, 8, LANES) * own[None]
@@ -98,7 +101,7 @@
             for group in range(groups):
                 lanes = slice(group * LANES, (group + 1) * LANES)
                 part = z[group * PIECE : (group + 1) * PIECE]
-                z_ref[here, lanes] = (part * live[here, lanes]).astype(BF16)
+                z_ref[group, here, :] = (part * live[here, lanes]).astype(BF16)
 
 
 def factor(alignment, mask, weight):
@@ -106,13 +109,13 @@
     hidden = weight.shape[0]
     return pl.pallas_call(
         factor_kernel,
-        out_shape=jax.ShapeDtypeStruct((seqs, rows * hidden), BF16),
+        out_shape=jax.ShapeDtypeStruct((rows * hidden // LANES, seqs, LANES), BF16),
         in_specs=[pl.BlockSpec(memory_space=pl.ANY), vmem(), vmem()],
         out_specs=vmem(),
         scratch_shapes=[
-            pltpu.VMEM(alignment.shape, BF16),
+            pltpu.VMEM((channels // LANES, seqs, rows, LANES), BF16),
             pltpu.VMEM((seqs * rows, LANES), BF16),
-            pltpu.SemaphoreType.DMA((STEPS,)),
+            pltpu.SemaphoreType.DMA((STEPS, channels // LANES)),
         ],
         compiler_params=pltpu.CompilerParams(vmem_limit_bytes=119 << 19),
         cost_estimate=pl.CostEstimate(
@@ -131,7 +134,11 @@
     classes = table_ref.shape[0]
     row_start = lax.axis_index("dap") * rows
     col_start = lax.axis_index("sub") * cols
-    zlt_ref[...] = zl_ref[...].T
+    for group in range(zl_ref.shape[0]):
+        turned = zl_ref[group].T
+        for half in range(zlt_ref.shape[0]):
+            lanes = slice(half * LANES, (half + 1) * LANES)
+            zlt_ref[half, group * LANES : (group + 1) * LANES, :] = turned[:, lanes]
     proj_out_ref[...] = proj_ref[...].reshape(proj_out_ref.shape).astype(BF16)
     which = iota((pairs, residues), 0)
     place = iota((pairs, residues), 1)
@@ -166,7 +173,7 @@
     return pl.pallas_call(
         prepare_kernel,
         out_shape=(
-            jax.ShapeDtypeStruct(zl.shape[::-1], BF16),
+            jax.ShapeDtypeStruct((zl.shape[1] // LANES, zl.shape[0] * LANES, LANES), BF16),
             shape,
             shape,
             shape,
@@ -187,16 +194,18 @@
     (base_ref, inverse_ref, live_ref, proj_ref, tl_ref, tr_ref,
      both_ref, one_ref, outer_scr, flat_scr, one_scr) = refs
     pairs, channels = base_ref.shape
-    rows = zlt_ref.shape[0] // hidden
+    rows = zlt_ref.shape[1] // hidden
     rep = LANES // hidden
     me = lax.axis_index("dap")
     lane = iota((rows, LANES), 1)
     odd = (lane // hidden) % 2 == 1
     upper = lane // (2 * hidden) == 1
     half = 2 * hidden
+    left = jnp.concatenate([zlt_ref[part] for part in range(zlt_ref.shape[0])], axis=1)
     for step in range(ratio):
         block = lax.rem(me + step, ratio)
-        outer = dot(zlt_ref[...], zr_refs[step][...])
+        right = [zr_refs[step][group] for group in range(rows // rep)]
+        outer = dot(left, jnp.concatenate(right, axis=1))
         for group in range(rows // rep):
             outer_scr[group] = outer[:, group * LANES : (group + 1) * LANES]
         for group in range(rows // rep):
@@ -221,8 +230,9 @@
                         first = (group * rep + k) * rows
                     else:
                         first = pl.multiple_of(first, rows)
-                    flat_scr[pl.ds(first, rows), quad * LANES : (quad + 1) * LANES] = found[k].astype(BF16)
-    outer_mean = dot(flat_scr[...], proj_ref[...]) * inverse_ref[...]
+                    flat_scr[quad, pl.ds(first, rows), :] = found[k].astype(BF16)
+    flat = jnp.concatenate([flat_scr[quad] for quad in range(flat_scr.shape[0])], axis=1)
+    outer_mean = dot(flat, proj_ref[...]) * inverse_ref[...]
     one = (base_ref[...] + outer_mean).astype(BF16).astype(F32)
     one_scr[...] = one
     norm = layer_norm(one).astype(BF16)
@@ -245,8 +255,8 @@
         in_specs=[vmem()] * (7 + ratio),
         out_specs=[vmem()] * 2,
         scratch_shapes=[
-            pltpu.VMEM((zrs[0].shape[1] // LANES, zlt.shape[0], LANES), F32),
-            pltpu.VMEM((pairs, proj.shape[0]), BF16),
+            pltpu.VMEM((zrs[0].shape[0], zlt.shape[1], LANES), F32),
+            pltpu.VMEM((proj.shape[0] // LANES, pairs, LANES), BF16),
             pltpu.VMEM((pairs, channels), F32),
         ],
         compiler_params=pltpu.CompilerParams(vmem_limit_bytes=32 << 20),

time: 37.5 us -> 37.6 us (level)
  no operation moved by 1% of the time
where the time goes in v7:
time: 37.6 us; the launch traced here: 37.4 us
  Pallas kernels  15.9 us (42%)
  starting transfers between devices  13.2 us (35%)
  waiting for transfers between devices  6.86 us (18%)
  local copies, waits for them, and re-layouts  1.04 us (3%)
    ppermute x5, starting transfers between devices, fetch(): return lax.ppermute(values, ('dap', 'sub'), perm)  13.2 us
    pallas_call x2, Pallas kernels, factor(): pl.pallas_call(factor_kernel, out_shape=jax.ShapeDtypeStruct((rows * hidd...  11.3 us
    ppermute x5, waiting for transfers between devices, fetch(): return lax.ppermute(values, ('dap', 'sub'), perm)  6.86 us
    pallas_call x1, Pallas kernels, triangle_update(): pl.pallas_call(functools.partial(triangle_kernel, subs, ratio, cols), out...  2.21 us
    pallas_call x1, Pallas kernels, pair_update(): pl.pallas_call(functools.partial(pair_kernel, ratio, hidden), out_shape=(...  1.58 us
    unnamed x26, local copies, waits for them, and re-layouts  1.02 us
  transfers between devices with their start and end apart: 5, of which 3 were waited for; matrix products, arithmetic and copies ran while one was open for 0% of the time, Pallas kernels for 17%

profile of v7, /device:TPU:1, one launch (start us, length us, event | category | flops | bytes accessed | tf_op | source)
XLA Modules:
  0.0 37.4 jit_solution(1595298575989948608)
XLA Ops:
  0.0 5.6 %shard_map.147 = bf16[4,256,128]{2,1,0:T(8,128)(2,1)} custom-call(bf16[256,16,256]{2,1,0:T(8,128)(2,1)} %x_any.3, s32[64,256]{1,0:T(8,128)} %bitcast.5, bf16[32,256]{1,0:T(8,128)(2,1)} %bitcast.10), custom_call_target="tpu_custom_call" | custom-call | flops 1073741824 | bytes 4194304 | tf_op jit(solution)/shard_map/pallas_call | solution.py:110
  5.6 0.0 copy-start
  5.6 0.0 copy-start.4
  5.6 0.0 copy-start.5
  5.6 0.0 copy-start.10
  5.7 0.0 copy-start.11
  5.7 0.0 copy-start.12
  5.7 5.7 %collective-permute-start = (bf16[4,256,128]{2,1,0:T(8,128)(2,1)}, bf16[4,256,128]{2,1,0:T(8,128)(2,1)S(1)}, u32[]{:S(2)}, u32[]{:S(2)}) collective-permute-start(bf16[4,256,128]{2,1,0:T(8,128)(2,1)} %shard_map.147), channel_id=1, source_target_pairs={{0,0},{6,1},{11,2},{13,3},{2,4},{5,5},{9,6},{14,7},{1,8},{7,9},{10... | collective-permute-start | bytes 786440 | tf_op jit(solution)/shard_map/ppermute | solution.py:400
  11.4 0.0 copy-start.6
  11.4 0.0 copy-start.7
  11.5 0.0 copy-start.8
  11.5 0.0 copy-start.2
  11.5 0.0 copy-start.3
  11.5 0.0 copy-start.9
  11.5 5.7 %shard_map.145.zl_ref = bf16[4,256,128]{2,1,0:T(8,128)(2,1)} custom-call(bf16[256,16,256]{2,1,0:T(8,128)(2,1)} %x_any.3, s32[64,256]{1,0:T(8,128)} %bitcast.6, bf16[32,256]{1,0:T(8,128)(2,1)} %bitcast.11), custom_call_target="tpu_custom_call" | custom-call | flops 1073741824 | bytes 4194304 | tf_op jit(solution)/shard_map/pallas_call | solution.py:110
  17.2 0.0 copy-done
  17.2 0.0 copy-done.4
  17.2 0.0 copy-done.5
  17.2 0.0 copy-done.10
  17.2 0.0 copy-done.11
  17.2 0.0 copy-done.12
  17.3 0.0 copy-start.1
  17.3 0.9 %copy-done.1 = bf16[4,256,128]{2,1,0:T(8,128)(2,1)S(1)} copy-done((bf16[4,256,128]{2,1,0:T(8,128)(2,1)S(1)}, bf16[4,256,128]{2,1,0:T(8,128)(2,1)}, u32[]{:S(2)}) %copy-start.1) | copy-done | bytes 262168
  18.2 0.5 %shard_map.146 = (bf16[2,512,128]{2,1,0:T(8,128)(2,1)S(1)}, f32[256,128]{1,0:T(8,128)S(1)}, f32[256,128]{1,0:T(8,128)S(1)}, f32[256,128]{1,0:T(8,128)S(1)}, bf16[1024,128]{1,0:T(8,128)(2,1)S(1)}) custom-call(bf16[4,256,128]{2,1,0:T(8,128)(2,1)S(1)} %copy-done.1, s32[64,256]{1,0:T(8,128)S(1)} %bitcast.7, bf16[16,16,128]{2,1,0:T(8,128)(2,1)S(1)} %copy-done.5, ...), custom_call_target="tpu_custom_call" | custom-call | flops 134217728 | bytes 2097152 | tf_op jit(solution)/shard_map/pallas_call | solution.py:173
  18.7 0.0 collective-permute-done.refs_0_
  18.7 0.0 copy-done.6
  18.7 0.0 copy-done.7
  18.8 1.6 %shard_map.148 = (bf16[2,256,128]{2,1,0:T(8,128)(2,1)S(1)}, bf16[256,128]{1,0:T(8,128)(2,1)S(1)}) custom-call(bf16[2,512,128]{2,1,0:T(8,128)(2,1)S(1)} %get-tuple-element.12.zlt_ref, bf16[4,256,128]{2,1,0:T(8,128)(2,1)S(1)} %collective-permute-done.refs_0_, f32[256,128]{1,0:T(8,128)S(1)} %get-tuple-element.13.refs_1_, ...), custom_call_target="tpu_custom_call" | custom-call | flops 268435456 | bytes 2097152 | tf_op jit(solution)/shard_map/pallas_call | solution.py:252
  20.3 0.1 collective-permute-start.1
  20.4 1.3 %collective-permute-done.1 = bf16[2,256,128]{2,1,0:T(8,128)(2,1)S(1)} collective-permute-done((bf16[2,256,128]{2,1,0:T(8,128)(2,1)S(1)}, bf16[2,256,128]{2,1,0:T(8,128)(2,1)S(1)}, u32[]{:S(2)}, u32[]{:S(2)}) %collective-permute-start.1) | collective-permute-done | bytes 131104 | tf_op jit(solution)/shard_map/ppermute | solution.py:400
  21.8 2.3 %collective-permute-start.2 = (bf16[2,256,128]{2,1,0:T(8,128)(2,1)S(1)}, bf16[2,256,128]{2,1,0:T(8,128)(2,1)S(1)}, u32[]{:S(2)}, u32[]{:S(2)}) collective-permute-start(bf16[2,256,128]{2,1,0:T(8,128)(2,1)S(1)} %pad_maximum_fusion.refs_0_), channel_id=1, source_target_pairs={{2,0},{3,1},{0,2},{1,3},{6,4},{7,5},{4,6},{5,7},{10,8},{11,9},{8,1... | collective-permute-start | bytes 393224 | tf_op jit(solution)/shard_map/ppermute | solution.py:400
  24.1 3.3 %collective-permute-start.4 = (bf16[2,256,128]{2,1,0:T(8,128)(2,1)S(1)}, bf16[2,256,128]{2,1,0:T(8,128)(2,1)S(1)}, u32[]{:S(2)}, u32[]{:S(2)}) collective-permute-start(bf16[2,256,128]{2,1,0:T(8,128)(2,1)S(1)} %pad_maximum_fusion.1), channel_id=1, source_target_pairs={{2,0},{4,1},{9,2},{15,3},{0,4},{7,5},{11,6},{12,7},{3,8},{5,9},{8,... | collective-permute-start | bytes 393224 | tf_op jit(solution)/shard_map/ppermute | solution.py:400
  27.3 1.9 %collective-permute-start.3 = (bf16[2,256,128]{2,1,0:T(8,128)(2,1)S(1)}, bf16[2,256,128]{2,1,0:T(8,128)(2,1)S(1)}, u32[]{:S(2)}, u32[]{:S(2)}) collective-permute-start(bf16[2,256,128]{2,1,0:T(8,128)(2,1)S(1)} %pad_maximum_fusion.1), channel_id=1, source_target_pairs={{0,0},{6,1},{11,2},{13,3},{2,4},{5,5},{9,6},{14,7},{1,8},{7,9},{10... | collective-permute-start | bytes 393224 | tf_op jit(solution)/shard_map/ppermute | solution.py:400
  29.2 0.0 copy-done.8
  29.3 0.3 shard_map.149.refs_5_
  29.6 0.0 collective-permute-done.2.refs_1_
  29.6 0.3 collective-permute-done.4.refs_3_
  29.9 5.2 %collective-permute-done.3.refs_2_ = bf16[2,256,128]{2,1,0:T(8,128)(2,1)S(1)} collective-permute-done((bf16[2,256,128]{2,1,0:T(8,128)(2,1)S(1)}, bf16[2,256,128]{2,1,0:T(8,128)(2,1)S(1)}, u32[]{:S(2)}, u32[]{:S(2)}) %collective-permute-start.3) | collective-permute-done | bytes 131104 | tf_op jit(solution)/shard_map/ppermute | solution.py:400
  35.1 0.0 copy-done.2
  35.1 0.0 copy-done.3
  35.1 0.0 copy-done.9
  35.1 2.2 %shard_map.150 = bf16[16,16,128]{2,1,0:T(8,128)(2,1)} custom-call(bf16[2,256,128]{2,1,0:T(8,128)(2,1)S(1)} %pad_maximum_fusion.refs_0_, bf16[2,256,128]{2,1,0:T(8,128)(2,1)S(1)} %collective-permute-done.2.refs_1_, bf16[2,256,128]{2,1,0:T(8,128)(2,1)S(1)} %collective-permute-done.3.refs_2_, bf16[2,256,128]{2,1,0:T(8,128)(2,1)S(1)} %collective-permute-done.4.refs_3_, ...), custom_call_target="tpu_custom_call" | custom-call | flops 134217728 | bytes 2097152 | tf_op jit(solution)/shard_map/pallas_call | solution.py:356
  (4 shorter events, 0.1 us)
Async XLA Ops:
  5.6 11.6 %copy-start = (f32[32,32,128]{2,1,0:T(8,128)S(1)}, f32[32,32,128]{2,1,0:T(8,128)}, u32[]{:S(2)}) copy-start(f32[32,32,128]{2,1,0:T(8,128)} %proj_ref.1) | copy-start | bytes 1572868
  5.6 11.6 %copy-start.4 = (s32[256,64]{0,1:T(8,128)S(1)}, s32[256,64]{0,1:T(8,128)}, u32[]{:S(2)}) copy-start(s32[256,64]{0,1:T(8,128)} %param.16) | copy-start | bytes 196612
  5.6 11.6 %copy-start.5 = (bf16[16,16,128]{2,1,0:T(8,128)(2,1)S(1)}, bf16[16,16,128]{2,1,0:T(8,128)(2,1)}, u32[]{:S(2)}) copy-start(bf16[16,16,128]{2,1,0:T(8,128)(2,1)} %pair_ref.1) | copy-start | bytes 196612
  5.6 11.6 %copy-start.10 = (bf16[66,128]{1,0:T(8,128)(2,1)S(1)}, bf16[66,128]{1,0:T(8,128)(2,1)}, u32[]{:S(2)}) copy-start(bf16[66,128]{1,0:T(8,128)(2,1)} %table_ref.1) | copy-start | bytes 50692
  5.7 11.6 %copy-start.11 = (s32[64]{0:T(128)S(1)}, s32[64]{0:T(128)}, u32[]{:S(2)}) copy-start(s32[64]{0:T(128)} %param.18) | copy-start | bytes 772
  5.7 11.6 %copy-start.12 = (s32[64]{0:T(128)S(1)}, s32[64]{0:T(128)}, u32[]{:S(2)}) copy-start(s32[64]{0:T(128)} %param.19) | copy-start | bytes 772
  5.7 13.0 %collective-permute-start = (bf16[4,256,128]{2,1,0:T(8,128)(2,1)}, bf16[4,256,128]{2,1,0:T(8,128)(2,1)S(1)}, u32[]{:S(2)}, u32[]{:S(2)}) collective-permute-start(bf16[4,256,128]{2,1,0:T(8,128)(2,1)} %shard_map.147), channel_id=1, source_target_pairs={{0,0},{6,1},{11,2},{13,3},{2,4},{5,5},{9,6},{14,7},{1,8},{7,9},{10... | collective-permute-start | bytes 786440 | tf_op jit(solution)/shard_map/ppermute | solution.py:400
  11.4 7.3 %copy-start.6 = (bf16[128,256]{1,0:T(8,128)(2,1)S(1)}, bf16[128,256]{1,0:T(8,128)(2,1)}, u32[]{:S(2)}) copy-start(bf16[128,256]{1,0:T(8,128)(2,1)} %refs_5_.1) | copy-start | bytes 196612
  11.4 7.3 %copy-start.7 = (bf16[128,256]{1,0:T(8,128)(2,1)S(1)}, bf16[128,256]{1,0:T(8,128)(2,1)}, u32[]{:S(2)}) copy-start(bf16[128,256]{1,0:T(8,128)(2,1)} %refs_6_.2) | copy-start | bytes 196612
  11.5 17.8 %copy-start.8 = (bf16[128,128]{1,0:T(8,128)(2,1)S(1)}, bf16[128,128]{1,0:T(8,128)(2,1)}, u32[]{:S(2)}) copy-start(bf16[128,128]{1,0:T(8,128)(2,1)} %weight_ref.1) | copy-start | bytes 98308
  11.5 23.7 %copy-start.2 = (bf16[128,512]{1,0:T(8,128)(2,1)S(1)}, bf16[128,512]{1,0:T(8,128)(2,1)}, u32[]{:S(2)}) copy-start(bf16[128,512]{1,0:T(8,128)(2,1)} %refs_7_.1) | copy-start | bytes 393220
  11.5 23.7 %copy-start.3 = (bf16[512,128]{1,0:T(8,128)(2,1)S(1)}, bf16[512,128]{1,0:T(8,128)(2,1)}, u32[]{:S(2)}) copy-start(bf16[512,128]{1,0:T(8,128)(2,1)} %refs_8_.1) | copy-start | bytes 393220
  11.5 23.7 %copy-start.9 = (bf16[128,128]{1,0:T(8,128)(2,1)S(1)}, bf16[128,128]{1,0:T(8,128)(2,1)}, u32[]{:S(2)}) copy-start(bf16[128,128]{1,0:T(8,128)(2,1)} %refs_6_.3) | copy-start | bytes 98308
  17.3 1.0 %copy-start.1 = (bf16[4,256,128]{2,1,0:T(8,128)(2,1)S(1)}, bf16[4,256,128]{2,1,0:T(8,128)(2,1)}, u32[]{:S(2)}) copy-start(bf16[4,256,128]{2,1,0:T(8,128)(2,1)} %shard_map.145.zl_ref) | copy-start | bytes 786436
  20.3 1.4 %collective-permute-start.1 = (bf16[2,256,128]{2,1,0:T(8,128)(2,1)S(1)}, bf16[2,256,128]{2,1,0:T(8,128)(2,1)S(1)}, u32[]{:S(2)}, u32[]{:S(2)}) collective-permute-start(bf16[2,256,128]{2,1,0:T(8,128)(2,1)S(1)} %get-tuple-element.17), channel_id=1, source_target_pairs={{1,0},{0,1},{3,2},{2,3},{5,4},{4,5},{7,6},{6,7},{9,8},{8,9},{11,10... | collective-permute-start | bytes 393224 | tf_op jit(solution)/shard_map/ppermute | solution.py:400
  21.8 7.8 %collective-permute-start.2 = (bf16[2,256,128]{2,1,0:T(8,128)(2,1)S(1)}, bf16[2,256,128]{2,1,0:T(8,128)(2,1)S(1)}, u32[]{:S(2)}, u32[]{:S(2)}) collective-permute-start(bf16[2,256,128]{2,1,0:T(8,128)(2,1)S(1)} %pad_maximum_fusion.refs_0_), channel_id=1, source_target_pairs={{2,0},{3,1},{0,2},{1,3},{6,4},{7,5},{4,6},{5,7},{10,8},{11,9},{8,1... | collective-permute-start | bytes 393224 | tf_op jit(solution)/shard_map/ppermute | solution.py:400
  24.1 5.9 %collective-permute-start.4 = (bf16[2,256,128]{2,1,0:T(8,128)(2,1)S(1)}, bf16[2,256,128]{2,1,0:T(8,128)(2,1)S(1)}, u32[]{:S(2)}, u32[]{:S(2)}) collective-permute-start(bf16[2,256,128]{2,1,0:T(8,128)(2,1)S(1)} %pad_maximum_fusion.1), channel_id=1, source_target_pairs={{2,0},{4,1},{9,2},{15,3},{0,4},{7,5},{11,6},{12,7},{3,8},{5,9},{8,... | collective-permute-start | bytes 393224 | tf_op jit(solution)/shard_map/ppermute | solution.py:400
  27.3 7.8 %collective-permute-start.3 = (bf16[2,256,128]{2,1,0:T(8,128)(2,1)S(1)}, bf16[2,256,128]{2,1,0:T(8,128)(2,1)S(1)}, u32[]{:S(2)}, u32[]{:S(2)}) collective-permute-start(bf16[2,256,128]{2,1,0:T(8,128)(2,1)S(1)} %pad_maximum_fusion.1), channel_id=1, source_target_pairs={{0,0},{6,1},{11,2},{13,3},{2,4},{5,5},{9,6},{14,7},{1,8},{7,9},{10... | collective-permute-start | bytes 393224 | tf_op jit(solution)/shard_map/ppermute | solution.py:400

commit v8 on v7

--- a/solution.py
+++ b/solution.py
@@ -11,6 +11,7 @@
 LANES = 128
 PIECE = 16
 STEPS = 4
+TILE = 64
 EPSILON = 1e-05
 BF16 = jnp.bfloat16
 F32 = jnp.float32
@@ -53,7 +54,10 @@
     return lax.bitwise_and(index, size - 1)
 
 
-def factor_kernel(x_any, mask_ref, weight_ref, z_ref, x_scr, y_scr, sems):
+def factor_kernel(
+    x_any, mask_ref, weight_ref, z_ref,
+    x_scr, y_scr, mean_scr, square_scr, spread_scr, out_scr, live_scr, sems,
+):
     halves, seqs, rows, _ = x_scr.shape
     hidden, channels = weight_ref.shape
     rep = LANES // hidden
@@ -73,35 +77,54 @@
     sums = dot(jnp.ones((8, channels), BF16), w)[:1, :LANES]
     start = lax.axis_index("dap") * rows
     spread = iota((residues, width), 0) == start + over(iota((residues, width), 1), hidden)
-    live = dot_tn(mask_ref[...].astype(BF16), spread.astype(BF16))
+    live_scr[...] = dot_tn(mask_ref[...].astype(BF16), spread.astype(BF16))
     to, at = iota((groups * PIECE, PIECE * rows), 0), iota((groups * PIECE, PIECE * rows), 1)
     gather = within(to, PIECE) == over(at, rows)
     gather = (gather & (over(to, PIECE) == over(within(at, rows), rep))).astype(BF16)
-    own = over(iota((8, LANES), 1), hidden) == within(iota((8, LANES), 0), rep)
+    own = over(iota((TILE, LANES), 1), hidden) == within(iota((TILE, LANES), 0), rep)
     own = own.astype(F32)
     ones = jnp.ones((LANES, LANES), BF16)
+
+    def square(tile, _):
+        here = pl.ds(pl.multiple_of(tile * TILE, TILE), TILE)
+        mean = mean_scr[here, :] * (1.0 / channels)
+        total = jnp.zeros_like(mean)
+        for half in range(halves):
+            part = x_scr[half, pl.ds(tile * (TILE // rows), TILE // rows)].reshape(TILE, LANES)
+            centered = part.astype(F32) - mean
+            total = total + centered * centered
+        square_scr[here, :] = total.astype(BF16)
+        return _
+
+    def normalise(tile, _):
+        here = pl.ds(pl.multiple_of(tile * TILE, TILE), TILE)
+        scale = lax.rsqrt(spread_scr[here, :] * (1.0 / channels) + EPSILON) * own
+        mean = mean_scr[here, :] * (1.0 / channels)
+        out_scr[here, :] = ((y_scr[here, :] - mean * sums) * scale).astype(BF16)
+        return _
+
+    tiles = step * rows // TILE
     for turn in range(STEPS):
         x = []
         for half in range(halves):
             copies[turn * halves + half].wait()
             x.append(x_scr[half, turn * step : (turn + 1) * step].reshape(step * rows, LANES))
         y = dot(jnp.concatenate(x, axis=1), w)
-        mean = y[:, LANES:] * (1.0 / channels)
-        square = jnp.zeros_like(mean)
-        for half in range(halves):
-            centered = x[half].astype(F32) - mean
-            square = square + centered * centered
-        spread = dot(square.astype(BF16), ones)
-        scale = lax.rsqrt(spread * (1.0 / channels) + EPSILON).reshape(-1, 8, LANES) * own[None]
-        scaled = (y[:, :LANES] - mean * sums) * scale.reshape(mean.shape)
-        y_scr[turn * step * rows : (turn + 1) * step * rows, :] = scaled.astype(BF16)
-        for piece in range(turn * step // PIECE, (turn + 1) * step // PIECE):
-            z = dot(gather, y_scr[piece * PIECE * rows : (piece + 1) * PIECE * rows, :])
-            here = slice(piece * PIECE, (piece + 1) * PIECE)
-            for group in range(groups):
-                lanes = slice(group * LANES, (group + 1) * LANES)
-                part = z[group * PIECE : (group + 1) * PIECE]
-                z_ref[group, here, :] = (part * live[here, lanes]).astype(BF16)
+        here = slice(turn * step * rows, (turn + 1) * step * rows)
+        y_scr[here, :] = y[:, :LANES]
+        mean_scr[here, :] = y[:, LANES:]
+        lax.fori_loop(turn * tiles, (turn + 1) * tiles, square, None, unroll=4)
+    for turn in range(STEPS):
+        here = slice(turn * step * rows, (turn + 1) * step * rows)
+        spread_scr[here, :] = dot(square_scr[here, :], ones)
+    lax.fori_loop(0, STEPS * tiles, normalise, None, unroll=4)
+    for piece in range(seqs // PIECE):
+        z = dot(gather, out_scr[piece * PIECE * rows : (piece + 1) * PIECE * rows, :])
+        here = slice(piece * PIECE, (piece + 1) * PIECE)
+        for group in range(groups):
+            lanes = slice(group * LANES, (group + 1) * LANES)
+            part = z[group * PIECE : (group + 1) * PIECE]
+            z_ref[group, here, :] = (part * live_scr[here, lanes]).astype(BF16)
 
 
 def factor(alignment, mask, weight):
@@ -114,7 +137,12 @@
         out_specs=vmem(),
         scratch_shapes=[
             pltpu.VMEM((channels // LANES, seqs, rows, LANES), BF16),
+            pltpu.VMEM((seqs * rows, LANES), F32),
+            pltpu.VMEM((seqs * rows, LANES), F32),
             pltpu.VMEM((seqs * rows, LANES), BF16),
+            pltpu.VMEM((seqs * rows, LANES), F32),
+            pltpu.VMEM((seqs * rows, LANES), BF16),
+            pltpu.VMEM((seqs, rows * hidden), F32),
             pltpu.SemaphoreType.DMA((STEPS, channels // LANES)),
         ],
         compiler_params=pltpu.CompilerParams(vmem_limit_bytes=119 << 19),

time: 37.6 us -> 39.2 us (1.043)
  Pallas kernels: 15.9 us -> 17.7 us
  starting transfers between devices: 13.2 us -> 12.4 us
  waiting for transfers between devices: 6.86 us -> 7.5 us
    pallas_call x2, Pallas kernels: 11.3 us -> 13.1 us  [factor(): pl.pallas_call(factor_kernel, out_shape=jax.ShapeDtypeStruct((rows * hidd...]
    ppermute x5, starting transfers between devices: 13.2 us -> 12.4 us  [fetch(): return lax.ppermute(values, ('dap', 'sub'), perm)]
    ppermute x5, waiting for transfers between devices: 6.86 us -> 7.5 us  [fetch(): return lax.ppermute(values, ('dap', 'sub'), perm)]
  transfers between devices with their start and end apart: 5 -> 5, of which waited for: 3 -> 3; matrix products, arithmetic and copies ran while one was open for 0% -> 0% of each run, Pallas kernels for 17% -> 19%
where the time goes in v8:
time: 39.2 us; the launch traced here: 38.9 us
  Pallas kernels  17.7 us (45%)
  starting transfers between devices  12.4 us (32%)
  waiting for transfers between devices  7.5 us (19%)
  local copies, waits for them, and re-layouts  1.04 us (3%)
    pallas_call x2, Pallas kernels, factor(): pl.pallas_call(factor_kernel, out_shape=jax.ShapeDtypeStruct((rows * hidd...  13.1 us
    ppermute x5, starting transfers between devices, fetch(): return lax.ppermute(values, ('dap', 'sub'), perm)  12.4 us
    ppermute x5, waiting for transfers between devices, fetch(): return lax.ppermute(values, ('dap', 'sub'), perm)  7.5 us
    pallas_call x1, Pallas kernels, triangle_update(): pl.pallas_call(functools.partial(triangle_kernel, subs, ratio, cols), out...  2.21 us
    pallas_call x1, Pallas kernels, pair_update(): pl.pallas_call(functools.partial(pair_kernel, ratio, hidden), out_shape=(...  1.58 us
    unnamed x26, local copies, waits for them, and re-layouts  1.02 us
  transfers between devices with their start and end apart: 5, of which 3 were waited for; matrix products, arithmetic and copies ran while one was open for 0% of the time, Pallas kernels for 19%

profile of v8, /device:TPU:1, one launch (start us, length us, event | category | flops | bytes accessed | tf_op | source)
XLA Modules:
  0.0 38.9 jit_solution(14684866267254920154)
XLA Ops:
  0.0 6.5 %shard_map.147 = bf16[4,256,128]{2,1,0:T(8,128)(2,1)} custom-call(bf16[256,16,256]{2,1,0:T(8,128)(2,1)} %x_any.3, s32[64,256]{1,0:T(8,128)} %bitcast.5, bf16[32,256]{1,0:T(8,128)(2,1)} %bitcast.10), custom_call_target="tpu_custom_call" | custom-call | flops 1073741824 | bytes 4194304 | tf_op jit(solution)/shard_map/pallas_call | solution.py:133
  6.5 0.0 copy-start
  6.5 0.0 copy-start.4
  6.5 0.0 copy-start.5
  6.5 0.0 copy-start.10
  6.6 0.0 copy-start.11
  6.6 0.0 copy-start.12
  6.6 5.7 %collective-permute-start = (bf16[4,256,128]{2,1,0:T(8,128)(2,1)}, bf16[4,256,128]{2,1,0:T(8,128)(2,1)S(1)}, u32[]{:S(2)}, u32[]{:S(2)}) collective-permute-start(bf16[4,256,128]{2,1,0:T(8,128)(2,1)} %shard_map.147), channel_id=1, source_target_pairs={{0,0},{6,1},{11,2},{13,3},{2,4},{5,5},{9,6},{14,7},{1,8},{7,9},{10... | collective-permute-start | bytes 786440 | tf_op jit(solution)/shard_map/ppermute | solution.py:428
  12.3 0.0 copy-start.6
  12.3 0.0 copy-start.7
  12.4 0.0 copy-start.8
  12.4 0.0 copy-start.2
  12.4 0.0 copy-start.3
  12.4 0.0 copy-start.9
  12.4 6.6 %shard_map.145.zl_ref = bf16[4,256,128]{2,1,0:T(8,128)(2,1)} custom-call(bf16[256,16,256]{2,1,0:T(8,128)(2,1)} %x_any.3, s32[64,256]{1,0:T(8,128)} %bitcast.6, bf16[32,256]{1,0:T(8,128)(2,1)} %bitcast.11), custom_call_target="tpu_custom_call" | custom-call | flops 1073741824 | bytes 4194304 | tf_op jit(solution)/shard_map/pallas_call | solution.py:133
  19.0 0.0 copy-done
  19.0 0.0 copy-done.4
  19.0 0.0 copy-done.5
  19.0 0.0 copy-done.10
  19.0 0.0 copy-done.11
  19.0 0.0 copy-done.12
  19.1 0.0 copy-start.1
  19.1 0.9 %copy-done.1 = bf16[4,256,128]{2,1,0:T(8,128)(2,1)S(1)} copy-done((bf16[4,256,128]{2,1,0:T(8,128)(2,1)S(1)}, bf16[4,256,128]{2,1,0:T(8,128)(2,1)}, u32[]{:S(2)}) %copy-start.1) | copy-done | bytes 262168
  20.0 0.5 %shard_map.146 = (bf16[2,512,128]{2,1,0:T(8,128)(2,1)S(1)}, f32[256,128]{1,0:T(8,128)S(1)}, f32[256,128]{1,0:T(8,128)S(1)}, f32[256,128]{1,0:T(8,128)S(1)}, bf16[1024,128]{1,0:T(8,128)(2,1)S(1)}) custom-call(bf16[4,256,128]{2,1,0:T(8,128)(2,1)S(1)} %copy-done.1, s32[64,256]{1,0:T(8,128)S(1)} %bitcast.7, bf16[16,16,128]{2,1,0:T(8,128)(2,1)S(1)} %copy-done.5, ...), custom_call_target="tpu_custom_call" | custom-call | flops 134217728 | bytes 2097152 | tf_op jit(solution)/shard_map/pallas_call | solution.py:201
  20.5 0.0 collective-permute-done.refs_0_
  20.5 0.0 copy-done.6
  20.5 0.0 copy-done.7
  20.6 1.6 %shard_map.148 = (bf16[2,256,128]{2,1,0:T(8,128)(2,1)S(1)}, bf16[256,128]{1,0:T(8,128)(2,1)S(1)}) custom-call(bf16[2,512,128]{2,1,0:T(8,128)(2,1)S(1)} %get-tuple-element.12.zlt_ref, bf16[4,256,128]{2,1,0:T(8,128)(2,1)S(1)} %collective-permute-done.refs_0_, f32[256,128]{1,0:T(8,128)S(1)} %get-tuple-element.13.refs_1_, ...), custom_call_target="tpu_custom_call" | custom-call | flops 268435456 | bytes 2097152 | tf_op jit(solution)/shard_map/pallas_call | solution.py:280
  22.1 0.1 collective-permute-start.1
  22.2 1.3 %collective-permute-done.1 = bf16[2,256,128]{2,1,0:T(8,128)(2,1)S(1)} collective-permute-done((bf16[2,256,128]{2,1,0:T(8,128)(2,1)S(1)}, bf16[2,256,128]{2,1,0:T(8,128)(2,1)S(1)}, u32[]{:S(2)}, u32[]{:S(2)}) %collective-permute-start.1) | collective-permute-done | bytes 131104 | tf_op jit(solution)/shard_map/ppermute | solution.py:428
  23.6 2.3 %collective-permute-start.2 = (bf16[2,256,128]{2,1,0:T(8,128)(2,1)S(1)}, bf16[2,256,128]{2,1,0:T(8,128)(2,1)S(1)}, u32[]{:S(2)}, u32[]{:S(2)}) collective-permute-start(bf16[2,256,128]{2,1,0:T(8,128)(2,1)S(1)} %pad_maximum_fusion.refs_0_), channel_id=1, source_target_pairs={{2,0},{3,1},{0,2},{1,3},{6,4},{7,5},{4,6},{5,7},{10,8},{11,9},{8,1... | collective-permute-start | bytes 393224 | tf_op jit(solution)/shard_map/ppermute | solution.py:428
  25.9 2.4 %collective-permute-start.4 = (bf16[2,256,128]{2,1,0:T(8,128)(2,1)S(1)}, bf16[2,256,128]{2,1,0:T(8,128)(2,1)S(1)}, u32[]{:S(2)}, u32[]{:S(2)}) collective-permute-start(bf16[2,256,128]{2,1,0:T(8,128)(2,1)S(1)} %pad_maximum_fusion.1), channel_id=1, source_target_pairs={{2,0},{4,1},{9,2},{15,3},{0,4},{7,5},{11,6},{12,7},{3,8},{5,9},{8,... | collective-permute-start | bytes 393224 | tf_op jit(solution)/shard_map/ppermute | solution.py:428
  28.2 1.9 %collective-permute-start.3 = (bf16[2,256,128]{2,1,0:T(8,128)(2,1)S(1)}, bf16[2,256,128]{2,1,0:T(8,128)(2,1)S(1)}, u32[]{:S(2)}, u32[]{:S(2)}) collective-permute-start(bf16[2,256,128]{2,1,0:T(8,128)(2,1)S(1)} %pad_maximum_fusion.1), channel_id=1, source_target_pairs={{0,0},{6,1},{11,2},{13,3},{2,4},{5,5},{9,6},{14,7},{1,8},{7,9},{10... | collective-permute-start | bytes 393224 | tf_op jit(solution)/shard_map/ppermute | solution.py:428
  30.2 0.0 copy-done.8
  30.2 0.3 shard_map.149.refs_5_
  30.5 0.0 collective-permute-done.2.refs_1_
  30.5 0.7 %collective-permute-done.4.refs_3_ = bf16[2,256,128]{2,1,0:T(8,128)(2,1)S(1)} collective-permute-done((bf16[2,256,128]{2,1,0:T(8,128)(2,1)S(1)}, bf16[2,256,128]{2,1,0:T(8,128)(2,1)S(1)}, u32[]{:S(2)}, u32[]{:S(2)}) %collective-permute-start.4) | collective-permute-done | bytes 131104 | tf_op jit(solution)/shard_map/ppermute | solution.py:428
  31.2 5.5 %collective-permute-done.3.refs_2_ = bf16[2,256,128]{2,1,0:T(8,128)(2,1)S(1)} collective-permute-done((bf16[2,256,128]{2,1,0:T(8,128)(2,1)S(1)}, bf16[2,256,128]{2,1,0:T(8,128)(2,1)S(1)}, u32[]{:S(2)}, u32[]{:S(2)}) %collective-permute-start.3) | collective-permute-done | bytes 131104 | tf_op jit(solution)/shard_map/ppermute | solution.py:428
  36.7 0.0 copy-done.2
  36.7 0.0 copy-done.3
  36.7 0.0 copy-done.9
  36.7 2.2 %shard_map.150 = bf16[16,16,128]{2,1,0:T(8,128)(2,1)} custom-call(bf16[2,256,128]{2,1,0:T(8,128)(2,1)S(1)} %pad_maximum_fusion.refs_0_, bf16[2,256,128]{2,1,0:T(8,128)(2,1)S(1)} %collective-permute-done.2.refs_1_, bf16[2,256,128]{2,1,0:T(8,128)(2,1)S(1)} %collective-permute-done.3.refs_2_, bf16[2,256,128]{2,1,0:T(8,128)(2,1)S(1)} %collective-permute-done.4.refs_3_, ...), custom_call_target="tpu_custom_call" | custom-call | flops 134217728 | bytes 2097152 | tf_op jit(solution)/shard_map/pallas_call | solution.py:384
  (4 shorter events, 0.1 us)
Async XLA Ops:
  6.5 12.5 %copy-start = (f32[32,32,128]{2,1,0:T(8,128)S(1)}, f32[32,32,128]{2,1,0:T(8,128)}, u32[]{:S(2)}) copy-start(f32[32,32,128]{2,1,0:T(8,128)} %proj_ref.1) | copy-start | bytes 1572868
  6.5 12.5 %copy-start.4 = (s32[256,64]{0,1:T(8,128)S(1)}, s32[256,64]{0,1:T(8,128)}, u32[]{:S(2)}) copy-start(s32[256,64]{0,1:T(8,128)} %param.16) | copy-start | bytes 196612
  6.5 12.5 %copy-start.5 = (bf16[16,16,128]{2,1,0:T(8,128)(2,1)S(1)}, bf16[16,16,128]{2,1,0:T(8,128)(2,1)}, u32[]{:S(2)}) copy-start(bf16[16,16,128]{2,1,0:T(8,128)(2,1)} %pair_ref.1) | copy-start | bytes 196612
  6.5 12.5 %copy-start.10 = (bf16[66,128]{1,0:T(8,128)(2,1)S(1)}, bf16[66,128]{1,0:T(8,128)(2,1)}, u32[]{:S(2)}) copy-start(bf16[66,128]{1,0:T(8,128)(2,1)} %table_ref.1) | copy-start | bytes 50692
  6.6 12.5 %copy-start.11 = (s32[64]{0:T(128)S(1)}, s32[64]{0:T(128)}, u32[]{:S(2)}) copy-start(s32[64]{0:T(128)} %param.18) | copy-start | bytes 772
  6.6 12.5 %copy-start.12 = (s32[64]{0:T(128)S(1)}, s32[64]{0:T(128)}, u32[]{:S(2)}) copy-start(s32[64]{0:T(128)} %param.19) | copy-start | bytes 772
  6.6 13.9 %collective-permute-start = (bf16[4,256,128]{2,1,0:T(8,128)(2,1)}, bf16[4,256,128]{2,1,0:T(8,128)(2,1)S(1)}, u32[]{:S(2)}, u32[]{:S(2)}) collective-permute-start(bf16[4,256,128]{2,1,0:T(8,128)(2,1)} %shard_map.147), channel_id=1, source_target_pairs={{0,0},{6,1},{11,2},{13,3},{2,4},{5,5},{9,6},{14,7},{1,8},{7,9},{10... | collective-permute-start | bytes 786440 | tf_op jit(solution)/shard_map/ppermute | solution.py:428
  12.3 8.2 %copy-start.6 = (bf16[128,256]{1,0:T(8,128)(2,1)S(1)}, bf16[128,256]{1,0:T(8,128)(2,1)}, u32[]{:S(2)}) copy-start(bf16[128,256]{1,0:T(8,128)(2,1)} %refs_5_.1) | copy-start | bytes 196612
  12.3 8.2 %copy-start.7 = (bf16[128,256]{1,0:T(8,128)(2,1)S(1)}, bf16[128,256]{1,0:T(8,128)(2,1)}, u32[]{:S(2)}) copy-start(bf16[128,256]{1,0:T(8,128)(2,1)} %refs_6_.2) | copy-start | bytes 196612
  12.4 17.8 %copy-start.8 = (bf16[128,128]{1,0:T(8,128)(2,1)S(1)}, bf16[128,128]{1,0:T(8,128)(2,1)}, u32[]{:S(2)}) copy-start(bf16[128,128]{1,0:T(8,128)(2,1)} %weight_ref.1) | copy-start | bytes 98308
  12.4 24.3 %copy-start.2 = (bf16[128,512]{1,0:T(8,128)(2,1)S(1)}, bf16[128,512]{1,0:T(8,128)(2,1)}, u32[]{:S(2)}) copy-start(bf16[128,512]{1,0:T(8,128)(2,1)} %refs_7_.1) | copy-start | bytes 393220
  12.4 24.3 %copy-start.3 = (bf16[512,128]{1,0:T(8,128)(2,1)S(1)}, bf16[512,128]{1,0:T(8,128)(2,1)}, u32[]{:S(2)}) copy-start(bf16[512,128]{1,0:T(8,128)(2,1)} %refs_8_.1) | copy-start | bytes 393220
  12.4 24.3 %copy-start.9 = (bf16[128,128]{1,0:T(8,128)(2,1)S(1)}, bf16[128,128]{1,0:T(8,128)(2,1)}, u32[]{:S(2)}) copy-start(bf16[128,128]{1,0:T(8,128)(2,1)} %refs_6_.3) | copy-start | bytes 98308
  19.1 1.0 %copy-start.1 = (bf16[4,256,128]{2,1,0:T(8,128)(2,1)S(1)}, bf16[4,256,128]{2,1,0:T(8,128)(2,1)}, u32[]{:S(2)}) copy-start(bf16[4,256,128]{2,1,0:T(8,128)(2,1)} %shard_map.145.zl_ref) | copy-start | bytes 786436
  22.1 1.4 %collective-permute-start.1 = (bf16[2,256,128]{2,1,0:T(8,128)(2,1)S(1)}, bf16[2,256,128]{2,1,0:T(8,128)(2,1)S(1)}, u32[]{:S(2)}, u32[]{:S(2)}) collective-permute-start(bf16[2,256,128]{2,1,0:T(8,128)(2,1)S(1)} %get-tuple-element.17), channel_id=1, source_target_pairs={{1,0},{0,1},{3,2},{2,3},{5,4},{4,5},{7,6},{6,7},{9,8},{8,9},{11,10... | collective-permute-start | bytes 393224 | tf_op jit(solution)/shard_map/ppermute | solution.py:428
  23.6 6.9 %collective-permute-start.2 = (bf16[2,256,128]{2,1,0:T(8,128)(2,1)S(1)}, bf16[2,256,128]{2,1,0:T(8,128)(2,1)S(1)}, u32[]{:S(2)}, u32[]{:S(2)}) collective-permute-start(bf16[2,256,128]{2,1,0:T(8,128)(2,1)S(1)} %pad_maximum_fusion.refs_0_), channel_id=1, source_target_pairs={{2,0},{3,1},{0,2},{1,3},{6,4},{7,5},{4,6},{5,7},{10,8},{11,9},{8,1... | collective-permute-start | bytes 393224 | tf_op jit(solution)/shard_map/ppermute | solution.py:428
  25.9 5.3 %collective-permute-start.4 = (bf16[2,256,128]{2,1,0:T(8,128)(2,1)S(1)}, bf16[2,256,128]{2,1,0:T(8,128)(2,1)S(1)}, u32[]{:S(2)}, u32[]{:S(2)}) collective-permute-start(bf16[2,256,128]{2,1,0:T(8,128)(2,1)S(1)} %pad_maximum_fusion.1), channel_id=1, source_target_pairs={{2,0},{4,1},{9,2},{15,3},{0,4},{7,5},{11,6},{12,7},{3,8},{5,9},{8,... | collective-permute-start | bytes 393224 | tf_op jit(solution)/shard_map/ppermute | solution.py:428
  28.2 8.5 %collective-permute-start.3 = (bf16[2,256,128]{2,1,0:T(8,128)(2,1)S(1)}, bf16[2,256,128]{2,1,0:T(8,128)(2,1)S(1)}, u32[]{:S(2)}, u32[]{:S(2)}) collective-permute-start(bf16[2,256,128]{2,1,0:T(8,128)(2,1)S(1)} %pad_maximum_fusion.1), channel_id=1, source_target_pairs={{0,0},{6,1},{11,2},{13,3},{2,4},{5,5},{9,6},{14,7},{1,8},{7,9},{10... | collective-permute-start | bytes 393224 | tf_op jit(solution)/shard_map/ppermute | solution.py:428

commit v9 on v7

--- a/solution.py
+++ b/solution.py
@@ -9,7 +9,6 @@
 
 REL_CLIP = 32
 LANES = 128
-PIECE = 16
 STEPS = 4
 EPSILON = 1e-05
 BF16 = jnp.bfloat16
@@ -74,11 +73,7 @@
     start = lax.axis_index("dap") * rows
     spread = iota((residues, width), 0) == start + over(iota((residues, width), 1), hidden)
     live = dot_tn(mask_ref[...].astype(BF16), spread.astype(BF16))
-    to, at = iota((groups * PIECE, PIECE * rows), 0), iota((groups * PIECE, PIECE * rows), 1)
-    gather = within(to, PIECE) == over(at, rows)
-    gather = (gather & (over(to, PIECE) == over(within(at, rows), rep))).astype(BF16)
-    own = over(iota((8, LANES), 1), hidden) == within(iota((8, LANES), 0), rep)
-    own = own.astype(F32)
+    block = over(iota((step, LANES), 1), hidden)
     ones = jnp.ones((LANES, LANES), BF16)
     for turn in range(STEPS):
         x = []
@@ -92,16 +87,16 @@
             centered = x[half].astype(F32) - mean
             square = square + centered * centered
         spread = dot(square.astype(BF16), ones)
-        scale = lax.rsqrt(spread * (1.0 / channels) + EPSILON).reshape(-1, 8, LANES) * own[None]
-        scaled = (y[:, :LANES] - mean * sums) * scale.reshape(mean.shape)
-        y_scr[turn * step * rows : (turn + 1) * step * rows, :] = scaled.astype(BF16)
-        for piece in range(turn * step // PIECE, (turn + 1) * step // PIECE):
-            z = dot(gather, y_scr[piece * PIECE * rows : (piece + 1) * PIECE * rows, :])
-            here = slice(piece * PIECE, (piece + 1) * PIECE)
-            for group in range(groups):
-                lanes = slice(group * LANES, (group + 1) * LANES)
-                part = z[group * PIECE : (group + 1) * PIECE]
-                z_ref[group, here, :] = (part * live[here, lanes]).astype(BF16)
+        scale = lax.rsqrt(spread * (1.0 / channels) + EPSILON)
+        y_scr[turn] = (y[:, :LANES] - mean * sums) * scale
+        here = slice(turn * step, (turn + 1) * step)
+        for group in range(groups):
+            z = y_scr[turn, pl.ds(group * rep, step, stride=rows), :]
+            for k in range(1, rep):
+                next_z = y_scr[turn, pl.ds(group * rep + k, step, stride=rows), :]
+                z = jnp.where(block == k, next_z, z)
+            lanes = slice(group * LANES, (group + 1) * LANES)
+            z_ref[group, here, :] = (z * live[here, lanes]).astype(BF16)
 
 
 def factor(alignment, mask, weight):
@@ -114,7 +109,7 @@
         out_specs=vmem(),
         scratch_shapes=[
             pltpu.VMEM((channels // LANES, seqs, rows, LANES), BF16),
-            pltpu.VMEM((seqs * rows, LANES), BF16),
+            pltpu.VMEM((STEPS, seqs * rows // STEPS, LANES), F32),
             pltpu.SemaphoreType.DMA((STEPS, channels // LANES)),
         ],
         compiler_params=pltpu.CompilerParams(vmem_limit_bytes=119 << 19),
@@ -309,8 +304,8 @@
 
 def triangle_kernel(subs, ratio, cols, *refs):
     twos = subs // 2
+    rights, refs = refs[: twos * ratio], refs[twos * ratio :]
     lefts, refs = refs[:twos], refs[twos:]
-    rights, refs = refs[: twos * ratio], refs[twos * ratio :]
     (one_ref, gate_ref, out_ref, up_ref, down_ref, result_ref, left_scr, right_scr, sum_scr) = refs
     pairs, channels = one_ref.shape
     rows = pairs // cols
@@ -367,7 +362,7 @@
         cost_estimate=pl.CostEstimate(
             flops=2 * pairs * channels * 2048, bytes_accessed=2 << 20, transcendentals=pairs * 128
         ),
-    )(*lefts, *rights, one, gate, out, up, down)
+    )(*rights, *lefts, one, gate, out, up, down)
 
 
 def per_device(

time: 37.6 us -> 35.4 us (0.941)
  waiting for transfers between devices: 6.86 us -> 4.74 us
  Pallas kernels: 15.9 us -> 15.2 us
  starting transfers between devices: 13.2 us -> 13.7 us
    ppermute x5, waiting for transfers between devices: 6.86 us -> 4.74 us  [fetch(): return lax.ppermute(values, ('dap', 'sub'), perm)]
    pallas_call x2, Pallas kernels: 11.3 us -> 10.6 us  [factor(): pl.pallas_call(factor_kernel, out_shape=jax.ShapeDtypeStruct((rows * hidd...]
    ppermute x5, starting transfers between devices: 13.2 us -> 13.7 us  [fetch(): return lax.ppermute(values, ('dap', 'sub'), perm)]
  transfers between devices with their start and end apart: 5 -> 5, of which waited for: 3 -> 2; matrix products, arithmetic and copies ran while one was open for 0% -> 0% of each run, Pallas kernels for 17% -> 18%
where the time goes in v9:
time: 35.4 us; the launch traced here: 35.1 us
  Pallas kernels  15.2 us (43%)
  starting transfers between devices  13.7 us (39%)
  waiting for transfers between devices  4.74 us (13%)
  local copies, waits for them, and re-layouts  1.04 us (3%)
    ppermute x5, starting transfers between devices, fetch(): return lax.ppermute(values, ('dap', 'sub'), perm)  13.7 us
    pallas_call x2, Pallas kernels, factor(): pl.pallas_call(factor_kernel, out_shape=jax.ShapeDtypeStruct((rows * hidd...  10.6 us
    ppermute x5, waiting for transfers between devices, fetch(): return lax.ppermute(values, ('dap', 'sub'), perm)  4.74 us
    pallas_call x1, Pallas kernels, triangle_update(): pl.pallas_call(functools.partial(triangle_kernel, subs, ratio, cols), out...  2.21 us
    pallas_call x1, Pallas kernels, pair_update(): pl.pallas_call(functools.partial(pair_kernel, ratio, hidden), out_shape=(...  1.58 us
    unnamed x26, local copies, waits for them, and re-layouts  1.02 us
  transfers between devices with their start and end apart: 5, of which 2 were waited for; matrix products, arithmetic and copies ran while one was open for 0% of the time, Pallas kernels for 18%

profile of v9, /device:TPU:1, one launch (start us, length us, event | category | flops | bytes accessed | tf_op | source)
XLA Modules:
  0.0 35.1 jit_solution(8362669559003866887)
XLA Ops:
  0.0 5.3 %shard_map.147 = bf16[4,256,128]{2,1,0:T(8,128)(2,1)} custom-call(bf16[256,16,256]{2,1,0:T(8,128)(2,1)} %x_any.3, s32[64,256]{1,0:T(8,128)} %bitcast.5, bf16[32,256]{1,0:T(8,128)(2,1)} %bitcast.10), custom_call_target="tpu_custom_call" | custom-call | flops 1073741824 | bytes 4194304 | tf_op jit(solution)/shard_map/pallas_call | solution.py:105
  5.3 0.0 copy-start
  5.3 0.0 copy-start.4
  5.3 0.0 copy-start.5
  5.3 0.0 copy-start.10
  5.3 0.0 copy-start.11
  5.3 0.0 copy-start.12
  5.3 5.7 %collective-permute-start = (bf16[4,256,128]{2,1,0:T(8,128)(2,1)}, bf16[4,256,128]{2,1,0:T(8,128)(2,1)S(1)}, u32[]{:S(2)}, u32[]{:S(2)}) collective-permute-start(bf16[4,256,128]{2,1,0:T(8,128)(2,1)} %shard_map.147), channel_id=1, source_target_pairs={{0,0},{6,1},{11,2},{13,3},{2,4},{5,5},{9,6},{14,7},{1,8},{7,9},{10... | collective-permute-start | bytes 786440 | tf_op jit(solution)/shard_map/ppermute | solution.py:395
  11.1 0.0 copy-start.6
  11.1 0.0 copy-start.7
  11.1 0.0 copy-start.8
  11.1 0.0 copy-start.2
  11.1 0.0 copy-start.3
  11.2 0.0 copy-start.9
  11.2 5.4 %shard_map.145.zl_ref = bf16[4,256,128]{2,1,0:T(8,128)(2,1)} custom-call(bf16[256,16,256]{2,1,0:T(8,128)(2,1)} %x_any.3, s32[64,256]{1,0:T(8,128)} %bitcast.6, bf16[32,256]{1,0:T(8,128)(2,1)} %bitcast.11), custom_call_target="tpu_custom_call" | custom-call | flops 1073741824 | bytes 4194304 | tf_op jit(solution)/shard_map/pallas_call | solution.py:105
  16.5 0.0 copy-done
  16.5 0.0 copy-done.4
  16.6 0.0 copy-done.5
  16.6 0.0 copy-done.10
  16.6 0.0 copy-done.11
  16.6 0.0 copy-done.12
  16.6 0.0 copy-start.1
  16.6 0.9 %copy-done.1 = bf16[4,256,128]{2,1,0:T(8,128)(2,1)S(1)} copy-done((bf16[4,256,128]{2,1,0:T(8,128)(2,1)S(1)}, bf16[4,256,128]{2,1,0:T(8,128)(2,1)}, u32[]{:S(2)}) %copy-start.1) | copy-done | bytes 262168
  17.5 0.5 %shard_map.146 = (bf16[2,512,128]{2,1,0:T(8,128)(2,1)S(1)}, f32[256,128]{1,0:T(8,128)S(1)}, f32[256,128]{1,0:T(8,128)S(1)}, f32[256,128]{1,0:T(8,128)S(1)}, bf16[1024,128]{1,0:T(8,128)(2,1)S(1)}) custom-call(bf16[4,256,128]{2,1,0:T(8,128)(2,1)S(1)} %copy-done.1, s32[64,256]{1,0:T(8,128)S(1)} %bitcast.7, bf16[16,16,128]{2,1,0:T(8,128)(2,1)S(1)} %copy-done.5, ...), custom_call_target="tpu_custom_call" | custom-call | flops 134217728 | bytes 2097152 | tf_op jit(solution)/shard_map/pallas_call | solution.py:168
  18.1 0.0 collective-permute-done.refs_0_
  18.1 0.0 copy-done.6
  18.1 0.0 copy-done.7
  18.1 1.6 %shard_map.148 = (bf16[2,256,128]{2,1,0:T(8,128)(2,1)S(1)}, bf16[256,128]{1,0:T(8,128)(2,1)S(1)}) custom-call(bf16[2,512,128]{2,1,0:T(8,128)(2,1)S(1)} %get-tuple-element.12.zlt_ref, bf16[4,256,128]{2,1,0:T(8,128)(2,1)S(1)} %collective-permute-done.refs_0_, f32[256,128]{1,0:T(8,128)S(1)} %get-tuple-element.13.refs_1_, ...), custom_call_target="tpu_custom_call" | custom-call | flops 268435456 | bytes 2097152 | tf_op jit(solution)/shard_map/pallas_call | solution.py:247
  19.7 0.1 collective-permute-start.1
  19.8 1.3 %collective-permute-done.1 = bf16[2,256,128]{2,1,0:T(8,128)(2,1)S(1)} collective-permute-done((bf16[2,256,128]{2,1,0:T(8,128)(2,1)S(1)}, bf16[2,256,128]{2,1,0:T(8,128)(2,1)S(1)}, u32[]{:S(2)}, u32[]{:S(2)}) %collective-permute-start.1) | collective-permute-done | bytes 131104 | tf_op jit(solution)/shard_map/ppermute | solution.py:395
  21.1 4.1 %collective-permute-start.3 = (bf16[2,256,128]{2,1,0:T(8,128)(2,1)S(1)}, bf16[2,256,128]{2,1,0:T(8,128)(2,1)S(1)}, u32[]{:S(2)}, u32[]{:S(2)}) collective-permute-start(bf16[2,256,128]{2,1,0:T(8,128)(2,1)S(1)} %pad_maximum_fusion), channel_id=1, source_target_pairs={{2,0},{4,1},{9,2},{15,3},{0,4},{7,5},{11,6},{12,7},{3,8},{5,9},{8,... | collective-permute-start | bytes 393224 | tf_op jit(solution)/shard_map/ppermute | solution.py:395
  25.3 1.9 %collective-permute-start.2 = (bf16[2,256,128]{2,1,0:T(8,128)(2,1)S(1)}, bf16[2,256,128]{2,1,0:T(8,128)(2,1)S(1)}, u32[]{:S(2)}, u32[]{:S(2)}) collective-permute-start(bf16[2,256,128]{2,1,0:T(8,128)(2,1)S(1)} %pad_maximum_fusion), channel_id=1, source_target_pairs={{0,0},{6,1},{11,2},{13,3},{2,4},{5,5},{9,6},{14,7},{1,8},{7,9},{10... | collective-permute-start | bytes 393224 | tf_op jit(solution)/shard_map/ppermute | solution.py:395
  27.2 1.9 %collective-permute-start.4 = (bf16[2,256,128]{2,1,0:T(8,128)(2,1)S(1)}, bf16[2,256,128]{2,1,0:T(8,128)(2,1)S(1)}, u32[]{:S(2)}, u32[]{:S(2)}) collective-permute-start(bf16[2,256,128]{2,1,0:T(8,128)(2,1)S(1)} %pad_maximum_fusion.1.refs_2_), channel_id=1, source_target_pairs={{2,0},{3,1},{0,2},{1,3},{6,4},{7,5},{4,6},{5,7},{10,8},{11,9},{8,1... | collective-permute-start | bytes 393224 | tf_op jit(solution)/shard_map/ppermute | solution.py:395
  29.1 0.0 copy-done.8
  29.1 0.3 shard_map.149.refs_5_
  29.4 0.0 collective-permute-done.3.refs_1_
  29.4 3.4 %collective-permute-done.2.refs_0_ = bf16[2,256,128]{2,1,0:T(8,128)(2,1)S(1)} collective-permute-done((bf16[2,256,128]{2,1,0:T(8,128)(2,1)S(1)}, bf16[2,256,128]{2,1,0:T(8,128)(2,1)S(1)}, u32[]{:S(2)}, u32[]{:S(2)}) %collective-permute-start.2) | collective-permute-done | bytes 131104 | tf_op jit(solution)/shard_map/ppermute | solution.py:395
  32.9 0.0 collective-permute-done.4.refs_3_
  32.9 0.0 copy-done.2
  32.9 0.0 copy-done.3
  32.9 0.0 copy-done.9
  32.9 2.2 %shard_map.150 = bf16[16,16,128]{2,1,0:T(8,128)(2,1)} custom-call(bf16[2,256,128]{2,1,0:T(8,128)(2,1)S(1)} %collective-permute-done.2.refs_0_, bf16[2,256,128]{2,1,0:T(8,128)(2,1)S(1)} %collective-permute-done.3.refs_1_, bf16[2,256,128]{2,1,0:T(8,128)(2,1)S(1)} %pad_maximum_fusion.1.refs_2_, bf16[2,256,128]{2,1,0:T(8,128)(2,1)S(1)} %collective-permute-done.4.refs_3_, ...), custom_call_target="tpu_custom_call" | custom-call | flops 134217728 | bytes 2097152 | tf_op jit(solution)/shard_map/pallas_call | solution.py:351
  (4 shorter events, 0.1 us)
Async XLA Ops:
  5.3 11.3 %copy-start = (f32[32,32,128]{2,1,0:T(8,128)S(1)}, f32[32,32,128]{2,1,0:T(8,128)}, u32[]{:S(2)}) copy-start(f32[32,32,128]{2,1,0:T(8,128)} %proj_ref.1) | copy-start | bytes 1572868
  5.3 11.3 %copy-start.4 = (s32[256,64]{0,1:T(8,128)S(1)}, s32[256,64]{0,1:T(8,128)}, u32[]{:S(2)}) copy-start(s32[256,64]{0,1:T(8,128)} %param.16) | copy-start | bytes 196612
  5.3 11.3 %copy-start.5 = (bf16[16,16,128]{2,1,0:T(8,128)(2,1)S(1)}, bf16[16,16,128]{2,1,0:T(8,128)(2,1)}, u32[]{:S(2)}) copy-start(bf16[16,16,128]{2,1,0:T(8,128)(2,1)} %pair_ref.1) | copy-start | bytes 196612
  5.3 11.3 %copy-start.10 = (bf16[66,128]{1,0:T(8,128)(2,1)S(1)}, bf16[66,128]{1,0:T(8,128)(2,1)}, u32[]{:S(2)}) copy-start(bf16[66,128]{1,0:T(8,128)(2,1)} %table_ref.1) | copy-start | bytes 50692
  5.3 11.2 %copy-start.11 = (s32[64]{0:T(128)S(1)}, s32[64]{0:T(128)}, u32[]{:S(2)}) copy-start(s32[64]{0:T(128)} %param.18) | copy-start | bytes 772
  5.3 11.2 %copy-start.12 = (s32[64]{0:T(128)S(1)}, s32[64]{0:T(128)}, u32[]{:S(2)}) copy-start(s32[64]{0:T(128)} %param.19) | copy-start | bytes 772
  5.3 12.7 %collective-permute-start = (bf16[4,256,128]{2,1,0:T(8,128)(2,1)}, bf16[4,256,128]{2,1,0:T(8,128)(2,1)S(1)}, u32[]{:S(2)}, u32[]{:S(2)}) collective-permute-start(bf16[4,256,128]{2,1,0:T(8,128)(2,1)} %shard_map.147), channel_id=1, source_target_pairs={{0,0},{6,1},{11,2},{13,3},{2,4},{5,5},{9,6},{14,7},{1,8},{7,9},{10... | collective-permute-start | bytes 786440 | tf_op jit(solution)/shard_map/ppermute | solution.py:395
  11.1 7.0 %copy-start.6 = (bf16[128,256]{1,0:T(8,128)(2,1)S(1)}, bf16[128,256]{1,0:T(8,128)(2,1)}, u32[]{:S(2)}) copy-start(bf16[128,256]{1,0:T(8,128)(2,1)} %refs_5_.1) | copy-start | bytes 196612
  11.1 7.0 %copy-start.7 = (bf16[128,256]{1,0:T(8,128)(2,1)S(1)}, bf16[128,256]{1,0:T(8,128)(2,1)}, u32[]{:S(2)}) copy-start(bf16[128,256]{1,0:T(8,128)(2,1)} %refs_6_.2) | copy-start | bytes 196612
  11.1 18.0 %copy-start.8 = (bf16[128,128]{1,0:T(8,128)(2,1)S(1)}, bf16[128,128]{1,0:T(8,128)(2,1)}, u32[]{:S(2)}) copy-start(bf16[128,128]{1,0:T(8,128)(2,1)} %weight_ref.1) | copy-start | bytes 98308
  11.1 21.7 %copy-start.2 = (bf16[128,512]{1,0:T(8,128)(2,1)S(1)}, bf16[128,512]{1,0:T(8,128)(2,1)}, u32[]{:S(2)}) copy-start(bf16[128,512]{1,0:T(8,128)(2,1)} %refs_7_.1) | copy-start | bytes 393220
  11.1 21.7 %copy-start.3 = (bf16[512,128]{1,0:T(8,128)(2,1)S(1)}, bf16[512,128]{1,0:T(8,128)(2,1)}, u32[]{:S(2)}) copy-start(bf16[512,128]{1,0:T(8,128)(2,1)} %refs_8_.1) | copy-start | bytes 393220
  11.2 21.7 %copy-start.9 = (bf16[128,128]{1,0:T(8,128)(2,1)S(1)}, bf16[128,128]{1,0:T(8,128)(2,1)}, u32[]{:S(2)}) copy-start(bf16[128,128]{1,0:T(8,128)(2,1)} %refs_6_.3) | copy-start | bytes 98308
  16.6 1.0 %copy-start.1 = (bf16[4,256,128]{2,1,0:T(8,128)(2,1)S(1)}, bf16[4,256,128]{2,1,0:T(8,128)(2,1)}, u32[]{:S(2)}) copy-start(bf16[4,256,128]{2,1,0:T(8,128)(2,1)} %shard_map.145.zl_ref) | copy-start | bytes 786436
  19.7 1.4 %collective-permute-start.1 = (bf16[2,256,128]{2,1,0:T(8,128)(2,1)S(1)}, bf16[2,256,128]{2,1,0:T(8,128)(2,1)S(1)}, u32[]{:S(2)}, u32[]{:S(2)}) collective-permute-start(bf16[2,256,128]{2,1,0:T(8,128)(2,1)S(1)} %get-tuple-element.17), channel_id=1, source_target_pairs={{1,0},{0,1},{3,2},{2,3},{5,4},{4,5},{7,6},{6,7},{9,8},{8,9},{11,10... | collective-permute-start | bytes 393224 | tf_op jit(solution)/shard_map/ppermute | solution.py:395
  21.1 8.3 %collective-permute-start.3 = (bf16[2,256,128]{2,1,0:T(8,128)(2,1)S(1)}, bf16[2,256,128]{2,1,0:T(8,128)(2,1)S(1)}, u32[]{:S(2)}, u32[]{:S(2)}) collective-permute-start(bf16[2,256,128]{2,1,0:T(8,128)(2,1)S(1)} %pad_maximum_fusion), channel_id=1, source_target_pairs={{2,0},{4,1},{9,2},{15,3},{0,4},{7,5},{11,6},{12,7},{3,8},{5,9},{8,... | collective-permute-start | bytes 393224 | tf_op jit(solution)/shard_map/ppermute | solution.py:395
  25.3 7.6 %collective-permute-start.2 = (bf16[2,256,128]{2,1,0:T(8,128)(2,1)S(1)}, bf16[2,256,128]{2,1,0:T(8,128)(2,1)S(1)}, u32[]{:S(2)}, u32[]{:S(2)}) collective-permute-start(bf16[2,256,128]{2,1,0:T(8,128)(2,1)S(1)} %pad_maximum_fusion), channel_id=1, source_target_pairs={{0,0},{6,1},{11,2},{13,3},{2,4},{5,5},{9,6},{14,7},{1,8},{7,9},{10... | collective-permute-start | bytes 393224 | tf_op jit(solution)/shard_map/ppermute | solution.py:395
  27.2 5.7 %collective-permute-start.4 = (bf16[2,256,128]{2,1,0:T(8,128)(2,1)S(1)}, bf16[2,256,128]{2,1,0:T(8,128)(2,1)S(1)}, u32[]{:S(2)}, u32[]{:S(2)}) collective-permute-start(bf16[2,256,128]{2,1,0:T(8,128)(2,1)S(1)} %pad_maximum_fusion.1.refs_2_), channel_id=1, source_target_pairs={{2,0},{3,1},{0,2},{1,3},{6,4},{7,5},{4,6},{5,7},{10,8},{11,9},{8,1... | collective-permute-start | bytes 393224 | tf_op jit(solution)/shard_map/ppermute | solution.py:395

commit v10 on v9

--- a/solution.py
+++ b/solution.py
@@ -52,21 +52,14 @@
     return lax.bitwise_and(index, size - 1)
 
 
-def factor_kernel(x_any, mask_ref, weight_ref, z_ref, x_scr, y_scr, sems):
-    halves, seqs, rows, _ = x_scr.shape
-    hidden, channels = weight_ref.shape
+def factor_kernel(x_ref, mask_ref, weight_ref, z_ref, y_scr):
+    seqs, rows, channels = x_ref.shape
+    hidden = weight_ref.shape[0]
     rep = LANES // hidden
     groups = rows // rep
     residues = mask_ref.shape[0]
     width = rows * hidden
     step = seqs // STEPS
-    copies = []
-    for turn in range(STEPS):
-        part = pl.ds(turn * step, step)
-        for half in range(halves):
-            source = x_any.at[part, :, pl.ds(half * LANES, LANES)]
-            copies.append(pltpu.make_async_copy(source, x_scr.at[half, part], sems.at[turn, half]))
-            copies[-1].start()
     weight = jnp.concatenate([weight_ref[...]] * rep, axis=0).T
     w = jnp.concatenate([weight, jnp.ones((channels, LANES), BF16)], axis=1)
     sums = dot(jnp.ones((8, channels), BF16), w)[:1, :LANES]
@@ -76,15 +69,12 @@
     block = over(iota((step, LANES), 1), hidden)
     ones = jnp.ones((LANES, LANES), BF16)
     for turn in range(STEPS):
-        x = []
-        for half in range(halves):
-            copies[turn * halves + half].wait()
-            x.append(x_scr[half, turn * step : (turn + 1) * step].reshape(step * rows, LANES))
-        y = dot(jnp.concatenate(x, axis=1), w)
+        x = x_ref[turn * step : (turn + 1) * step].reshape(step * rows, channels)
+        y = dot(x, w)
         mean = y[:, LANES:] * (1.0 / channels)
         square = jnp.zeros_like(mean)
-        for half in range(halves):
-            centered = x[half].astype(F32) - mean
+        for half in range(channels // LANES):
+            centered = x[:, half * LANES : (half + 1) * LANES].astype(F32) - mean
             square = square + centered * centered
         spread = dot(square.astype(BF16), ones)
         scale = lax.rsqrt(spread * (1.0 / channels) + EPSILON)
@@ -105,14 +95,12 @@
     return pl.pallas_call(
         factor_kernel,
         out_shape=jax.ShapeDtypeStruct((rows * hidden // LANES, seqs, LANES), BF16),
-        in_specs=[pl.BlockSpec(memory_space=pl.ANY), vmem(), vmem()],
+        in_specs=[vmem()] * 3,
         out_specs=vmem(),
         scratch_shapes=[
-            pltpu.VMEM((channels // LANES, seqs, rows, LANES), BF16),
             pltpu.VMEM((STEPS, seqs * rows // STEPS, LANES), F32),
-            pltpu.SemaphoreType.DMA((STEPS, channels // LANES)),
         ],
-        compiler_params=pltpu.CompilerParams(vmem_limit_bytes=119 << 19),
+        compiler_params=pltpu.CompilerParams(vmem_limit_bytes=24 << 20),
         cost_estimate=pl.CostEstimate(
             flops=2 * seqs * rows * channels * 512, bytes_accessed=4 << 20, transcendentals=0
         ),

time: 35.4 us -> 35.2 us (level)
  Pallas kernels: 15.2 us -> 8.97 us
  waiting for transfers between devices: 4.74 us -> 7.19 us
  local copies, waits for them, and re-layouts: 1.04 us -> 3.24 us
  starting transfers between devices: 13.7 us -> 15.2 us
    pallas_call x2, Pallas kernels: 10.6 us -> 4.34 us  [factor(): pl.pallas_call(factor_kernel, out_shape=jax.ShapeDtypeStruct((rows * hidd...]
    ppermute x5, waiting for transfers between devices: 4.74 us -> 7.19 us  [fetch(): return lax.ppermute(values, ('dap', 'sub'), perm)]
    unnamed x26 -> x30, local copies, waits for them, and re-layouts: 1.02 us -> 3.22 us
    ppermute x5, starting transfers between devices: 13.7 us -> 15.2 us  [fetch(): return lax.ppermute(values, ('dap', 'sub'), perm)]
  transfers between devices with their start and end apart: 5 -> 5, of which waited for: 2 -> 4; matrix products, arithmetic and copies ran while one was open for 0% -> 0% of each run, Pallas kernels for 18% -> 9%
where the time goes in v10:
time: 35.2 us; the launch traced here: 34.9 us
  starting transfers between devices  15.2 us (43%)
  Pallas kernels  8.97 us (25%)
  waiting for transfers between devices  7.19 us (20%)
  local copies, waits for them, and re-layouts  3.24 us (9%)
    ppermute x5, starting transfers between devices, fetch(): return lax.ppermute(values, ('dap', 'sub'), perm)  15.2 us
    ppermute x5, waiting for transfers between devices, fetch(): return lax.ppermute(values, ('dap', 'sub'), perm)  7.19 us
    pallas_call x2, Pallas kernels, factor(): pl.pallas_call(factor_kernel, out_shape=jax.ShapeDtypeStruct((rows * hidd...  4.34 us
    unnamed x30, local copies, waits for them, and re-layouts  3.22 us
    pallas_call x1, Pallas kernels, triangle_update(): pl.pallas_call(functools.partial(triangle_kernel, subs, ratio, cols), out...  2.21 us
    pallas_call x1, Pallas kernels, pair_update(): pl.pallas_call(functools.partial(pair_kernel, ratio, hidden), out_shape=(...  1.58 us
  transfers between devices with their start and end apart: 5, of which 4 were waited for; matrix products, arithmetic and copies ran while one was open for 0% of the time, Pallas kernels for 9%

profile of v10, /device:TPU:1, one launch (start us, length us, event | category | flops | bytes accessed | tf_op | source)
XLA Modules:
  0.0 34.9 jit_solution(13663651488081862400)
XLA Ops:
  0.0 0.0 copy-start.3
  0.0 0.8 %copy-done.3 = s32[256,64]{0,1:T(8,128)S(1)} copy-done((s32[256,64]{0,1:T(8,128)S(1)}, s32[256,64]{0,1:T(8,128)}, u32[]{:S(2)}) %copy-start.3) | copy-done | bytes 65560
  0.8 0.0 copy-start.12
  0.8 1.6 %copy-done.12 = bf16[256,16,256]{2,1,0:T(8,128)(2,1)S(1)} copy-done((bf16[256,16,256]{2,1,0:T(8,128)(2,1)S(1)}, bf16[256,16,256]{2,1,0:T(8,128)(2,1)}, u32[]{:S(2)}) %copy-start.12) | copy-done | bytes 2097176
  2.4 0.0 copy-start.13
  2.4 0.7 %copy-done.13 = bf16[256,32]{0,1:T(8,128)(2,1)S(1)} copy-done((bf16[256,32]{0,1:T(8,128)(2,1)S(1)}, bf16[256,32]{0,1:T(8,128)(2,1)}, u32[]{:S(2)}) %copy-start.13) | copy-done | bytes 16408
  3.1 0.0 copy-start.14
  3.2 2.2 %shard_map.147 = bf16[4,256,128]{2,1,0:T(8,128)(2,1)S(1)} custom-call(bf16[256,16,256]{2,1,0:T(8,128)(2,1)S(1)} %copy-done.12, s32[64,256]{1,0:T(8,128)S(1)} %bitcast.5, bf16[32,256]{1,0:T(8,128)(2,1)S(1)} %bitcast.10), custom_call_target="tpu_custom_call" | custom-call | flops 1073741824 | bytes 4194304 | tf_op jit(solution)/shard_map/pallas_call | solution.py:95
  5.3 0.0 copy-start
  5.3 0.0 copy-start.4
  5.4 0.0 copy-start.9
  5.4 0.0 copy-start.10
  5.4 0.0 copy-start.11
  5.4 5.7 %collective-permute-start = (bf16[4,256,128]{2,1,0:T(8,128)(2,1)S(1)}, bf16[4,256,128]{2,1,0:T(8,128)(2,1)S(1)}, u32[]{:S(2)}, u32[]{:S(2)}) collective-permute-start(bf16[4,256,128]{2,1,0:T(8,128)(2,1)S(1)} %shard_map.147), channel_id=1, source_target_pairs={{0,0},{6,1},{11,2},{13,3},{2,4},{5,5},{9,6},{14,7},{1,8},{7,9},{10... | collective-permute-start | bytes 786440 | tf_op jit(solution)/shard_map/ppermute | solution.py:383
  11.1 0.0 copy-done.14
  11.1 0.0 copy-start.5
  11.2 0.0 copy-start.6
  11.2 2.2 %shard_map.145.zl_ref = bf16[4,256,128]{2,1,0:T(8,128)(2,1)S(1)} custom-call(bf16[256,16,256]{2,1,0:T(8,128)(2,1)S(1)} %copy-done.12, s32[64,256]{1,0:T(8,128)S(1)} %bitcast.6, bf16[32,256]{1,0:T(8,128)(2,1)S(1)} %bitcast.11), custom_call_target="tpu_custom_call" | custom-call | flops 1073741824 | bytes 4194304 | tf_op jit(solution)/shard_map/pallas_call | solution.py:95
  13.3 0.0 copy-start.7
  13.4 0.0 copy-start.1
  13.4 0.0 copy-start.2
  13.4 0.0 copy-start.8
  13.4 0.0 copy-done
  13.4 0.0 copy-done.4
  13.4 0.0 copy-done.9
  13.4 0.0 copy-done.10
  13.4 0.0 copy-done.11
  13.4 0.5 %shard_map.146 = (bf16[2,512,128]{2,1,0:T(8,128)(2,1)S(1)}, f32[256,128]{1,0:T(8,128)S(1)}, f32[256,128]{1,0:T(8,128)S(1)}, f32[256,128]{1,0:T(8,128)S(1)}, bf16[1024,128]{1,0:T(8,128)(2,1)S(1)}) custom-call(bf16[4,256,128]{2,1,0:T(8,128)(2,1)S(1)} %shard_map.145.zl_ref, s32[64,256]{1,0:T(8,128)S(1)} %bitcast.7, bf16[16,16,128]{2,1,0:T(8,128)(2,1)S(1)} %copy-done.4, ...), custom_call_target="tpu_custom_call" | custom-call | flops 134217728 | bytes 2097152 | tf_op jit(solution)/shard_map/pallas_call | solution.py:156
  14.0 2.4 %collective-permute-done.refs_0_ = bf16[4,256,128]{2,1,0:T(8,128)(2,1)S(1)} collective-permute-done((bf16[4,256,128]{2,1,0:T(8,128)(2,1)S(1)}, bf16[4,256,128]{2,1,0:T(8,128)(2,1)S(1)}, u32[]{:S(2)}, u32[]{:S(2)}) %collective-permute-start) | collective-permute-done | bytes 262176 | tf_op jit(solution)/shard_map/ppermute | solution.py:383
  16.4 0.0 copy-done.5
  16.4 0.0 copy-done.6
  16.4 1.6 %shard_map.148 = (bf16[2,256,128]{2,1,0:T(8,128)(2,1)S(1)}, bf16[256,128]{1,0:T(8,128)(2,1)S(1)}) custom-call(bf16[2,512,128]{2,1,0:T(8,128)(2,1)S(1)} %get-tuple-element.12.zlt_ref, bf16[4,256,128]{2,1,0:T(8,128)(2,1)S(1)} %collective-permute-done.refs_0_, f32[256,128]{1,0:T(8,128)S(1)} %get-tuple-element.13.refs_1_, ...), custom_call_target="tpu_custom_call" | custom-call | flops 268435456 | bytes 2097152 | tf_op jit(solution)/shard_map/pallas_call | solution.py:235
  18.0 0.1 collective-permute-start.1
  18.1 1.3 %collective-permute-done.1 = bf16[2,256,128]{2,1,0:T(8,128)(2,1)S(1)} collective-permute-done((bf16[2,256,128]{2,1,0:T(8,128)(2,1)S(1)}, bf16[2,256,128]{2,1,0:T(8,128)(2,1)S(1)}, u32[]{:S(2)}, u32[]{:S(2)}) %collective-permute-start.1) | collective-permute-done | bytes 131104 | tf_op jit(solution)/shard_map/ppermute | solution.py:383
  19.5 5.6 %collective-permute-start.3 = (bf16[2,256,128]{2,1,0:T(8,128)(2,1)S(1)}, bf16[2,256,128]{2,1,0:T(8,128)(2,1)S(1)}, u32[]{:S(2)}, u32[]{:S(2)}) collective-permute-start(bf16[2,256,128]{2,1,0:T(8,128)(2,1)S(1)} %pad_maximum_fusion), channel_id=1, source_target_pairs={{2,0},{4,1},{9,2},{15,3},{0,4},{7,5},{11,6},{12,7},{3,8},{5,9},{8,... | collective-permute-start | bytes 393224 | tf_op jit(solution)/shard_map/ppermute | solution.py:383
  25.1 1.9 %collective-permute-start.2 = (bf16[2,256,128]{2,1,0:T(8,128)(2,1)S(1)}, bf16[2,256,128]{2,1,0:T(8,128)(2,1)S(1)}, u32[]{:S(2)}, u32[]{:S(2)}) collective-permute-start(bf16[2,256,128]{2,1,0:T(8,128)(2,1)S(1)} %pad_maximum_fusion), channel_id=1, source_target_pairs={{0,0},{6,1},{11,2},{13,3},{2,4},{5,5},{9,6},{14,7},{1,8},{7,9},{10... | collective-permute-start | bytes 393224 | tf_op jit(solution)/shard_map/ppermute | solution.py:383
  27.0 1.9 %collective-permute-start.4 = (bf16[2,256,128]{2,1,0:T(8,128)(2,1)S(1)}, bf16[2,256,128]{2,1,0:T(8,128)(2,1)S(1)}, u32[]{:S(2)}, u32[]{:S(2)}) collective-permute-start(bf16[2,256,128]{2,1,0:T(8,128)(2,1)S(1)} %pad_maximum_fusion.1.refs_2_), channel_id=1, source_target_pairs={{2,0},{3,1},{0,2},{1,3},{6,4},{7,5},{4,6},{5,7},{10,8},{11,9},{8,1... | collective-permute-start | bytes 393224 | tf_op jit(solution)/shard_map/ppermute | solution.py:383
  28.9 0.0 copy-done.7
  28.9 0.3 shard_map.149.refs_5_
  29.3 0.0 collective-permute-done.3.refs_1_
  29.3 3.2 %collective-permute-done.2.refs_0_ = bf16[2,256,128]{2,1,0:T(8,128)(2,1)S(1)} collective-permute-done((bf16[2,256,128]{2,1,0:T(8,128)(2,1)S(1)}, bf16[2,256,128]{2,1,0:T(8,128)(2,1)S(1)}, u32[]{:S(2)}, u32[]{:S(2)}) %collective-permute-start.2) | collective-permute-done | bytes 131104 | tf_op jit(solution)/shard_map/ppermute | solution.py:383
  32.5 0.2 collective-permute-done.4.refs_3_
  32.7 0.0 copy-done.1
  32.7 0.0 copy-done.2
  32.7 0.0 copy-done.8
  32.7 2.2 %shard_map.150 = bf16[16,16,128]{2,1,0:T(8,128)(2,1)} custom-call(bf16[2,256,128]{2,1,0:T(8,128)(2,1)S(1)} %collective-permute-done.2.refs_0_, bf16[2,256,128]{2,1,0:T(8,128)(2,1)S(1)} %collective-permute-done.3.refs_1_, bf16[2,256,128]{2,1,0:T(8,128)(2,1)S(1)} %pad_maximum_fusion.1.refs_2_, bf16[2,256,128]{2,1,0:T(8,128)(2,1)S(1)} %collective-permute-done.4.refs_3_, ...), custom_call_target="tpu_custom_call" | custom-call | flops 134217728 | bytes 2097152 | tf_op jit(solution)/shard_map/pallas_call | solution.py:339
  (4 shorter events, 0.1 us)
Async XLA Ops:
  0.0 0.8 %copy-start.3 = (s32[256,64]{0,1:T(8,128)S(1)}, s32[256,64]{0,1:T(8,128)}, u32[]{:S(2)}) copy-start(s32[256,64]{0,1:T(8,128)} %param.16) | copy-start | bytes 196612
  0.8 1.6 %copy-start.12 = (bf16[256,16,256]{2,1,0:T(8,128)(2,1)S(1)}, bf16[256,16,256]{2,1,0:T(8,128)(2,1)}, u32[]{:S(2)}) copy-start(bf16[256,16,256]{2,1,0:T(8,128)(2,1)} %x_ref.3) | copy-start | bytes 6291460
  2.4 0.7 %copy-start.13 = (bf16[256,32]{0,1:T(8,128)(2,1)S(1)}, bf16[256,32]{0,1:T(8,128)(2,1)}, u32[]{:S(2)}) copy-start(bf16[256,32]{0,1:T(8,128)(2,1)} %param.21) | copy-start | bytes 49156
  3.1 8.0 %copy-start.14 = (bf16[256,32]{0,1:T(8,128)(2,1)S(1)}, bf16[256,32]{0,1:T(8,128)(2,1)}, u32[]{:S(2)}) copy-start(bf16[256,32]{0,1:T(8,128)(2,1)} %param.20) | copy-start | bytes 49156
  5.3 8.1 %copy-start = (f32[32,32,128]{2,1,0:T(8,128)S(1)}, f32[32,32,128]{2,1,0:T(8,128)}, u32[]{:S(2)}) copy-start(f32[32,32,128]{2,1,0:T(8,128)} %proj_ref.1) | copy-start | bytes 1572868
  5.3 8.1 %copy-start.4 = (bf16[16,16,128]{2,1,0:T(8,128)(2,1)S(1)}, bf16[16,16,128]{2,1,0:T(8,128)(2,1)}, u32[]{:S(2)}) copy-start(bf16[16,16,128]{2,1,0:T(8,128)(2,1)} %pair_ref.1) | copy-start | bytes 196612
  5.4 8.1 %copy-start.9 = (bf16[66,128]{1,0:T(8,128)(2,1)S(1)}, bf16[66,128]{1,0:T(8,128)(2,1)}, u32[]{:S(2)}) copy-start(bf16[66,128]{1,0:T(8,128)(2,1)} %table_ref.1) | copy-start | bytes 50692
  5.4 8.1 %copy-start.10 = (s32[64]{0:T(128)S(1)}, s32[64]{0:T(128)}, u32[]{:S(2)}) copy-start(s32[64]{0:T(128)} %param.18) | copy-start | bytes 772
  5.4 8.1 %copy-start.11 = (s32[64]{0:T(128)S(1)}, s32[64]{0:T(128)}, u32[]{:S(2)}) copy-start(s32[64]{0:T(128)} %param.19) | copy-start | bytes 772
  5.4 11.0 %collective-permute-start = (bf16[4,256,128]{2,1,0:T(8,128)(2,1)S(1)}, bf16[4,256,128]{2,1,0:T(8,128)(2,1)S(1)}, u32[]{:S(2)}, u32[]{:S(2)}) collective-permute-start(bf16[4,256,128]{2,1,0:T(8,128)(2,1)S(1)} %shard_map.147), channel_id=1, source_target_pairs={{0,0},{6,1},{11,2},{13,3},{2,4},{5,5},{9,6},{14,7},{1,8},{7,9},{10... | collective-permute-start | bytes 786440 | tf_op jit(solution)/shard_map/ppermute | solution.py:383
  11.1 5.3 %copy-start.5 = (bf16[128,256]{1,0:T(8,128)(2,1)S(1)}, bf16[128,256]{1,0:T(8,128)(2,1)}, u32[]{:S(2)}) copy-start(bf16[128,256]{1,0:T(8,128)(2,1)} %refs_5_.1) | copy-start | bytes 196612
  11.2 5.3 %copy-start.6 = (bf16[128,256]{1,0:T(8,128)(2,1)S(1)}, bf16[128,256]{1,0:T(8,128)(2,1)}, u32[]{:S(2)}) copy-start(bf16[128,256]{1,0:T(8,128)(2,1)} %refs_6_.2) | copy-start | bytes 196612
  13.3 15.6 %copy-start.7 = (bf16[128,128]{1,0:T(8,128)(2,1)S(1)}, bf16[128,128]{1,0:T(8,128)(2,1)}, u32[]{:S(2)}) copy-start(bf16[128,128]{1,0:T(8,128)(2,1)} %weight_ref.1) | copy-start | bytes 98308
  13.4 19.3 %copy-start.1 = (bf16[128,512]{1,0:T(8,128)(2,1)S(1)}, bf16[128,512]{1,0:T(8,128)(2,1)}, u32[]{:S(2)}) copy-start(bf16[128,512]{1,0:T(8,128)(2,1)} %refs_7_.1) | copy-start | bytes 393220
  13.4 19.3 %copy-start.2 = (bf16[512,128]{1,0:T(8,128)(2,1)S(1)}, bf16[512,128]{1,0:T(8,128)(2,1)}, u32[]{:S(2)}) copy-start(bf16[512,128]{1,0:T(8,128)(2,1)} %refs_8_.1) | copy-start | bytes 393220
  13.4 19.3 %copy-start.8 = (bf16[128,128]{1,0:T(8,128)(2,1)S(1)}, bf16[128,128]{1,0:T(8,128)(2,1)}, u32[]{:S(2)}) copy-start(bf16[128,128]{1,0:T(8,128)(2,1)} %refs_6_.3) | copy-start | bytes 98308
  18.0 1.4 %collective-permute-start.1 = (bf16[2,256,128]{2,1,0:T(8,128)(2,1)S(1)}, bf16[2,256,128]{2,1,0:T(8,128)(2,1)S(1)}, u32[]{:S(2)}, u32[]{:S(2)}) collective-permute-start(bf16[2,256,128]{2,1,0:T(8,128)(2,1)S(1)} %get-tuple-element.17), channel_id=1, source_target_pairs={{1,0},{0,1},{3,2},{2,3},{5,4},{4,5},{7,6},{6,7},{9,8},{8,9},{11,10... | collective-permute-start | bytes 393224 | tf_op jit(solution)/shard_map/ppermute | solution.py:383
  19.5 9.8 %collective-permute-start.3 = (bf16[2,256,128]{2,1,0:T(8,128)(2,1)S(1)}, bf16[2,256,128]{2,1,0:T(8,128)(2,1)S(1)}, u32[]{:S(2)}, u32[]{:S(2)}) collective-permute-start(bf16[2,256,128]{2,1,0:T(8,128)(2,1)S(1)} %pad_maximum_fusion), channel_id=1, source_target_pairs={{2,0},{4,1},{9,2},{15,3},{0,4},{7,5},{11,6},{12,7},{3,8},{5,9},{8,... | collective-permute-start | bytes 393224 | tf_op jit(solution)/shard_map/ppermute | solution.py:383
  25.1 7.4 %collective-permute-start.2 = (bf16[2,256,128]{2,1,0:T(8,128)(2,1)S(1)}, bf16[2,256,128]{2,1,0:T(8,128)(2,1)S(1)}, u32[]{:S(2)}, u32[]{:S(2)}) collective-permute-start(bf16[2,256,128]{2,1,0:T(8,128)(2,1)S(1)} %pad_maximum_fusion), channel_id=1, source_target_pairs={{0,0},{6,1},{11,2},{13,3},{2,4},{5,5},{9,6},{14,7},{1,8},{7,9},{10... | collective-permute-start | bytes 393224 | tf_op jit(solution)/shard_map/ppermute | solution.py:383
  27.0 5.7 %collective-permute-start.4 = (bf16[2,256,128]{2,1,0:T(8,128)(2,1)S(1)}, bf16[2,256,128]{2,1,0:T(8,128)(2,1)S(1)}, u32[]{:S(2)}, u32[]{:S(2)}) collective-permute-start(bf16[2,256,128]{2,1,0:T(8,128)(2,1)S(1)} %pad_maximum_fusion.1.refs_2_), channel_id=1, source_target_pairs={{2,0},{3,1},{0,2},{1,3},{6,4},{7,5},{4,6},{5,7},{10,8},{11,9},{8,1... | collective-permute-start | bytes 393224 | tf_op jit(solution)/shard_map/ppermute | solution.py:383

commit v11 on v10

--- a/solution.py
+++ b/solution.py
@@ -9,7 +9,7 @@
 
 REL_CLIP = 32
 LANES = 128
-STEPS = 4
+PARTS = 2
 EPSILON = 1e-05
 BF16 = jnp.bfloat16
 F32 = jnp.float32
@@ -52,24 +52,25 @@
     return lax.bitwise_and(index, size - 1)
 
 
-def factor_kernel(x_ref, mask_ref, weight_ref, z_ref, y_scr):
-    seqs, rows, channels = x_ref.shape
-    hidden = weight_ref.shape[0]
+def factor_kernel(first, hidden, x_ref, weight_ref, *refs):
+    mask_ref = refs[0] if len(refs) == 3 else None
+    z_ref, y_scr = refs[-2:]
+    groups, seqs, _ = z_ref.shape
+    _, rows, channels = x_ref.shape
     rep = LANES // hidden
-    groups = rows // rep
-    residues = mask_ref.shape[0]
     width = rows * hidden
-    step = seqs // STEPS
-    weight = jnp.concatenate([weight_ref[...]] * rep, axis=0).T
-    w = jnp.concatenate([weight, jnp.ones((channels, LANES), BF16)], axis=1)
+    step = y_scr.shape[1] // rows
+    w = jnp.concatenate([weight_ref[...].T, jnp.ones((channels, LANES), BF16)], axis=1)
     sums = dot(jnp.ones((8, channels), BF16), w)[:1, :LANES]
-    start = lax.axis_index("dap") * rows
-    spread = iota((residues, width), 0) == start + over(iota((residues, width), 1), hidden)
-    live = dot_tn(mask_ref[...].astype(BF16), spread.astype(BF16))
+    if mask_ref is not None:
+        residues = mask_ref.shape[0]
+        start = lax.axis_index("dap") * rows
+        spread = iota((residues, width), 0) == start + over(iota((residues, width), 1), hidden)
+        live = dot_tn(mask_ref[...].astype(BF16), spread.astype(BF16))
     block = over(iota((step, LANES), 1), hidden)
     ones = jnp.ones((LANES, LANES), BF16)
-    for turn in range(STEPS):
-        x = x_ref[turn * step : (turn + 1) * step].reshape(step * rows, channels)
+    for turn in range(seqs // step):
+        x = x_ref[first + turn * step : first + (turn + 1) * step].reshape(step * rows, channels)
         y = dot(x, w)
         mean = y[:, LANES:] * (1.0 / channels)
         square = jnp.zeros_like(mean)
@@ -85,31 +86,31 @@
             for k in range(1, rep):
                 next_z = y_scr[turn, pl.ds(group * rep + k, step, stride=rows), :]
                 z = jnp.where(block == k, next_z, z)
-            lanes = slice(group * LANES, (group + 1) * LANES)
-            z_ref[group, here, :] = (z * live[here, lanes]).astype(BF16)
-
-
-def factor(alignment, mask, weight):
-    seqs, rows, channels = alignment.shape
-    hidden = weight.shape[0]
+            if mask_ref is not None:
+                z = z * live[here, group * LANES : (group + 1) * LANES]
+            z_ref[group, here, :] = z.astype(BF16)
+
+
+def factor(alignment, weight, hidden, first, seqs, mask=None):
+    _, rows, channels = alignment.shape
+    step = seqs // 4 if mask is not None else seqs // 2
+    operands = (alignment, weight) if mask is None else (alignment, weight, mask)
     return pl.pallas_call(
-        factor_kernel,
+        functools.partial(factor_kernel, first, hidden),
         out_shape=jax.ShapeDtypeStruct((rows * hidden // LANES, seqs, LANES), BF16),
-        in_specs=[vmem()] * 3,
+        in_specs=[vmem()] * len(operands),
         out_specs=vmem(),
-        scratch_shapes=[
-            pltpu.VMEM((STEPS, seqs * rows // STEPS, LANES), F32),
-        ],
+        scratch_shapes=[pltpu.VMEM((seqs // step, step * rows, LANES), F32)],
         compiler_params=pltpu.CompilerParams(vmem_limit_bytes=24 << 20),
         cost_estimate=pl.CostEstimate(
-            flops=2 * seqs * rows * channels * 512, bytes_accessed=4 << 20, transcendentals=0
-        ),
-    )(alignment, mask, weight)
+            flops=2 * seqs * rows * channels * 512, bytes_accessed=seqs << 14, transcendentals=0
+        ),
+    )(*operands)
 
 
 def prepare_kernel(
     zl_ref, mask_ref, pair_ref, live_ref, chain_ref, table_ref, proj_ref,
-    zlt_ref, base_ref, inverse_ref, live_out_ref, proj_out_ref, pair_scr, table_scr,
+    zlt_ref, base_ref, inverse_ref, live_out_ref, proj_out_ref, seen_ref, pair_scr, table_scr,
 ):
     rows, cols, _ = pair_ref.shape
     pairs = rows * cols
@@ -123,6 +124,15 @@
             lanes = slice(half * LANES, (half + 1) * LANES)
             zlt_ref[half, group * LANES : (group + 1) * LANES, :] = turned[:, lanes]
     proj_out_ref[...] = proj_ref[...].reshape(proj_out_ref.shape).astype(BF16)
+    groups = zl_ref.shape[0]
+    width = groups * LANES
+    hidden = width // rows
+    for block in range(cols // rows):
+        column = col_start + block * rows + over(iota((residues, width), 1), hidden)
+        spread = (iota((residues, width), 0) == column).astype(BF16)
+        seen = dot_tn(mask_ref[...].astype(BF16), spread).astype(BF16)
+        for group in range(groups):
+            seen_ref[block * groups + group] = seen[:, group * LANES : (group + 1) * LANES]
     which = iota((pairs, residues), 0)
     place = iota((pairs, residues), 1)
     pick_row = (place == row_start + within(which, rows)).astype(BF16)
@@ -161,9 +171,10 @@
             shape,
             shape,
             jax.ShapeDtypeStruct((depth, channels), BF16),
+            jax.ShapeDtypeStruct((cols // rows * zl.shape[0], *zl.shape[1:]), BF16),
         ),
         in_specs=[vmem()] * 7,
-        out_specs=[vmem()] * 5,
+        out_specs=[vmem()] * 6,
         scratch_shapes=[pltpu.VMEM((pairs, channels), F32), pltpu.VMEM((LANES, channels), F32)],
         compiler_params=pltpu.CompilerParams(vmem_limit_bytes=24 << 20),
         cost_estimate=pl.CostEstimate(
@@ -173,8 +184,8 @@
 
 
 def pair_kernel(ratio, hidden, zlt_ref, *refs):
-    zr_refs, refs = refs[:ratio], refs[ratio:]
-    (base_ref, inverse_ref, live_ref, proj_ref, tl_ref, tr_ref,
+    zr_refs, refs = refs[: ratio * PARTS], refs[ratio * PARTS :]
+    (seen_ref, base_ref, inverse_ref, live_ref, proj_ref, tl_ref, tr_ref,
      both_ref, one_ref, outer_scr, flat_scr, one_scr) = refs
     pairs, channels = base_ref.shape
     rows = zlt_ref.shape[1] // hidden
@@ -187,7 +198,10 @@
     left = jnp.concatenate([zlt_ref[part] for part in range(zlt_ref.shape[0])], axis=1)
     for step in range(ratio):
         block = lax.rem(me + step, ratio)
-        right = [zr_refs[step][group] for group in range(rows // rep)]
+        right = []
+        for group in range(rows // rep):
+            parts = [zr_refs[step * PARTS + part][group] for part in range(PARTS)]
+            right.append(jnp.concatenate(parts, axis=0) * seen_ref[block * (rows // rep) + group])
         outer = dot(left, jnp.concatenate(right, axis=1))
         for group in range(rows // rep):
             outer_scr[group] = outer[:, group * LANES : (group + 1) * LANES]
@@ -228,14 +242,14 @@
         one_ref[row * cols : (row + 1) * cols, :] = one_scr[pl.ds(row, cols, stride=rows), :].astype(BF16)
 
 
-def pair_update(hidden, zlt, zrs, base, inverse, live, proj, triangle_left, triangle_right):
+def pair_update(hidden, zlt, zrs, seen, base, inverse, live, proj, triangle_left, triangle_right):
     pairs, channels = base.shape
-    ratio = len(zrs)
+    ratio = len(zrs) // PARTS
     shape = jax.ShapeDtypeStruct((pairs, channels), BF16)
     return pl.pallas_call(
         functools.partial(pair_kernel, ratio, hidden),
         out_shape=(jax.ShapeDtypeStruct((2, pairs, channels), BF16), shape),
-        in_specs=[vmem()] * (7 + ratio),
+        in_specs=[vmem()] * (8 + len(zrs)),
         out_specs=[vmem()] * 2,
         scratch_shapes=[
             pltpu.VMEM((zrs[0].shape[0], zlt.shape[1], LANES), F32),
@@ -246,7 +260,7 @@
         cost_estimate=pl.CostEstimate(
             flops=2 * pairs * 1024 * 512, bytes_accessed=2 << 20, transcendentals=pairs * 256
         ),
-    )(zlt, *zrs, base, inverse, live, proj, triangle_left, triangle_right)
+    )(zlt, *zrs, seen, base, inverse, live, proj, triangle_left, triangle_right)
 
 
 def other(sub):
@@ -385,18 +399,27 @@
     def owner(a, b, turn):
         return ratio * b + (a + turn) % ratio
 
+    hidden = outer_left.shape[1]
+    seqs = alignment.shape[0]
+    part_seqs = seqs // PARTS
     mask = alignment_mask.T
-    zr = factor(alignment, mask, outer_right.T)
+    wide_left, wide_right = (
+        jnp.tile(weight.T, (LANES // hidden, 1)) for weight in (outer_left, outer_right)
+    )
+    zr_parts = [
+        factor(alignment, wide_right, hidden, part * part_seqs, part_seqs) for part in range(PARTS)
+    ]
     zrs = [
         fetch(zr, lambda a, b, turn=turn: (owner(a, b, turn), sender(a, b, subs, ratio)))
         for turn in range(ratio)
+        for zr in zr_parts
     ]
-    zl = factor(alignment, mask, outer_left.T)
-    zlt, base, inverse, live, proj = prepare(
+    zl = factor(alignment, wide_left, hidden, 0, seqs, mask)
+    zlt, base, inverse, live, proj, seen = prepare(
         zl, mask, pair_input, residue_mask, chain_index, relative_table, outer_proj
     )
     own, one = pair_update(
-        outer_left.shape[1], zlt, zrs, base, inverse, live, proj, triangle_left, triangle_right
+        hidden, zlt, zrs, seen, base, inverse, live, proj, triangle_left, triangle_right
     )
     near = fetch(own, lambda a, b: (a, other(b)))
     left = jnp.stack([own[0], near[0]])

time: 35.2 us -> 36.3 us (1.031)
  the two profiles are of different devices: /device:TPU:1 before, /device:TPU:2 now
where the time goes in v11:
time: 36.3 us; the launch traced here: 36 us
  starting transfers between devices  12.4 us (34%)
  waiting for transfers between devices  11.7 us (32%)
  Pallas kernels  9.26 us (26%)
  local copies, waits for them, and re-layouts  2.41 us (7%)
    ppermute x6, starting transfers between devices, fetch(): return lax.ppermute(values, ('dap', 'sub'), perm)  12.4 us
    ppermute x6, waiting for transfers between devices, fetch(): return lax.ppermute(values, ('dap', 'sub'), perm)  11.7 us
    pallas_call x3, Pallas kernels, factor(): pl.pallas_call(functools.partial(factor_kernel, first, hidden), out_shape...  4.51 us
    pallas_call x1, Pallas kernels, triangle_update(): pl.pallas_call(functools.partial(triangle_kernel, subs, ratio, cols), out...  2.21 us
    unnamed x28, local copies, waits for them, and re-layouts  1.67 us
    pallas_call x1, Pallas kernels, pair_update(): pl.pallas_call(functools.partial(pair_kernel, ratio, hidden), out_shape=(...  1.58 us
    another operation x2, local copies, waits for them, and re-layouts, per_device(): jnp.tile(weight.T, (LANES // hidden, 1))  0.73 us
  transfers between devices with their start and end apart: 6, of which 5 were waited for; matrix products, arithmetic and copies ran while one was open for 0% of the time, Pallas kernels for 12%

profile of v11, /device:TPU:2, one launch (start us, length us, event | category | flops | bytes accessed | tf_op | source)
XLA Modules:
  0.0 36.0 jit_solution(8294755642721675953)
XLA Ops:
  0.0 0.7 %tile.20 = bf16[4,32,256]{2,1,0:T(8,128)(2,1)S(1)} broadcast(bf16[32,256]{1,0:T(8,128)(2,1)} %bitcast.14), dimensions={1,2} | broadcast | bytes 81920 | tf_op jit(solution)/shard_map/tile | solution.py:407
  0.7 0.0 copy-start
  0.7 1.6 %copy-done = bf16[256,16,256]{2,1,0:T(8,128)(2,1)S(1)} copy-done((bf16[256,16,256]{2,1,0:T(8,128)(2,1)S(1)}, bf16[256,16,256]{2,1,0:T(8,128)(2,1)}, u32[]{:S(2)}) %copy-start) | copy-done | bytes 2097176
  2.3 0.0 copy-start.13
  2.3 0.0 copy-start.4
  2.3 1.2 %shard_map.147 = bf16[4,128,128]{2,1,0:T(8,128)(2,1)S(1)} custom-call(bf16[256,16,256]{2,1,0:T(8,128)(2,1)S(1)} %copy-done, bf16[128,256]{1,0:T(8,128)(2,1)S(1)} %bitcast.7), custom_call_target="tpu_custom_call" | custom-call | flops 536870912 | bytes 2097152 | tf_op jit(solution)/shard_map/pallas_call | solution.py:98
  3.5 3.5 %collective-permute-start = (bf16[4,128,128]{2,1,0:T(8,128)(2,1)S(1)}, bf16[4,128,128]{2,1,0:T(8,128)(2,1)S(1)}, u32[]{:S(2)}, u32[]{:S(2)}) collective-permute-start(bf16[4,128,128]{2,1,0:T(8,128)(2,1)S(1)} %shard_map.147), channel_id=1, source_target_pairs={{0,0},{6,1},{11,2},{13,3},{2,4},{5,5},{9,6},{14,7},{1,8},{7,9},{10... | collective-permute-start | bytes 393224 | tf_op jit(solution)/shard_map/ppermute | solution.py:397
  7.0 1.2 %shard_map.148 = bf16[4,128,128]{2,1,0:T(8,128)(2,1)S(1)} custom-call(bf16[256,16,256]{2,1,0:T(8,128)(2,1)S(1)} %copy-done, bf16[128,256]{1,0:T(8,128)(2,1)S(1)} %bitcast.8), custom_call_target="tpu_custom_call" | custom-call | flops 536870912 | bytes 2097152 | tf_op jit(solution)/shard_map/pallas_call | solution.py:98
  8.1 0.0 copy-start.1
  8.2 0.0 copy-start.5
  8.2 0.0 copy-start.10
  8.2 0.0 copy-start.11
  8.2 0.0 copy-start.12
  8.2 4.1 %collective-permute-start.1 = (bf16[4,128,128]{2,1,0:T(8,128)(2,1)S(1)}, bf16[4,128,128]{2,1,0:T(8,128)(2,1)S(1)}, u32[]{:S(2)}, u32[]{:S(2)}) collective-permute-start(bf16[4,128,128]{2,1,0:T(8,128)(2,1)S(1)} %shard_map.148), channel_id=1, source_target_pairs={{0,0},{6,1},{11,2},{13,3},{2,4},{5,5},{9,6},{14,7},{1,8},{7,9},{10... | collective-permute-start | bytes 393224 | tf_op jit(solution)/shard_map/ppermute | solution.py:397
  12.3 0.0 copy-done.13
  12.3 0.0 copy-done.4
  12.3 0.0 copy-start.6
  12.3 0.0 copy-start.7
  12.3 2.2 %shard_map.145.zl_ref = bf16[4,256,128]{2,1,0:T(8,128)(2,1)S(1)} custom-call(bf16[256,16,256]{2,1,0:T(8,128)(2,1)S(1)} %copy-done, bf16[128,256]{1,0:T(8,128)(2,1)S(1)} %bitcast.11, s32[64,256]{1,0:T(8,128)S(1)} %bitcast.9), custom_call_target="tpu_custom_call" | custom-call | flops 1073741824 | bytes 4194304 | tf_op jit(solution)/shard_map/pallas_call | solution.py:98
  14.5 0.0 copy-start.8
  14.5 0.0 copy-start.2
  14.5 0.0 copy-start.3
  14.5 0.0 copy-start.9
  14.6 0.0 copy-done.1
  14.6 0.0 copy-done.5
  14.6 0.0 copy-done.10
  14.6 0.0 copy-done.11
  14.6 0.0 copy-done.12
  14.6 0.6 %shard_map.146 = (bf16[2,512,128]{2,1,0:T(8,128)(2,1)S(1)}, f32[256,128]{1,0:T(8,128)S(1)}, f32[256,128]{1,0:T(8,128)S(1)}, f32[256,128]{1,0:T(8,128)S(1)}, bf16...) custom-call(bf16[4,256,128]{2,1,0:T(8,128)(2,1)S(1)} %shard_map.145.zl_ref, s32[64,256]{1,0:T(8,128)S(1)} %bitcast.10, ...), custom_call_target="tpu_custom_call" | custom-call | flops 134217728 | bytes 2097152 | tf_op jit(solution)/shard_map/pallas_call | solution.py:166
  15.3 0.0 collective-permute-done.refs_0_
  15.3 1.7 %collective-permute-done.1.refs_1_ = bf16[4,128,128]{2,1,0:T(8,128)(2,1)S(1)} collective-permute-done((bf16[4,128,128]{2,1,0:T(8,128)(2,1)S(1)}, bf16[4,128,128]{2,1,0:T(8,128)(2,1)S(1)}, u32[]{:S(2)}, u32[]{:S(2)}) %collective-permute-start.1) | collective-permute-done | bytes 131104 | tf_op jit(solution)/shard_map/ppermute | solution.py:397
  16.9 0.0 copy-done.6
  16.9 0.0 copy-done.7
  16.9 1.6 %shard_map.149 = (bf16[2,256,128]{2,1,0:T(8,128)(2,1)S(1)}, bf16[256,128]{1,0:T(8,128)(2,1)S(1)}) custom-call(bf16[2,512,128]{2,1,0:T(8,128)(2,1)S(1)} %get-tuple-element.13.zlt_ref, bf16[4,128,128]{2,1,0:T(8,128)(2,1)S(1)} %collective-permute-done.refs_0_, bf16[4,128,128]{2,1,0:T(8,128)(2,1)S(1)} %collective-permute-done.1.refs_1_, ...), custom_call_target="tpu_custom_call" | custom-call | flops 268435456 | bytes 2097152 | tf_op jit(solution)/shard_map/pallas_call | solution.py:249
  18.5 2.0 %collective-permute-start.2 = (bf16[2,256,128]{2,1,0:T(8,128)(2,1)S(1)}, bf16[2,256,128]{2,1,0:T(8,128)(2,1)S(1)}, u32[]{:S(2)}, u32[]{:S(2)}) collective-permute-start(bf16[2,256,128]{2,1,0:T(8,128)(2,1)S(1)} %get-tuple-element.19), channel_id=1, source_target_pairs={{1,0},{0,1},{3,2},{2,3},{5,4},{4,5},{7,6},{6,7},{9,8},{8,9},{11,10... | collective-permute-start | bytes 393224 | tf_op jit(solution)/shard_map/ppermute | solution.py:397
  20.6 1.0 %collective-permute-done.2 = bf16[2,256,128]{2,1,0:T(8,128)(2,1)S(1)} collective-permute-done((bf16[2,256,128]{2,1,0:T(8,128)(2,1)S(1)}, bf16[2,256,128]{2,1,0:T(8,128)(2,1)S(1)}, u32[]{:S(2)}, u32[]{:S(2)}) %collective-permute-start.2) | collective-permute-done | bytes 131104 | tf_op jit(solution)/shard_map/ppermute | solution.py:397
  21.6 0.1 collective-permute-start.5
  21.7 2.7 %collective-permute-start.3 = (bf16[2,256,128]{2,1,0:T(8,128)(2,1)S(1)}, bf16[2,256,128]{2,1,0:T(8,128)(2,1)S(1)}, u32[]{:S(2)}, u32[]{:S(2)}) collective-permute-start(bf16[2,256,128]{2,1,0:T(8,128)(2,1)S(1)} %pad_maximum_fusion), channel_id=1, source_target_pairs={{0,0},{6,1},{11,2},{13,3},{2,4},{5,5},{9,6},{14,7},{1,8},{7,9},{10... | collective-permute-start | bytes 393224 | tf_op jit(solution)/shard_map/ppermute | solution.py:397
  24.3 0.1 collective-permute-start.4
  24.4 0.0 copy-done.8
  24.4 0.3 shard_map.150.refs_5_
  24.8 2.6 %collective-permute-done.5.refs_3_ = bf16[2,256,128]{2,1,0:T(8,128)(2,1)S(1)} collective-permute-done((bf16[2,256,128]{2,1,0:T(8,128)(2,1)S(1)}, bf16[2,256,128]{2,1,0:T(8,128)(2,1)S(1)}, u32[]{:S(2)}, u32[]{:S(2)}) %collective-permute-start.5) | collective-permute-done | bytes 131104 | tf_op jit(solution)/shard_map/ppermute | solution.py:397
  27.4 2.9 %collective-permute-done.3.refs_0_ = bf16[2,256,128]{2,1,0:T(8,128)(2,1)S(1)} collective-permute-done((bf16[2,256,128]{2,1,0:T(8,128)(2,1)S(1)}, bf16[2,256,128]{2,1,0:T(8,128)(2,1)S(1)}, u32[]{:S(2)}, u32[]{:S(2)}) %collective-permute-start.3) | collective-permute-done | bytes 131104 | tf_op jit(solution)/shard_map/ppermute | solution.py:397
  30.3 3.6 %collective-permute-done.4.refs_1_ = bf16[2,256,128]{2,1,0:T(8,128)(2,1)S(1)} collective-permute-done((bf16[2,256,128]{2,1,0:T(8,128)(2,1)S(1)}, bf16[2,256,128]{2,1,0:T(8,128)(2,1)S(1)}, u32[]{:S(2)}, u32[]{:S(2)}) %collective-permute-start.4) | collective-permute-done | bytes 131104 | tf_op jit(solution)/shard_map/ppermute | solution.py:397
  33.8 0.0 copy-done.2
  33.8 0.0 copy-done.3
  33.8 0.0 copy-done.9
  33.8 2.2 %shard_map.151 = bf16[16,16,128]{2,1,0:T(8,128)(2,1)} custom-call(bf16[2,256,128]{2,1,0:T(8,128)(2,1)S(1)} %collective-permute-done.3.refs_0_, bf16[2,256,128]{2,1,0:T(8,128)(2,1)S(1)} %collective-permute-done.4.refs_1_, bf16[2,256,128]{2,1,0:T(8,128)(2,1)S(1)} %pad_maximum_fusion.1.refs_2_, bf16[2,256,128]{2,1,0:T(8,128)(2,1)S(1)} %collective-permute-done.5.refs_3_, ...), custom_call_target="tpu_custom_call" | custom-call | flops 134217728 | bytes 2097152 | tf_op jit(solution)/shard_map/pallas_call | solution.py:353
  (5 shorter events, 0.1 us)
Async XLA Ops:
  0.7 1.6 %copy-start = (bf16[256,16,256]{2,1,0:T(8,128)(2,1)S(1)}, bf16[256,16,256]{2,1,0:T(8,128)(2,1)}, u32[]{:S(2)}) copy-start(bf16[256,16,256]{2,1,0:T(8,128)(2,1)} %x_ref.5) | copy-start | bytes 6291460
  2.3 10.0 %copy-start.13 = (bf16[256,32]{0,1:T(8,128)(2,1)S(1)}, bf16[256,32]{0,1:T(8,128)(2,1)}, u32[]{:S(2)}) copy-start(bf16[256,32]{0,1:T(8,128)(2,1)} %param.20) | copy-start | bytes 49156
  2.3 10.0 %copy-start.4 = (s32[256,64]{0,1:T(8,128)S(1)}, s32[256,64]{0,1:T(8,128)}, u32[]{:S(2)}) copy-start(s32[256,64]{0,1:T(8,128)} %param.16) | copy-start | bytes 196612
  3.5 11.8 %collective-permute-start = (bf16[4,128,128]{2,1,0:T(8,128)(2,1)S(1)}, bf16[4,128,128]{2,1,0:T(8,128)(2,1)S(1)}, u32[]{:S(2)}, u32[]{:S(2)}) collective-permute-start(bf16[4,128,128]{2,1,0:T(8,128)(2,1)S(1)} %shard_map.147), channel_id=1, source_target_pairs={{0,0},{6,1},{11,2},{13,3},{2,4},{5,5},{9,6},{14,7},{1,8},{7,9},{10... | collective-permute-start | bytes 393224 | tf_op jit(solution)/shard_map/ppermute | solution.py:397
  8.1 6.4 %copy-start.1 = (f32[32,32,128]{2,1,0:T(8,128)S(1)}, f32[32,32,128]{2,1,0:T(8,128)}, u32[]{:S(2)}) copy-start(f32[32,32,128]{2,1,0:T(8,128)} %proj_ref.1) | copy-start | bytes 1572868
  8.2 6.4 %copy-start.5 = (bf16[16,16,128]{2,1,0:T(8,128)(2,1)S(1)}, bf16[16,16,128]{2,1,0:T(8,128)(2,1)}, u32[]{:S(2)}) copy-start(bf16[16,16,128]{2,1,0:T(8,128)(2,1)} %pair_ref.1) | copy-start | bytes 196612
  8.2 6.4 %copy-start.10 = (bf16[66,128]{1,0:T(8,128)(2,1)S(1)}, bf16[66,128]{1,0:T(8,128)(2,1)}, u32[]{:S(2)}) copy-start(bf16[66,128]{1,0:T(8,128)(2,1)} %table_ref.1) | copy-start | bytes 50692
  8.2 6.4 %copy-start.11 = (s32[64]{0:T(128)S(1)}, s32[64]{0:T(128)}, u32[]{:S(2)}) copy-start(s32[64]{0:T(128)} %param.18) | copy-start | bytes 772
  8.2 6.4 %copy-start.12 = (s32[64]{0:T(128)S(1)}, s32[64]{0:T(128)}, u32[]{:S(2)}) copy-start(s32[64]{0:T(128)} %param.19) | copy-start | bytes 772
  8.2 8.7 %collective-permute-start.1 = (bf16[4,128,128]{2,1,0:T(8,128)(2,1)S(1)}, bf16[4,128,128]{2,1,0:T(8,128)(2,1)S(1)}, u32[]{:S(2)}, u32[]{:S(2)}) collective-permute-start(bf16[4,128,128]{2,1,0:T(8,128)(2,1)S(1)} %shard_map.148), channel_id=1, source_target_pairs={{0,0},{6,1},{11,2},{13,3},{2,4},{5,5},{9,6},{14,7},{1,8},{7,9},{10... | collective-permute-start | bytes 393224 | tf_op jit(solution)/shard_map/ppermute | solution.py:397
  12.3 4.6 %copy-start.6 = (bf16[128,256]{1,0:T(8,128)(2,1)S(1)}, bf16[128,256]{1,0:T(8,128)(2,1)}, u32[]{:S(2)}) copy-start(bf16[128,256]{1,0:T(8,128)(2,1)} %refs_7_.2) | copy-start | bytes 196612
  12.3 4.6 %copy-start.7 = (bf16[128,256]{1,0:T(8,128)(2,1)S(1)}, bf16[128,256]{1,0:T(8,128)(2,1)}, u32[]{:S(2)}) copy-start(bf16[128,256]{1,0:T(8,128)(2,1)} %refs_8_.2) | copy-start | bytes 196612
  14.5 9.9 %copy-start.8 = (bf16[128,128]{1,0:T(8,128)(2,1)S(1)}, bf16[128,128]{1,0:T(8,128)(2,1)}, u32[]{:S(2)}) copy-start(bf16[128,128]{1,0:T(8,128)(2,1)} %weight_ref.1) | copy-start | bytes 98308
  14.5 19.3 %copy-start.2 = (bf16[128,512]{1,0:T(8,128)(2,1)S(1)}, bf16[128,512]{1,0:T(8,128)(2,1)}, u32[]{:S(2)}) copy-start(bf16[128,512]{1,0:T(8,128)(2,1)} %refs_7_.3) | copy-start | bytes 393220
  14.5 19.3 %copy-start.3 = (bf16[512,128]{1,0:T(8,128)(2,1)S(1)}, bf16[512,128]{1,0:T(8,128)(2,1)}, u32[]{:S(2)}) copy-start(bf16[512,128]{1,0:T(8,128)(2,1)} %refs_8_.3) | copy-start | bytes 393220
  14.5 19.3 %copy-start.9 = (bf16[128,128]{1,0:T(8,128)(2,1)S(1)}, bf16[128,128]{1,0:T(8,128)(2,1)}, u32[]{:S(2)}) copy-start(bf16[128,128]{1,0:T(8,128)(2,1)} %refs_6_.1) | copy-start | bytes 98308
  18.5 3.0 %collective-permute-start.2 = (bf16[2,256,128]{2,1,0:T(8,128)(2,1)S(1)}, bf16[2,256,128]{2,1,0:T(8,128)(2,1)S(1)}, u32[]{:S(2)}, u32[]{:S(2)}) collective-permute-start(bf16[2,256,128]{2,1,0:T(8,128)(2,1)S(1)} %get-tuple-element.19), channel_id=1, source_target_pairs={{1,0},{0,1},{3,2},{2,3},{5,4},{4,5},{7,6},{6,7},{9,8},{8,9},{11,10... | collective-permute-start | bytes 393224 | tf_op jit(solution)/shard_map/ppermute | solution.py:397
  21.6 5.8 %collective-permute-start.5 = (bf16[2,256,128]{2,1,0:T(8,128)(2,1)S(1)}, bf16[2,256,128]{2,1,0:T(8,128)(2,1)S(1)}, u32[]{:S(2)}, u32[]{:S(2)}) collective-permute-start(bf16[2,256,128]{2,1,0:T(8,128)(2,1)S(1)} %pad_maximum_fusion.1.refs_2_), channel_id=1, source_target_pairs={{2,0},{3,1},{0,2},{1,3},{6,4},{7,5},{4,6},{5,7},{10,8},{11,9},{8,1... | collective-permute-start | bytes 393224 | tf_op jit(solution)/shard_map/ppermute | solution.py:397
  21.7 8.6 %collective-permute-start.3 = (bf16[2,256,128]{2,1,0:T(8,128)(2,1)S(1)}, bf16[2,256,128]{2,1,0:T(8,128)(2,1)S(1)}, u32[]{:S(2)}, u32[]{:S(2)}) collective-permute-start(bf16[2,256,128]{2,1,0:T(8,128)(2,1)S(1)} %pad_maximum_fusion), channel_id=1, source_target_pairs={{0,0},{6,1},{11,2},{13,3},{2,4},{5,5},{9,6},{14,7},{1,8},{7,9},{10... | collective-permute-start | bytes 393224 | tf_op jit(solution)/shard_map/ppermute | solution.py:397
  24.3 9.5 %collective-permute-start.4 = (bf16[2,256,128]{2,1,0:T(8,128)(2,1)S(1)}, bf16[2,256,128]{2,1,0:T(8,128)(2,1)S(1)}, u32[]{:S(2)}, u32[]{:S(2)}) collective-permute-start(bf16[2,256,128]{2,1,0:T(8,128)(2,1)S(1)} %pad_maximum_fusion), channel_id=1, source_target_pairs={{2,0},{4,1},{9,2},{15,3},{0,4},{7,5},{11,6},{12,7},{3,8},{5,9},{8,... | collective-permute-start | bytes 393224 | tf_op jit(solution)/shard_map/ppermute | solution.py:397

commit v12 on v11

--- a/solution.py
+++ b/solution.py
@@ -9,7 +9,7 @@
 
 REL_CLIP = 32
 LANES = 128
-PARTS = 2
+PARTS = 1
 EPSILON = 1e-05
 BF16 = jnp.bfloat16
 F32 = jnp.float32
@@ -68,7 +68,8 @@
         spread = iota((residues, width), 0) == start + over(iota((residues, width), 1), hidden)
         live = dot_tn(mask_ref[...].astype(BF16), spread.astype(BF16))
     block = over(iota((step, LANES), 1), hidden)
-    ones = jnp.ones((LANES, LANES), BF16)
+    side = (2 * LANES, 2 * LANES)
+    ones = (over(iota(side, 0), LANES) == over(iota(side, 1), LANES)).astype(BF16)
     for turn in range(seqs // step):
         x = x_ref[first + turn * step : first + (turn + 1) * step].reshape(step * rows, channels)
         y = dot(x, w)
@@ -77,7 +78,10 @@
         for half in range(channels // LANES):
             centered = x[:, half * LANES : (half + 1) * LANES].astype(F32) - mean
             square = square + centered * centered
+        tops = square.shape[0] // 2
+        square = jnp.concatenate([square[:tops], square[tops:]], axis=1)
         spread = dot(square.astype(BF16), ones)
+        spread = jnp.concatenate([spread[:, :LANES], spread[:, LANES:]], axis=0)
         scale = lax.rsqrt(spread * (1.0 / channels) + EPSILON)
         y_scr[turn] = (y[:, :LANES] - mean * sums) * scale
         here = slice(turn * step, (turn + 1) * step)
@@ -93,7 +97,7 @@
 
 def factor(alignment, weight, hidden, first, seqs, mask=None):
     _, rows, channels = alignment.shape
-    step = seqs // 4 if mask is not None else seqs // 2
+    step = seqs // 4
     operands = (alignment, weight) if mask is None else (alignment, weight, mask)
     return pl.pallas_call(
         functools.partial(factor_kernel, first, hidden),
@@ -285,7 +289,7 @@
     )(one, weight)
 
 
-SENDERS = ((0, 2, 1, 3), (2, 1, 3, 0), (3, 1, 2, 0), (1, 2, 0, 3))
+SENDERS = ((0, 2, 3, 1), (2, 1, 0, 3), (0, 3, 2, 1), (2, 0, 1, 3))
 
 
 def sender(a, b, subs, ratio):

time: 36.3 us -> 35 us (0.964)
  the two profiles are of different devices: /device:TPU:2 before, /device:TPU:1 now
where the time goes in v12:
time: 35 us; the launch traced here: 34.8 us
  starting transfers between devices  15 us (43%)
  Pallas kernels  9.35 us (27%)
  waiting for transfers between devices  7.72 us (22%)
  local copies, waits for them, and re-layouts  2.46 us (7%)
    ppermute x5, starting transfers between devices, fetch(): return lax.ppermute(values, ('dap', 'sub'), perm)  15 us
    ppermute x5, waiting for transfers between devices, fetch(): return lax.ppermute(values, ('dap', 'sub'), perm)  7.72 us
    pallas_call x2, Pallas kernels, factor(): pl.pallas_call(functools.partial(factor_kernel, first, hidden), out_shape...  4.59 us
    pallas_call x1, Pallas kernels, triangle_update(): pl.pallas_call(functools.partial(triangle_kernel, subs, ratio, cols), out...  2.21 us
    unnamed x28, local copies, waits for them, and re-layouts  1.67 us
    pallas_call x1, Pallas kernels, pair_update(): pl.pallas_call(functools.partial(pair_kernel, ratio, hidden), out_shape=(...  1.59 us
    another operation x2, local copies, waits for them, and re-layouts, per_device(): jnp.tile(weight.T, (LANES // hidden, 1))  0.77 us
  transfers between devices with their start and end apart: 5, of which 3 were waited for; matrix products, arithmetic and copies ran while one was open for 0% of the time, Pallas kernels for 9%

profile of v12, /device:TPU:1, one launch (start us, length us, event | category | flops | bytes accessed | tf_op | source)
XLA Modules:
  0.0 34.8 jit_solution(16174164087621454456)
XLA Ops:
  0.0 0.0 copy-start.3
  0.0 0.0 copy-start.13
  0.0 0.8 %tile.20 = bf16[4,32,256]{2,1,0:T(8,128)(2,1)S(1)} broadcast(bf16[32,256]{1,0:T(8,128)(2,1)} %bitcast.13), dimensions={1,2} | broadcast | bytes 81920 | tf_op jit(solution)/shard_map/tile | solution.py:411
  0.8 0.0 copy-start.12
  0.8 1.6 %copy-done.12 = bf16[256,16,256]{2,1,0:T(8,128)(2,1)S(1)} copy-done((bf16[256,16,256]{2,1,0:T(8,128)(2,1)S(1)}, bf16[256,16,256]{2,1,0:T(8,128)(2,1)}, u32[]{:S(2)}) %copy-start.12) | copy-done | bytes 2097176
  2.4 2.3 %shard_map.147 = bf16[4,256,128]{2,1,0:T(8,128)(2,1)S(1)} custom-call(bf16[256,16,256]{2,1,0:T(8,128)(2,1)S(1)} %copy-done.12, bf16[128,256]{1,0:T(8,128)(2,1)S(1)} %bitcast.9), custom_call_target="tpu_custom_call" | custom-call | flops 1073741824 | bytes 4194304 | tf_op jit(solution)/shard_map/pallas_call | solution.py:102
  4.6 0.0 copy-start
  4.7 0.0 copy-start.4
  4.7 0.0 copy-start.9
  4.7 0.0 copy-start.10
  4.7 0.0 copy-start.11
  4.7 6.7 %collective-permute-start = (bf16[4,256,128]{2,1,0:T(8,128)(2,1)S(1)}, bf16[4,256,128]{2,1,0:T(8,128)(2,1)S(1)}, u32[]{:S(2)}, u32[]{:S(2)}) collective-permute-start(bf16[4,256,128]{2,1,0:T(8,128)(2,1)S(1)} %shard_map.147), channel_id=1, source_target_pairs={{0,0},{6,1},{8,2},{14,3},{2,4},{5,5},{11,6},{12,7},{3,8},{4,9},{10... | collective-permute-start | bytes 786440 | tf_op jit(solution)/shard_map/ppermute | solution.py:401
  11.5 0.0 copy-done.13
  11.5 0.0 copy-done.3
  11.5 0.0 copy-start.5
  11.5 0.0 copy-start.6
  11.5 2.3 %shard_map.145.zl_ref = bf16[4,256,128]{2,1,0:T(8,128)(2,1)S(1)} custom-call(bf16[256,16,256]{2,1,0:T(8,128)(2,1)S(1)} %copy-done.12, bf16[128,256]{1,0:T(8,128)(2,1)S(1)} %bitcast.10, s32[64,256]{1,0:T(8,128)S(1)} %bitcast.7), custom_call_target="tpu_custom_call" | custom-call | flops 1073741824 | bytes 4194304 | tf_op jit(solution)/shard_map/pallas_call | solution.py:102
  13.8 0.0 copy-start.7
  13.9 0.0 copy-start.1
  13.9 0.0 copy-start.2
  13.9 0.0 copy-start.8
  13.9 0.0 copy-done
  13.9 0.0 copy-done.4
  13.9 0.0 copy-done.9
  13.9 0.0 copy-done.10
  13.9 0.0 copy-done.11
  13.9 0.6 %shard_map.146 = (bf16[2,512,128]{2,1,0:T(8,128)(2,1)S(1)}, f32[256,128]{1,0:T(8,128)S(1)}, f32[256,128]{1,0:T(8,128)S(1)}, f32[256,128]{1,0:T(8,128)S(1)}, bf16...) custom-call(bf16[4,256,128]{2,1,0:T(8,128)(2,1)S(1)} %shard_map.145.zl_ref, s32[64,256]{1,0:T(8,128)S(1)} %bitcast.8, ...), custom_call_target="tpu_custom_call" | custom-call | flops 134217728 | bytes 2097152 | tf_op jit(solution)/shard_map/pallas_call | solution.py:170
  14.6 2.6 %collective-permute-done.refs_0_ = bf16[4,256,128]{2,1,0:T(8,128)(2,1)S(1)} collective-permute-done((bf16[4,256,128]{2,1,0:T(8,128)(2,1)S(1)}, bf16[4,256,128]{2,1,0:T(8,128)(2,1)S(1)}, u32[]{:S(2)}, u32[]{:S(2)}) %collective-permute-start) | collective-permute-done | bytes 262176 | tf_op jit(solution)/shard_map/ppermute | solution.py:401
  17.2 0.0 copy-done.5
  17.2 0.0 copy-done.6
  17.2 1.6 %shard_map.148 = (bf16[2,256,128]{2,1,0:T(8,128)(2,1)S(1)}, bf16[256,128]{1,0:T(8,128)(2,1)S(1)}) custom-call(bf16[2,512,128]{2,1,0:T(8,128)(2,1)S(1)} %get-tuple-element.13.zlt_ref, bf16[4,256,128]{2,1,0:T(8,128)(2,1)S(1)} %collective-permute-done.refs_0_, bf16[4,256,128]{2,1,0:T(8,128)(2,1)S(1)} %get-tuple-element.14.refs_1_, ...), custom_call_target="tpu_custom_call" | custom-call | flops 268435456 | bytes 2097152 | tf_op jit(solution)/shard_map/pallas_call | solution.py:253
  18.8 0.1 collective-permute-start.1
  18.9 1.3 %collective-permute-done.1 = bf16[2,256,128]{2,1,0:T(8,128)(2,1)S(1)} collective-permute-done((bf16[2,256,128]{2,1,0:T(8,128)(2,1)S(1)}, bf16[2,256,128]{2,1,0:T(8,128)(2,1)S(1)}, u32[]{:S(2)}, u32[]{:S(2)}) %collective-permute-start.1) | collective-permute-done | bytes 131104 | tf_op jit(solution)/shard_map/ppermute | solution.py:401
  20.3 3.2 %collective-permute-start.3 = (bf16[2,256,128]{2,1,0:T(8,128)(2,1)S(1)}, bf16[2,256,128]{2,1,0:T(8,128)(2,1)S(1)}, u32[]{:S(2)}, u32[]{:S(2)}) collective-permute-start(bf16[2,256,128]{2,1,0:T(8,128)(2,1)S(1)} %pad_maximum_fusion), channel_id=1, source_target_pairs={{2,0},{4,1},{10,2},{12,3},{0,4},{7,5},{9,6},{14,7},{1,8},{6,9},{8,... | collective-permute-start | bytes 393224 | tf_op jit(solution)/shard_map/ppermute | solution.py:401
  23.5 4.8 %collective-permute-start.2 = (bf16[2,256,128]{2,1,0:T(8,128)(2,1)S(1)}, bf16[2,256,128]{2,1,0:T(8,128)(2,1)S(1)}, u32[]{:S(2)}, u32[]{:S(2)}) collective-permute-start(bf16[2,256,128]{2,1,0:T(8,128)(2,1)S(1)} %pad_maximum_fusion), channel_id=1, source_target_pairs={{0,0},{6,1},{8,2},{14,3},{2,4},{5,5},{11,6},{12,7},{3,8},{4,9},{10... | collective-permute-start | bytes 393224 | tf_op jit(solution)/shard_map/ppermute | solution.py:401
  28.4 0.1 collective-permute-start.4
  28.4 0.0 copy-done.7
  28.4 0.3 shard_map.149.refs_5_
  28.8 0.0 collective-permute-done.3.refs_1_
  28.8 3.8 %collective-permute-done.2.refs_0_ = bf16[2,256,128]{2,1,0:T(8,128)(2,1)S(1)} collective-permute-done((bf16[2,256,128]{2,1,0:T(8,128)(2,1)S(1)}, bf16[2,256,128]{2,1,0:T(8,128)(2,1)S(1)}, u32[]{:S(2)}, u32[]{:S(2)}) %collective-permute-start.2) | collective-permute-done | bytes 131104 | tf_op jit(solution)/shard_map/ppermute | solution.py:401
  32.6 0.0 collective-permute-done.4.refs_3_
  32.6 0.0 copy-done.1
  32.6 0.0 copy-done.2
  32.6 0.0 copy-done.8
  32.6 2.2 %shard_map.150 = bf16[16,16,128]{2,1,0:T(8,128)(2,1)} custom-call(bf16[2,256,128]{2,1,0:T(8,128)(2,1)S(1)} %collective-permute-done.2.refs_0_, bf16[2,256,128]{2,1,0:T(8,128)(2,1)S(1)} %collective-permute-done.3.refs_1_, bf16[2,256,128]{2,1,0:T(8,128)(2,1)S(1)} %pad_maximum_fusion.1.refs_2_, bf16[2,256,128]{2,1,0:T(8,128)(2,1)S(1)} %collective-permute-done.4.refs_3_, ...), custom_call_target="tpu_custom_call" | custom-call | flops 134217728 | bytes 2097152 | tf_op jit(solution)/shard_map/pallas_call | solution.py:357
  (5 shorter events, 0.1 us)
Async XLA Ops:
  0.0 11.5 %copy-start.3 = (s32[256,64]{0,1:T(8,128)S(1)}, s32[256,64]{0,1:T(8,128)}, u32[]{:S(2)}) copy-start(s32[256,64]{0,1:T(8,128)} %param.16) | copy-start | bytes 196612
  0.0 11.5 %copy-start.13 = (bf16[256,32]{0,1:T(8,128)(2,1)S(1)}, bf16[256,32]{0,1:T(8,128)(2,1)}, u32[]{:S(2)}) copy-start(bf16[256,32]{0,1:T(8,128)(2,1)} %param.20) | copy-start | bytes 49156
  0.8 1.6 %copy-start.12 = (bf16[256,16,256]{2,1,0:T(8,128)(2,1)S(1)}, bf16[256,16,256]{2,1,0:T(8,128)(2,1)}, u32[]{:S(2)}) copy-start(bf16[256,16,256]{2,1,0:T(8,128)(2,1)} %x_ref.3) | copy-start | bytes 6291460
  4.6 9.3 %copy-start = (f32[32,32,128]{2,1,0:T(8,128)S(1)}, f32[32,32,128]{2,1,0:T(8,128)}, u32[]{:S(2)}) copy-start(f32[32,32,128]{2,1,0:T(8,128)} %proj_ref.1) | copy-start | bytes 1572868
  4.7 9.3 %copy-start.4 = (bf16[16,16,128]{2,1,0:T(8,128)(2,1)S(1)}, bf16[16,16,128]{2,1,0:T(8,128)(2,1)}, u32[]{:S(2)}) copy-start(bf16[16,16,128]{2,1,0:T(8,128)(2,1)} %pair_ref.1) | copy-start | bytes 196612
  4.7 9.2 %copy-start.9 = (bf16[66,128]{1,0:T(8,128)(2,1)S(1)}, bf16[66,128]{1,0:T(8,128)(2,1)}, u32[]{:S(2)}) copy-start(bf16[66,128]{1,0:T(8,128)(2,1)} %table_ref.1) | copy-start | bytes 50692
  4.7 9.2 %copy-start.10 = (s32[64]{0:T(128)S(1)}, s32[64]{0:T(128)}, u32[]{:S(2)}) copy-start(s32[64]{0:T(128)} %param.18) | copy-start | bytes 772
  4.7 9.2 %copy-start.11 = (s32[64]{0:T(128)S(1)}, s32[64]{0:T(128)}, u32[]{:S(2)}) copy-start(s32[64]{0:T(128)} %param.19) | copy-start | bytes 772
  4.7 12.5 %collective-permute-start = (bf16[4,256,128]{2,1,0:T(8,128)(2,1)S(1)}, bf16[4,256,128]{2,1,0:T(8,128)(2,1)S(1)}, u32[]{:S(2)}, u32[]{:S(2)}) collective-permute-start(bf16[4,256,128]{2,1,0:T(8,128)(2,1)S(1)} %shard_map.147), channel_id=1, source_target_pairs={{0,0},{6,1},{8,2},{14,3},{2,4},{5,5},{11,6},{12,7},{3,8},{4,9},{10... | collective-permute-start | bytes 786440 | tf_op jit(solution)/shard_map/ppermute | solution.py:401
  11.5 5.7 %copy-start.5 = (bf16[128,256]{1,0:T(8,128)(2,1)S(1)}, bf16[128,256]{1,0:T(8,128)(2,1)}, u32[]{:S(2)}) copy-start(bf16[128,256]{1,0:T(8,128)(2,1)} %refs_6_.2) | copy-start | bytes 196612
  11.5 5.7 %copy-start.6 = (bf16[128,256]{1,0:T(8,128)(2,1)S(1)}, bf16[128,256]{1,0:T(8,128)(2,1)}, u32[]{:S(2)}) copy-start(bf16[128,256]{1,0:T(8,128)(2,1)} %refs_7_.2) | copy-start | bytes 196612
  13.8 14.6 %copy-start.7 = (bf16[128,128]{1,0:T(8,128)(2,1)S(1)}, bf16[128,128]{1,0:T(8,128)(2,1)}, u32[]{:S(2)}) copy-start(bf16[128,128]{1,0:T(8,128)(2,1)} %weight_ref.1) | copy-start | bytes 98308
  13.9 18.7 %copy-start.1 = (bf16[128,512]{1,0:T(8,128)(2,1)S(1)}, bf16[128,512]{1,0:T(8,128)(2,1)}, u32[]{:S(2)}) copy-start(bf16[128,512]{1,0:T(8,128)(2,1)} %refs_7_.3) | copy-start | bytes 393220
  13.9 18.7 %copy-start.2 = (bf16[512,128]{1,0:T(8,128)(2,1)S(1)}, bf16[512,128]{1,0:T(8,128)(2,1)}, u32[]{:S(2)}) copy-start(bf16[512,128]{1,0:T(8,128)(2,1)} %refs_8_.1) | copy-start | bytes 393220
  13.9 18.7 %copy-start.8 = (bf16[128,128]{1,0:T(8,128)(2,1)S(1)}, bf16[128,128]{1,0:T(8,128)(2,1)}, u32[]{:S(2)}) copy-start(bf16[128,128]{1,0:T(8,128)(2,1)} %refs_6_.3) | copy-start | bytes 98308
  18.8 1.4 %collective-permute-start.1 = (bf16[2,256,128]{2,1,0:T(8,128)(2,1)S(1)}, bf16[2,256,128]{2,1,0:T(8,128)(2,1)S(1)}, u32[]{:S(2)}, u32[]{:S(2)}) collective-permute-start(bf16[2,256,128]{2,1,0:T(8,128)(2,1)S(1)} %get-tuple-element.19), channel_id=1, source_target_pairs={{1,0},{0,1},{3,2},{2,3},{5,4},{4,5},{7,6},{6,7},{9,8},{8,9},{11,10... | collective-permute-start | bytes 393224 | tf_op jit(solution)/shard_map/ppermute | solution.py:401
  20.3 8.5 %collective-permute-start.3 = (bf16[2,256,128]{2,1,0:T(8,128)(2,1)S(1)}, bf16[2,256,128]{2,1,0:T(8,128)(2,1)S(1)}, u32[]{:S(2)}, u32[]{:S(2)}) collective-permute-start(bf16[2,256,128]{2,1,0:T(8,128)(2,1)S(1)} %pad_maximum_fusion), channel_id=1, source_target_pairs={{2,0},{4,1},{10,2},{12,3},{0,4},{7,5},{9,6},{14,7},{1,8},{6,9},{8,... | collective-permute-start | bytes 393224 | tf_op jit(solution)/shard_map/ppermute | solution.py:401
  23.5 9.1 %collective-permute-start.2 = (bf16[2,256,128]{2,1,0:T(8,128)(2,1)S(1)}, bf16[2,256,128]{2,1,0:T(8,128)(2,1)S(1)}, u32[]{:S(2)}, u32[]{:S(2)}) collective-permute-start(bf16[2,256,128]{2,1,0:T(8,128)(2,1)S(1)} %pad_maximum_fusion), channel_id=1, source_target_pairs={{0,0},{6,1},{8,2},{14,3},{2,4},{5,5},{11,6},{12,7},{3,8},{4,9},{10... | collective-permute-start | bytes 393224 | tf_op jit(solution)/shard_map/ppermute | solution.py:401
  28.4 4.2 %collective-permute-start.4 = (bf16[2,256,128]{2,1,0:T(8,128)(2,1)S(1)}, bf16[2,256,128]{2,1,0:T(8,128)(2,1)S(1)}, u32[]{:S(2)}, u32[]{:S(2)}) collective-permute-start(bf16[2,256,128]{2,1,0:T(8,128)(2,1)S(1)} %pad_maximum_fusion.1.refs_2_), channel_id=1, source_target_pairs={{2,0},{3,1},{0,2},{1,3},{6,4},{7,5},{4,6},{5,7},{10,8},{11,9},{8,1... | collective-permute-start | bytes 393224 | tf_op jit(solution)/shard_map/ppermute | solution.py:401

commit v13 on v12

--- a/solution.py
+++ b/solution.py
@@ -9,7 +9,6 @@
 
 REL_CLIP = 32
 LANES = 128
-PARTS = 1
 EPSILON = 1e-05
 BF16 = jnp.bfloat16
 F32 = jnp.float32
@@ -52,36 +51,49 @@
     return lax.bitwise_and(index, size - 1)
 
 
-def factor_kernel(first, hidden, x_ref, weight_ref, *refs):
+def repeat_kernel(weight_ref, out_ref):
+    rep = LANES // weight_ref.shape[0]
+    out_ref[...] = jnp.concatenate([weight_ref[...]] * rep, axis=0).T
+
+
+def repeat_weight(weight):
+    return pl.pallas_call(
+        repeat_kernel,
+        out_shape=jax.ShapeDtypeStruct((weight.shape[1], LANES), BF16),
+        in_specs=[vmem()],
+        out_specs=vmem(),
+        compiler_params=pltpu.CompilerParams(vmem_limit_bytes=2 << 20),
+        cost_estimate=pl.CostEstimate(flops=1 << 30, bytes_accessed=1 << 17, transcendentals=0),
+    )(weight)
+
+
+def factor_kernel(x_ref, weight_ref, *refs):
     mask_ref = refs[0] if len(refs) == 3 else None
     z_ref, y_scr = refs[-2:]
     groups, seqs, _ = z_ref.shape
     _, rows, channels = x_ref.shape
-    rep = LANES // hidden
+    rep = rows // groups
+    hidden = LANES // rep
     width = rows * hidden
     step = y_scr.shape[1] // rows
-    w = jnp.concatenate([weight_ref[...].T, jnp.ones((channels, LANES), BF16)], axis=1)
-    sums = dot(jnp.ones((8, channels), BF16), w)[:1, :LANES]
+    w = jnp.concatenate([weight_ref[...], jnp.ones((channels, LANES), BF16)], axis=1)
+    ones = jnp.ones((LANES, LANES), BF16)
+    sums = dot(jnp.ones((8, channels), BF16), weight_ref[...])[:1]
+    block = over(iota((step, LANES), 1), hidden)
     if mask_ref is not None:
         residues = mask_ref.shape[0]
-        start = lax.axis_index("dap") * rows
-        spread = iota((residues, width), 0) == start + over(iota((residues, width), 1), hidden)
-        live = dot_tn(mask_ref[...].astype(BF16), spread.astype(BF16))
-    block = over(iota((step, LANES), 1), hidden)
-    side = (2 * LANES, 2 * LANES)
-    ones = (over(iota(side, 0), LANES) == over(iota(side, 1), LANES)).astype(BF16)
+        column = lax.axis_index("dap") * rows + over(iota((residues, width), 1), hidden)
+        lanes_of = (iota((residues, width), 0) == column).astype(BF16)
+        live = dot_tn(mask_ref[...].astype(BF16), lanes_of)
     for turn in range(seqs // step):
-        x = x_ref[first + turn * step : first + (turn + 1) * step].reshape(step * rows, channels)
+        x = x_ref[turn * step : (turn + 1) * step].reshape(step * rows, channels)
         y = dot(x, w)
         mean = y[:, LANES:] * (1.0 / channels)
         square = jnp.zeros_like(mean)
         for half in range(channels // LANES):
             centered = x[:, half * LANES : (half + 1) * LANES].astype(F32) - mean
             square = square + centered * centered
-        tops = square.shape[0] // 2
-        square = jnp.concatenate([square[:tops], square[tops:]], axis=1)
         spread = dot(square.astype(BF16), ones)
-        spread = jnp.concatenate([spread[:, :LANES], spread[:, LANES:]], axis=0)
         scale = lax.rsqrt(spread * (1.0 / channels) + EPSILON)
         y_scr[turn] = (y[:, :LANES] - mean * sums) * scale
         here = slice(turn * step, (turn + 1) * step)
@@ -95,12 +107,12 @@
             z_ref[group, here, :] = z.astype(BF16)
 
 
-def factor(alignment, weight, hidden, first, seqs, mask=None):
-    _, rows, channels = alignment.shape
+def factor(alignment, weight, hidden, mask=None):
+    seqs, rows, channels = alignment.shape
     step = seqs // 4
     operands = (alignment, weight) if mask is None else (alignment, weight, mask)
     return pl.pallas_call(
-        functools.partial(factor_kernel, first, hidden),
+        factor_kernel,
         out_shape=jax.ShapeDtypeStruct((rows * hidden // LANES, seqs, LANES), BF16),
         in_specs=[vmem()] * len(operands),
         out_specs=vmem(),
@@ -188,9 +200,9 @@
 
 
 def pair_kernel(ratio, hidden, zlt_ref, *refs):
-    zr_refs, refs = refs[: ratio * PARTS], refs[ratio * PARTS :]
+    zr_refs, refs = refs[:ratio], refs[ratio:]
     (seen_ref, base_ref, inverse_ref, live_ref, proj_ref, tl_ref, tr_ref,
-     both_ref, one_ref, outer_scr, flat_scr, one_scr) = refs
+     both_ref, left_ref, one_ref, outer_scr, flat_scr, one_scr) = refs
     pairs, channels = base_ref.shape
     rows = zlt_ref.shape[1] // hidden
     rep = LANES // hidden
@@ -204,8 +216,7 @@
         block = lax.rem(me + step, ratio)
         right = []
         for group in range(rows // rep):
-            parts = [zr_refs[step * PARTS + part][group] for part in range(PARTS)]
-            right.append(jnp.concatenate(parts, axis=0) * seen_ref[block * (rows // rep) + group])
+            right.append(zr_refs[step][group] * seen_ref[block * (rows // rep) + group])
         outer = dot(left, jnp.concatenate(right, axis=1))
         for group in range(rows // rep):
             outer_scr[group] = outer[:, group * LANES : (group + 1) * LANES]
@@ -241,6 +252,8 @@
         both = dot(norm, weight[...])
         factor = jax.nn.sigmoid(both[:, :channels]) * both[:, channels:] * live_ref[...]
         both_ref[side] = factor.astype(BF16)
+        if side == 0:
+            left_ref[...] = factor.astype(BF16)
     cols = pairs // rows
     for row in range(rows):
         one_ref[row * cols : (row + 1) * cols, :] = one_scr[pl.ds(row, cols, stride=rows), :].astype(BF16)
@@ -248,13 +261,13 @@
 
 def pair_update(hidden, zlt, zrs, seen, base, inverse, live, proj, triangle_left, triangle_right):
     pairs, channels = base.shape
-    ratio = len(zrs) // PARTS
+    ratio = len(zrs)
     shape = jax.ShapeDtypeStruct((pairs, channels), BF16)
     return pl.pallas_call(
         functools.partial(pair_kernel, ratio, hidden),
-        out_shape=(jax.ShapeDtypeStruct((2, pairs, channels), BF16), shape),
+        out_shape=(jax.ShapeDtypeStruct((2, pairs, channels), BF16), shape, shape),
         in_specs=[vmem()] * (8 + len(zrs)),
-        out_specs=[vmem()] * 2,
+        out_specs=[vmem()] * 3,
         scratch_shapes=[
             pltpu.VMEM((zrs[0].shape[0], zlt.shape[1], LANES), F32),
             pltpu.VMEM((proj.shape[0] // LANES, pairs, LANES), BF16),
@@ -271,24 +284,6 @@
     return sub + 1 - 2 * (sub % 2)
 
 
-def gate_kernel(one_ref, weight_ref, gate_ref):
-    norm = layer_norm(one_ref[...].astype(F32)).astype(BF16)
-    gate_ref[...] = jax.nn.sigmoid(dot(norm, weight_ref[...]))
-
-
-def output_gate(one, weight):
-    return pl.pallas_call(
-        gate_kernel,
-        out_shape=jax.ShapeDtypeStruct(one.shape, F32),
-        in_specs=[vmem()] * 2,
-        out_specs=vmem(),
-        compiler_params=pltpu.CompilerParams(vmem_limit_bytes=4 << 20),
-        cost_estimate=pl.CostEstimate(
-            flops=2 * one.size * LANES, bytes_accessed=1 << 18, transcendentals=one.size
-        ),
-    )(one, weight)
-
-
 SENDERS = ((0, 2, 3, 1), (2, 1, 0, 3), (0, 3, 2, 1), (2, 0, 1, 3))
 
 
@@ -308,39 +303,66 @@
     return found
 
 
-def triangle_kernel(subs, ratio, cols, *refs):
-    twos = subs // 2
-    rights, refs = refs[: twos * ratio], refs[twos * ratio :]
-    lefts, refs = refs[:twos], refs[twos:]
-    (one_ref, gate_ref, out_ref, up_ref, down_ref, result_ref, left_scr, right_scr, sum_scr) = refs
-    pairs, channels = one_ref.shape
-    rows = pairs // cols
+def add_terms(sums, start, lefts, rights, steps, ratio, cols, left_scr):
+    subs = left_scr.shape[0]
+    _, channels = sums.shape
+    rows = left_scr.shape[1] // cols
     here, there = lax.axis_index("dap"), lax.axis_index("sub")
     first_sub = sender_index(here, there, subs, ratio)
-    for step in range(twos):
+    own, near, across, beyond = lefts
+    left_scr[there] = own[0].astype(F32)
+    left_scr[other(there)] = near[0].astype(F32)
+    for step in range(1, subs // 2):
         sub = lax.rem(there + 2 * step, subs)
-        left_scr[sub] = lefts[step][0].astype(F32)
-        left_scr[other(sub)] = lefts[step][1].astype(F32)
+        left_scr[sub] = across[step - 1][...].astype(F32)
+        left_scr[other(sub)] = beyond[step - 1][...].astype(F32)
     for turn in range(ratio):
-        block = lax.rem(here + turn, ratio)
-        for step in range(twos):
+        block = lax.rem(here + turn, ratio) if ratio > 1 else 0
+        places = [i * cols + block * rows for i in range(rows)]
+        if ratio > 1:
+            places = [pl.multiple_of(place, rows) for place in places]
+        if start is None:
+            totals = tuple(jnp.zeros((rows, channels), F32) for _ in range(rows))
+        else:
+            totals = tuple(start[pl.ds(place, rows), :] for place in places)
+        for index, step in enumerate(steps):
             sub = lax.rem(first_sub + 2 * step, subs)
-            right_scr[block * subs + sub] = rights[turn * twos + step][0].astype(F32)
-            right_scr[block * subs + other(sub)] = rights[turn * twos + step][1].astype(F32)
-    for block in range(ratio):
-        totals = tuple(jnp.zeros((rows, channels), F32) for _ in range(rows))
-        for sub in range(subs):
-
-            def body(k, totals, sub=sub, block=block):
-                first = pl.multiple_of(k * rows, rows)
-                right = right_scr[block * subs + sub, pl.ds(first, rows), :]
-                return tuple(
-                    totals[i] + left_scr[sub, pl.ds(first + i, 1), :] * right for i in range(rows)
-                )
-
-            totals = lax.fori_loop(0, cols, body, totals, unroll=4)
-        for i in range(rows):
-            sum_scr[i * cols + block * rows : i * cols + (block + 1) * rows, :] = totals[i]
+            pair = rights[turn * len(steps) + index]
+            for member, slot in enumerate((sub, other(sub))):
+
+                def body(k, totals, slot=slot, member=member, pair=pair):
+                    first = pl.multiple_of(k * rows, rows)
+                    right = pair[member, pl.ds(first, rows), :].astype(F32)
+                    return tuple(
+                        totals[i] + left_scr[slot, pl.ds(first + i, 1), :] * right
+                        for i in range(rows)
+                    )
+
+                totals = lax.fori_loop(0, cols, body, totals, unroll=4)
+        for place, total in zip(places, totals):
+            sums[pl.ds(place, rows), :] = total
+
+
+def split_lefts(refs, twos):
+    count = twos - 1
+    lefts = (refs[0], refs[1], refs[2 : 2 + count], refs[2 + count : 2 + 2 * count])
+    return lefts, refs[2 + 2 * count :]
+
+
+def first_kernel(steps, twos, ratio, cols, *refs):
+    lefts, refs = split_lefts(refs, twos)
+    rights, refs = refs[: ratio * len(steps)], refs[ratio * len(steps) :]
+    one_ref, weight_ref, sums_ref, gate_ref, left_scr = refs
+    add_terms(sums_ref, None, lefts, rights, steps, ratio, cols, left_scr)
+    norm = layer_norm(one_ref[...].astype(F32)).astype(BF16)
+    gate_ref[...] = jax.nn.sigmoid(dot(norm, weight_ref[...]))
+
+
+def last_kernel(steps, twos, ratio, cols, *refs):
+    lefts, refs = split_lefts(refs, twos)
+    rights, refs = refs[: ratio * len(steps)], refs[ratio * len(steps) :]
+    (start_ref, one_ref, gate_ref, out_ref, up_ref, down_ref, result_ref, left_scr, sum_scr) = refs
+    add_terms(sum_scr, start_ref, lefts, rights, steps, ratio, cols, left_scr)
     one = one_ref[...].astype(F32)
     hidden = layer_norm(sum_scr[...].astype(BF16).astype(F32)).astype(BF16)
     two = (one + gate_ref[...] * dot(hidden, out_ref[...])).astype(BF16).astype(F32)
@@ -349,26 +371,42 @@
     result_ref[...] = result.reshape(result_ref.shape)
 
 
-def triangle_update(lefts, rights, one, cols, gate, out, up, down):
+def triangle_update(lefts, rights, one, cols, gate_weight, out, up, down):
     pairs, channels = one.shape
     rows = pairs // cols
-    subs = 2 * len(lefts)
-    ratio = len(rights) // len(lefts)
+    twos = len(lefts) // 2
+    subs = 2 * twos
+    ratio = len(rights) // twos
+    late, early = range(twos // 2), range(twos // 2, twos)
+    limit = (12 << 20) if ratio == 1 else (50 << 20)
+    left_scr = pltpu.VMEM((subs, pairs, channels), F32)
+    shape = jax.ShapeDtypeStruct((pairs, channels), F32)
+
+    def chosen(steps):
+        return [rights[turn * twos + step] for turn in range(ratio) for step in steps]
+
+    sums, gate = pl.pallas_call(
+        functools.partial(first_kernel, early, twos, ratio, cols),
+        out_shape=(shape, shape),
+        in_specs=[vmem()] * (len(lefts) + ratio * len(early) + 2),
+        out_specs=[vmem()] * 2,
+        scratch_shapes=[left_scr],
+        compiler_params=pltpu.CompilerParams(vmem_limit_bytes=limit),
+        cost_estimate=pl.CostEstimate(
+            flops=2 * pairs * channels * 1024, bytes_accessed=1 << 20, transcendentals=pairs * 128
+        ),
+    )(*lefts, *chosen(early), one, gate_weight)
     return pl.pallas_call(
-        functools.partial(triangle_kernel, subs, ratio, cols),
+        functools.partial(last_kernel, late, twos, ratio, cols),
         out_shape=jax.ShapeDtypeStruct((rows, cols, channels), BF16),
-        in_specs=[vmem()] * (len(lefts) + len(rights) + 5),
+        in_specs=[vmem()] * (len(lefts) + ratio * len(late) + 6),
         out_specs=vmem(),
-        scratch_shapes=[
-            pltpu.VMEM((subs, pairs, channels), F32),
-            pltpu.VMEM((subs * ratio, pairs, channels), F32),
-            pltpu.VMEM((pairs, channels), F32),
-        ],
-        compiler_params=pltpu.CompilerParams(vmem_limit_bytes=(16 << 20) if ratio == 1 else (50 << 20)),
+        scratch_shapes=[left_scr, pltpu.VMEM((pairs, channels), F32)],
+        compiler_params=pltpu.CompilerParams(vmem_limit_bytes=limit),
         cost_estimate=pl.CostEstimate(
             flops=2 * pairs * channels * 2048, bytes_accessed=2 << 20, transcendentals=pairs * 128
         ),
-    )(*rights, *lefts, one, gate, out, up, down)
+    )(*lefts, *chosen(late), sums, one, gate, out, up, down)
 
 
 def per_device(
@@ -404,29 +442,24 @@
         return ratio * b + (a + turn) % ratio
 
     hidden = outer_left.shape[1]
-    seqs = alignment.shape[0]
-    part_seqs = seqs // PARTS
     mask = alignment_mask.T
-    wide_left, wide_right = (
-        jnp.tile(weight.T, (LANES // hidden, 1)) for weight in (outer_left, outer_right)
-    )
-    zr_parts = [
-        factor(alignment, wide_right, hidden, part * part_seqs, part_seqs) for part in range(PARTS)
-    ]
+    zr = factor(alignment, repeat_weight(outer_right.T), hidden)
     zrs = [
         fetch(zr, lambda a, b, turn=turn: (owner(a, b, turn), sender(a, b, subs, ratio)))
         for turn in range(ratio)
-        for zr in zr_parts
     ]
-    zl = factor(alignment, wide_left, hidden, 0, seqs, mask)
+    zl = factor(alignment, repeat_weight(outer_left.T), hidden, mask)
     zlt, base, inverse, live, proj, seen = prepare(
         zl, mask, pair_input, residue_mask, chain_index, relative_table, outer_proj
     )
-    own, one = pair_update(
+    own, left, one = pair_update(
         hidden, zlt, zrs, seen, base, inverse, live, proj, triangle_left, triangle_right
     )
     near = fetch(own, lambda a, b: (a, other(b)))
-    left = jnp.stack([own[0], near[0]])
+    across = [
+        fetch(left, lambda a, b, m=step: (a, (b + 2 * m) % subs)) for step in range(1, subs // 2)
+    ]
+    beyond = [fetch(block, lambda a, b: (a, other(b))) for block in across]
     right = jnp.stack([own[1], near[1]])
     rights = [
         fetch(
@@ -438,12 +471,15 @@
         for turn in range(ratio)
         for step in range(subs // 2)
     ]
-    lefts = [left] + [
-        fetch(left, lambda a, b, m=step: (a, (b + 2 * m) % subs)) for step in range(1, subs // 2)
-    ]
-    gate = output_gate(one, triangle_gate)
     return triangle_update(
-        lefts, rights, one, cols, gate, triangle_out, transition_up, transition_down
+        [own, near, *across, *beyond],
+        rights,
+        one,
+        cols,
+        triangle_gate,
+        triangle_out,
+        transition_up,
+        transition_down,
     )
 
 

time: 35 us -> 32.9 us (0.940)
  the two profiles are of different devices: /device:TPU:1 before, /device:TPU:3 now
where the time goes in v13:
time: 32.9 us; the launch traced here: 32.7 us
  starting transfers between devices  12.5 us (38%)
  Pallas kernels  9.21 us (28%)
  waiting for transfers between devices  9.1 us (28%)
  local copies, waits for them, and re-layouts  1.62 us (5%)
    ppermute x6, starting transfers between devices, fetch(): return lax.ppermute(values, ('dap', 'sub'), perm)  12.5 us
    ppermute x6, waiting for transfers between devices, fetch(): return lax.ppermute(values, ('dap', 'sub'), perm)  9.1 us
    pallas_call x2, Pallas kernels, factor(): pl.pallas_call(factor_kernel, out_shape=jax.ShapeDtypeStruct((rows * hidd...  4.25 us
    pallas_call x1, Pallas kernels, triangle_update(): pl.pallas_call(functools.partial(last_kernel, late, twos, ratio, cols), o...  1.87 us
    unnamed x30, local copies, waits for them, and re-layouts  1.61 us
    pallas_call x1, Pallas kernels, pair_update(): pl.pallas_call(functools.partial(pair_kernel, ratio, hidden), out_shape=(...  1.6 us
    pallas_call x1, Pallas kernels, triangle_update(): pl.pallas_call(functools.partial(first_kernel, early, twos, ratio, cols),...  0.73 us
  transfers between devices with their start and end apart: 6, of which 5 were waited for; matrix products, arithmetic and copies ran while one was open for 0% of the time, Pallas kernels for 11%

profile of v13, /device:TPU:3, one launch (start us, length us, event | category | flops | bytes accessed | tf_op | source)
XLA Modules:
  0.0 32.7 jit_solution(16256172301387596601)
XLA Ops:
  0.0 0.0 copy-start.12
  0.0 0.0 copy-start.13
  0.0 0.9 %copy-done.13 = bf16[256,32]{0,1:T(8,128)(2,1)S(1)} copy-done((bf16[256,32]{0,1:T(8,128)(2,1)S(1)}, bf16[256,32]{0,1:T(8,128)(2,1)}, u32[]{:S(2)}) %copy-start.13) | copy-done | bytes 16408
  0.9 0.1 shard_map.148.weight_ref
  0.9 0.7 %copy-done.12 = bf16[256,16,256]{2,1,0:T(8,128)(2,1)S(1)} copy-done((bf16[256,16,256]{2,1,0:T(8,128)(2,1)S(1)}, bf16[256,16,256]{2,1,0:T(8,128)(2,1)}, u32[]{:S(2)}) %copy-start.12) | copy-done | bytes 2097176
  1.6 0.0 copy-start.14
  1.6 2.0 %shard_map.149 = bf16[4,256,128]{2,1,0:T(8,128)(2,1)S(1)} custom-call(bf16[256,16,256]{2,1,0:T(8,128)(2,1)S(1)} %copy-done.12, bf16[256,128]{1,0:T(8,128)(2,1)S(1)} %shard_map.148.weight_ref), custom_call_target="tpu_custom_call" | custom-call | flops 1073741824 | bytes 4194304 | tf_op jit(solution)/shard_map/pallas_call | solution.py:114
  3.7 0.0 copy-start.3
  3.7 4.9 %collective-permute-start = (bf16[4,256,128]{2,1,0:T(8,128)(2,1)S(1)}, bf16[4,256,128]{2,1,0:T(8,128)(2,1)S(1)}, u32[]{:S(2)}, u32[]{:S(2)}) collective-permute-start(bf16[4,256,128]{2,1,0:T(8,128)(2,1)S(1)} %shard_map.149), channel_id=1, source_target_pairs={{0,0},{6,1},{8,2},{14,3},{2,4},{5,5},{11,6},{12,7},{3,8},{4,9},{10... | collective-permute-start | bytes 786440 | tf_op jit(solution)/shard_map/ppermute | solution.py:439
  8.6 0.0 copy-done.14
  8.6 0.1 shard_map.145.weight_ref
  8.6 0.0 copy-start
  8.7 0.0 copy-start.4
  8.7 0.0 copy-start.9
  8.7 0.0 copy-start.10
  8.7 0.0 copy-start.11
  8.7 0.0 copy-done.3
  8.7 0.0 copy-start.5
  8.7 0.0 copy-start.6
  8.7 2.2 %shard_map.146.zl_ref = bf16[4,256,128]{2,1,0:T(8,128)(2,1)S(1)} custom-call(bf16[256,16,256]{2,1,0:T(8,128)(2,1)S(1)} %copy-done.12, bf16[256,128]{1,0:T(8,128)(2,1)S(1)} %shard_map.145.weight_ref, s32[64,256]{1,0:T(8,128)S(1)} %bitcast.5), custom_call_target="tpu_custom_call" | custom-call | flops 1073741824 | bytes 4194304 | tf_op jit(solution)/shard_map/pallas_call | solution.py:114
  10.9 0.0 copy-start.7
  11.0 0.0 copy-start.1
  11.0 0.0 copy-start.2
  11.0 0.0 copy-start.8
  11.0 0.0 copy-done
  11.0 0.0 copy-done.4
  11.0 0.0 copy-done.9
  11.0 0.0 copy-done.10
  11.0 0.0 copy-done.11
  11.0 0.6 %shard_map.147 = (bf16[2,512,128]{2,1,0:T(8,128)(2,1)S(1)}, f32[256,128]{1,0:T(8,128)S(1)}, f32[256,128]{1,0:T(8,128)S(1)}, f32[256,128]{1,0:T(8,128)S(1)}, bf16...) custom-call(bf16[4,256,128]{2,1,0:T(8,128)(2,1)S(1)} %shard_map.146.zl_ref, s32[64,256]{1,0:T(8,128)S(1)} %bitcast.6, ...), custom_call_target="tpu_custom_call" | custom-call | flops 134217728 | bytes 2097152 | tf_op jit(solution)/shard_map/pallas_call | solution.py:182
  11.7 2.5 %collective-permute-done.refs_0_ = bf16[4,256,128]{2,1,0:T(8,128)(2,1)S(1)} collective-permute-done((bf16[4,256,128]{2,1,0:T(8,128)(2,1)S(1)}, bf16[4,256,128]{2,1,0:T(8,128)(2,1)S(1)}, u32[]{:S(2)}, u32[]{:S(2)}) %collective-permute-start) | collective-permute-done | bytes 262176 | tf_op jit(solution)/shard_map/ppermute | solution.py:439
  14.2 0.0 copy-done.5
  14.2 0.0 copy-done.6
  14.2 1.6 %shard_map.150 = (bf16[2,256,128]{2,1,0:T(8,128)(2,1)S(1)}, bf16[256,128]{1,0:T(8,128)(2,1)S(1)}, bf16[256,128]{1,0:T(8,128)(2,1)S(1)}) custom-call(bf16[2,512,128]{2,1,0:T(8,128)(2,1)S(1)} %get-tuple-element.16.zlt_ref, bf16[4,256,128]{2,1,0:T(8,128)(2,1)S(1)} %collective-permute-done.refs_0_, bf16[4,256,128]{2,1,0:T(8,128)(2,1)S(1)} %get-tuple-element.17.refs_1_, ...), custom_call_target="tpu_custom_call" | custom-call | flops 268435456 | bytes 2097152 | tf_op jit(solution)/shard_map/pallas_call | solution.py:266
  15.8 3.2 %collective-permute-start.1 = (bf16[2,256,128]{2,1,0:T(8,128)(2,1)S(1)}, bf16[2,256,128]{2,1,0:T(8,128)(2,1)S(1)}, u32[]{:S(2)}, u32[]{:S(2)}) collective-permute-start(bf16[2,256,128]{2,1,0:T(8,128)(2,1)S(1)} %get-tuple-element.22.refs_0_), channel_id=1, source_target_pairs={{1,0},{0,1},{3,2},{2,3},{5,4},{4,5},{7,6},{6,7},{9,8},{8,9},{11,10... | collective-permute-start | bytes 393224 | tf_op jit(solution)/shard_map/ppermute | solution.py:439
  19.0 0.0 collective-permute-start.2
  19.0 1.0 %collective-permute-done.1.refs_1_ = bf16[2,256,128]{2,1,0:T(8,128)(2,1)S(1)} collective-permute-done((bf16[2,256,128]{2,1,0:T(8,128)(2,1)S(1)}, bf16[2,256,128]{2,1,0:T(8,128)(2,1)S(1)}, u32[]{:S(2)}, u32[]{:S(2)}) %collective-permute-start.1) | collective-permute-done | bytes 131104 | tf_op jit(solution)/shard_map/ppermute | solution.py:439
  20.0 2.4 %collective-permute-start.5 = (bf16[2,256,128]{2,1,0:T(8,128)(2,1)S(1)}, bf16[2,256,128]{2,1,0:T(8,128)(2,1)S(1)}, u32[]{:S(2)}, u32[]{:S(2)}) collective-permute-start(bf16[2,256,128]{2,1,0:T(8,128)(2,1)S(1)} %pad_maximum_fusion), channel_id=1, source_target_pairs={{2,0},{4,1},{10,2},{12,3},{0,4},{7,5},{9,6},{14,7},{1,8},{6,9},{8,... | collective-permute-start | bytes 393224 | tf_op jit(solution)/shard_map/ppermute | solution.py:439
  22.4 1.9 %collective-permute-start.4 = (bf16[2,256,128]{2,1,0:T(8,128)(2,1)S(1)}, bf16[2,256,128]{2,1,0:T(8,128)(2,1)S(1)}, u32[]{:S(2)}, u32[]{:S(2)}) collective-permute-start(bf16[2,256,128]{2,1,0:T(8,128)(2,1)S(1)} %pad_maximum_fusion), channel_id=1, source_target_pairs={{0,0},{6,1},{8,2},{14,3},{2,4},{5,5},{11,6},{12,7},{3,8},{4,9},{10... | collective-permute-start | bytes 393224 | tf_op jit(solution)/shard_map/ppermute | solution.py:439
  24.3 0.0 collective-permute-done.2.refs_2_
  24.3 0.1 collective-permute-start.3
  24.4 1.2 %collective-permute-done.3.refs_3_ = bf16[256,128]{1,0:T(8,128)(2,1)S(1)} collective-permute-done((bf16[256,128]{1,0:T(8,128)(2,1)S(1)}, bf16[256,128]{1,0:T(8,128)(2,1)S(1)}, u32[]{:S(2)}, u32[]{:S(2)}) %collective-permute-start.3) | collective-permute-done | bytes 65568 | tf_op jit(solution)/shard_map/ppermute | solution.py:439
  25.7 1.5 %collective-permute-done.5.refs_4_ = bf16[2,256,128]{2,1,0:T(8,128)(2,1)S(1)} collective-permute-done((bf16[2,256,128]{2,1,0:T(8,128)(2,1)S(1)}, bf16[2,256,128]{2,1,0:T(8,128)(2,1)S(1)}, u32[]{:S(2)}, u32[]{:S(2)}) %collective-permute-start.5) | collective-permute-done | bytes 131104 | tf_op jit(solution)/shard_map/ppermute | solution.py:439
  27.2 0.0 copy-done.7
  27.2 0.7 %shard_map.151 = (f32[256,128]{1,0:T(8,128)S(1)}, f32[256,128]{1,0:T(8,128)S(1)}) custom-call(bf16[2,256,128]{2,1,0:T(8,128)(2,1)S(1)} %get-tuple-element.22.refs_0_, bf16[2,256,128]{2,1,0:T(8,128)(2,1)S(1)} %collective-permute-done.1.refs_1_, bf16[256,128]{1,0:T(8,128)(2,1)S(1)} %collective-permute-done.2.refs_2_, ...), custom_call_target="tpu_custom_call" | custom-call | flops 67108864 | bytes 1048576 | tf_op jit(solution)/shard_map/pallas_call | solution.py:388
  27.9 2.8 %collective-permute-done.4.refs_4_ = bf16[2,256,128]{2,1,0:T(8,128)(2,1)S(1)} collective-permute-done((bf16[2,256,128]{2,1,0:T(8,128)(2,1)S(1)}, bf16[2,256,128]{2,1,0:T(8,128)(2,1)S(1)}, u32[]{:S(2)}, u32[]{:S(2)}) %collective-permute-start.4) | collective-permute-done | bytes 131104 | tf_op jit(solution)/shard_map/ppermute | solution.py:439
  30.8 0.0 copy-done.1
  30.8 0.0 copy-done.2
  30.8 0.0 copy-done.8
  30.8 1.9 %shard_map.152 = bf16[16,16,128]{2,1,0:T(8,128)(2,1)} custom-call(bf16[2,256,128]{2,1,0:T(8,128)(2,1)S(1)} %get-tuple-element.22.refs_0_, bf16[2,256,128]{2,1,0:T(8,128)(2,1)S(1)} %collective-permute-done.1.refs_1_, bf16[256,128]{1,0:T(8,128)(2,1)S(1)} %collective-permute-done.2.refs_2_, bf16[256,128]{1,0:T(8,128)(2,1)S(1)} %collective-permute-done.3.refs_3_, ...), custom_call_target="tpu_custom_call" | custom-call | flops 134217728 | bytes 2097152 | tf_op jit(solution)/shard_map/pallas_call | solution.py:399
  (3 shorter events, 0.0 us)
Async XLA Ops:
  0.0 1.6 %copy-start.12 = (bf16[256,16,256]{2,1,0:T(8,128)(2,1)S(1)}, bf16[256,16,256]{2,1,0:T(8,128)(2,1)}, u32[]{:S(2)}) copy-start(bf16[256,16,256]{2,1,0:T(8,128)(2,1)} %x_ref.3) | copy-start | bytes 6291460
  0.0 0.9 %copy-start.13 = (bf16[256,32]{0,1:T(8,128)(2,1)S(1)}, bf16[256,32]{0,1:T(8,128)(2,1)}, u32[]{:S(2)}) copy-start(bf16[256,32]{0,1:T(8,128)(2,1)} %param.21) | copy-start | bytes 49156
  1.6 7.0 %copy-start.14 = (bf16[256,32]{0,1:T(8,128)(2,1)S(1)}, bf16[256,32]{0,1:T(8,128)(2,1)}, u32[]{:S(2)}) copy-start(bf16[256,32]{0,1:T(8,128)(2,1)} %param.20) | copy-start | bytes 49156
  3.7 5.0 %copy-start.3 = (s32[256,64]{0,1:T(8,128)S(1)}, s32[256,64]{0,1:T(8,128)}, u32[]{:S(2)}) copy-start(s32[256,64]{0,1:T(8,128)} %param.16) | copy-start | bytes 196612
  3.7 10.6 %collective-permute-start = (bf16[4,256,128]{2,1,0:T(8,128)(2,1)S(1)}, bf16[4,256,128]{2,1,0:T(8,128)(2,1)S(1)}, u32[]{:S(2)}, u32[]{:S(2)}) collective-permute-start(bf16[4,256,128]{2,1,0:T(8,128)(2,1)S(1)} %shard_map.149), channel_id=1, source_target_pairs={{0,0},{6,1},{8,2},{14,3},{2,4},{5,5},{11,6},{12,7},{3,8},{4,9},{10... | collective-permute-start | bytes 786440 | tf_op jit(solution)/shard_map/ppermute | solution.py:439
  8.6 2.4 %copy-start = (f32[32,32,128]{2,1,0:T(8,128)S(1)}, f32[32,32,128]{2,1,0:T(8,128)}, u32[]{:S(2)}) copy-start(f32[32,32,128]{2,1,0:T(8,128)} %proj_ref.1) | copy-start | bytes 1572868
  8.7 2.4 %copy-start.4 = (bf16[16,16,128]{2,1,0:T(8,128)(2,1)S(1)}, bf16[16,16,128]{2,1,0:T(8,128)(2,1)}, u32[]{:S(2)}) copy-start(bf16[16,16,128]{2,1,0:T(8,128)(2,1)} %pair_ref.1) | copy-start | bytes 196612
  8.7 2.4 %copy-start.9 = (bf16[66,128]{1,0:T(8,128)(2,1)S(1)}, bf16[66,128]{1,0:T(8,128)(2,1)}, u32[]{:S(2)}) copy-start(bf16[66,128]{1,0:T(8,128)(2,1)} %table_ref.1) | copy-start | bytes 50692
  8.7 2.4 %copy-start.10 = (s32[64]{0:T(128)S(1)}, s32[64]{0:T(128)}, u32[]{:S(2)}) copy-start(s32[64]{0:T(128)} %param.18) | copy-start | bytes 772
  8.7 2.3 %copy-start.11 = (s32[64]{0:T(128)S(1)}, s32[64]{0:T(128)}, u32[]{:S(2)}) copy-start(s32[64]{0:T(128)} %param.19) | copy-start | bytes 772
  8.7 5.5 %copy-start.5 = (bf16[128,256]{1,0:T(8,128)(2,1)S(1)}, bf16[128,256]{1,0:T(8,128)(2,1)}, u32[]{:S(2)}) copy-start(bf16[128,256]{1,0:T(8,128)(2,1)} %refs_6_.2) | copy-start | bytes 196612
  8.7 5.5 %copy-start.6 = (bf16[128,256]{1,0:T(8,128)(2,1)S(1)}, bf16[128,256]{1,0:T(8,128)(2,1)}, u32[]{:S(2)}) copy-start(bf16[128,256]{1,0:T(8,128)(2,1)} %refs_7_.1) | copy-start | bytes 196612
  10.9 16.2 %copy-start.7 = (bf16[128,128]{1,0:T(8,128)(2,1)S(1)}, bf16[128,128]{1,0:T(8,128)(2,1)}, u32[]{:S(2)}) copy-start(bf16[128,128]{1,0:T(8,128)(2,1)} %refs_6_.3) | copy-start | bytes 98308
  11.0 19.8 %copy-start.1 = (bf16[128,512]{1,0:T(8,128)(2,1)S(1)}, bf16[128,512]{1,0:T(8,128)(2,1)}, u32[]{:S(2)}) copy-start(bf16[128,512]{1,0:T(8,128)(2,1)} %refs_9_.1) | copy-start | bytes 393220
  11.0 19.8 %copy-start.2 = (bf16[512,128]{1,0:T(8,128)(2,1)S(1)}, bf16[512,128]{1,0:T(8,128)(2,1)}, u32[]{:S(2)}) copy-start(bf16[512,128]{1,0:T(8,128)(2,1)} %refs_10_.1) | copy-start | bytes 393220
  11.0 19.8 %copy-start.8 = (bf16[128,128]{1,0:T(8,128)(2,1)S(1)}, bf16[128,128]{1,0:T(8,128)(2,1)}, u32[]{:S(2)}) copy-start(bf16[128,128]{1,0:T(8,128)(2,1)} %refs_8_.1) | copy-start | bytes 98308
  15.8 4.2 %collective-permute-start.1 = (bf16[2,256,128]{2,1,0:T(8,128)(2,1)S(1)}, bf16[2,256,128]{2,1,0:T(8,128)(2,1)S(1)}, u32[]{:S(2)}, u32[]{:S(2)}) collective-permute-start(bf16[2,256,128]{2,1,0:T(8,128)(2,1)S(1)} %get-tuple-element.22.refs_0_), channel_id=1, source_target_pairs={{1,0},{0,1},{3,2},{2,3},{5,4},{4,5},{7,6},{6,7},{9,8},{8,9},{11,10... | collective-permute-start | bytes 393224 | tf_op jit(solution)/shard_map/ppermute | solution.py:439
  19.0 5.3 %collective-permute-start.2 = (bf16[256,128]{1,0:T(8,128)(2,1)S(1)}, bf16[256,128]{1,0:T(8,128)(2,1)S(1)}, u32[]{:S(2)}, u32[]{:S(2)}) collective-permute-start(bf16[256,128]{1,0:T(8,128)(2,1)S(1)} %get-tuple-element.23), channel_id=1, source_target_pairs={{2,0},{3,1},{0,2},{1,3},{6,4},{7,5},{4,6},{5,7},{10,8},{11,9},{8,1... | collective-permute-start | bytes 196616 | tf_op jit(solution)/shard_map/ppermute | solution.py:439
  20.0 7.1 %collective-permute-start.5 = (bf16[2,256,128]{2,1,0:T(8,128)(2,1)S(1)}, bf16[2,256,128]{2,1,0:T(8,128)(2,1)S(1)}, u32[]{:S(2)}, u32[]{:S(2)}) collective-permute-start(bf16[2,256,128]{2,1,0:T(8,128)(2,1)S(1)} %pad_maximum_fusion), channel_id=1, source_target_pairs={{2,0},{4,1},{10,2},{12,3},{0,4},{7,5},{9,6},{14,7},{1,8},{6,9},{8,... | collective-permute-start | bytes 393224 | tf_op jit(solution)/shard_map/ppermute | solution.py:439
  22.4 8.4 %collective-permute-start.4 = (bf16[2,256,128]{2,1,0:T(8,128)(2,1)S(1)}, bf16[2,256,128]{2,1,0:T(8,128)(2,1)S(1)}, u32[]{:S(2)}, u32[]{:S(2)}) collective-permute-start(bf16[2,256,128]{2,1,0:T(8,128)(2,1)S(1)} %pad_maximum_fusion), channel_id=1, source_target_pairs={{0,0},{6,1},{8,2},{14,3},{2,4},{5,5},{11,6},{12,7},{3,8},{4,9},{10... | collective-permute-start | bytes 393224 | tf_op jit(solution)/shard_map/ppermute | solution.py:439
  24.3 1.3 %collective-permute-start.3 = (bf16[256,128]{1,0:T(8,128)(2,1)S(1)}, bf16[256,128]{1,0:T(8,128)(2,1)S(1)}, u32[]{:S(2)}, u32[]{:S(2)}) collective-permute-start(bf16[256,128]{1,0:T(8,128)(2,1)S(1)} %collective-permute-done.2.refs_2_), channel_id=1, source_target_pairs={{1,0},{0,1},{3,2},{2,3},{5,4},{4,5},{7,6},{6,7},{9,8},{8,9},{11,10... | collective-permute-start | bytes 196616 | tf_op jit(solution)/shard_map/ppermute | solution.py:439

commit v14 on v13

--- a/solution.py
+++ b/solution.py
@@ -9,6 +9,7 @@
 
 REL_CLIP = 32
 LANES = 128
+HALVES = 2
 EPSILON = 1e-05
 BF16 = jnp.bfloat16
 F32 = jnp.float32
@@ -109,7 +110,7 @@
 
 def factor(alignment, weight, hidden, mask=None):
     seqs, rows, channels = alignment.shape
-    step = seqs // 4
+    step = seqs // 8
     operands = (alignment, weight) if mask is None else (alignment, weight, mask)
     return pl.pallas_call(
         factor_kernel,
@@ -212,48 +213,51 @@
     upper = lane // (2 * hidden) == 1
     half = 2 * hidden
     left = jnp.concatenate([zlt_ref[part] for part in range(zlt_ref.shape[0])], axis=1)
+    groups = rows // rep
     for step in range(ratio):
-        block = lax.rem(me + step, ratio)
-        right = []
-        for group in range(rows // rep):
-            right.append(zr_refs[step][group] * seen_ref[block * (rows // rep) + group])
+        block = lax.rem(me + step, ratio) if ratio > 1 else 0
+        right = [zr_refs[step][group] * seen_ref[block * groups + group] for group in range(groups)]
         outer = dot(left, jnp.concatenate(right, axis=1))
-        for group in range(rows // rep):
+        for group in range(groups):
             outer_scr[group] = outer[:, group * LANES : (group + 1) * LANES]
-        for group in range(rows // rep):
-            for quad in range(hidden // rep):
-                s0, s1, s2, s3 = (
-                    outer_scr[group, pl.ds(quad * rep + k, rows, stride=hidden), :] for k in range(rep)
-                )
-                t0 = jnp.where(upper, pltpu.roll(s2, half, 1), s0)
-                t1 = jnp.where(upper, pltpu.roll(s3, half, 1), s1)
-                t2 = jnp.where(upper, s2, pltpu.roll(s0, half, 1))
-                t3 = jnp.where(upper, s3, pltpu.roll(s1, half, 1))
-                back = LANES - hidden
-                found = (
-                    jnp.where(odd, pltpu.roll(t1, hidden, 1), t0),
-                    jnp.where(odd, t1, pltpu.roll(t0, back, 1)),
-                    jnp.where(odd, pltpu.roll(t3, hidden, 1), t2),
-                    jnp.where(odd, t3, pltpu.roll(t2, back, 1)),
-                )
-                for k in range(rep):
-                    first = block * rows * rows + (group * rep + k) * rows
-                    if ratio == 1:
-                        first = (group * rep + k) * rows
-                    else:
-                        first = pl.multiple_of(first, rows)
-                    flat_scr[quad, pl.ds(first, rows), :] = found[k].astype(BF16)
-    flat = jnp.concatenate([flat_scr[quad] for quad in range(flat_scr.shape[0])], axis=1)
-    outer_mean = dot(flat, proj_ref[...]) * inverse_ref[...]
-    one = (base_ref[...] + outer_mean).astype(BF16).astype(F32)
-    one_scr[...] = one
-    norm = layer_norm(one).astype(BF16)
-    for side, weight in enumerate((tl_ref, tr_ref)):
-        both = dot(norm, weight[...])
-        factor = jax.nn.sigmoid(both[:, :channels]) * both[:, channels:] * live_ref[...]
-        both_ref[side] = factor.astype(BF16)
-        if side == 0:
-            left_ref[...] = factor.astype(BF16)
+        for part in range(HALVES):
+            span = rows * rows // HALVES
+            for group in range(part * groups // HALVES, (part + 1) * groups // HALVES):
+                for quad in range(hidden // rep):
+                    s0, s1, s2, s3 = (
+                        outer_scr[group, pl.ds(quad * rep + k, rows, stride=hidden), :]
+                        for k in range(rep)
+                    )
+                    t0 = jnp.where(upper, pltpu.roll(s2, half, 1), s0)
+                    t1 = jnp.where(upper, pltpu.roll(s3, half, 1), s1)
+                    t2 = jnp.where(upper, s2, pltpu.roll(s0, half, 1))
+                    t3 = jnp.where(upper, s3, pltpu.roll(s1, half, 1))
+                    back = LANES - hidden
+                    found = (
+                        jnp.where(odd, pltpu.roll(t1, hidden, 1), t0),
+                        jnp.where(odd, t1, pltpu.roll(t0, back, 1)),
+                        jnp.where(odd, pltpu.roll(t3, hidden, 1), t2),
+                        jnp.where(odd, t3, pltpu.roll(t2, back, 1)),
+                    )
+                    for k in range(rep):
+                        place = ((group * rep + k) * rows) % span
+                        flat_scr[part, quad, place : place + rows, :] = found[k].astype(BF16)
+            first = block * rows * rows + part * span
+            if ratio > 1:
+                first = pl.multiple_of(first, span)
+            here = pl.ds(first, span)
+            flat = [flat_scr[part, quad] for quad in range(hidden // rep)]
+            projected = dot(jnp.concatenate(flat, axis=1), proj_ref[...])
+            one = (base_ref[here, :] + projected * inverse_ref[here, :]).astype(BF16).astype(F32)
+            one_scr[here, :] = one
+            norm = layer_norm(one).astype(BF16)
+            live = live_ref[here, :]
+            for side, weight in enumerate((tl_ref, tr_ref)):
+                both = dot(norm, weight[...])
+                factor = jax.nn.sigmoid(both[:, :channels]) * both[:, channels:] * live
+                both_ref[side, here, :] = factor.astype(BF16)
+                if side == 0:
+                    left_ref[here, :] = factor.astype(BF16)
     cols = pairs // rows
     for row in range(rows):
         one_ref[row * cols : (row + 1) * cols, :] = one_scr[pl.ds(row, cols, stride=rows), :].astype(BF16)
@@ -262,6 +266,7 @@
 def pair_update(hidden, zlt, zrs, seen, base, inverse, live, proj, triangle_left, triangle_right):
     pairs, channels = base.shape
     ratio = len(zrs)
+    rows = zlt.shape[1] // hidden
     shape = jax.ShapeDtypeStruct((pairs, channels), BF16)
     return pl.pallas_call(
         functools.partial(pair_kernel, ratio, hidden),
@@ -270,7 +275,7 @@
         out_specs=[vmem()] * 3,
         scratch_shapes=[
             pltpu.VMEM((zrs[0].shape[0], zlt.shape[1], LANES), F32),
-            pltpu.VMEM((proj.shape[0] // LANES, pairs, LANES), BF16),
+            pltpu.VMEM((HALVES, hidden * hidden // LANES, rows * rows // HALVES, LANES), BF16),
             pltpu.VMEM((pairs, channels), F32),
         ],
         compiler_params=pltpu.CompilerParams(vmem_limit_bytes=32 << 20),
@@ -303,12 +308,9 @@
     return found
 
 
-def add_terms(sums, start, lefts, rights, steps, ratio, cols, left_scr):
+def widen(lefts, left_scr):
     subs = left_scr.shape[0]
-    _, channels = sums.shape
-    rows = left_scr.shape[1] // cols
-    here, there = lax.axis_index("dap"), lax.axis_index("sub")
-    first_sub = sender_index(here, there, subs, ratio)
+    there = lax.axis_index("sub")
     own, near, across, beyond = lefts
     left_scr[there] = own[0].astype(F32)
     left_scr[other(there)] = near[0].astype(F32)
@@ -316,6 +318,14 @@
         sub = lax.rem(there + 2 * step, subs)
         left_scr[sub] = across[step - 1][...].astype(F32)
         left_scr[other(sub)] = beyond[step - 1][...].astype(F32)
+
+
+def add_terms(sums, start, rights, steps, ratio, cols, left_scr):
+    subs = left_scr.shape[0]
+    _, channels = sums.shape
+    rows = left_scr.shape[1] // cols
+    here, there = lax.axis_index("dap"), lax.axis_index("sub")
+    first_sub = sender_index(here, there, subs, ratio)
     for turn in range(ratio):
         block = lax.rem(here + turn, ratio) if ratio > 1 else 0
         places = [i * cols + block * rows for i in range(rows)]
@@ -352,23 +362,33 @@
 def first_kernel(steps, twos, ratio, cols, *refs):
     lefts, refs = split_lefts(refs, twos)
     rights, refs = refs[: ratio * len(steps)], refs[ratio * len(steps) :]
-    one_ref, weight_ref, sums_ref, gate_ref, left_scr = refs
-    add_terms(sums_ref, None, lefts, rights, steps, ratio, cols, left_scr)
+    one_ref, weight_ref, left_ref, sums_ref, gate_ref = refs
+    widen(lefts, left_ref)
+    add_terms(sums_ref, None, rights, steps, ratio, cols, left_ref)
     norm = layer_norm(one_ref[...].astype(F32)).astype(BF16)
     gate_ref[...] = jax.nn.sigmoid(dot(norm, weight_ref[...]))
 
 
-def last_kernel(steps, twos, ratio, cols, *refs):
-    lefts, refs = split_lefts(refs, twos)
+def last_kernel(steps, ratio, cols, left_ref, *refs):
     rights, refs = refs[: ratio * len(steps)], refs[ratio * len(steps) :]
-    (start_ref, one_ref, gate_ref, out_ref, up_ref, down_ref, result_ref, left_scr, sum_scr) = refs
-    add_terms(sum_scr, start_ref, lefts, rights, steps, ratio, cols, left_scr)
-    one = one_ref[...].astype(F32)
-    hidden = layer_norm(sum_scr[...].astype(BF16).astype(F32)).astype(BF16)
-    two = (one + gate_ref[...] * dot(hidden, out_ref[...])).astype(BF16).astype(F32)
-    wide = jnp.maximum(dot(layer_norm(two).astype(BF16), up_ref[...]), 0.0).astype(BF16)
-    result = (two + dot(wide, down_ref[...])).astype(BF16)
-    result_ref[...] = result.reshape(result_ref.shape)
+    (start_ref, one_ref, gate_ref, out_ref, up_ref, down_ref, result_ref, sum_scr) = refs
+    add_terms(sum_scr, start_ref, rights, steps, ratio, cols, left_ref)
+    pairs, channels = one_ref.shape
+    span = pairs // HALVES
+    parts = [slice(part * span, (part + 1) * span) for part in range(HALVES)]
+    hidden = [layer_norm(sum_scr[part, :].astype(BF16).astype(F32)).astype(BF16) for part in parts]
+    update = [dot(value, out_ref[...]) for value in hidden]
+    two = [
+        (one_ref[part, :].astype(F32) + gate_ref[part, :] * value).astype(BF16).astype(F32)
+        for part, value in zip(parts, update)
+    ]
+    norm = [layer_norm(value).astype(BF16) for value in two]
+    wide = [jnp.maximum(dot(value, up_ref[...]), 0.0).astype(BF16) for value in norm]
+    result = [value + dot(inner, down_ref[...]) for value, inner in zip(two, wide)]
+    lines = span // cols
+    for part, value in enumerate(result):
+        value = value.astype(BF16).reshape(lines, cols, channels)
+        result_ref[part * lines : (part + 1) * lines] = value
 
 
 def triangle_update(lefts, rights, one, cols, gate_weight, out, up, down):
@@ -379,34 +399,32 @@
     ratio = len(rights) // twos
     late, early = range(twos // 2), range(twos // 2, twos)
     limit = (12 << 20) if ratio == 1 else (50 << 20)
-    left_scr = pltpu.VMEM((subs, pairs, channels), F32)
     shape = jax.ShapeDtypeStruct((pairs, channels), F32)
 
     def chosen(steps):
         return [rights[turn * twos + step] for turn in range(ratio) for step in steps]
 
-    sums, gate = pl.pallas_call(
+    left, sums, gate = pl.pallas_call(
         functools.partial(first_kernel, early, twos, ratio, cols),
-        out_shape=(shape, shape),
+        out_shape=(jax.ShapeDtypeStruct((subs, pairs, channels), F32), shape, shape),
         in_specs=[vmem()] * (len(lefts) + ratio * len(early) + 2),
-        out_specs=[vmem()] * 2,
-        scratch_shapes=[left_scr],
+        out_specs=[vmem()] * 3,
         compiler_params=pltpu.CompilerParams(vmem_limit_bytes=limit),
         cost_estimate=pl.CostEstimate(
             flops=2 * pairs * channels * 1024, bytes_accessed=1 << 20, transcendentals=pairs * 128
         ),
     )(*lefts, *chosen(early), one, gate_weight)
     return pl.pallas_call(
-        functools.partial(last_kernel, late, twos, ratio, cols),
+        functools.partial(last_kernel, late, ratio, cols),
         out_shape=jax.ShapeDtypeStruct((rows, cols, channels), BF16),
-        in_specs=[vmem()] * (len(lefts) + ratio * len(late) + 6),
+        in_specs=[vmem()] * (1 + ratio * len(late) + 6),
         out_specs=vmem(),
-        scratch_shapes=[left_scr, pltpu.VMEM((pairs, channels), F32)],
+        scratch_shapes=[pltpu.VMEM((pairs, channels), F32)],
         compiler_params=pltpu.CompilerParams(vmem_limit_bytes=limit),
         cost_estimate=pl.CostEstimate(
             flops=2 * pairs * channels * 2048, bytes_accessed=2 << 20, transcendentals=pairs * 128
         ),
-    )(*lefts, *chosen(late), sums, one, gate, out, up, down)
+    )(left, *chosen(late), sums, one, gate, out, up, down)
 
 
 def per_device(

time: 32.9 us -> 33.2 us (level)
  the two profiles are of different devices: /device:TPU:3 before, /device:TPU:7 now
where the time goes in v14:
time: 33.2 us; the launch traced here: 33 us
  starting transfers between devices  12.5 us (38%)
  Pallas kernels  9.77 us (29%)
  waiting for transfers between devices  8.86 us (27%)
  local copies, waits for them, and re-layouts  1.62 us (5%)
    ppermute x6, starting transfers between devices, fetch(): return lax.ppermute(values, ('dap', 'sub'), perm)  12.5 us
    ppermute x6, waiting for transfers between devices, fetch(): return lax.ppermute(values, ('dap', 'sub'), perm)  8.86 us
    pallas_call x2, Pallas kernels, factor(): pl.pallas_call(factor_kernel, out_shape=jax.ShapeDtypeStruct((rows * hidd...  4.73 us
    pallas_call x1, Pallas kernels, triangle_update(): pl.pallas_call(functools.partial(last_kernel, late, ratio, cols), out_sha...  1.84 us
    pallas_call x1, Pallas kernels, pair_update(): pl.pallas_call(functools.partial(pair_kernel, ratio, hidden), out_shape=(...  1.7 us
    unnamed x30, local copies, waits for them, and re-layouts  1.61 us
    pallas_call x1, Pallas kernels, triangle_update(): pl.pallas_call(functools.partial(first_kernel, early, twos, ratio, cols),...  0.72 us
  transfers between devices with their start and end apart: 6, of which 5 were waited for; matrix products, arithmetic and copies ran while one was open for 0% of the time, Pallas kernels for 12%

profile of v14, /device:TPU:7, one launch (start us, length us, event | category | flops | bytes accessed | tf_op | source)
XLA Modules:
  0.0 33.0 jit_solution(4008717431093171919)
XLA Ops:
  0.0 0.0 copy-start.12
  0.0 0.0 copy-start.13
  0.0 0.9 %copy-done.13 = bf16[256,32]{0,1:T(8,128)(2,1)S(1)} copy-done((bf16[256,32]{0,1:T(8,128)(2,1)S(1)}, bf16[256,32]{0,1:T(8,128)(2,1)}, u32[]{:S(2)}) %copy-start.13) | copy-done | bytes 16408
  0.9 0.1 shard_map.148.weight_ref
  0.9 0.7 %copy-done.12 = bf16[256,16,256]{2,1,0:T(8,128)(2,1)S(1)} copy-done((bf16[256,16,256]{2,1,0:T(8,128)(2,1)S(1)}, bf16[256,16,256]{2,1,0:T(8,128)(2,1)}, u32[]{:S(2)}) %copy-start.12) | copy-done | bytes 2097176
  1.6 0.0 copy-start.14
  1.6 2.3 %shard_map.149 = bf16[4,256,128]{2,1,0:T(8,128)(2,1)S(1)} custom-call(bf16[256,16,256]{2,1,0:T(8,128)(2,1)S(1)} %copy-done.12, bf16[256,128]{1,0:T(8,128)(2,1)S(1)} %shard_map.148.weight_ref), custom_call_target="tpu_custom_call" | custom-call | flops 1073741824 | bytes 4194304 | tf_op jit(solution)/shard_map/pallas_call | solution.py:115
  3.9 0.0 copy-start.3
  3.9 4.9 %collective-permute-start = (bf16[4,256,128]{2,1,0:T(8,128)(2,1)S(1)}, bf16[4,256,128]{2,1,0:T(8,128)(2,1)S(1)}, u32[]{:S(2)}, u32[]{:S(2)}) collective-permute-start(bf16[4,256,128]{2,1,0:T(8,128)(2,1)S(1)} %shard_map.149), channel_id=1, source_target_pairs={{0,0},{6,1},{8,2},{14,3},{2,4},{5,5},{11,6},{12,7},{3,8},{4,9},{10... | collective-permute-start | bytes 786440 | tf_op jit(solution)/shard_map/ppermute | solution.py:457
  8.8 0.0 copy-done.14
  8.8 0.1 shard_map.145.weight_ref
  8.9 0.0 copy-start
  8.9 0.0 copy-start.4
  8.9 0.0 copy-start.9
  8.9 0.0 copy-start.10
  8.9 0.0 copy-start.11
  8.9 0.0 copy-done.3
  9.0 0.0 copy-start.5
  9.0 0.0 copy-start.6
  9.0 2.4 %shard_map.146.zl_ref = bf16[4,256,128]{2,1,0:T(8,128)(2,1)S(1)} custom-call(bf16[256,16,256]{2,1,0:T(8,128)(2,1)S(1)} %copy-done.12, bf16[256,128]{1,0:T(8,128)(2,1)S(1)} %shard_map.145.weight_ref, s32[64,256]{1,0:T(8,128)S(1)} %bitcast.5), custom_call_target="tpu_custom_call" | custom-call | flops 1073741824 | bytes 4194304 | tf_op jit(solution)/shard_map/pallas_call | solution.py:115
  11.4 0.0 copy-start.7
  11.4 0.0 copy-start.1
  11.5 0.0 copy-start.2
  11.5 0.0 copy-start.8
  11.5 0.0 copy-done
  11.5 0.0 copy-done.4
  11.5 0.0 copy-done.9
  11.5 0.0 copy-done.10
  11.5 0.0 copy-done.11
  11.5 0.6 %shard_map.147 = (bf16[2,512,128]{2,1,0:T(8,128)(2,1)S(1)}, f32[256,128]{1,0:T(8,128)S(1)}, f32[256,128]{1,0:T(8,128)S(1)}, f32[256,128]{1,0:T(8,128)S(1)}, bf16...) custom-call(bf16[4,256,128]{2,1,0:T(8,128)(2,1)S(1)} %shard_map.146.zl_ref, s32[64,256]{1,0:T(8,128)S(1)} %bitcast.6, ...), custom_call_target="tpu_custom_call" | custom-call | flops 134217728 | bytes 2097152 | tf_op jit(solution)/shard_map/pallas_call | solution.py:183
  12.2 2.3 %collective-permute-done.refs_0_ = bf16[4,256,128]{2,1,0:T(8,128)(2,1)S(1)} collective-permute-done((bf16[4,256,128]{2,1,0:T(8,128)(2,1)S(1)}, bf16[4,256,128]{2,1,0:T(8,128)(2,1)S(1)}, u32[]{:S(2)}, u32[]{:S(2)}) %collective-permute-start) | collective-permute-done | bytes 262176 | tf_op jit(solution)/shard_map/ppermute | solution.py:457
  14.5 0.0 copy-done.5
  14.5 0.0 copy-done.6
  14.5 1.7 %shard_map.150 = (bf16[2,256,128]{2,1,0:T(8,128)(2,1)S(1)}, bf16[256,128]{1,0:T(8,128)(2,1)S(1)}, bf16[256,128]{1,0:T(8,128)(2,1)S(1)}) custom-call(bf16[2,512,128]{2,1,0:T(8,128)(2,1)S(1)} %get-tuple-element.17.zlt_ref, bf16[4,256,128]{2,1,0:T(8,128)(2,1)S(1)} %collective-permute-done.refs_0_, bf16[4,256,128]{2,1,0:T(8,128)(2,1)S(1)} %get-tuple-element.18.refs_1_, ...), custom_call_target="tpu_custom_call" | custom-call | flops 268435456 | bytes 2097152 | tf_op jit(solution)/shard_map/pallas_call | solution.py:271
  16.2 3.2 %collective-permute-start.1 = (bf16[2,256,128]{2,1,0:T(8,128)(2,1)S(1)}, bf16[2,256,128]{2,1,0:T(8,128)(2,1)S(1)}, u32[]{:S(2)}, u32[]{:S(2)}) collective-permute-start(bf16[2,256,128]{2,1,0:T(8,128)(2,1)S(1)} %get-tuple-element.23.refs_0_), channel_id=1, source_target_pairs={{1,0},{0,1},{3,2},{2,3},{5,4},{4,5},{7,6},{6,7},{9,8},{8,9},{11,10... | collective-permute-start | bytes 393224 | tf_op jit(solution)/shard_map/ppermute | solution.py:457
  19.4 0.0 collective-permute-start.2
  19.4 1.0 %collective-permute-done.1.refs_1_ = bf16[2,256,128]{2,1,0:T(8,128)(2,1)S(1)} collective-permute-done((bf16[2,256,128]{2,1,0:T(8,128)(2,1)S(1)}, bf16[2,256,128]{2,1,0:T(8,128)(2,1)S(1)}, u32[]{:S(2)}, u32[]{:S(2)}) %collective-permute-start.1) | collective-permute-done | bytes 131104 | tf_op jit(solution)/shard_map/ppermute | solution.py:457
  20.4 2.4 %collective-permute-start.4 = (bf16[2,256,128]{2,1,0:T(8,128)(2,1)S(1)}, bf16[2,256,128]{2,1,0:T(8,128)(2,1)S(1)}, u32[]{:S(2)}, u32[]{:S(2)}) collective-permute-start(bf16[2,256,128]{2,1,0:T(8,128)(2,1)S(1)} %pad_maximum_fusion), channel_id=1, source_target_pairs={{2,0},{4,1},{10,2},{12,3},{0,4},{7,5},{9,6},{14,7},{1,8},{6,9},{8,... | collective-permute-start | bytes 393224 | tf_op jit(solution)/shard_map/ppermute | solution.py:457
  22.7 1.9 %collective-permute-start.5 = (bf16[2,256,128]{2,1,0:T(8,128)(2,1)S(1)}, bf16[2,256,128]{2,1,0:T(8,128)(2,1)S(1)}, u32[]{:S(2)}, u32[]{:S(2)}) collective-permute-start(bf16[2,256,128]{2,1,0:T(8,128)(2,1)S(1)} %pad_maximum_fusion), channel_id=1, source_target_pairs={{0,0},{6,1},{8,2},{14,3},{2,4},{5,5},{11,6},{12,7},{3,8},{4,9},{10... | collective-permute-start | bytes 393224 | tf_op jit(solution)/shard_map/ppermute | solution.py:457
  24.7 0.0 collective-permute-done.2.refs_2_
  24.7 0.1 collective-permute-start.3
  24.8 1.2 %collective-permute-done.3.refs_3_ = bf16[256,128]{1,0:T(8,128)(2,1)S(1)} collective-permute-done((bf16[256,128]{1,0:T(8,128)(2,1)S(1)}, bf16[256,128]{1,0:T(8,128)(2,1)S(1)}, u32[]{:S(2)}, u32[]{:S(2)}) %collective-permute-start.3) | collective-permute-done | bytes 65568 | tf_op jit(solution)/shard_map/ppermute | solution.py:457
  26.0 1.5 %collective-permute-done.4.refs_4_ = bf16[2,256,128]{2,1,0:T(8,128)(2,1)S(1)} collective-permute-done((bf16[2,256,128]{2,1,0:T(8,128)(2,1)S(1)}, bf16[2,256,128]{2,1,0:T(8,128)(2,1)S(1)}, u32[]{:S(2)}, u32[]{:S(2)}) %collective-permute-start.4) | collective-permute-done | bytes 131104 | tf_op jit(solution)/shard_map/ppermute | solution.py:457
  27.5 0.0 copy-done.7
  27.5 0.7 %shard_map.151 = (f32[4,256,128]{2,1,0:T(8,128)S(1)}, f32[256,128]{1,0:T(8,128)S(1)}, f32[256,128]{1,0:T(8,128)S(1)}) custom-call(bf16[2,256,128]{2,1,0:T(8,128)(2,1)S(1)} %get-tuple-element.23.refs_0_, bf16[2,256,128]{2,1,0:T(8,128)(2,1)S(1)} %collective-permute-done.1.refs_1_, bf16[256,128]{1,0:T(8,128)(2,1)S(1)} %collective-permute-done.2.refs_2_, ...), custom_call_target="tpu_custom_call" | custom-call | flops 67108864 | bytes 1048576 | tf_op jit(solution)/shard_map/pallas_call | solution.py:407
  28.3 2.9 %collective-permute-done.5.refs_0_ = bf16[2,256,128]{2,1,0:T(8,128)(2,1)S(1)} collective-permute-done((bf16[2,256,128]{2,1,0:T(8,128)(2,1)S(1)}, bf16[2,256,128]{2,1,0:T(8,128)(2,1)S(1)}, u32[]{:S(2)}, u32[]{:S(2)}) %collective-permute-start.5) | collective-permute-done | bytes 131104 | tf_op jit(solution)/shard_map/ppermute | solution.py:457
  31.1 0.0 copy-done.1
  31.1 0.0 copy-done.2
  31.1 0.0 copy-done.8
  31.1 1.8 %shard_map.152 = bf16[16,16,128]{2,1,0:T(8,128)(2,1)} custom-call(f32[4,256,128]{2,1,0:T(8,128)S(1)} %get-tuple-element.26.left_ref, bf16[2,256,128]{2,1,0:T(8,128)(2,1)S(1)} %collective-permute-done.5.refs_0_, f32[256,128]{1,0:T(8,128)S(1)} %get-tuple-element.27.refs_1_, bf16[256,128]{1,0:T(8,128)(2,1)S(1)} %get-tuple-element.25.refs_5_.refs_2_, ...), custom_call_target="tpu_custom_call" | custom-call | flops 134217728 | bytes 2097152 | tf_op jit(solution)/shard_map/pallas_call | solution.py:417
  (3 shorter events, 0.0 us)
Async XLA Ops:
  0.0 1.6 %copy-start.12 = (bf16[256,16,256]{2,1,0:T(8,128)(2,1)S(1)}, bf16[256,16,256]{2,1,0:T(8,128)(2,1)}, u32[]{:S(2)}) copy-start(bf16[256,16,256]{2,1,0:T(8,128)(2,1)} %x_ref.3) | copy-start | bytes 6291460
  0.0 0.9 %copy-start.13 = (bf16[256,32]{0,1:T(8,128)(2,1)S(1)}, bf16[256,32]{0,1:T(8,128)(2,1)}, u32[]{:S(2)}) copy-start(bf16[256,32]{0,1:T(8,128)(2,1)} %param.21) | copy-start | bytes 49156
  1.6 7.2 %copy-start.14 = (bf16[256,32]{0,1:T(8,128)(2,1)S(1)}, bf16[256,32]{0,1:T(8,128)(2,1)}, u32[]{:S(2)}) copy-start(bf16[256,32]{0,1:T(8,128)(2,1)} %param.20) | copy-start | bytes 49156
  3.9 5.0 %copy-start.3 = (s32[256,64]{0,1:T(8,128)S(1)}, s32[256,64]{0,1:T(8,128)}, u32[]{:S(2)}) copy-start(s32[256,64]{0,1:T(8,128)} %param.16) | copy-start | bytes 196612
  3.9 10.6 %collective-permute-start = (bf16[4,256,128]{2,1,0:T(8,128)(2,1)S(1)}, bf16[4,256,128]{2,1,0:T(8,128)(2,1)S(1)}, u32[]{:S(2)}, u32[]{:S(2)}) collective-permute-start(bf16[4,256,128]{2,1,0:T(8,128)(2,1)S(1)} %shard_map.149), channel_id=1, source_target_pairs={{0,0},{6,1},{8,2},{14,3},{2,4},{5,5},{11,6},{12,7},{3,8},{4,9},{10... | collective-permute-start | bytes 786440 | tf_op jit(solution)/shard_map/ppermute | solution.py:457
  8.9 2.6 %copy-start = (f32[32,32,128]{2,1,0:T(8,128)S(1)}, f32[32,32,128]{2,1,0:T(8,128)}, u32[]{:S(2)}) copy-start(f32[32,32,128]{2,1,0:T(8,128)} %proj_ref.1) | copy-start | bytes 1572868
  8.9 2.6 %copy-start.4 = (bf16[16,16,128]{2,1,0:T(8,128)(2,1)S(1)}, bf16[16,16,128]{2,1,0:T(8,128)(2,1)}, u32[]{:S(2)}) copy-start(bf16[16,16,128]{2,1,0:T(8,128)(2,1)} %pair_ref.1) | copy-start | bytes 196612
  8.9 2.6 %copy-start.9 = (bf16[66,128]{1,0:T(8,128)(2,1)S(1)}, bf16[66,128]{1,0:T(8,128)(2,1)}, u32[]{:S(2)}) copy-start(bf16[66,128]{1,0:T(8,128)(2,1)} %table_ref.1) | copy-start | bytes 50692
  8.9 2.6 %copy-start.10 = (s32[64]{0:T(128)S(1)}, s32[64]{0:T(128)}, u32[]{:S(2)}) copy-start(s32[64]{0:T(128)} %param.18) | copy-start | bytes 772
  8.9 2.6 %copy-start.11 = (s32[64]{0:T(128)S(1)}, s32[64]{0:T(128)}, u32[]{:S(2)}) copy-start(s32[64]{0:T(128)} %param.19) | copy-start | bytes 772
  9.0 5.5 %copy-start.5 = (bf16[128,256]{1,0:T(8,128)(2,1)S(1)}, bf16[128,256]{1,0:T(8,128)(2,1)}, u32[]{:S(2)}) copy-start(bf16[128,256]{1,0:T(8,128)(2,1)} %refs_6_.3) | copy-start | bytes 196612
  9.0 5.5 %copy-start.6 = (bf16[128,256]{1,0:T(8,128)(2,1)S(1)}, bf16[128,256]{1,0:T(8,128)(2,1)}, u32[]{:S(2)}) copy-start(bf16[128,256]{1,0:T(8,128)(2,1)} %refs_7_.1) | copy-start | bytes 196612
  11.4 16.1 %copy-start.7 = (bf16[128,128]{1,0:T(8,128)(2,1)S(1)}, bf16[128,128]{1,0:T(8,128)(2,1)}, u32[]{:S(2)}) copy-start(bf16[128,128]{1,0:T(8,128)(2,1)} %refs_6_.4) | copy-start | bytes 98308
  11.4 19.7 %copy-start.1 = (bf16[128,512]{1,0:T(8,128)(2,1)S(1)}, bf16[128,512]{1,0:T(8,128)(2,1)}, u32[]{:S(2)}) copy-start(bf16[128,512]{1,0:T(8,128)(2,1)} %refs_5_.1) | copy-start | bytes 393220
  11.5 19.7 %copy-start.2 = (bf16[512,128]{1,0:T(8,128)(2,1)S(1)}, bf16[512,128]{1,0:T(8,128)(2,1)}, u32[]{:S(2)}) copy-start(bf16[512,128]{1,0:T(8,128)(2,1)} %refs_6_.5) | copy-start | bytes 393220
  11.5 19.7 %copy-start.8 = (bf16[128,128]{1,0:T(8,128)(2,1)S(1)}, bf16[128,128]{1,0:T(8,128)(2,1)}, u32[]{:S(2)}) copy-start(bf16[128,128]{1,0:T(8,128)(2,1)} %refs_4_.1) | copy-start | bytes 98308
  16.2 4.2 %collective-permute-start.1 = (bf16[2,256,128]{2,1,0:T(8,128)(2,1)S(1)}, bf16[2,256,128]{2,1,0:T(8,128)(2,1)S(1)}, u32[]{:S(2)}, u32[]{:S(2)}) collective-permute-start(bf16[2,256,128]{2,1,0:T(8,128)(2,1)S(1)} %get-tuple-element.23.refs_0_), channel_id=1, source_target_pairs={{1,0},{0,1},{3,2},{2,3},{5,4},{4,5},{7,6},{6,7},{9,8},{8,9},{11,10... | collective-permute-start | bytes 393224 | tf_op jit(solution)/shard_map/ppermute | solution.py:457
  19.4 5.3 %collective-permute-start.2 = (bf16[256,128]{1,0:T(8,128)(2,1)S(1)}, bf16[256,128]{1,0:T(8,128)(2,1)S(1)}, u32[]{:S(2)}, u32[]{:S(2)}) collective-permute-start(bf16[256,128]{1,0:T(8,128)(2,1)S(1)} %get-tuple-element.24), channel_id=1, source_target_pairs={{2,0},{3,1},{0,2},{1,3},{6,4},{7,5},{4,6},{5,7},{10,8},{11,9},{8,1... | collective-permute-start | bytes 196616 | tf_op jit(solution)/shard_map/ppermute | solution.py:457
  20.4 7.1 %collective-permute-start.4 = (bf16[2,256,128]{2,1,0:T(8,128)(2,1)S(1)}, bf16[2,256,128]{2,1,0:T(8,128)(2,1)S(1)}, u32[]{:S(2)}, u32[]{:S(2)}) collective-permute-start(bf16[2,256,128]{2,1,0:T(8,128)(2,1)S(1)} %pad_maximum_fusion), channel_id=1, source_target_pairs={{2,0},{4,1},{10,2},{12,3},{0,4},{7,5},{9,6},{14,7},{1,8},{6,9},{8,... | collective-permute-start | bytes 393224 | tf_op jit(solution)/shard_map/ppermute | solution.py:457
  22.7 8.4 %collective-permute-start.5 = (bf16[2,256,128]{2,1,0:T(8,128)(2,1)S(1)}, bf16[2,256,128]{2,1,0:T(8,128)(2,1)S(1)}, u32[]{:S(2)}, u32[]{:S(2)}) collective-permute-start(bf16[2,256,128]{2,1,0:T(8,128)(2,1)S(1)} %pad_maximum_fusion), channel_id=1, source_target_pairs={{0,0},{6,1},{8,2},{14,3},{2,4},{5,5},{11,6},{12,7},{3,8},{4,9},{10... | collective-permute-start | bytes 393224 | tf_op jit(solution)/shard_map/ppermute | solution.py:457
  24.7 1.3 %collective-permute-start.3 = (bf16[256,128]{1,0:T(8,128)(2,1)S(1)}, bf16[256,128]{1,0:T(8,128)(2,1)S(1)}, u32[]{:S(2)}, u32[]{:S(2)}) collective-permute-start(bf16[256,128]{1,0:T(8,128)(2,1)S(1)} %collective-permute-done.2.refs_2_), channel_id=1, source_target_pairs={{1,0},{0,1},{3,2},{2,3},{5,4},{4,5},{7,6},{6,7},{9,8},{8,9},{11,10... | collective-permute-start | bytes 196616 | tf_op jit(solution)/shard_map/ppermute | solution.py:457

commit v15 on v13

--- a/solution.py
+++ b/solution.py
@@ -9,6 +9,7 @@
 
 REL_CLIP = 32
 LANES = 128
+PARTS = 2
 EPSILON = 1e-05
 BF16 = jnp.bfloat16
 F32 = jnp.float32
@@ -67,13 +68,13 @@
     )(weight)
 
 
-def factor_kernel(x_ref, weight_ref, *refs):
-    mask_ref = refs[0] if len(refs) == 3 else None
-    z_ref, y_scr = refs[-2:]
-    groups, seqs, _ = z_ref.shape
+def factor_kernel(masked, hidden, x_ref, weight_ref, *refs):
+    mask_ref = refs[0] if masked else None
+    z_refs, y_scr = refs[masked:-1], refs[-1]
+    each, seqs, _ = z_refs[0].shape
+    groups = each * len(z_refs)
     _, rows, channels = x_ref.shape
     rep = rows // groups
-    hidden = LANES // rep
     width = rows * hidden
     step = y_scr.shape[1] // rows
     w = jnp.concatenate([weight_ref[...], jnp.ones((channels, LANES), BF16)], axis=1)
@@ -104,18 +105,19 @@
                 z = jnp.where(block == k, next_z, z)
             if mask_ref is not None:
                 z = z * live[here, group * LANES : (group + 1) * LANES]
-            z_ref[group, here, :] = z.astype(BF16)
-
-
-def factor(alignment, weight, hidden, mask=None):
+            z_refs[group // each][group % each, here, :] = z.astype(BF16)
+
+
+def factor(alignment, weight, hidden, parts, mask=None):
     seqs, rows, channels = alignment.shape
-    step = seqs // 4
+    step = seqs // 2
     operands = (alignment, weight) if mask is None else (alignment, weight, mask)
+    shape = jax.ShapeDtypeStruct((rows * hidden // LANES // parts, seqs, LANES), BF16)
     return pl.pallas_call(
-        factor_kernel,
-        out_shape=jax.ShapeDtypeStruct((rows * hidden // LANES, seqs, LANES), BF16),
+        functools.partial(factor_kernel, mask is not None, hidden),
+        out_shape=(shape,) * parts,
         in_specs=[vmem()] * len(operands),
-        out_specs=vmem(),
+        out_specs=[vmem()] * parts,
         scratch_shapes=[pltpu.VMEM((seqs // step, step * rows, LANES), F32)],
         compiler_params=pltpu.CompilerParams(vmem_limit_bytes=24 << 20),
         cost_estimate=pl.CostEstimate(
@@ -200,7 +202,7 @@
 
 
 def pair_kernel(ratio, hidden, zlt_ref, *refs):
-    zr_refs, refs = refs[:ratio], refs[ratio:]
+    zr_refs, refs = refs[: ratio * PARTS], refs[ratio * PARTS :]
     (seen_ref, base_ref, inverse_ref, live_ref, proj_ref, tl_ref, tr_ref,
      both_ref, left_ref, one_ref, outer_scr, flat_scr, one_scr) = refs
     pairs, channels = base_ref.shape
@@ -216,7 +218,9 @@
         block = lax.rem(me + step, ratio)
         right = []
         for group in range(rows // rep):
-            right.append(zr_refs[step][group] * seen_ref[block * (rows // rep) + group])
+            each = rows // rep // PARTS
+            factor = zr_refs[step * PARTS + group // each][group % each]
+            right.append(factor * seen_ref[block * (rows // rep) + group])
         outer = dot(left, jnp.concatenate(right, axis=1))
         for group in range(rows // rep):
             outer_scr[group] = outer[:, group * LANES : (group + 1) * LANES]
@@ -261,7 +265,7 @@
 
 def pair_update(hidden, zlt, zrs, seen, base, inverse, live, proj, triangle_left, triangle_right):
     pairs, channels = base.shape
-    ratio = len(zrs)
+    ratio = len(zrs) // PARTS
     shape = jax.ShapeDtypeStruct((pairs, channels), BF16)
     return pl.pallas_call(
         functools.partial(pair_kernel, ratio, hidden),
@@ -269,7 +273,7 @@
         in_specs=[vmem()] * (8 + len(zrs)),
         out_specs=[vmem()] * 3,
         scratch_shapes=[
-            pltpu.VMEM((zrs[0].shape[0], zlt.shape[1], LANES), F32),
+            pltpu.VMEM((zrs[0].shape[0] * PARTS, zlt.shape[1], LANES), F32),
             pltpu.VMEM((proj.shape[0] // LANES, pairs, LANES), BF16),
             pltpu.VMEM((pairs, channels), F32),
         ],
@@ -443,12 +447,18 @@
 
     hidden = outer_left.shape[1]
     mask = alignment_mask.T
-    zr = factor(alignment, repeat_weight(outer_right.T), hidden)
+    zr = factor(alignment, repeat_weight(outer_right.T), hidden, PARTS)
     zrs = [
-        fetch(zr, lambda a, b, turn=turn: (owner(a, b, turn), sender(a, b, subs, ratio)))
+        fetch(
+            zr[part],
+            lambda a, b, t=turn, p=part: (
+                owner(a, b, t), (sender(a, b, subs, ratio) + 2 * p) % subs
+            ),
+        )
         for turn in range(ratio)
+        for part in range(PARTS)
     ]
-    zl = factor(alignment, repeat_weight(outer_left.T), hidden, mask)
+    (zl,) = factor(alignment, repeat_weight(outer_left.T), hidden, 1, mask)
     zlt, base, inverse, live, proj, seen = prepare(
         zl, mask, pair_input, residue_mask, chain_index, relative_table, outer_proj
     )

time: 32.9 us -> 33.3 us (1.012)
  the two profiles are of different devices: /device:TPU:3 before, /device:TPU:1 now
where the time goes in v15:
time: 33.3 us; the launch traced here: 33.1 us
  starting transfers between devices  15.4 us (46%)
  Pallas kernels  9.13 us (27%)
  waiting for transfers between devices  6.66 us (20%)
  local copies, waits for them, and re-layouts  1.62 us (5%)
    ppermute x7, starting transfers between devices, fetch(): return lax.ppermute(values, ('dap', 'sub'), perm)  15.4 us
    ppermute x7, waiting for transfers between devices, fetch(): return lax.ppermute(values, ('dap', 'sub'), perm)  6.66 us
    pallas_call x2, Pallas kernels, factor(): pl.pallas_call(functools.partial(factor_kernel, mask is not None, hidden)...  4.17 us
    pallas_call x1, Pallas kernels, triangle_update(): pl.pallas_call(functools.partial(last_kernel, late, twos, ratio, cols), o...  1.87 us
    unnamed x30, local copies, waits for them, and re-layouts  1.61 us
    pallas_call x1, Pallas kernels, pair_update(): pl.pallas_call(functools.partial(pair_kernel, ratio, hidden), out_shape=(...  1.59 us
    pallas_call x1, Pallas kernels, triangle_update(): pl.pallas_call(functools.partial(first_kernel, early, twos, ratio, cols),...  0.73 us
  transfers between devices with their start and end apart: 7, of which 3 were waited for; matrix products, arithmetic and copies ran while one was open for 0% of the time, Pallas kernels for 11%

profile of v15, /device:TPU:1, one launch (start us, length us, event | category | flops | bytes accessed | tf_op | source)
XLA Modules:
  0.0 33.1 jit_solution(11839985268476337674)
XLA Ops:
  0.0 0.0 copy-start.12
  0.0 0.0 copy-start.13
  0.0 0.9 %copy-done.13 = bf16[256,32]{0,1:T(8,128)(2,1)S(1)} copy-done((bf16[256,32]{0,1:T(8,128)(2,1)S(1)}, bf16[256,32]{0,1:T(8,128)(2,1)}, u32[]{:S(2)}) %copy-start.13) | copy-done | bytes 16408
  0.9 0.1 shard_map.148.weight_ref
  0.9 0.7 %copy-done.12 = bf16[256,16,256]{2,1,0:T(8,128)(2,1)S(1)} copy-done((bf16[256,16,256]{2,1,0:T(8,128)(2,1)S(1)}, bf16[256,16,256]{2,1,0:T(8,128)(2,1)}, u32[]{:S(2)}) %copy-start.12) | copy-done | bytes 2097176
  1.6 0.0 copy-start.14
  1.6 2.0 %shard_map.149 = (bf16[2,256,128]{2,1,0:T(8,128)(2,1)S(1)}, bf16[2,256,128]{2,1,0:T(8,128)(2,1)S(1)}) custom-call(bf16[256,16,256]{2,1,0:T(8,128)(2,1)S(1)} %copy-done.12, bf16[256,128]{1,0:T(8,128)(2,1)S(1)} %shard_map.148.weight_ref), custom_call_target="tpu_custom_call" | custom-call | flops 1073741824 | bytes 4194304 | tf_op jit(solution)/shard_map/pallas_call | solution.py:116
  3.6 0.0 copy-start.3
  3.6 6.8 %collective-permute-start = (bf16[2,256,128]{2,1,0:T(8,128)(2,1)S(1)}, bf16[2,256,128]{2,1,0:T(8,128)(2,1)S(1)}, u32[]{:S(2)}, u32[]{:S(2)}) collective-permute-start(bf16[2,256,128]{2,1,0:T(8,128)(2,1)S(1)} %get-tuple-element.19), channel_id=1, source_target_pairs={{0,0},{6,1},{8,2},{14,3},{2,4},{5,5},{11,6},{12,7},{3,8},{4,9},{10... | collective-permute-start | bytes 393224 | tf_op jit(solution)/shard_map/ppermute | solution.py:443
  10.4 0.3 collective-permute-start.1
  10.7 0.0 copy-done.14
  10.7 0.1 shard_map.145.weight_ref
  10.8 0.0 copy-start
  10.8 0.0 copy-start.4
  10.8 0.0 copy-start.9
  10.8 0.0 copy-start.10
  10.8 0.0 copy-start.11
  10.8 0.0 copy-done.3
  10.9 0.0 copy-start.5
  10.9 0.0 copy-start.6
  10.9 2.2 %shard_map.146.zl_ref = bf16[4,256,128]{2,1,0:T(8,128)(2,1)S(1)} custom-call(bf16[256,16,256]{2,1,0:T(8,128)(2,1)S(1)} %copy-done.12, bf16[256,128]{1,0:T(8,128)(2,1)S(1)} %shard_map.145.weight_ref, s32[64,256]{1,0:T(8,128)S(1)} %bitcast.5), custom_call_target="tpu_custom_call" | custom-call | flops 1073741824 | bytes 4194304 | tf_op jit(solution)/shard_map/pallas_call | solution.py:116
  13.0 0.0 copy-start.7
  13.1 0.0 copy-start.1
  13.1 0.0 copy-start.2
  13.1 0.0 copy-start.8
  13.1 0.0 copy-done
  13.1 0.0 copy-done.4
  13.1 0.0 copy-done.9
  13.1 0.0 copy-done.10
  13.1 0.0 copy-done.11
  13.1 0.6 %shard_map.147 = (bf16[2,512,128]{2,1,0:T(8,128)(2,1)S(1)}, f32[256,128]{1,0:T(8,128)S(1)}, f32[256,128]{1,0:T(8,128)S(1)}, f32[256,128]{1,0:T(8,128)S(1)}, bf16...) custom-call(bf16[4,256,128]{2,1,0:T(8,128)(2,1)S(1)} %shard_map.146.zl_ref, s32[64,256]{1,0:T(8,128)S(1)} %bitcast.6, ...), custom_call_target="tpu_custom_call" | custom-call | flops 134217728 | bytes 2097152 | tf_op jit(solution)/shard_map/pallas_call | solution.py:184
  13.8 0.0 collective-permute-done.refs_0_
  13.8 3.0 %collective-permute-done.1.refs_1_ = bf16[2,256,128]{2,1,0:T(8,128)(2,1)S(1)} collective-permute-done((bf16[2,256,128]{2,1,0:T(8,128)(2,1)S(1)}, bf16[2,256,128]{2,1,0:T(8,128)(2,1)S(1)}, u32[]{:S(2)}, u32[]{:S(2)}) %collective-permute-start.1) | collective-permute-done | bytes 131104 | tf_op jit(solution)/shard_map/ppermute | solution.py:443
  16.8 0.0 copy-done.5
  16.8 0.0 copy-done.6
  16.9 1.6 %shard_map.150 = (bf16[2,256,128]{2,1,0:T(8,128)(2,1)S(1)}, bf16[256,128]{1,0:T(8,128)(2,1)S(1)}, bf16[256,128]{1,0:T(8,128)(2,1)S(1)}) custom-call(bf16[2,512,128]{2,1,0:T(8,128)(2,1)S(1)} %get-tuple-element.18.zlt_ref, bf16[2,256,128]{2,1,0:T(8,128)(2,1)S(1)} %collective-permute-done.refs_0_, bf16[2,256,128]{2,1,0:T(8,128)(2,1)S(1)} %collective-permute-done.1.refs_1_, ...), custom_call_target="tpu_custom_call" | custom-call | flops 268435456 | bytes 2097152 | tf_op jit(solution)/shard_map/pallas_call | solution.py:270
  18.5 0.1 collective-permute-start.2
  18.5 2.0 %collective-permute-start.3 = (bf16[256,128]{1,0:T(8,128)(2,1)S(1)}, bf16[256,128]{1,0:T(8,128)(2,1)S(1)}, u32[]{:S(2)}, u32[]{:S(2)}) collective-permute-start(bf16[256,128]{1,0:T(8,128)(2,1)S(1)} %get-tuple-element.27), channel_id=1, source_target_pairs={{2,0},{3,1},{0,2},{1,3},{6,4},{7,5},{4,6},{5,7},{10,8},{11,9},{8,1... | collective-permute-start | bytes 196616 | tf_op jit(solution)/shard_map/ppermute | solution.py:443
  20.5 0.0 collective-permute-done.2.refs_1_
  20.6 1.3 %collective-permute-start.6 = (bf16[2,256,128]{2,1,0:T(8,128)(2,1)S(1)}, bf16[2,256,128]{2,1,0:T(8,128)(2,1)S(1)}, u32[]{:S(2)}, u32[]{:S(2)}) collective-permute-start(bf16[2,256,128]{2,1,0:T(8,128)(2,1)S(1)} %pad_maximum_fusion), channel_id=1, source_target_pairs={{2,0},{4,1},{10,2},{12,3},{0,4},{7,5},{9,6},{14,7},{1,8},{6,9},{8,... | collective-permute-start | bytes 393224 | tf_op jit(solution)/shard_map/ppermute | solution.py:443
  21.9 4.9 %collective-permute-start.5 = (bf16[2,256,128]{2,1,0:T(8,128)(2,1)S(1)}, bf16[2,256,128]{2,1,0:T(8,128)(2,1)S(1)}, u32[]{:S(2)}, u32[]{:S(2)}) collective-permute-start(bf16[2,256,128]{2,1,0:T(8,128)(2,1)S(1)} %pad_maximum_fusion), channel_id=1, source_target_pairs={{0,0},{6,1},{8,2},{14,3},{2,4},{5,5},{11,6},{12,7},{3,8},{4,9},{10... | collective-permute-start | bytes 393224 | tf_op jit(solution)/shard_map/ppermute | solution.py:443
  26.7 0.0 collective-permute-done.3.refs_2_
  26.8 0.1 collective-permute-start.4
  26.8 1.2 %collective-permute-done.4.refs_3_ = bf16[256,128]{1,0:T(8,128)(2,1)S(1)} collective-permute-done((bf16[256,128]{1,0:T(8,128)(2,1)S(1)}, bf16[256,128]{1,0:T(8,128)(2,1)S(1)}, u32[]{:S(2)}, u32[]{:S(2)}) %collective-permute-start.4) | collective-permute-done | bytes 65568 | tf_op jit(solution)/shard_map/ppermute | solution.py:443
  28.1 0.0 collective-permute-done.6.refs_4_
  28.1 0.0 copy-done.7
  28.1 0.7 %shard_map.151 = (f32[256,128]{1,0:T(8,128)S(1)}, f32[256,128]{1,0:T(8,128)S(1)}) custom-call(bf16[2,256,128]{2,1,0:T(8,128)(2,1)S(1)} %get-tuple-element.26.refs_0_, bf16[2,256,128]{2,1,0:T(8,128)(2,1)S(1)} %collective-permute-done.2.refs_1_, bf16[256,128]{1,0:T(8,128)(2,1)S(1)} %collective-permute-done.3.refs_2_, ...), custom_call_target="tpu_custom_call" | custom-call | flops 67108864 | bytes 1048576 | tf_op jit(solution)/shard_map/pallas_call | solution.py:392
  28.8 2.4 %collective-permute-done.5.refs_4_ = bf16[2,256,128]{2,1,0:T(8,128)(2,1)S(1)} collective-permute-done((bf16[2,256,128]{2,1,0:T(8,128)(2,1)S(1)}, bf16[2,256,128]{2,1,0:T(8,128)(2,1)S(1)}, u32[]{:S(2)}, u32[]{:S(2)}) %collective-permute-start.5) | collective-permute-done | bytes 131104 | tf_op jit(solution)/shard_map/ppermute | solution.py:443
  31.2 0.0 copy-done.1
  31.2 0.0 copy-done.2
  31.2 0.0 copy-done.8
  31.2 1.9 %shard_map.152 = bf16[16,16,128]{2,1,0:T(8,128)(2,1)} custom-call(bf16[2,256,128]{2,1,0:T(8,128)(2,1)S(1)} %get-tuple-element.26.refs_0_, bf16[2,256,128]{2,1,0:T(8,128)(2,1)S(1)} %collective-permute-done.2.refs_1_, bf16[256,128]{1,0:T(8,128)(2,1)S(1)} %collective-permute-done.3.refs_2_, bf16[256,128]{1,0:T(8,128)(2,1)S(1)} %collective-permute-done.4.refs_3_, ...), custom_call_target="tpu_custom_call" | custom-call | flops 134217728 | bytes 2097152 | tf_op jit(solution)/shard_map/pallas_call | solution.py:403
  (3 shorter events, 0.0 us)
Async XLA Ops:
  0.0 1.6 %copy-start.12 = (bf16[256,16,256]{2,1,0:T(8,128)(2,1)S(1)}, bf16[256,16,256]{2,1,0:T(8,128)(2,1)}, u32[]{:S(2)}) copy-start(bf16[256,16,256]{2,1,0:T(8,128)(2,1)} %x_ref.3) | copy-start | bytes 6291460
  0.0 0.9 %copy-start.13 = (bf16[256,32]{0,1:T(8,128)(2,1)S(1)}, bf16[256,32]{0,1:T(8,128)(2,1)}, u32[]{:S(2)}) copy-start(bf16[256,32]{0,1:T(8,128)(2,1)} %param.21) | copy-start | bytes 49156
  1.6 9.1 %copy-start.14 = (bf16[256,32]{0,1:T(8,128)(2,1)S(1)}, bf16[256,32]{0,1:T(8,128)(2,1)}, u32[]{:S(2)}) copy-start(bf16[256,32]{0,1:T(8,128)(2,1)} %param.20) | copy-start | bytes 49156
  3.6 7.2 %copy-start.3 = (s32[256,64]{0,1:T(8,128)S(1)}, s32[256,64]{0,1:T(8,128)}, u32[]{:S(2)}) copy-start(s32[256,64]{0,1:T(8,128)} %param.16) | copy-start | bytes 196612
  3.6 10.2 %collective-permute-start = (bf16[2,256,128]{2,1,0:T(8,128)(2,1)S(1)}, bf16[2,256,128]{2,1,0:T(8,128)(2,1)S(1)}, u32[]{:S(2)}, u32[]{:S(2)}) collective-permute-start(bf16[2,256,128]{2,1,0:T(8,128)(2,1)S(1)} %get-tuple-element.19), channel_id=1, source_target_pairs={{0,0},{6,1},{8,2},{14,3},{2,4},{5,5},{11,6},{12,7},{3,8},{4,9},{10... | collective-permute-start | bytes 393224 | tf_op jit(solution)/shard_map/ppermute | solution.py:443
  10.4 6.4 %collective-permute-start.1 = (bf16[2,256,128]{2,1,0:T(8,128)(2,1)S(1)}, bf16[2,256,128]{2,1,0:T(8,128)(2,1)S(1)}, u32[]{:S(2)}, u32[]{:S(2)}) collective-permute-start(bf16[2,256,128]{2,1,0:T(8,128)(2,1)S(1)} %get-tuple-element.20), channel_id=1, source_target_pairs={{2,0},{4,1},{10,2},{12,3},{0,4},{7,5},{9,6},{14,7},{1,8},{6,9},{8,... | collective-permute-start | bytes 393224 | tf_op jit(solution)/shard_map/ppermute | solution.py:443
  10.8 2.3 %copy-start = (f32[32,32,128]{2,1,0:T(8,128)S(1)}, f32[32,32,128]{2,1,0:T(8,128)}, u32[]{:S(2)}) copy-start(f32[32,32,128]{2,1,0:T(8,128)} %proj_ref.1) | copy-start | bytes 1572868
  10.8 2.3 %copy-start.4 = (bf16[16,16,128]{2,1,0:T(8,128)(2,1)S(1)}, bf16[16,16,128]{2,1,0:T(8,128)(2,1)}, u32[]{:S(2)}) copy-start(bf16[16,16,128]{2,1,0:T(8,128)(2,1)} %pair_ref.1) | copy-start | bytes 196612
  10.8 2.3 %copy-start.9 = (bf16[66,128]{1,0:T(8,128)(2,1)S(1)}, bf16[66,128]{1,0:T(8,128)(2,1)}, u32[]{:S(2)}) copy-start(bf16[66,128]{1,0:T(8,128)(2,1)} %table_ref.1) | copy-start | bytes 50692
  10.8 2.3 %copy-start.10 = (s32[64]{0:T(128)S(1)}, s32[64]{0:T(128)}, u32[]{:S(2)}) copy-start(s32[64]{0:T(128)} %param.18) | copy-start | bytes 772
  10.8 2.3 %copy-start.11 = (s32[64]{0:T(128)S(1)}, s32[64]{0:T(128)}, u32[]{:S(2)}) copy-start(s32[64]{0:T(128)} %param.19) | copy-start | bytes 772
  10.9 6.0 %copy-start.5 = (bf16[128,256]{1,0:T(8,128)(2,1)S(1)}, bf16[128,256]{1,0:T(8,128)(2,1)}, u32[]{:S(2)}) copy-start(bf16[128,256]{1,0:T(8,128)(2,1)} %refs_7_.1) | copy-start | bytes 196612
  10.9 6.0 %copy-start.6 = (bf16[128,256]{1,0:T(8,128)(2,1)S(1)}, bf16[128,256]{1,0:T(8,128)(2,1)}, u32[]{:S(2)}) copy-start(bf16[128,256]{1,0:T(8,128)(2,1)} %refs_8_.2) | copy-start | bytes 196612
  13.0 15.0 %copy-start.7 = (bf16[128,128]{1,0:T(8,128)(2,1)S(1)}, bf16[128,128]{1,0:T(8,128)(2,1)}, u32[]{:S(2)}) copy-start(bf16[128,128]{1,0:T(8,128)(2,1)} %refs_6_.1) | copy-start | bytes 98308
  13.1 18.1 %copy-start.1 = (bf16[128,512]{1,0:T(8,128)(2,1)S(1)}, bf16[128,512]{1,0:T(8,128)(2,1)}, u32[]{:S(2)}) copy-start(bf16[128,512]{1,0:T(8,128)(2,1)} %refs_9_.1) | copy-start | bytes 393220
  13.1 18.1 %copy-start.2 = (bf16[512,128]{1,0:T(8,128)(2,1)S(1)}, bf16[512,128]{1,0:T(8,128)(2,1)}, u32[]{:S(2)}) copy-start(bf16[512,128]{1,0:T(8,128)(2,1)} %refs_10_.1) | copy-start | bytes 393220
  13.1 18.1 %copy-start.8 = (bf16[128,128]{1,0:T(8,128)(2,1)S(1)}, bf16[128,128]{1,0:T(8,128)(2,1)}, u32[]{:S(2)}) copy-start(bf16[128,128]{1,0:T(8,128)(2,1)} %refs_8_.3) | copy-start | bytes 98308
  18.5 2.1 %collective-permute-start.2 = (bf16[2,256,128]{2,1,0:T(8,128)(2,1)S(1)}, bf16[2,256,128]{2,1,0:T(8,128)(2,1)S(1)}, u32[]{:S(2)}, u32[]{:S(2)}) collective-permute-start(bf16[2,256,128]{2,1,0:T(8,128)(2,1)S(1)} %get-tuple-element.26.refs_0_), channel_id=1, source_target_pairs={{1,0},{0,1},{3,2},{2,3},{5,4},{4,5},{7,6},{6,7},{9,8},{8,9},{11,10... | collective-permute-start | bytes 393224 | tf_op jit(solution)/shard_map/ppermute | solution.py:443
  18.5 8.2 %collective-permute-start.3 = (bf16[256,128]{1,0:T(8,128)(2,1)S(1)}, bf16[256,128]{1,0:T(8,128)(2,1)S(1)}, u32[]{:S(2)}, u32[]{:S(2)}) collective-permute-start(bf16[256,128]{1,0:T(8,128)(2,1)S(1)} %get-tuple-element.27), channel_id=1, source_target_pairs={{2,0},{3,1},{0,2},{1,3},{6,4},{7,5},{4,6},{5,7},{10,8},{11,9},{8,1... | collective-permute-start | bytes 196616 | tf_op jit(solution)/shard_map/ppermute | solution.py:443
  20.6 7.5 %collective-permute-start.6 = (bf16[2,256,128]{2,1,0:T(8,128)(2,1)S(1)}, bf16[2,256,128]{2,1,0:T(8,128)(2,1)S(1)}, u32[]{:S(2)}, u32[]{:S(2)}) collective-permute-start(bf16[2,256,128]{2,1,0:T(8,128)(2,1)S(1)} %pad_maximum_fusion), channel_id=1, source_target_pairs={{2,0},{4,1},{10,2},{12,3},{0,4},{7,5},{9,6},{14,7},{1,8},{6,9},{8,... | collective-permute-start | bytes 393224 | tf_op jit(solution)/shard_map/ppermute | solution.py:443
  21.9 9.3 %collective-permute-start.5 = (bf16[2,256,128]{2,1,0:T(8,128)(2,1)S(1)}, bf16[2,256,128]{2,1,0:T(8,128)(2,1)S(1)}, u32[]{:S(2)}, u32[]{:S(2)}) collective-permute-start(bf16[2,256,128]{2,1,0:T(8,128)(2,1)S(1)} %pad_maximum_fusion), channel_id=1, source_target_pairs={{0,0},{6,1},{8,2},{14,3},{2,4},{5,5},{11,6},{12,7},{3,8},{4,9},{10... | collective-permute-start | bytes 393224 | tf_op jit(solution)/shard_map/ppermute | solution.py:443
  26.8 1.3 %collective-permute-start.4 = (bf16[256,128]{1,0:T(8,128)(2,1)S(1)}, bf16[256,128]{1,0:T(8,128)(2,1)S(1)}, u32[]{:S(2)}, u32[]{:S(2)}) collective-permute-start(bf16[256,128]{1,0:T(8,128)(2,1)S(1)} %collective-permute-done.3.refs_2_), channel_id=1, source_target_pairs={{1,0},{0,1},{3,2},{2,3},{5,4},{4,5},{7,6},{6,7},{9,8},{8,9},{11,10... | collective-permute-start | bytes 196616 | tf_op jit(solution)/shard_map/ppermute | solution.py:443

commit v16 on v15

--- a/solution.py
+++ b/solution.py
@@ -52,50 +52,42 @@
     return lax.bitwise_and(index, size - 1)
 
 
-def repeat_kernel(weight_ref, out_ref):
-    rep = LANES // weight_ref.shape[0]
-    out_ref[...] = jnp.concatenate([weight_ref[...]] * rep, axis=0).T
-
-
-def repeat_weight(weight):
-    return pl.pallas_call(
-        repeat_kernel,
-        out_shape=jax.ShapeDtypeStruct((weight.shape[1], LANES), BF16),
-        in_specs=[vmem()],
-        out_specs=vmem(),
-        compiler_params=pltpu.CompilerParams(vmem_limit_bytes=2 << 20),
-        cost_estimate=pl.CostEstimate(flops=1 << 30, bytes_accessed=1 << 17, transcendentals=0),
-    )(weight)
-
-
-def factor_kernel(masked, hidden, x_ref, weight_ref, *refs):
+def factor_kernel(masked, x_any, weight_any, *refs):
     mask_ref = refs[0] if masked else None
-    z_refs, y_scr = refs[masked:-1], refs[-1]
+    z_refs, (x_scr, y_scr, weight_scr, sems) = refs[masked:-4], refs[-4:]
     each, seqs, _ = z_refs[0].shape
     groups = each * len(z_refs)
-    _, rows, channels = x_ref.shape
+    steps, step, rows, channels = x_scr.shape
+    hidden = weight_scr.shape[0]
     rep = rows // groups
     width = rows * hidden
-    step = y_scr.shape[1] // rows
-    w = jnp.concatenate([weight_ref[...], jnp.ones((channels, LANES), BF16)], axis=1)
-    ones = jnp.ones((LANES, LANES), BF16)
-    sums = dot(jnp.ones((8, channels), BF16), weight_ref[...])[:1]
+    fetches = [pltpu.make_async_copy(weight_any, weight_scr, sems.at[steps])]
+    for turn in range(steps):
+        part = x_any.at[pl.ds(turn * step, step)]
+        fetches.append(pltpu.make_async_copy(part, x_scr.at[turn], sems.at[turn]))
+    for fetch in fetches:
+        fetch.start()
+    ones = jnp.full((LANES, LANES), 1.0 / channels, BF16)
     block = over(iota((step, LANES), 1), hidden)
-    if mask_ref is not None:
+    if masked:
         residues = mask_ref.shape[0]
         column = lax.axis_index("dap") * rows + over(iota((residues, width), 1), hidden)
         lanes_of = (iota((residues, width), 0) == column).astype(BF16)
         live = dot_tn(mask_ref[...].astype(BF16), lanes_of)
-    for turn in range(seqs // step):
-        x = x_ref[turn * step : (turn + 1) * step].reshape(step * rows, channels)
+    fetches[0].wait()
+    weight = jnp.concatenate([weight_scr[...]] * rep, axis=0).T
+    w = jnp.concatenate([weight, jnp.full((channels, LANES), 1.0 / channels, BF16)], axis=1)
+    sums = dot(jnp.ones((8, channels), BF16), weight)[:1]
+    for turn in range(steps):
+        fetches[turn + 1].wait()
+        x = x_scr[turn].reshape(step * rows, channels)
         y = dot(x, w)
-        mean = y[:, LANES:] * (1.0 / channels)
+        mean = y[:, LANES:]
         square = jnp.zeros_like(mean)
         for half in range(channels // LANES):
             centered = x[:, half * LANES : (half + 1) * LANES].astype(F32) - mean
             square = square + centered * centered
-        spread = dot(square.astype(BF16), ones)
-        scale = lax.rsqrt(spread * (1.0 / channels) + EPSILON)
+        scale = lax.rsqrt(dot(square.astype(BF16), ones) + EPSILON)
         y_scr[turn] = (y[:, :LANES] - mean * sums) * scale
         here = slice(turn * step, (turn + 1) * step)
         for group in range(groups):
@@ -103,23 +95,30 @@
             for k in range(1, rep):
                 next_z = y_scr[turn, pl.ds(group * rep + k, step, stride=rows), :]
                 z = jnp.where(block == k, next_z, z)
-            if mask_ref is not None:
+            if masked:
                 z = z * live[here, group * LANES : (group + 1) * LANES]
             z_refs[group // each][group % each, here, :] = z.astype(BF16)
 
 
-def factor(alignment, weight, hidden, parts, mask=None):
+def factor(alignment, weight, parts, mask=None):
     seqs, rows, channels = alignment.shape
-    step = seqs // 2
+    hidden = weight.shape[0]
+    steps = 4
     operands = (alignment, weight) if mask is None else (alignment, weight, mask)
+    away = pl.BlockSpec(memory_space=pl.ANY)
     shape = jax.ShapeDtypeStruct((rows * hidden // LANES // parts, seqs, LANES), BF16)
     return pl.pallas_call(
-        functools.partial(factor_kernel, mask is not None, hidden),
+        functools.partial(factor_kernel, mask is not None),
         out_shape=(shape,) * parts,
-        in_specs=[vmem()] * len(operands),
+        in_specs=[away, away, vmem()][: len(operands)],
         out_specs=[vmem()] * parts,
-        scratch_shapes=[pltpu.VMEM((seqs // step, step * rows, LANES), F32)],
-        compiler_params=pltpu.CompilerParams(vmem_limit_bytes=24 << 20),
+        scratch_shapes=[
+            pltpu.VMEM((steps, seqs // steps, rows, channels), BF16),
+            pltpu.VMEM((steps, seqs // steps * rows, LANES), F32),
+            pltpu.VMEM(weight.shape, BF16),
+            pltpu.SemaphoreType.DMA((steps + 1,)),
+        ],
+        compiler_params=pltpu.CompilerParams(vmem_limit_bytes=119 << 19),
         cost_estimate=pl.CostEstimate(
             flops=2 * seqs * rows * channels * 512, bytes_accessed=seqs << 14, transcendentals=0
         ),
@@ -447,7 +446,7 @@
 
     hidden = outer_left.shape[1]
     mask = alignment_mask.T
-    zr = factor(alignment, repeat_weight(outer_right.T), hidden, PARTS)
+    zr = factor(alignment, outer_right.T, PARTS)
     zrs = [
         fetch(
             zr[part],
@@ -458,7 +457,7 @@
         for turn in range(ratio)
         for part in range(PARTS)
     ]
-    (zl,) = factor(alignment, repeat_weight(outer_left.T), hidden, 1, mask)
+    (zl,) = factor(alignment, outer_left.T, 1, mask)
     zlt, base, inverse, live, proj, seen = prepare(
         zl, mask, pair_input, residue_mask, chain_index, relative_table, outer_proj
     )

time: 33.3 us -> 34 us (1.021)
  the two profiles are of different devices: /device:TPU:1 before, /device:TPU:3 now
where the time goes in v16:
time: 34 us; the launch traced here: 33.6 us
  Pallas kernels  14.2 us (42%)
  starting transfers between devices  11.6 us (34%)
  waiting for transfers between devices  6.59 us (19%)
  local copies, waits for them, and re-layouts  1.02 us (3%)
    ppermute x7, starting transfers between devices, fetch(): return lax.ppermute(values, ('dap', 'sub'), perm)  11.6 us
    pallas_call x2, Pallas kernels, factor(): pl.pallas_call(functools.partial(factor_kernel, mask is not None), out_sh...  9.35 us
    ppermute x7, waiting for transfers between devices, fetch(): return lax.ppermute(values, ('dap', 'sub'), perm)  6.59 us
    pallas_call x1, Pallas kernels, triangle_update(): pl.pallas_call(functools.partial(last_kernel, late, twos, ratio, cols), o...  1.87 us
    pallas_call x1, Pallas kernels, pair_update(): pl.pallas_call(functools.partial(pair_kernel, ratio, hidden), out_shape=(...  1.6 us
    unnamed x26, local copies, waits for them, and re-layouts  1.01 us
    pallas_call x1, Pallas kernels, triangle_update(): pl.pallas_call(functools.partial(first_kernel, early, twos, ratio, cols),...  0.73 us
  transfers between devices with their start and end apart: 7, of which 4 were waited for; matrix products, arithmetic and copies ran while one was open for 0% of the time, Pallas kernels for 19%

profile of v16, /device:TPU:3, one launch (start us, length us, event | category | flops | bytes accessed | tf_op | source)
XLA Modules:
  0.0 33.6 jit_solution(17869586471339960098)
XLA Ops:
  0.0 4.2 %shard_map.147 = (bf16[2,256,128]{2,1,0:T(8,128)(2,1)}, bf16[2,256,128]{2,1,0:T(8,128)(2,1)}) custom-call(bf16[256,16,256]{2,1,0:T(8,128)(2,1)} %x_any.3, bf16[32,256]{1,0:T(8,128)(2,1)} %bitcast.9), custom_call_target="tpu_custom_call" | custom-call | flops 1073741824 | bytes 4194304 | tf_op jit(solution)/shard_map/pallas_call | solution.py:110
  4.2 0.0 copy-start
  4.2 0.0 copy-start.4
  4.2 0.0 copy-start.5
  4.3 0.0 copy-start.10
  4.3 0.0 copy-start.11
  4.3 0.0 copy-start.12
  4.3 4.9 %collective-permute-start = (bf16[2,256,128]{2,1,0:T(8,128)(2,1)}, bf16[2,256,128]{2,1,0:T(8,128)(2,1)S(1)}, u32[]{:S(2)}, u32[]{:S(2)}) collective-permute-start(bf16[2,256,128]{2,1,0:T(8,128)(2,1)} %get-tuple-element.19), channel_id=1, source_target_pairs={{0,0},{6,1},{8,2},{14,3},{2,4},{5,5},{11,6},{12,7},{3,8},{4,9},{10... | collective-permute-start | bytes 393224 | tf_op jit(solution)/shard_map/ppermute | solution.py:442
  9.2 1.8 %collective-permute-start.1 = (bf16[2,256,128]{2,1,0:T(8,128)(2,1)}, bf16[2,256,128]{2,1,0:T(8,128)(2,1)S(1)}, u32[]{:S(2)}, u32[]{:S(2)}) collective-permute-start(bf16[2,256,128]{2,1,0:T(8,128)(2,1)} %get-tuple-element.20), channel_id=1, source_target_pairs={{2,0},{4,1},{10,2},{12,3},{0,4},{7,5},{9,6},{14,7},{1,8},{6,9},{8,... | collective-permute-start | bytes 393224 | tf_op jit(solution)/shard_map/ppermute | solution.py:442
  11.0 0.0 copy-start.6
  11.0 0.0 copy-start.7
  11.0 0.0 copy-start.8
  11.0 0.0 copy-start.2
  11.0 0.0 copy-start.3
  11.0 0.0 copy-start.9
  11.0 5.1 %shard_map.145.zl_ref = bf16[4,256,128]{2,1,0:T(8,128)(2,1)} custom-call(bf16[256,16,256]{2,1,0:T(8,128)(2,1)} %x_any.3, bf16[32,256]{1,0:T(8,128)(2,1)} %bitcast.10, s32[64,256]{1,0:T(8,128)} %bitcast.5), custom_call_target="tpu_custom_call" | custom-call | flops 1073741824 | bytes 4194304 | tf_op jit(solution)/shard_map/pallas_call | solution.py:110
  16.1 0.0 copy-done
  16.2 0.0 copy-done.4
  16.2 0.0 copy-done.5
  16.2 0.0 copy-done.10
  16.2 0.0 copy-done.11
  16.2 0.0 copy-done.12
  16.2 0.0 copy-start.1
  16.2 0.9 %copy-done.1 = bf16[4,256,128]{2,1,0:T(8,128)(2,1)S(1)} copy-done((bf16[4,256,128]{2,1,0:T(8,128)(2,1)S(1)}, bf16[4,256,128]{2,1,0:T(8,128)(2,1)}, u32[]{:S(2)}) %copy-start.1) | copy-done | bytes 262168
  17.2 0.6 %shard_map.146 = (bf16[2,512,128]{2,1,0:T(8,128)(2,1)S(1)}, f32[256,128]{1,0:T(8,128)S(1)}, f32[256,128]{1,0:T(8,128)S(1)}, f32[256,128]{1,0:T(8,128)S(1)}, bf16...) custom-call(bf16[4,256,128]{2,1,0:T(8,128)(2,1)S(1)} %copy-done.1, s32[64,256]{1,0:T(8,128)S(1)} %bitcast.6, ...), custom_call_target="tpu_custom_call" | custom-call | flops 134217728 | bytes 2097152 | tf_op jit(solution)/shard_map/pallas_call | solution.py:183
  17.8 0.0 collective-permute-done.refs_0_
  17.8 0.0 collective-permute-done.1.refs_1_
  17.8 0.0 copy-done.6
  17.8 0.0 copy-done.7
  17.8 1.6 %shard_map.148 = (bf16[2,256,128]{2,1,0:T(8,128)(2,1)S(1)}, bf16[256,128]{1,0:T(8,128)(2,1)S(1)}, bf16[256,128]{1,0:T(8,128)(2,1)S(1)}) custom-call(bf16[2,512,128]{2,1,0:T(8,128)(2,1)S(1)} %get-tuple-element.18.zlt_ref, bf16[2,256,128]{2,1,0:T(8,128)(2,1)S(1)} %collective-permute-done.refs_0_, bf16[2,256,128]{2,1,0:T(8,128)(2,1)S(1)} %collective-permute-done.1.refs_1_, ...), custom_call_target="tpu_custom_call" | custom-call | flops 268435456 | bytes 2097152 | tf_op jit(solution)/shard_map/pallas_call | solution.py:269
  19.4 0.1 collective-permute-start.2
  19.5 0.1 collective-permute-start.3
  19.6 1.2 %collective-permute-done.2.refs_1_ = bf16[2,256,128]{2,1,0:T(8,128)(2,1)S(1)} collective-permute-done((bf16[2,256,128]{2,1,0:T(8,128)(2,1)S(1)}, bf16[2,256,128]{2,1,0:T(8,128)(2,1)S(1)}, u32[]{:S(2)}, u32[]{:S(2)}) %collective-permute-start.2) | collective-permute-done | bytes 131104 | tf_op jit(solution)/shard_map/ppermute | solution.py:442
  20.9 2.8 %collective-permute-start.6 = (bf16[2,256,128]{2,1,0:T(8,128)(2,1)S(1)}, bf16[2,256,128]{2,1,0:T(8,128)(2,1)S(1)}, u32[]{:S(2)}, u32[]{:S(2)}) collective-permute-start(bf16[2,256,128]{2,1,0:T(8,128)(2,1)S(1)} %pad_maximum_fusion), channel_id=1, source_target_pairs={{2,0},{4,1},{10,2},{12,3},{0,4},{7,5},{9,6},{14,7},{1,8},{6,9},{8,... | collective-permute-start | bytes 393224 | tf_op jit(solution)/shard_map/ppermute | solution.py:442
  23.7 1.9 %collective-permute-start.5 = (bf16[2,256,128]{2,1,0:T(8,128)(2,1)S(1)}, bf16[2,256,128]{2,1,0:T(8,128)(2,1)S(1)}, u32[]{:S(2)}, u32[]{:S(2)}) collective-permute-start(bf16[2,256,128]{2,1,0:T(8,128)(2,1)S(1)} %pad_maximum_fusion), channel_id=1, source_target_pairs={{0,0},{6,1},{8,2},{14,3},{2,4},{5,5},{11,6},{12,7},{3,8},{4,9},{10... | collective-permute-start | bytes 393224 | tf_op jit(solution)/shard_map/ppermute | solution.py:442
  25.6 0.0 collective-permute-done.3.refs_2_
  25.6 0.1 collective-permute-start.4
  25.7 1.2 %collective-permute-done.4.refs_3_ = bf16[256,128]{1,0:T(8,128)(2,1)S(1)} collective-permute-done((bf16[256,128]{1,0:T(8,128)(2,1)S(1)}, bf16[256,128]{1,0:T(8,128)(2,1)S(1)}, u32[]{:S(2)}, u32[]{:S(2)}) %collective-permute-start.4) | collective-permute-done | bytes 65568 | tf_op jit(solution)/shard_map/ppermute | solution.py:442
  26.9 1.1 %collective-permute-done.6.refs_4_ = bf16[2,256,128]{2,1,0:T(8,128)(2,1)S(1)} collective-permute-done((bf16[2,256,128]{2,1,0:T(8,128)(2,1)S(1)}, bf16[2,256,128]{2,1,0:T(8,128)(2,1)S(1)}, u32[]{:S(2)}, u32[]{:S(2)}) %collective-permute-start.6) | collective-permute-done | bytes 131104 | tf_op jit(solution)/shard_map/ppermute | solution.py:442
  28.0 0.0 copy-done.8
  28.0 0.7 %shard_map.149 = (f32[256,128]{1,0:T(8,128)S(1)}, f32[256,128]{1,0:T(8,128)S(1)}) custom-call(bf16[2,256,128]{2,1,0:T(8,128)(2,1)S(1)} %get-tuple-element.26.refs_0_, bf16[2,256,128]{2,1,0:T(8,128)(2,1)S(1)} %collective-permute-done.2.refs_1_, bf16[256,128]{1,0:T(8,128)(2,1)S(1)} %collective-permute-done.3.refs_2_, ...), custom_call_target="tpu_custom_call" | custom-call | flops 67108864 | bytes 1048576 | tf_op jit(solution)/shard_map/pallas_call | solution.py:391
  28.8 3.0 %collective-permute-done.5.refs_4_ = bf16[2,256,128]{2,1,0:T(8,128)(2,1)S(1)} collective-permute-done((bf16[2,256,128]{2,1,0:T(8,128)(2,1)S(1)}, bf16[2,256,128]{2,1,0:T(8,128)(2,1)S(1)}, u32[]{:S(2)}, u32[]{:S(2)}) %collective-permute-start.5) | collective-permute-done | bytes 131104 | tf_op jit(solution)/shard_map/ppermute | solution.py:442
  31.8 0.0 copy-done.2
  31.8 0.0 copy-done.3
  31.8 0.0 copy-done.9
  31.8 1.9 %shard_map.150 = bf16[16,16,128]{2,1,0:T(8,128)(2,1)} custom-call(bf16[2,256,128]{2,1,0:T(8,128)(2,1)S(1)} %get-tuple-element.26.refs_0_, bf16[2,256,128]{2,1,0:T(8,128)(2,1)S(1)} %collective-permute-done.2.refs_1_, bf16[256,128]{1,0:T(8,128)(2,1)S(1)} %collective-permute-done.3.refs_2_, bf16[256,128]{1,0:T(8,128)(2,1)S(1)} %collective-permute-done.4.refs_3_, ...), custom_call_target="tpu_custom_call" | custom-call | flops 134217728 | bytes 2097152 | tf_op jit(solution)/shard_map/pallas_call | solution.py:402
  (3 shorter events, 0.0 us)
Async XLA Ops:
  4.2 11.9 %copy-start = (f32[32,32,128]{2,1,0:T(8,128)S(1)}, f32[32,32,128]{2,1,0:T(8,128)}, u32[]{:S(2)}) copy-start(f32[32,32,128]{2,1,0:T(8,128)} %proj_ref.1) | copy-start | bytes 1572868
  4.2 11.9 %copy-start.4 = (s32[256,64]{0,1:T(8,128)S(1)}, s32[256,64]{0,1:T(8,128)}, u32[]{:S(2)}) copy-start(s32[256,64]{0,1:T(8,128)} %param.16) | copy-start | bytes 196612
  4.2 11.9 %copy-start.5 = (bf16[16,16,128]{2,1,0:T(8,128)(2,1)S(1)}, bf16[16,16,128]{2,1,0:T(8,128)(2,1)}, u32[]{:S(2)}) copy-start(bf16[16,16,128]{2,1,0:T(8,128)(2,1)} %pair_ref.1) | copy-start | bytes 196612
  4.3 11.9 %copy-start.10 = (bf16[66,128]{1,0:T(8,128)(2,1)S(1)}, bf16[66,128]{1,0:T(8,128)(2,1)}, u32[]{:S(2)}) copy-start(bf16[66,128]{1,0:T(8,128)(2,1)} %table_ref.1) | copy-start | bytes 50692
  4.3 11.9 %copy-start.11 = (s32[64]{0:T(128)S(1)}, s32[64]{0:T(128)}, u32[]{:S(2)}) copy-start(s32[64]{0:T(128)} %param.18) | copy-start | bytes 772
  4.3 11.9 %copy-start.12 = (s32[64]{0:T(128)S(1)}, s32[64]{0:T(128)}, u32[]{:S(2)}) copy-start(s32[64]{0:T(128)} %param.19) | copy-start | bytes 772
  4.3 13.5 %collective-permute-start = (bf16[2,256,128]{2,1,0:T(8,128)(2,1)}, bf16[2,256,128]{2,1,0:T(8,128)(2,1)S(1)}, u32[]{:S(2)}, u32[]{:S(2)}) collective-permute-start(bf16[2,256,128]{2,1,0:T(8,128)(2,1)} %get-tuple-element.19), channel_id=1, source_target_pairs={{0,0},{6,1},{8,2},{14,3},{2,4},{5,5},{11,6},{12,7},{3,8},{4,9},{10... | collective-permute-start | bytes 393224 | tf_op jit(solution)/shard_map/ppermute | solution.py:442
  9.2 8.6 %collective-permute-start.1 = (bf16[2,256,128]{2,1,0:T(8,128)(2,1)}, bf16[2,256,128]{2,1,0:T(8,128)(2,1)S(1)}, u32[]{:S(2)}, u32[]{:S(2)}) collective-permute-start(bf16[2,256,128]{2,1,0:T(8,128)(2,1)} %get-tuple-element.20), channel_id=1, source_target_pairs={{2,0},{4,1},{10,2},{12,3},{0,4},{7,5},{9,6},{14,7},{1,8},{6,9},{8,... | collective-permute-start | bytes 393224 | tf_op jit(solution)/shard_map/ppermute | solution.py:442
  11.0 6.9 %copy-start.6 = (bf16[128,256]{1,0:T(8,128)(2,1)S(1)}, bf16[128,256]{1,0:T(8,128)(2,1)}, u32[]{:S(2)}) copy-start(bf16[128,256]{1,0:T(8,128)(2,1)} %refs_7_.1) | copy-start | bytes 196612
  11.0 6.9 %copy-start.7 = (bf16[128,256]{1,0:T(8,128)(2,1)S(1)}, bf16[128,256]{1,0:T(8,128)(2,1)}, u32[]{:S(2)}) copy-start(bf16[128,256]{1,0:T(8,128)(2,1)} %refs_8_.2) | copy-start | bytes 196612
  11.0 17.1 %copy-start.8 = (bf16[128,128]{1,0:T(8,128)(2,1)S(1)}, bf16[128,128]{1,0:T(8,128)(2,1)}, u32[]{:S(2)}) copy-start(bf16[128,128]{1,0:T(8,128)(2,1)} %refs_6_.1) | copy-start | bytes 98308
  11.0 20.8 %copy-start.2 = (bf16[128,512]{1,0:T(8,128)(2,1)S(1)}, bf16[128,512]{1,0:T(8,128)(2,1)}, u32[]{:S(2)}) copy-start(bf16[128,512]{1,0:T(8,128)(2,1)} %refs_9_.1) | copy-start | bytes 393220
  11.0 20.8 %copy-start.3 = (bf16[512,128]{1,0:T(8,128)(2,1)S(1)}, bf16[512,128]{1,0:T(8,128)(2,1)}, u32[]{:S(2)}) copy-start(bf16[512,128]{1,0:T(8,128)(2,1)} %refs_10_.1) | copy-start | bytes 393220
  11.0 20.8 %copy-start.9 = (bf16[128,128]{1,0:T(8,128)(2,1)S(1)}, bf16[128,128]{1,0:T(8,128)(2,1)}, u32[]{:S(2)}) copy-start(bf16[128,128]{1,0:T(8,128)(2,1)} %refs_8_.3) | copy-start | bytes 98308
  16.2 1.0 %copy-start.1 = (bf16[4,256,128]{2,1,0:T(8,128)(2,1)S(1)}, bf16[4,256,128]{2,1,0:T(8,128)(2,1)}, u32[]{:S(2)}) copy-start(bf16[4,256,128]{2,1,0:T(8,128)(2,1)} %shard_map.145.zl_ref) | copy-start | bytes 786436
  19.4 1.4 %collective-permute-start.2 = (bf16[2,256,128]{2,1,0:T(8,128)(2,1)S(1)}, bf16[2,256,128]{2,1,0:T(8,128)(2,1)S(1)}, u32[]{:S(2)}, u32[]{:S(2)}) collective-permute-start(bf16[2,256,128]{2,1,0:T(8,128)(2,1)S(1)} %get-tuple-element.26.refs_0_), channel_id=1, source_target_pairs={{1,0},{0,1},{3,2},{2,3},{5,4},{4,5},{7,6},{6,7},{9,8},{8,9},{11,10... | collective-permute-start | bytes 393224 | tf_op jit(solution)/shard_map/ppermute | solution.py:442
  19.5 6.0 %collective-permute-start.3 = (bf16[256,128]{1,0:T(8,128)(2,1)S(1)}, bf16[256,128]{1,0:T(8,128)(2,1)S(1)}, u32[]{:S(2)}, u32[]{:S(2)}) collective-permute-start(bf16[256,128]{1,0:T(8,128)(2,1)S(1)} %get-tuple-element.27), channel_id=1, source_target_pairs={{2,0},{3,1},{0,2},{1,3},{6,4},{7,5},{4,6},{5,7},{10,8},{11,9},{8,1... | collective-permute-start | bytes 196616 | tf_op jit(solution)/shard_map/ppermute | solution.py:442
  20.9 7.1 %collective-permute-start.6 = (bf16[2,256,128]{2,1,0:T(8,128)(2,1)S(1)}, bf16[2,256,128]{2,1,0:T(8,128)(2,1)S(1)}, u32[]{:S(2)}, u32[]{:S(2)}) collective-permute-start(bf16[2,256,128]{2,1,0:T(8,128)(2,1)S(1)} %pad_maximum_fusion), channel_id=1, source_target_pairs={{2,0},{4,1},{10,2},{12,3},{0,4},{7,5},{9,6},{14,7},{1,8},{6,9},{8,... | collective-permute-start | bytes 393224 | tf_op jit(solution)/shard_map/ppermute | solution.py:442
  23.7 8.1 %collective-permute-start.5 = (bf16[2,256,128]{2,1,0:T(8,128)(2,1)S(1)}, bf16[2,256,128]{2,1,0:T(8,128)(2,1)S(1)}, u32[]{:S(2)}, u32[]{:S(2)}) collective-permute-start(bf16[2,256,128]{2,1,0:T(8,128)(2,1)S(1)} %pad_maximum_fusion), channel_id=1, source_target_pairs={{0,0},{6,1},{8,2},{14,3},{2,4},{5,5},{11,6},{12,7},{3,8},{4,9},{10... | collective-permute-start | bytes 393224 | tf_op jit(solution)/shard_map/ppermute | solution.py:442
  25.6 1.3 %collective-permute-start.4 = (bf16[256,128]{1,0:T(8,128)(2,1)S(1)}, bf16[256,128]{1,0:T(8,128)(2,1)S(1)}, u32[]{:S(2)}, u32[]{:S(2)}) collective-permute-start(bf16[256,128]{1,0:T(8,128)(2,1)S(1)} %collective-permute-done.3.refs_2_), channel_id=1, source_target_pairs={{1,0},{0,1},{3,2},{2,3},{5,4},{4,5},{7,6},{6,7},{9,8},{8,9},{11,10... | collective-permute-start | bytes 196616 | tf_op jit(solution)/shard_map/ppermute | solution.py:442

commit v17 on v15

--- a/solution.py
+++ b/solution.py
@@ -77,8 +77,8 @@
     rep = rows // groups
     width = rows * hidden
     step = y_scr.shape[1] // rows
-    w = jnp.concatenate([weight_ref[...], jnp.ones((channels, LANES), BF16)], axis=1)
-    ones = jnp.ones((LANES, LANES), BF16)
+    share = jnp.full((channels, LANES), 1.0 / channels, BF16)
+    w = jnp.concatenate([weight_ref[...], share], axis=1)
     sums = dot(jnp.ones((8, channels), BF16), weight_ref[...])[:1]
     block = over(iota((step, LANES), 1), hidden)
     if mask_ref is not None:
@@ -89,13 +89,12 @@
     for turn in range(seqs // step):
         x = x_ref[turn * step : (turn + 1) * step].reshape(step * rows, channels)
         y = dot(x, w)
-        mean = y[:, LANES:] * (1.0 / channels)
+        mean = y[:, LANES:]
         square = jnp.zeros_like(mean)
         for half in range(channels // LANES):
             centered = x[:, half * LANES : (half + 1) * LANES].astype(F32) - mean
             square = square + centered * centered
-        spread = dot(square.astype(BF16), ones)
-        scale = lax.rsqrt(spread * (1.0 / channels) + EPSILON)
+        scale = lax.rsqrt(dot(square.astype(BF16), share[:LANES]) + EPSILON)
         y_scr[turn] = (y[:, :LANES] - mean * sums) * scale
         here = slice(turn * step, (turn + 1) * step)
         for group in range(groups):
@@ -203,8 +202,8 @@
 
 def pair_kernel(ratio, hidden, zlt_ref, *refs):
     zr_refs, refs = refs[: ratio * PARTS], refs[ratio * PARTS :]
-    (seen_ref, base_ref, inverse_ref, live_ref, proj_ref, tl_ref, tr_ref,
-     both_ref, left_ref, one_ref, outer_scr, flat_scr, one_scr) = refs
+    (seen_ref, base_ref, inverse_ref, live_ref, proj_ref, weight_ref,
+     right_ref, one_ref, outer_scr, flat_scr) = refs
     pairs, channels = base_ref.shape
     rows = zlt_ref.shape[1] // hidden
     rep = LANES // hidden
@@ -250,38 +249,63 @@
     flat = jnp.concatenate([flat_scr[quad] for quad in range(flat_scr.shape[0])], axis=1)
     outer_mean = dot(flat, proj_ref[...]) * inverse_ref[...]
     one = (base_ref[...] + outer_mean).astype(BF16).astype(F32)
-    one_scr[...] = one
-    norm = layer_norm(one).astype(BF16)
-    for side, weight in enumerate((tl_ref, tr_ref)):
-        both = dot(norm, weight[...])
-        factor = jax.nn.sigmoid(both[:, :channels]) * both[:, channels:] * live_ref[...]
-        both_ref[side] = factor.astype(BF16)
-        if side == 0:
-            left_ref[...] = factor.astype(BF16)
-    cols = pairs // rows
+    one_ref[...] = one
+    right_ref[...] = gated(layer_norm(one).astype(BF16), weight_ref, live_ref)
+
+
+def gated(norm, weight_ref, live_ref):
+    both = dot(norm, weight_ref[...])
+    channels = both.shape[1] // 2
+    return (jax.nn.sigmoid(both[:, :channels]) * both[:, channels:] * live_ref[...]).astype(BF16)
+
+
+def side_kernel(one_ref, live_ref, left_weight, gate_weight, left_ref, gate_ref, pair_ref, norm_scr):
+    pairs, _ = one_ref.shape
+    rows, cols = pair_ref.shape[:2]
+    norm = layer_norm(one_ref[...]).astype(BF16)
+    left_ref[...] = gated(norm, left_weight, live_ref)
+    norm_scr[...] = jax.nn.sigmoid(dot(norm, gate_weight[...]))
     for row in range(rows):
-        one_ref[row * cols : (row + 1) * cols, :] = one_scr[pl.ds(row, cols, stride=rows), :].astype(BF16)
-
-
-def pair_update(hidden, zlt, zrs, seen, base, inverse, live, proj, triangle_left, triangle_right):
+        pair_ref[row] = one_ref[pl.ds(row, cols, stride=rows), :]
+        gate_ref[row] = norm_scr[pl.ds(row, cols, stride=rows), :]
+
+
+def side_update(one, live, left_weight, gate_weight, rows):
+    pairs, channels = one.shape
+    by_row = jax.ShapeDtypeStruct((rows, pairs // rows, channels), F32)
+    return pl.pallas_call(
+        side_kernel,
+        out_shape=(jax.ShapeDtypeStruct((pairs, channels), BF16), by_row, by_row),
+        in_specs=[vmem()] * 4,
+        out_specs=[vmem()] * 3,
+        scratch_shapes=[pltpu.VMEM((pairs, channels), F32)],
+        compiler_params=pltpu.CompilerParams(vmem_limit_bytes=8 << 20),
+        cost_estimate=pl.CostEstimate(
+            flops=2 * pairs * channels * 384, bytes_accessed=1 << 19, transcendentals=pairs * 256
+        ),
+    )(one, live, left_weight, gate_weight)
+
+
+def pair_update(hidden, zlt, zrs, seen, base, inverse, live, proj, weight):
     pairs, channels = base.shape
     ratio = len(zrs) // PARTS
-    shape = jax.ShapeDtypeStruct((pairs, channels), BF16)
     return pl.pallas_call(
         functools.partial(pair_kernel, ratio, hidden),
-        out_shape=(jax.ShapeDtypeStruct((2, pairs, channels), BF16), shape, shape),
-        in_specs=[vmem()] * (8 + len(zrs)),
-        out_specs=[vmem()] * 3,
+        out_shape=(
+            jax.ShapeDtypeStruct((pairs, channels), BF16),
+            jax.ShapeDtypeStruct((pairs, channels), F32),
+        ),
+        in_specs=[vmem()] * (7 + len(zrs)),
+        out_specs=[vmem()] * 2,
         scratch_shapes=[
             pltpu.VMEM((zrs[0].shape[0] * PARTS, zlt.shape[1], LANES), F32),
             pltpu.VMEM((proj.shape[0] // LANES, pairs, LANES), BF16),
-            pltpu.VMEM((pairs, channels), F32),
         ],
         compiler_params=pltpu.CompilerParams(vmem_limit_bytes=32 << 20),
         cost_estimate=pl.CostEstimate(
             flops=2 * pairs * 1024 * 512, bytes_accessed=2 << 20, transcendentals=pairs * 256
         ),
-    )(zlt, *zrs, seen, base, inverse, live, proj, triangle_left, triangle_right)
+    )(zlt, *zrs, seen, base, inverse, live, proj, weight)
 
 
 def other(sub):
@@ -313,13 +337,11 @@
     rows = left_scr.shape[1] // cols
     here, there = lax.axis_index("dap"), lax.axis_index("sub")
     first_sub = sender_index(here, there, subs, ratio)
-    own, near, across, beyond = lefts
-    left_scr[there] = own[0].astype(F32)
-    left_scr[other(there)] = near[0].astype(F32)
-    for step in range(1, subs // 2):
+    own, near = lefts
+    for step in range(subs // 2):
         sub = lax.rem(there + 2 * step, subs)
-        left_scr[sub] = across[step - 1][...].astype(F32)
-        left_scr[other(sub)] = beyond[step - 1][...].astype(F32)
+        left_scr[sub] = own[step].astype(F32)
+        left_scr[other(sub)] = near[step].astype(F32)
     for turn in range(ratio):
         block = lax.rem(here + turn, ratio) if ratio > 1 else 0
         places = [i * cols + block * rows for i in range(rows)]
@@ -347,38 +369,28 @@
             sums[pl.ds(place, rows), :] = total
 
 
-def split_lefts(refs, twos):
-    count = twos - 1
-    lefts = (refs[0], refs[1], refs[2 : 2 + count], refs[2 + count : 2 + 2 * count])
-    return lefts, refs[2 + 2 * count :]
-
-
-def first_kernel(steps, twos, ratio, cols, *refs):
-    lefts, refs = split_lefts(refs, twos)
-    rights, refs = refs[: ratio * len(steps)], refs[ratio * len(steps) :]
-    one_ref, weight_ref, sums_ref, gate_ref, left_scr = refs
-    add_terms(sums_ref, None, lefts, rights, steps, ratio, cols, left_scr)
-    norm = layer_norm(one_ref[...].astype(F32)).astype(BF16)
-    gate_ref[...] = jax.nn.sigmoid(dot(norm, weight_ref[...]))
-
-
-def last_kernel(steps, twos, ratio, cols, *refs):
-    lefts, refs = split_lefts(refs, twos)
+def first_kernel(steps, ratio, cols, *refs):
+    lefts, (sums_ref, left_scr) = refs[:2], refs[-2:]
+    add_terms(sums_ref, None, lefts, refs[2:-2], steps, ratio, cols, left_scr)
+
+
+def last_kernel(steps, ratio, cols, *refs):
+    lefts, refs = refs[:2], refs[2:]
     rights, refs = refs[: ratio * len(steps)], refs[ratio * len(steps) :]
     (start_ref, one_ref, gate_ref, out_ref, up_ref, down_ref, result_ref, left_scr, sum_scr) = refs
     add_terms(sum_scr, start_ref, lefts, rights, steps, ratio, cols, left_scr)
-    one = one_ref[...].astype(F32)
+    one, gate = (ref[...].reshape(sum_scr.shape) for ref in (one_ref, gate_ref))
     hidden = layer_norm(sum_scr[...].astype(BF16).astype(F32)).astype(BF16)
-    two = (one + gate_ref[...] * dot(hidden, out_ref[...])).astype(BF16).astype(F32)
+    two = (one + gate * dot(hidden, out_ref[...])).astype(BF16).astype(F32)
     wide = jnp.maximum(dot(layer_norm(two).astype(BF16), up_ref[...]), 0.0).astype(BF16)
     result = (two + dot(wide, down_ref[...])).astype(BF16)
     result_ref[...] = result.reshape(result_ref.shape)
 
 
-def triangle_update(lefts, rights, one, cols, gate_weight, out, up, down):
-    pairs, channels = one.shape
-    rows = pairs // cols
-    twos = len(lefts) // 2
+def triangle_update(lefts, rights, one, gate, out, up, down):
+    rows, cols, channels = one.shape
+    pairs = rows * cols
+    twos = lefts[0].shape[0]
     subs = 2 * twos
     ratio = len(rights) // twos
     late, early = range(twos // 2), range(twos // 2, twos)
@@ -389,21 +401,21 @@
     def chosen(steps):
         return [rights[turn * twos + step] for turn in range(ratio) for step in steps]
 
-    sums, gate = pl.pallas_call(
-        functools.partial(first_kernel, early, twos, ratio, cols),
-        out_shape=(shape, shape),
-        in_specs=[vmem()] * (len(lefts) + ratio * len(early) + 2),
-        out_specs=[vmem()] * 2,
+    sums = pl.pallas_call(
+        functools.partial(first_kernel, early, ratio, cols),
+        out_shape=shape,
+        in_specs=[vmem()] * (2 + ratio * len(early)),
+        out_specs=vmem(),
         scratch_shapes=[left_scr],
         compiler_params=pltpu.CompilerParams(vmem_limit_bytes=limit),
         cost_estimate=pl.CostEstimate(
-            flops=2 * pairs * channels * 1024, bytes_accessed=1 << 20, transcendentals=pairs * 128
-        ),
-    )(*lefts, *chosen(early), one, gate_weight)
+            flops=2 * pairs * channels * 1024, bytes_accessed=1 << 20, transcendentals=0
+        ),
+    )(*lefts, *chosen(early))
     return pl.pallas_call(
-        functools.partial(last_kernel, late, twos, ratio, cols),
+        functools.partial(last_kernel, late, ratio, cols),
         out_shape=jax.ShapeDtypeStruct((rows, cols, channels), BF16),
-        in_specs=[vmem()] * (len(lefts) + ratio * len(late) + 6),
+        in_specs=[vmem()] * (2 + ratio * len(late) + 6),
         out_specs=vmem(),
         scratch_shapes=[left_scr, pltpu.VMEM((pairs, channels), F32)],
         compiler_params=pltpu.CompilerParams(vmem_limit_bytes=limit),
@@ -432,7 +444,6 @@
 ):
     daps, subs = lax.axis_size("dap"), lax.axis_size("sub")
     ratio = daps // subs
-    cols = pair_input.shape[1]
 
     def fetch(values, source):
         perm = []
@@ -462,15 +473,17 @@
     zlt, base, inverse, live, proj, seen = prepare(
         zl, mask, pair_input, residue_mask, chain_index, relative_table, outer_proj
     )
-    own, left, one = pair_update(
-        hidden, zlt, zrs, seen, base, inverse, live, proj, triangle_left, triangle_right
+    right, one = pair_update(
+        hidden, zlt, zrs, seen, base, inverse, live, proj, triangle_right
     )
-    near = fetch(own, lambda a, b: (a, other(b)))
+    near_right = fetch(right, lambda a, b: (a, other(b)))
+    left, gate, pair = side_update(one, live, triangle_left, triangle_gate, pair_input.shape[0])
     across = [
         fetch(left, lambda a, b, m=step: (a, (b + 2 * m) % subs)) for step in range(1, subs // 2)
     ]
-    beyond = [fetch(block, lambda a, b: (a, other(b))) for block in across]
-    right = jnp.stack([own[1], near[1]])
+    left_pair = jnp.stack([left, *across])
+    near_left = fetch(left_pair, lambda a, b: (a, other(b)))
+    right = jnp.stack([right, near_right])
     rights = [
         fetch(
             right,
@@ -482,14 +495,7 @@
         for step in range(subs // 2)
     ]
     return triangle_update(
-        [own, near, *across, *beyond],
-        rights,
-        one,
-        cols,
-        triangle_gate,
-        triangle_out,
-        transition_up,
-        transition_down,
+        [left_pair, near_left], rights, pair, gate, triangle_out, transition_up, transition_down
     )
 
 

time: 33.3 us -> 34.9 us (1.048)
  the two profiles are of different devices: /device:TPU:1 before, /device:TPU:6 now
where the time goes in v17:
time: 34.9 us; the launch traced here: 34.7 us
  waiting for transfers between devices  15.6 us (45%)
  Pallas kernels  8.97 us (26%)
  starting transfers between devices  8.15 us (23%)
  local copies, waits for them, and re-layouts  1.61 us (5%)
    ppermute x7, waiting for transfers between devices, fetch(): return lax.ppermute(values, ('dap', 'sub'), perm)  15.6 us
    ppermute x7, starting transfers between devices, fetch(): return lax.ppermute(values, ('dap', 'sub'), perm)  8.15 us
    pallas_call x2, Pallas kernels, factor(): pl.pallas_call(functools.partial(factor_kernel, mask is not None, hidden)...  3.95 us
    pallas_call x1, Pallas kernels, triangle_update(): pl.pallas_call(functools.partial(last_kernel, late, ratio, cols), out_sha...  1.87 us
    unnamed x30, local copies, waits for them, and re-layouts  1.61 us
    pallas_call x1, Pallas kernels, pair_update(): pl.pallas_call(functools.partial(pair_kernel, ratio, hidden), out_shape=(...  1.56 us
  transfers between devices with their start and end apart: 7, of which 5 were waited for; matrix products, arithmetic and copies ran while one was open for 0% of the time, Pallas kernels for 10%

profile of v17, /device:TPU:6, one launch (start us, length us, event | category | flops | bytes accessed | tf_op | source)
XLA Modules:
  0.0 34.7 jit_solution(12790422590361325794)
XLA Ops:
  0.0 0.0 copy-start.12
  0.0 0.0 copy-start.13
  0.0 0.9 %copy-done.13 = bf16[256,32]{0,1:T(8,128)(2,1)S(1)} copy-done((bf16[256,32]{0,1:T(8,128)(2,1)S(1)}, bf16[256,32]{0,1:T(8,128)(2,1)}, u32[]{:S(2)}) %copy-start.13) | copy-done | bytes 16408
  0.9 0.1 shard_map.148.weight_ref
  0.9 0.7 %copy-done.12 = bf16[256,16,256]{2,1,0:T(8,128)(2,1)S(1)} copy-done((bf16[256,16,256]{2,1,0:T(8,128)(2,1)S(1)}, bf16[256,16,256]{2,1,0:T(8,128)(2,1)}, u32[]{:S(2)}) %copy-start.12) | copy-done | bytes 2097176
  1.6 0.0 copy-start.14
  1.6 1.9 %shard_map.149 = (bf16[2,256,128]{2,1,0:T(8,128)(2,1)S(1)}, bf16[2,256,128]{2,1,0:T(8,128)(2,1)S(1)}) custom-call(bf16[256,16,256]{2,1,0:T(8,128)(2,1)S(1)} %copy-done.12, bf16[256,128]{1,0:T(8,128)(2,1)S(1)} %shard_map.148.weight_ref), custom_call_target="tpu_custom_call" | custom-call | flops 1073741824 | bytes 4194304 | tf_op jit(solution)/shard_map/pallas_call | solution.py:115
  3.5 0.0 copy-start.3
  3.5 3.6 %collective-permute-start = (bf16[2,256,128]{2,1,0:T(8,128)(2,1)S(1)}, bf16[2,256,128]{2,1,0:T(8,128)(2,1)S(1)}, u32[]{:S(2)}, u32[]{:S(2)}) collective-permute-start(bf16[2,256,128]{2,1,0:T(8,128)(2,1)S(1)} %get-tuple-element.19), channel_id=1, source_target_pairs={{0,0},{6,1},{8,2},{14,3},{2,4},{5,5},{11,6},{12,7},{3,8},{4,9},{10... | collective-permute-start | bytes 393224 | tf_op jit(solution)/shard_map/ppermute | solution.py:454
  7.1 0.1 collective-permute-start.1
  7.2 0.0 copy-done.14
  7.2 0.1 shard_map.145.weight_ref
  7.3 0.0 copy-start
  7.3 0.0 copy-start.4
  7.3 0.0 copy-start.9
  7.3 0.0 copy-start.10
  7.3 0.0 copy-start.11
  7.3 0.0 copy-done.3
  7.3 0.0 copy-start.5
  7.4 2.1 %shard_map.146.zl_ref = bf16[4,256,128]{2,1,0:T(8,128)(2,1)S(1)} custom-call(bf16[256,16,256]{2,1,0:T(8,128)(2,1)S(1)} %copy-done.12, bf16[256,128]{1,0:T(8,128)(2,1)S(1)} %shard_map.145.weight_ref, s32[64,256]{1,0:T(8,128)S(1)} %bitcast.9), custom_call_target="tpu_custom_call" | custom-call | flops 1073741824 | bytes 4194304 | tf_op jit(solution)/shard_map/pallas_call | solution.py:115
  9.4 0.0 copy-start.6
  9.4 0.0 copy-start.8
  9.4 0.0 copy-start.1
  9.5 0.0 copy-start.2
  9.5 0.0 copy-start.7
  9.5 0.0 copy-done
  9.5 0.0 copy-done.4
  9.5 0.0 copy-done.9
  9.5 0.0 copy-done.10
  9.5 0.0 copy-done.11
  9.5 0.6 %shard_map.147 = (bf16[2,512,128]{2,1,0:T(8,128)(2,1)S(1)}, f32[256,128]{1,0:T(8,128)S(1)}, f32[256,128]{1,0:T(8,128)S(1)}, f32[256,128]{1,0:T(8,128)S(1)}, bf16...) custom-call(bf16[4,256,128]{2,1,0:T(8,128)(2,1)S(1)} %shard_map.146.zl_ref, s32[64,256]{1,0:T(8,128)S(1)} %bitcast.10, ...), custom_call_target="tpu_custom_call" | custom-call | flops 134217728 | bytes 2097152 | tf_op jit(solution)/shard_map/pallas_call | solution.py:183
  10.2 5.8 %collective-permute-done.refs_0_ = bf16[2,256,128]{2,1,0:T(8,128)(2,1)S(1)} collective-permute-done((bf16[2,256,128]{2,1,0:T(8,128)(2,1)S(1)}, bf16[2,256,128]{2,1,0:T(8,128)(2,1)S(1)}, u32[]{:S(2)}, u32[]{:S(2)}) %collective-permute-start) | collective-permute-done | bytes 131104 | tf_op jit(solution)/shard_map/ppermute | solution.py:454
  16.0 0.0 collective-permute-done.1.refs_1_
  16.0 0.0 copy-done.5
  16.0 1.6 %shard_map.150 = (bf16[256,128]{1,0:T(8,128)(2,1)S(1)}, f32[256,128]{1,0:T(8,128)S(1)}) custom-call(bf16[2,512,128]{2,1,0:T(8,128)(2,1)S(1)} %get-tuple-element.18.zlt_ref, bf16[2,256,128]{2,1,0:T(8,128)(2,1)S(1)} %collective-permute-done.refs_0_, bf16[2,256,128]{2,1,0:T(8,128)(2,1)S(1)} %collective-permute-done.1.refs_1_, ...), custom_call_target="tpu_custom_call" | custom-call | flops 268435456 | bytes 2097152 | tf_op jit(solution)/shard_map/pallas_call | solution.py:292
  17.6 0.1 collective-permute-start.4
  17.7 0.0 copy-done.6
  17.7 0.0 copy-done.8
  17.7 0.4 %shard_map.151 = (bf16[256,128]{1,0:T(8,128)(2,1)S(1)}, f32[16,16,128]{2,1,0:T(8,128)S(1)}, f32[16,16,128]{2,1,0:T(8,128)S(1)}) custom-call(f32[256,128]{1,0:T(8,128)S(1)} %get-tuple-element.26.one_ref, f32[256,128]{1,0:T(8,128)S(1)} %get-tuple-element.24.refs_5_.live_ref, bf16[128,256]{1,0:T(8,128)(2,1)S(1)} %copy-done.6, bf16[128,128]{1,0:T(8,128)(2,1)S(1)} %copy-done.8), custom_call_target="tpu_custom_call" | custom-call | flops 25165824 | bytes 524288 | tf_op jit(solution)/shard_map/pallas_call | solution.py:276
  18.1 0.3 collective-permute-start.2
  18.4 0.5 %collective-permute-done.4 = bf16[256,128]{1,0:T(8,128)(2,1)S(1)} collective-permute-done((bf16[256,128]{1,0:T(8,128)(2,1)S(1)}, bf16[256,128]{1,0:T(8,128)(2,1)S(1)}, u32[]{:S(2)}, u32[]{:S(2)}) %collective-permute-start.4) | collective-permute-done | bytes 65568 | tf_op jit(solution)/shard_map/ppermute | solution.py:454
  18.9 1.3 %collective-permute-start.6 = (bf16[2,256,128]{2,1,0:T(8,128)(2,1)S(1)}, bf16[2,256,128]{2,1,0:T(8,128)(2,1)S(1)}, u32[]{:S(2)}, u32[]{:S(2)}) collective-permute-start(bf16[2,256,128]{2,1,0:T(8,128)(2,1)S(1)} %pad_maximum_fusion.1), channel_id=1, source_target_pairs={{2,0},{4,1},{10,2},{12,3},{0,4},{7,5},{9,6},{14,7},{1,8},{6,9},{8,... | collective-permute-start | bytes 393224 | tf_op jit(solution)/shard_map/ppermute | solution.py:454
  20.3 2.4 %collective-permute-done.2 = bf16[256,128]{1,0:T(8,128)(2,1)S(1)} collective-permute-done((bf16[256,128]{1,0:T(8,128)(2,1)S(1)}, bf16[256,128]{1,0:T(8,128)(2,1)S(1)}, u32[]{:S(2)}, u32[]{:S(2)}) %collective-permute-start.2) | collective-permute-done | bytes 65568 | tf_op jit(solution)/shard_map/ppermute | solution.py:454
  22.6 0.1 collective-permute-start.3
  22.7 2.7 %collective-permute-start.5 = (bf16[2,256,128]{2,1,0:T(8,128)(2,1)S(1)}, bf16[2,256,128]{2,1,0:T(8,128)(2,1)S(1)}, u32[]{:S(2)}, u32[]{:S(2)}) collective-permute-start(bf16[2,256,128]{2,1,0:T(8,128)(2,1)S(1)} %pad_maximum_fusion.1), channel_id=1, source_target_pairs={{0,0},{6,1},{8,2},{14,3},{2,4},{5,5},{11,6},{12,7},{3,8},{4,9},{10... | collective-permute-start | bytes 393224 | tf_op jit(solution)/shard_map/ppermute | solution.py:454
  25.5 0.8 %collective-permute-done.6.refs_2_ = bf16[2,256,128]{2,1,0:T(8,128)(2,1)S(1)} collective-permute-done((bf16[2,256,128]{2,1,0:T(8,128)(2,1)S(1)}, bf16[2,256,128]{2,1,0:T(8,128)(2,1)S(1)}, u32[]{:S(2)}, u32[]{:S(2)}) %collective-permute-start.6) | collective-permute-done | bytes 131104 | tf_op jit(solution)/shard_map/ppermute | solution.py:454
  26.2 0.0 collective-permute-done.3.refs_1_
  26.2 0.4 %shard_map.152.refs_3_ = f32[256,128]{1,0:T(8,128)S(1)} custom-call(bf16[2,256,128]{2,1,0:T(8,128)(2,1)S(1)} %pad_maximum_fusion.refs_0_, bf16[2,256,128]{2,1,0:T(8,128)(2,1)S(1)} %collective-permute-done.3.refs_1_, bf16[2,256,128]{2,1,0:T(8,128)(2,1)S(1)} %collective-permute-done.6.refs_2_), custom_call_target="tpu_custom_call" | custom-call | flops 67108864 | bytes 1048576 | tf_op jit(solution)/shard_map/pallas_call | solution.py:404
  26.7 6.1 %collective-permute-done.5.refs_2_ = bf16[2,256,128]{2,1,0:T(8,128)(2,1)S(1)} collective-permute-done((bf16[2,256,128]{2,1,0:T(8,128)(2,1)S(1)}, bf16[2,256,128]{2,1,0:T(8,128)(2,1)S(1)}, u32[]{:S(2)}, u32[]{:S(2)}) %collective-permute-start.5) | collective-permute-done | bytes 131104 | tf_op jit(solution)/shard_map/ppermute | solution.py:454
  32.8 0.0 copy-done.1
  32.8 0.0 copy-done.2
  32.8 0.0 copy-done.7
  32.8 1.9 %shard_map.153 = bf16[16,16,128]{2,1,0:T(8,128)(2,1)} custom-call(bf16[2,256,128]{2,1,0:T(8,128)(2,1)S(1)} %pad_maximum_fusion.refs_0_, bf16[2,256,128]{2,1,0:T(8,128)(2,1)S(1)} %collective-permute-done.3.refs_1_, bf16[2,256,128]{2,1,0:T(8,128)(2,1)S(1)} %collective-permute-done.5.refs_2_, f32[256,128]{1,0:T(8,128)S(1)} %shard_map.152.refs_3_, ...), custom_call_target="tpu_custom_call" | custom-call | flops 134217728 | bytes 2097152 | tf_op jit(solution)/shard_map/pallas_call | solution.py:415
  (2 shorter events, 0.0 us)
Async XLA Ops:
  0.0 1.6 %copy-start.12 = (bf16[256,16,256]{2,1,0:T(8,128)(2,1)S(1)}, bf16[256,16,256]{2,1,0:T(8,128)(2,1)}, u32[]{:S(2)}) copy-start(bf16[256,16,256]{2,1,0:T(8,128)(2,1)} %x_ref.3) | copy-start | bytes 6291460
  0.0 0.9 %copy-start.13 = (bf16[256,32]{0,1:T(8,128)(2,1)S(1)}, bf16[256,32]{0,1:T(8,128)(2,1)}, u32[]{:S(2)}) copy-start(bf16[256,32]{0,1:T(8,128)(2,1)} %param.21) | copy-start | bytes 49156
  1.6 5.6 %copy-start.14 = (bf16[256,32]{0,1:T(8,128)(2,1)S(1)}, bf16[256,32]{0,1:T(8,128)(2,1)}, u32[]{:S(2)}) copy-start(bf16[256,32]{0,1:T(8,128)(2,1)} %param.20) | copy-start | bytes 49156
  3.5 3.8 %copy-start.3 = (s32[256,64]{0,1:T(8,128)S(1)}, s32[256,64]{0,1:T(8,128)}, u32[]{:S(2)}) copy-start(s32[256,64]{0,1:T(8,128)} %param.16) | copy-start | bytes 196612
  3.5 12.5 %collective-permute-start = (bf16[2,256,128]{2,1,0:T(8,128)(2,1)S(1)}, bf16[2,256,128]{2,1,0:T(8,128)(2,1)S(1)}, u32[]{:S(2)}, u32[]{:S(2)}) collective-permute-start(bf16[2,256,128]{2,1,0:T(8,128)(2,1)S(1)} %get-tuple-element.19), channel_id=1, source_target_pairs={{0,0},{6,1},{8,2},{14,3},{2,4},{5,5},{11,6},{12,7},{3,8},{4,9},{10... | collective-permute-start | bytes 393224 | tf_op jit(solution)/shard_map/ppermute | solution.py:454
  7.1 8.9 %collective-permute-start.1 = (bf16[2,256,128]{2,1,0:T(8,128)(2,1)S(1)}, bf16[2,256,128]{2,1,0:T(8,128)(2,1)S(1)}, u32[]{:S(2)}, u32[]{:S(2)}) collective-permute-start(bf16[2,256,128]{2,1,0:T(8,128)(2,1)S(1)} %get-tuple-element.20), channel_id=1, source_target_pairs={{2,0},{4,1},{10,2},{12,3},{0,4},{7,5},{9,6},{14,7},{1,8},{6,9},{8,... | collective-permute-start | bytes 393224 | tf_op jit(solution)/shard_map/ppermute | solution.py:454
  7.3 2.2 %copy-start = (f32[32,32,128]{2,1,0:T(8,128)S(1)}, f32[32,32,128]{2,1,0:T(8,128)}, u32[]{:S(2)}) copy-start(f32[32,32,128]{2,1,0:T(8,128)} %proj_ref.1) | copy-start | bytes 1572868
  7.3 2.2 %copy-start.4 = (bf16[16,16,128]{2,1,0:T(8,128)(2,1)S(1)}, bf16[16,16,128]{2,1,0:T(8,128)(2,1)}, u32[]{:S(2)}) copy-start(bf16[16,16,128]{2,1,0:T(8,128)(2,1)} %pair_ref.1) | copy-start | bytes 196612
  7.3 2.2 %copy-start.9 = (bf16[66,128]{1,0:T(8,128)(2,1)S(1)}, bf16[66,128]{1,0:T(8,128)(2,1)}, u32[]{:S(2)}) copy-start(bf16[66,128]{1,0:T(8,128)(2,1)} %table_ref.1) | copy-start | bytes 50692
  7.3 2.2 %copy-start.10 = (s32[64]{0:T(128)S(1)}, s32[64]{0:T(128)}, u32[]{:S(2)}) copy-start(s32[64]{0:T(128)} %param.18) | copy-start | bytes 772
  7.3 2.2 %copy-start.11 = (s32[64]{0:T(128)S(1)}, s32[64]{0:T(128)}, u32[]{:S(2)}) copy-start(s32[64]{0:T(128)} %param.19) | copy-start | bytes 772
  7.3 8.7 %copy-start.5 = (bf16[128,256]{1,0:T(8,128)(2,1)S(1)}, bf16[128,256]{1,0:T(8,128)(2,1)}, u32[]{:S(2)}) copy-start(bf16[128,256]{1,0:T(8,128)(2,1)} %refs_7_.2) | copy-start | bytes 196612
  9.4 8.2 %copy-start.6 = (bf16[128,256]{1,0:T(8,128)(2,1)S(1)}, bf16[128,256]{1,0:T(8,128)(2,1)}, u32[]{:S(2)}) copy-start(bf16[128,256]{1,0:T(8,128)(2,1)} %left_weight.1) | copy-start | bytes 196612
  9.4 8.2 %copy-start.8 = (bf16[128,128]{1,0:T(8,128)(2,1)S(1)}, bf16[128,128]{1,0:T(8,128)(2,1)}, u32[]{:S(2)}) copy-start(bf16[128,128]{1,0:T(8,128)(2,1)} %gate_weight.1) | copy-start | bytes 98308
  9.4 23.3 %copy-start.1 = (bf16[128,512]{1,0:T(8,128)(2,1)S(1)}, bf16[128,512]{1,0:T(8,128)(2,1)}, u32[]{:S(2)}) copy-start(bf16[128,512]{1,0:T(8,128)(2,1)} %refs_7_.3) | copy-start | bytes 393220
  9.5 23.3 %copy-start.2 = (bf16[512,128]{1,0:T(8,128)(2,1)S(1)}, bf16[512,128]{1,0:T(8,128)(2,1)}, u32[]{:S(2)}) copy-start(bf16[512,128]{1,0:T(8,128)(2,1)} %refs_8_.1) | copy-start | bytes 393220
  9.5 23.3 %copy-start.7 = (bf16[128,128]{1,0:T(8,128)(2,1)S(1)}, bf16[128,128]{1,0:T(8,128)(2,1)}, u32[]{:S(2)}) copy-start(bf16[128,128]{1,0:T(8,128)(2,1)} %refs_6_.1) | copy-start | bytes 98308
  17.6 1.3 %collective-permute-start.4 = (bf16[256,128]{1,0:T(8,128)(2,1)S(1)}, bf16[256,128]{1,0:T(8,128)(2,1)S(1)}, u32[]{:S(2)}, u32[]{:S(2)}) collective-permute-start(bf16[256,128]{1,0:T(8,128)(2,1)S(1)} %get-tuple-element.28), channel_id=1, source_target_pairs={{1,0},{0,1},{3,2},{2,3},{5,4},{4,5},{7,6},{6,7},{9,8},{8,9},{11,10... | collective-permute-start | bytes 196616 | tf_op jit(solution)/shard_map/ppermute | solution.py:454
  18.1 4.5 %collective-permute-start.2 = (bf16[256,128]{1,0:T(8,128)(2,1)S(1)}, bf16[256,128]{1,0:T(8,128)(2,1)S(1)}, u32[]{:S(2)}, u32[]{:S(2)}) collective-permute-start(bf16[256,128]{1,0:T(8,128)(2,1)S(1)} %get-tuple-element.27), channel_id=1, source_target_pairs={{2,0},{3,1},{0,2},{1,3},{6,4},{7,5},{4,6},{5,7},{10,8},{11,9},{8,1... | collective-permute-start | bytes 196616 | tf_op jit(solution)/shard_map/ppermute | solution.py:454
  18.9 7.3 %collective-permute-start.6 = (bf16[2,256,128]{2,1,0:T(8,128)(2,1)S(1)}, bf16[2,256,128]{2,1,0:T(8,128)(2,1)S(1)}, u32[]{:S(2)}, u32[]{:S(2)}) collective-permute-start(bf16[2,256,128]{2,1,0:T(8,128)(2,1)S(1)} %pad_maximum_fusion.1), channel_id=1, source_target_pairs={{2,0},{4,1},{10,2},{12,3},{0,4},{7,5},{9,6},{14,7},{1,8},{6,9},{8,... | collective-permute-start | bytes 393224 | tf_op jit(solution)/shard_map/ppermute | solution.py:454
  22.6 3.6 %collective-permute-start.3 = (bf16[2,256,128]{2,1,0:T(8,128)(2,1)S(1)}, bf16[2,256,128]{2,1,0:T(8,128)(2,1)S(1)}, u32[]{:S(2)}, u32[]{:S(2)}) collective-permute-start(bf16[2,256,128]{2,1,0:T(8,128)(2,1)S(1)} %pad_maximum_fusion.refs_0_), channel_id=1, source_target_pairs={{1,0},{0,1},{3,2},{2,3},{5,4},{4,5},{7,6},{6,7},{9,8},{8,9},{11,10... | collective-permute-start | bytes 393224 | tf_op jit(solution)/shard_map/ppermute | solution.py:454
  22.7 10.1 %collective-permute-start.5 = (bf16[2,256,128]{2,1,0:T(8,128)(2,1)S(1)}, bf16[2,256,128]{2,1,0:T(8,128)(2,1)S(1)}, u32[]{:S(2)}, u32[]{:S(2)}) collective-permute-start(bf16[2,256,128]{2,1,0:T(8,128)(2,1)S(1)} %pad_maximum_fusion.1), channel_id=1, source_target_pairs={{0,0},{6,1},{8,2},{14,3},{2,4},{5,5},{11,6},{12,7},{3,8},{4,9},{10... | collective-permute-start | bytes 393224 | tf_op jit(solution)/shard_map/ppermute | solution.py:454

commit v18 on v15

--- a/solution.py
+++ b/solution.py
@@ -77,8 +77,8 @@
     rep = rows // groups
     width = rows * hidden
     step = y_scr.shape[1] // rows
-    w = jnp.concatenate([weight_ref[...], jnp.ones((channels, LANES), BF16)], axis=1)
-    ones = jnp.ones((LANES, LANES), BF16)
+    share = jnp.full((channels, LANES), 1.0 / channels, BF16)
+    w = jnp.concatenate([weight_ref[...], share], axis=1)
     sums = dot(jnp.ones((8, channels), BF16), weight_ref[...])[:1]
     block = over(iota((step, LANES), 1), hidden)
     if mask_ref is not None:
@@ -89,13 +89,12 @@
     for turn in range(seqs // step):
         x = x_ref[turn * step : (turn + 1) * step].reshape(step * rows, channels)
         y = dot(x, w)
-        mean = y[:, LANES:] * (1.0 / channels)
+        mean = y[:, LANES:]
         square = jnp.zeros_like(mean)
         for half in range(channels // LANES):
             centered = x[:, half * LANES : (half + 1) * LANES].astype(F32) - mean
             square = square + centered * centered
-        spread = dot(square.astype(BF16), ones)
-        scale = lax.rsqrt(spread * (1.0 / channels) + EPSILON)
+        scale = lax.rsqrt(dot(square.astype(BF16), share[:LANES]) + EPSILON)
         y_scr[turn] = (y[:, :LANES] - mean * sums) * scale
         here = slice(turn * step, (turn + 1) * step)
         for group in range(groups):
@@ -128,7 +127,7 @@
 
 def prepare_kernel(
     zl_ref, mask_ref, pair_ref, live_ref, chain_ref, table_ref, proj_ref,
-    zlt_ref, base_ref, inverse_ref, live_out_ref, proj_out_ref, seen_ref, pair_scr, table_scr,
+    zlt_ref, base_ref, inverse_ref, live_out_ref, proj_out_ref, seen_ref, pair_scr, table_scr, turn_scr,
 ):
     rows, cols, _ = pair_ref.shape
     pairs = rows * cols
@@ -136,15 +135,20 @@
     classes = table_ref.shape[0]
     row_start = lax.axis_index("dap") * rows
     col_start = lax.axis_index("sub") * cols
-    for group in range(zl_ref.shape[0]):
-        turned = zl_ref[group].T
+    groups = zl_ref.shape[0]
+    hidden = groups * LANES // rows
+    for group in range(groups):
+        turned = zl_ref[group].astype(F32).T
         for half in range(zlt_ref.shape[0]):
             lanes = slice(half * LANES, (half + 1) * LANES)
-            zlt_ref[half, group * LANES : (group + 1) * LANES, :] = turned[:, lanes]
+            turn_scr[half, group * LANES : (group + 1) * LANES, :] = turned[:, lanes]
+    for half in range(zlt_ref.shape[0]):
+        for channel in range(hidden):
+            here = slice(channel * rows, (channel + 1) * rows)
+            picked = turn_scr[half, pl.ds(channel, rows, stride=hidden), :]
+            zlt_ref[half, here, :] = picked.astype(BF16)
     proj_out_ref[...] = proj_ref[...].reshape(proj_out_ref.shape).astype(BF16)
-    groups = zl_ref.shape[0]
     width = groups * LANES
-    hidden = width // rows
     for block in range(cols // rows):
         column = col_start + block * rows + over(iota((residues, width), 1), hidden)
         spread = (iota((residues, width), 0) == column).astype(BF16)
@@ -193,7 +197,11 @@
         ),
         in_specs=[vmem()] * 7,
         out_specs=[vmem()] * 6,
-        scratch_shapes=[pltpu.VMEM((pairs, channels), F32), pltpu.VMEM((LANES, channels), F32)],
+        scratch_shapes=[
+            pltpu.VMEM((pairs, channels), F32),
+            pltpu.VMEM((LANES, channels), F32),
+            pltpu.VMEM((zl.shape[1] // LANES, zl.shape[0] * LANES, LANES), F32),
+        ],
         compiler_params=pltpu.CompilerParams(vmem_limit_bytes=24 << 20),
         cost_estimate=pl.CostEstimate(
             flops=2 * pairs * 256 * 1024, bytes_accessed=2 << 20, transcendentals=0
@@ -204,7 +212,7 @@
 def pair_kernel(ratio, hidden, zlt_ref, *refs):
     zr_refs, refs = refs[: ratio * PARTS], refs[ratio * PARTS :]
     (seen_ref, base_ref, inverse_ref, live_ref, proj_ref, tl_ref, tr_ref,
-     both_ref, left_ref, one_ref, outer_scr, flat_scr, one_scr) = refs
+     both_ref, left_ref, one_ref, flat_scr, one_scr) = refs
     pairs, channels = base_ref.shape
     rows = zlt_ref.shape[1] // hidden
     rep = LANES // hidden
@@ -223,11 +231,11 @@
             right.append(factor * seen_ref[block * (rows // rep) + group])
         outer = dot(left, jnp.concatenate(right, axis=1))
         for group in range(rows // rep):
-            outer_scr[group] = outer[:, group * LANES : (group + 1) * LANES]
-        for group in range(rows // rep):
+            lanes = slice(group * LANES, (group + 1) * LANES)
             for quad in range(hidden // rep):
                 s0, s1, s2, s3 = (
-                    outer_scr[group, pl.ds(quad * rep + k, rows, stride=hidden), :] for k in range(rep)
+                    outer[(quad * rep + k) * rows : (quad * rep + k + 1) * rows, lanes]
+                    for k in range(rep)
                 )
                 t0 = jnp.where(upper, pltpu.roll(s2, half, 1), s0)
                 t1 = jnp.where(upper, pltpu.roll(s3, half, 1), s1)
@@ -273,7 +281,6 @@
         in_specs=[vmem()] * (8 + len(zrs)),
         out_specs=[vmem()] * 3,
         scratch_shapes=[
-            pltpu.VMEM((zrs[0].shape[0] * PARTS, zlt.shape[1], LANES), F32),
             pltpu.VMEM((proj.shape[0] // LANES, pairs, LANES), BF16),
             pltpu.VMEM((pairs, channels), F32),
         ],

time: 33.3 us -> 32.8 us (0.985)
    pallas_call x1, Pallas kernels: 1.59 us -> 1.19 us  [pair_update(): pl.pallas_call(functools.partial(pair_kernel, ratio, hidden), out_shape=(...]
  transfers between devices with their start and end apart: 7 -> 7, of which waited for: 3 -> 3; matrix products, arithmetic and copies ran while one was open for 0% -> 0% of each run, Pallas kernels for 11% -> 12%
where the time goes in v18:
time: 32.8 us; the launch traced here: 32.5 us
  starting transfers between devices  15.4 us (47%)
  Pallas kernels  8.83 us (27%)
  waiting for transfers between devices  6.45 us (20%)
  local copies, waits for them, and re-layouts  1.62 us (5%)
    ppermute x7, starting transfers between devices, fetch(): return lax.ppermute(values, ('dap', 'sub'), perm)  15.4 us
    ppermute x7, waiting for transfers between devices, fetch(): return lax.ppermute(values, ('dap', 'sub'), perm)  6.45 us
    pallas_call x2, Pallas kernels, factor(): pl.pallas_call(functools.partial(factor_kernel, mask is not None, hidden)...  3.96 us
    pallas_call x1, Pallas kernels, triangle_update(): pl.pallas_call(functools.partial(last_kernel, late, twos, ratio, cols), o...  1.87 us
    unnamed x30, local copies, waits for them, and re-layouts  1.61 us
    pallas_call x1, Pallas kernels, pair_update(): pl.pallas_call(functools.partial(pair_kernel, ratio, hidden), out_shape=(...  1.19 us
    pallas_call x1, Pallas kernels, prepare(): pl.pallas_call(prepare_kernel, out_shape=(jax.ShapeDtypeStruct((zl.shape[...  0.94 us
    pallas_call x1, Pallas kernels, triangle_update(): pl.pallas_call(functools.partial(first_kernel, early, twos, ratio, cols),...  0.73 us
  transfers between devices with their start and end apart: 7, of which 3 were waited for; matrix products, arithmetic and copies ran while one was open for 0% of the time, Pallas kernels for 12%

profile of v18, /device:TPU:1, one launch (start us, length us, event | category | flops | bytes accessed | tf_op | source)
XLA Modules:
  0.0 32.5 jit_solution(10506712146122499757)
XLA Ops:
  0.0 0.0 copy-start.12
  0.0 0.0 copy-start.13
  0.0 0.9 %copy-done.13 = bf16[256,32]{0,1:T(8,128)(2,1)S(1)} copy-done((bf16[256,32]{0,1:T(8,128)(2,1)S(1)}, bf16[256,32]{0,1:T(8,128)(2,1)}, u32[]{:S(2)}) %copy-start.13) | copy-done | bytes 16408
  0.9 0.1 shard_map.148.weight_ref
  0.9 0.7 %copy-done.12 = bf16[256,16,256]{2,1,0:T(8,128)(2,1)S(1)} copy-done((bf16[256,16,256]{2,1,0:T(8,128)(2,1)S(1)}, bf16[256,16,256]{2,1,0:T(8,128)(2,1)}, u32[]{:S(2)}) %copy-start.12) | copy-done | bytes 2097176
  1.6 0.0 copy-start.14
  1.6 1.9 %shard_map.149 = (bf16[2,256,128]{2,1,0:T(8,128)(2,1)S(1)}, bf16[2,256,128]{2,1,0:T(8,128)(2,1)S(1)}) custom-call(bf16[256,16,256]{2,1,0:T(8,128)(2,1)S(1)} %copy-done.12, bf16[256,128]{1,0:T(8,128)(2,1)S(1)} %shard_map.148.weight_ref), custom_call_target="tpu_custom_call" | custom-call | flops 1073741824 | bytes 4194304 | tf_op jit(solution)/shard_map/pallas_call | solution.py:115
  3.5 0.0 copy-start.3
  3.5 6.8 %collective-permute-start = (bf16[2,256,128]{2,1,0:T(8,128)(2,1)S(1)}, bf16[2,256,128]{2,1,0:T(8,128)(2,1)S(1)}, u32[]{:S(2)}, u32[]{:S(2)}) collective-permute-start(bf16[2,256,128]{2,1,0:T(8,128)(2,1)S(1)} %get-tuple-element.19), channel_id=1, source_target_pairs={{0,0},{6,1},{8,2},{14,3},{2,4},{5,5},{11,6},{12,7},{3,8},{4,9},{10... | collective-permute-start | bytes 393224 | tf_op jit(solution)/shard_map/ppermute | solution.py:450
  10.3 0.3 collective-permute-start.1
  10.6 0.0 copy-done.14
  10.6 0.1 shard_map.145.weight_ref
  10.7 0.0 copy-start
  10.7 0.0 copy-start.4
  10.7 0.0 copy-start.9
  10.7 0.0 copy-start.10
  10.7 0.0 copy-start.11
  10.7 0.0 copy-done.3
  10.7 0.0 copy-start.5
  10.8 0.0 copy-start.6
  10.8 2.1 %shard_map.146.zl_ref = bf16[4,256,128]{2,1,0:T(8,128)(2,1)S(1)} custom-call(bf16[256,16,256]{2,1,0:T(8,128)(2,1)S(1)} %copy-done.12, bf16[256,128]{1,0:T(8,128)(2,1)S(1)} %shard_map.145.weight_ref, s32[64,256]{1,0:T(8,128)S(1)} %bitcast.5), custom_call_target="tpu_custom_call" | custom-call | flops 1073741824 | bytes 4194304 | tf_op jit(solution)/shard_map/pallas_call | solution.py:115
  12.8 0.0 copy-start.7
  12.8 0.0 copy-start.1
  12.9 0.0 copy-start.2
  12.9 0.0 copy-start.8
  12.9 0.0 copy-done
  12.9 0.0 copy-done.4
  12.9 0.0 copy-done.9
  12.9 0.0 copy-done.10
  12.9 0.0 copy-done.11
  12.9 0.9 %shard_map.147 = (bf16[2,512,128]{2,1,0:T(8,128)(2,1)S(1)}, f32[256,128]{1,0:T(8,128)S(1)}, f32[256,128]{1,0:T(8,128)S(1)}, f32[256,128]{1,0:T(8,128)S(1)}, bf16...) custom-call(bf16[4,256,128]{2,1,0:T(8,128)(2,1)S(1)} %shard_map.146.zl_ref, s32[64,256]{1,0:T(8,128)S(1)} %bitcast.6, ...), custom_call_target="tpu_custom_call" | custom-call | flops 134217728 | bytes 2097152 | tf_op jit(solution)/shard_map/pallas_call | solution.py:188
  13.9 0.0 collective-permute-done.refs_0_
  13.9 2.8 %collective-permute-done.1.refs_1_ = bf16[2,256,128]{2,1,0:T(8,128)(2,1)S(1)} collective-permute-done((bf16[2,256,128]{2,1,0:T(8,128)(2,1)S(1)}, bf16[2,256,128]{2,1,0:T(8,128)(2,1)S(1)}, u32[]{:S(2)}, u32[]{:S(2)}) %collective-permute-start.1) | collective-permute-done | bytes 131104 | tf_op jit(solution)/shard_map/ppermute | solution.py:450
  16.7 0.0 copy-done.5
  16.7 0.0 copy-done.6
  16.7 1.2 %shard_map.150 = (bf16[2,256,128]{2,1,0:T(8,128)(2,1)S(1)}, bf16[256,128]{1,0:T(8,128)(2,1)S(1)}, bf16[256,128]{1,0:T(8,128)(2,1)S(1)}) custom-call(bf16[2,512,128]{2,1,0:T(8,128)(2,1)S(1)} %get-tuple-element.18.zlt_ref, bf16[2,256,128]{2,1,0:T(8,128)(2,1)S(1)} %collective-permute-done.refs_0_, bf16[2,256,128]{2,1,0:T(8,128)(2,1)S(1)} %collective-permute-done.1.refs_1_, ...), custom_call_target="tpu_custom_call" | custom-call | flops 268435456 | bytes 2097152 | tf_op jit(solution)/shard_map/pallas_call | solution.py:278
  17.9 0.1 collective-permute-start.2
  18.0 2.0 %collective-permute-start.3 = (bf16[256,128]{1,0:T(8,128)(2,1)S(1)}, bf16[256,128]{1,0:T(8,128)(2,1)S(1)}, u32[]{:S(2)}, u32[]{:S(2)}) collective-permute-start(bf16[256,128]{1,0:T(8,128)(2,1)S(1)} %get-tuple-element.27), channel_id=1, source_target_pairs={{2,0},{3,1},{0,2},{1,3},{6,4},{7,5},{4,6},{5,7},{10,8},{11,9},{8,1... | collective-permute-start | bytes 196616 | tf_op jit(solution)/shard_map/ppermute | solution.py:450
  20.0 0.0 collective-permute-done.2.refs_1_
  20.1 1.3 %collective-permute-start.6 = (bf16[2,256,128]{2,1,0:T(8,128)(2,1)S(1)}, bf16[2,256,128]{2,1,0:T(8,128)(2,1)S(1)}, u32[]{:S(2)}, u32[]{:S(2)}) collective-permute-start(bf16[2,256,128]{2,1,0:T(8,128)(2,1)S(1)} %pad_maximum_fusion), channel_id=1, source_target_pairs={{2,0},{4,1},{10,2},{12,3},{0,4},{7,5},{9,6},{14,7},{1,8},{6,9},{8,... | collective-permute-start | bytes 393224 | tf_op jit(solution)/shard_map/ppermute | solution.py:450
  21.4 4.9 %collective-permute-start.5 = (bf16[2,256,128]{2,1,0:T(8,128)(2,1)S(1)}, bf16[2,256,128]{2,1,0:T(8,128)(2,1)S(1)}, u32[]{:S(2)}, u32[]{:S(2)}) collective-permute-start(bf16[2,256,128]{2,1,0:T(8,128)(2,1)S(1)} %pad_maximum_fusion), channel_id=1, source_target_pairs={{0,0},{6,1},{8,2},{14,3},{2,4},{5,5},{11,6},{12,7},{3,8},{4,9},{10... | collective-permute-start | bytes 393224 | tf_op jit(solution)/shard_map/ppermute | solution.py:450
  26.2 0.0 collective-permute-done.3.refs_2_
  26.2 0.1 collective-permute-start.4
  26.3 1.2 %collective-permute-done.4.refs_3_ = bf16[256,128]{1,0:T(8,128)(2,1)S(1)} collective-permute-done((bf16[256,128]{1,0:T(8,128)(2,1)S(1)}, bf16[256,128]{1,0:T(8,128)(2,1)S(1)}, u32[]{:S(2)}, u32[]{:S(2)}) %collective-permute-start.4) | collective-permute-done | bytes 65568 | tf_op jit(solution)/shard_map/ppermute | solution.py:450
  27.6 0.0 collective-permute-done.6.refs_4_
  27.6 0.0 copy-done.7
  27.6 0.7 %shard_map.151 = (f32[256,128]{1,0:T(8,128)S(1)}, f32[256,128]{1,0:T(8,128)S(1)}) custom-call(bf16[2,256,128]{2,1,0:T(8,128)(2,1)S(1)} %get-tuple-element.26.refs_0_, bf16[2,256,128]{2,1,0:T(8,128)(2,1)S(1)} %collective-permute-done.2.refs_1_, bf16[256,128]{1,0:T(8,128)(2,1)S(1)} %collective-permute-done.3.refs_2_, ...), custom_call_target="tpu_custom_call" | custom-call | flops 67108864 | bytes 1048576 | tf_op jit(solution)/shard_map/pallas_call | solution.py:399
  28.3 2.4 %collective-permute-done.5.refs_4_ = bf16[2,256,128]{2,1,0:T(8,128)(2,1)S(1)} collective-permute-done((bf16[2,256,128]{2,1,0:T(8,128)(2,1)S(1)}, bf16[2,256,128]{2,1,0:T(8,128)(2,1)S(1)}, u32[]{:S(2)}, u32[]{:S(2)}) %collective-permute-start.5) | collective-permute-done | bytes 131104 | tf_op jit(solution)/shard_map/ppermute | solution.py:450
  30.7 0.0 copy-done.1
  30.7 0.0 copy-done.2
  30.7 0.0 copy-done.8
  30.7 1.9 %shard_map.152 = bf16[16,16,128]{2,1,0:T(8,128)(2,1)} custom-call(bf16[2,256,128]{2,1,0:T(8,128)(2,1)S(1)} %get-tuple-element.26.refs_0_, bf16[2,256,128]{2,1,0:T(8,128)(2,1)S(1)} %collective-permute-done.2.refs_1_, bf16[256,128]{1,0:T(8,128)(2,1)S(1)} %collective-permute-done.3.refs_2_, bf16[256,128]{1,0:T(8,128)(2,1)S(1)} %collective-permute-done.4.refs_3_, ...), custom_call_target="tpu_custom_call" | custom-call | flops 134217728 | bytes 2097152 | tf_op jit(solution)/shard_map/pallas_call | solution.py:410
  (3 shorter events, 0.0 us)
Async XLA Ops:
  0.0 1.6 %copy-start.12 = (bf16[256,16,256]{2,1,0:T(8,128)(2,1)S(1)}, bf16[256,16,256]{2,1,0:T(8,128)(2,1)}, u32[]{:S(2)}) copy-start(bf16[256,16,256]{2,1,0:T(8,128)(2,1)} %x_ref.3) | copy-start | bytes 6291460
  0.0 0.9 %copy-start.13 = (bf16[256,32]{0,1:T(8,128)(2,1)S(1)}, bf16[256,32]{0,1:T(8,128)(2,1)}, u32[]{:S(2)}) copy-start(bf16[256,32]{0,1:T(8,128)(2,1)} %param.21) | copy-start | bytes 49156
  1.6 9.0 %copy-start.14 = (bf16[256,32]{0,1:T(8,128)(2,1)S(1)}, bf16[256,32]{0,1:T(8,128)(2,1)}, u32[]{:S(2)}) copy-start(bf16[256,32]{0,1:T(8,128)(2,1)} %param.20) | copy-start | bytes 49156
  3.5 7.2 %copy-start.3 = (s32[256,64]{0,1:T(8,128)S(1)}, s32[256,64]{0,1:T(8,128)}, u32[]{:S(2)}) copy-start(s32[256,64]{0,1:T(8,128)} %param.16) | copy-start | bytes 196612
  3.5 10.4 %collective-permute-start = (bf16[2,256,128]{2,1,0:T(8,128)(2,1)S(1)}, bf16[2,256,128]{2,1,0:T(8,128)(2,1)S(1)}, u32[]{:S(2)}, u32[]{:S(2)}) collective-permute-start(bf16[2,256,128]{2,1,0:T(8,128)(2,1)S(1)} %get-tuple-element.19), channel_id=1, source_target_pairs={{0,0},{6,1},{8,2},{14,3},{2,4},{5,5},{11,6},{12,7},{3,8},{4,9},{10... | collective-permute-start | bytes 393224 | tf_op jit(solution)/shard_map/ppermute | solution.py:450
  10.3 6.4 %collective-permute-start.1 = (bf16[2,256,128]{2,1,0:T(8,128)(2,1)S(1)}, bf16[2,256,128]{2,1,0:T(8,128)(2,1)S(1)}, u32[]{:S(2)}, u32[]{:S(2)}) collective-permute-start(bf16[2,256,128]{2,1,0:T(8,128)(2,1)S(1)} %get-tuple-element.20), channel_id=1, source_target_pairs={{2,0},{4,1},{10,2},{12,3},{0,4},{7,5},{9,6},{14,7},{1,8},{6,9},{8,... | collective-permute-start | bytes 393224 | tf_op jit(solution)/shard_map/ppermute | solution.py:450
  10.7 2.2 %copy-start = (f32[32,32,128]{2,1,0:T(8,128)S(1)}, f32[32,32,128]{2,1,0:T(8,128)}, u32[]{:S(2)}) copy-start(f32[32,32,128]{2,1,0:T(8,128)} %proj_ref.1) | copy-start | bytes 1572868
  10.7 2.2 %copy-start.4 = (bf16[16,16,128]{2,1,0:T(8,128)(2,1)S(1)}, bf16[16,16,128]{2,1,0:T(8,128)(2,1)}, u32[]{:S(2)}) copy-start(bf16[16,16,128]{2,1,0:T(8,128)(2,1)} %pair_ref.1) | copy-start | bytes 196612
  10.7 2.2 %copy-start.9 = (bf16[66,128]{1,0:T(8,128)(2,1)S(1)}, bf16[66,128]{1,0:T(8,128)(2,1)}, u32[]{:S(2)}) copy-start(bf16[66,128]{1,0:T(8,128)(2,1)} %table_ref.1) | copy-start | bytes 50692
  10.7 2.2 %copy-start.10 = (s32[64]{0:T(128)S(1)}, s32[64]{0:T(128)}, u32[]{:S(2)}) copy-start(s32[64]{0:T(128)} %param.18) | copy-start | bytes 772
  10.7 2.2 %copy-start.11 = (s32[64]{0:T(128)S(1)}, s32[64]{0:T(128)}, u32[]{:S(2)}) copy-start(s32[64]{0:T(128)} %param.19) | copy-start | bytes 772
  10.7 6.0 %copy-start.5 = (bf16[128,256]{1,0:T(8,128)(2,1)S(1)}, bf16[128,256]{1,0:T(8,128)(2,1)}, u32[]{:S(2)}) copy-start(bf16[128,256]{1,0:T(8,128)(2,1)} %refs_7_.1) | copy-start | bytes 196612
  10.8 6.0 %copy-start.6 = (bf16[128,256]{1,0:T(8,128)(2,1)S(1)}, bf16[128,256]{1,0:T(8,128)(2,1)}, u32[]{:S(2)}) copy-start(bf16[128,256]{1,0:T(8,128)(2,1)} %refs_8_.2) | copy-start | bytes 196612
  12.8 14.7 %copy-start.7 = (bf16[128,128]{1,0:T(8,128)(2,1)S(1)}, bf16[128,128]{1,0:T(8,128)(2,1)}, u32[]{:S(2)}) copy-start(bf16[128,128]{1,0:T(8,128)(2,1)} %refs_6_.1) | copy-start | bytes 98308
  12.8 17.8 %copy-start.1 = (bf16[128,512]{1,0:T(8,128)(2,1)S(1)}, bf16[128,512]{1,0:T(8,128)(2,1)}, u32[]{:S(2)}) copy-start(bf16[128,512]{1,0:T(8,128)(2,1)} %refs_9_.1) | copy-start | bytes 393220
  12.9 17.8 %copy-start.2 = (bf16[512,128]{1,0:T(8,128)(2,1)S(1)}, bf16[512,128]{1,0:T(8,128)(2,1)}, u32[]{:S(2)}) copy-start(bf16[512,128]{1,0:T(8,128)(2,1)} %refs_10_.1) | copy-start | bytes 393220
  12.9 17.8 %copy-start.8 = (bf16[128,128]{1,0:T(8,128)(2,1)S(1)}, bf16[128,128]{1,0:T(8,128)(2,1)}, u32[]{:S(2)}) copy-start(bf16[128,128]{1,0:T(8,128)(2,1)} %refs_8_.3) | copy-start | bytes 98308
  17.9 2.1 %collective-permute-start.2 = (bf16[2,256,128]{2,1,0:T(8,128)(2,1)S(1)}, bf16[2,256,128]{2,1,0:T(8,128)(2,1)S(1)}, u32[]{:S(2)}, u32[]{:S(2)}) collective-permute-start(bf16[2,256,128]{2,1,0:T(8,128)(2,1)S(1)} %get-tuple-element.26.refs_0_), channel_id=1, source_target_pairs={{1,0},{0,1},{3,2},{2,3},{5,4},{4,5},{7,6},{6,7},{9,8},{8,9},{11,10... | collective-permute-start | bytes 393224 | tf_op jit(solution)/shard_map/ppermute | solution.py:450
  18.0 8.2 %collective-permute-start.3 = (bf16[256,128]{1,0:T(8,128)(2,1)S(1)}, bf16[256,128]{1,0:T(8,128)(2,1)S(1)}, u32[]{:S(2)}, u32[]{:S(2)}) collective-permute-start(bf16[256,128]{1,0:T(8,128)(2,1)S(1)} %get-tuple-element.27), channel_id=1, source_target_pairs={{2,0},{3,1},{0,2},{1,3},{6,4},{7,5},{4,6},{5,7},{10,8},{11,9},{8,1... | collective-permute-start | bytes 196616 | tf_op jit(solution)/shard_map/ppermute | solution.py:450
  20.1 7.5 %collective-permute-start.6 = (bf16[2,256,128]{2,1,0:T(8,128)(2,1)S(1)}, bf16[2,256,128]{2,1,0:T(8,128)(2,1)S(1)}, u32[]{:S(2)}, u32[]{:S(2)}) collective-permute-start(bf16[2,256,128]{2,1,0:T(8,128)(2,1)S(1)} %pad_maximum_fusion), channel_id=1, source_target_pairs={{2,0},{4,1},{10,2},{12,3},{0,4},{7,5},{9,6},{14,7},{1,8},{6,9},{8,... | collective-permute-start | bytes 393224 | tf_op jit(solution)/shard_map/ppermute | solution.py:450
  21.4 9.3 %collective-permute-start.5 = (bf16[2,256,128]{2,1,0:T(8,128)(2,1)S(1)}, bf16[2,256,128]{2,1,0:T(8,128)(2,1)S(1)}, u32[]{:S(2)}, u32[]{:S(2)}) collective-permute-start(bf16[2,256,128]{2,1,0:T(8,128)(2,1)S(1)} %pad_maximum_fusion), channel_id=1, source_target_pairs={{0,0},{6,1},{8,2},{14,3},{2,4},{5,5},{11,6},{12,7},{3,8},{4,9},{10... | collective-permute-start | bytes 393224 | tf_op jit(solution)/shard_map/ppermute | solution.py:450
  26.2 1.3 %collective-permute-start.4 = (bf16[256,128]{1,0:T(8,128)(2,1)S(1)}, bf16[256,128]{1,0:T(8,128)(2,1)S(1)}, u32[]{:S(2)}, u32[]{:S(2)}) collective-permute-start(bf16[256,128]{1,0:T(8,128)(2,1)S(1)} %collective-permute-done.3.refs_2_), channel_id=1, source_target_pairs={{1,0},{0,1},{3,2},{2,3},{5,4},{4,5},{7,6},{6,7},{9,8},{8,9},{11,10... | collective-permute-start | bytes 196616 | tf_op jit(solution)/shard_map/ppermute | solution.py:450

commit v19 on v18

--- a/solution.py
+++ b/solution.py
@@ -337,7 +337,7 @@
         else:
             totals = tuple(start[pl.ds(place, rows), :] for place in places)
         for index, step in enumerate(steps):
-            sub = lax.rem(first_sub + 2 * step, subs)
+            sub = lax.rem(first_sub + 2 * step + 2, subs)
             pair = rights[turn * len(steps) + index]
             for member, slot in enumerate((sub, other(sub))):
 
@@ -482,7 +482,7 @@
         fetch(
             right,
             lambda a, b, t=turn, m=step: (
-                owner(a, b, t), (sender(a, b, subs, ratio) + 2 * m) % subs
+                owner(a, b, t), (sender(a, b, subs, ratio) + 2 * m + 2) % subs
             ),
         )
         for turn in range(ratio)

time: 32.8 us -> 34.4 us (1.049)
  the two profiles are of different devices: /device:TPU:1 before, /device:TPU:2 now
where the time goes in v19:
time: 34.4 us; the launch traced here: 34.1 us
  waiting for transfers between devices  13.2 us (38%)
  starting transfers between devices  10.1 us (29%)
  Pallas kernels  8.82 us (26%)
  local copies, waits for them, and re-layouts  1.62 us (5%)
    ppermute x7, waiting for transfers between devices, fetch(): return lax.ppermute(values, ('dap', 'sub'), perm)  13.2 us
    ppermute x7, starting transfers between devices, fetch(): return lax.ppermute(values, ('dap', 'sub'), perm)  10.1 us
    pallas_call x2, Pallas kernels, factor(): pl.pallas_call(functools.partial(factor_kernel, mask is not None, hidden)...  3.96 us
    pallas_call x1, Pallas kernels, triangle_update(): pl.pallas_call(functools.partial(last_kernel, late, twos, ratio, cols), o...  1.87 us
    unnamed x30, local copies, waits for them, and re-layouts  1.61 us
    pallas_call x1, Pallas kernels, pair_update(): pl.pallas_call(functools.partial(pair_kernel, ratio, hidden), out_shape=(...  1.19 us
    pallas_call x1, Pallas kernels, prepare(): pl.pallas_call(prepare_kernel, out_shape=(jax.ShapeDtypeStruct((zl.shape[...  0.94 us
    pallas_call x1, Pallas kernels, triangle_update(): pl.pallas_call(functools.partial(first_kernel, early, twos, ratio, cols),...  0.73 us
  transfers between devices with their start and end apart: 7, of which 4 were waited for; matrix products, arithmetic and copies ran while one was open for 0% of the time, Pallas kernels for 11%

profile of v19, /device:TPU:2, one launch (start us, length us, event | category | flops | bytes accessed | tf_op | source)
XLA Modules:
  0.0 34.1 jit_solution(17331968483146728902)
XLA Ops:
  0.0 0.0 copy-start.12
  0.0 0.0 copy-start.13
  0.0 0.9 %copy-done.13 = bf16[256,32]{0,1:T(8,128)(2,1)S(1)} copy-done((bf16[256,32]{0,1:T(8,128)(2,1)S(1)}, bf16[256,32]{0,1:T(8,128)(2,1)}, u32[]{:S(2)}) %copy-start.13) | copy-done | bytes 16408
  0.9 0.1 shard_map.148.weight_ref
  0.9 0.7 %copy-done.12 = bf16[256,16,256]{2,1,0:T(8,128)(2,1)S(1)} copy-done((bf16[256,16,256]{2,1,0:T(8,128)(2,1)S(1)}, bf16[256,16,256]{2,1,0:T(8,128)(2,1)}, u32[]{:S(2)}) %copy-start.12) | copy-done | bytes 2097176
  1.6 0.0 copy-start.14
  1.6 1.9 %shard_map.149 = (bf16[2,256,128]{2,1,0:T(8,128)(2,1)S(1)}, bf16[2,256,128]{2,1,0:T(8,128)(2,1)S(1)}) custom-call(bf16[256,16,256]{2,1,0:T(8,128)(2,1)S(1)} %copy-done.12, bf16[256,128]{1,0:T(8,128)(2,1)S(1)} %shard_map.148.weight_ref), custom_call_target="tpu_custom_call" | custom-call | flops 1073741824 | bytes 4194304 | tf_op jit(solution)/shard_map/pallas_call | solution.py:115
  3.5 0.0 copy-start.3
  3.5 3.6 %collective-permute-start = (bf16[2,256,128]{2,1,0:T(8,128)(2,1)S(1)}, bf16[2,256,128]{2,1,0:T(8,128)(2,1)S(1)}, u32[]{:S(2)}, u32[]{:S(2)}) collective-permute-start(bf16[2,256,128]{2,1,0:T(8,128)(2,1)S(1)} %get-tuple-element.19), channel_id=1, source_target_pairs={{0,0},{6,1},{8,2},{14,3},{2,4},{5,5},{11,6},{12,7},{3,8},{4,9},{10... | collective-permute-start | bytes 393224 | tf_op jit(solution)/shard_map/ppermute | solution.py:450
  7.1 0.1 collective-permute-start.1
  7.2 0.0 copy-done.14
  7.2 0.1 shard_map.145.weight_ref
  7.3 0.0 copy-start
  7.3 0.0 copy-start.4
  7.3 0.0 copy-start.9
  7.3 0.0 copy-start.10
  7.3 0.0 copy-start.11
  7.3 0.0 copy-done.3
  7.3 0.0 copy-start.5
  7.4 0.0 copy-start.6
  7.4 2.1 %shard_map.146.zl_ref = bf16[4,256,128]{2,1,0:T(8,128)(2,1)S(1)} custom-call(bf16[256,16,256]{2,1,0:T(8,128)(2,1)S(1)} %copy-done.12, bf16[256,128]{1,0:T(8,128)(2,1)S(1)} %shard_map.145.weight_ref, s32[64,256]{1,0:T(8,128)S(1)} %bitcast.5), custom_call_target="tpu_custom_call" | custom-call | flops 1073741824 | bytes 4194304 | tf_op jit(solution)/shard_map/pallas_call | solution.py:115
  9.4 0.0 copy-start.7
  9.4 0.0 copy-start.1
  9.5 0.0 copy-start.2
  9.5 0.0 copy-start.8
  9.5 0.0 copy-done
  9.5 0.0 copy-done.4
  9.5 0.0 copy-done.9
  9.5 0.0 copy-done.10
  9.5 0.0 copy-done.11
  9.5 0.9 %shard_map.147 = (bf16[2,512,128]{2,1,0:T(8,128)(2,1)S(1)}, f32[256,128]{1,0:T(8,128)S(1)}, f32[256,128]{1,0:T(8,128)S(1)}, f32[256,128]{1,0:T(8,128)S(1)}, bf16...) custom-call(bf16[4,256,128]{2,1,0:T(8,128)(2,1)S(1)} %shard_map.146.zl_ref, s32[64,256]{1,0:T(8,128)S(1)} %bitcast.6, ...), custom_call_target="tpu_custom_call" | custom-call | flops 134217728 | bytes 2097152 | tf_op jit(solution)/shard_map/pallas_call | solution.py:188
  10.5 5.5 %collective-permute-done.refs_0_ = bf16[2,256,128]{2,1,0:T(8,128)(2,1)S(1)} collective-permute-done((bf16[2,256,128]{2,1,0:T(8,128)(2,1)S(1)}, bf16[2,256,128]{2,1,0:T(8,128)(2,1)S(1)}, u32[]{:S(2)}, u32[]{:S(2)}) %collective-permute-start) | collective-permute-done | bytes 131104 | tf_op jit(solution)/shard_map/ppermute | solution.py:450
  16.0 0.0 collective-permute-done.1.refs_1_
  16.0 0.0 copy-done.5
  16.0 0.0 copy-done.6
  16.0 1.2 %shard_map.150 = (bf16[2,256,128]{2,1,0:T(8,128)(2,1)S(1)}, bf16[256,128]{1,0:T(8,128)(2,1)S(1)}, bf16[256,128]{1,0:T(8,128)(2,1)S(1)}) custom-call(bf16[2,512,128]{2,1,0:T(8,128)(2,1)S(1)} %get-tuple-element.18.zlt_ref, bf16[2,256,128]{2,1,0:T(8,128)(2,1)S(1)} %collective-permute-done.refs_0_, bf16[2,256,128]{2,1,0:T(8,128)(2,1)S(1)} %collective-permute-done.1.refs_1_, ...), custom_call_target="tpu_custom_call" | custom-call | flops 268435456 | bytes 2097152 | tf_op jit(solution)/shard_map/pallas_call | solution.py:278
  17.2 0.1 collective-permute-start.2
  17.3 0.2 collective-permute-start.3
  17.6 1.1 %collective-permute-done.2.refs_1_ = bf16[2,256,128]{2,1,0:T(8,128)(2,1)S(1)} collective-permute-done((bf16[2,256,128]{2,1,0:T(8,128)(2,1)S(1)}, bf16[2,256,128]{2,1,0:T(8,128)(2,1)S(1)}, u32[]{:S(2)}, u32[]{:S(2)}) %collective-permute-start.2) | collective-permute-done | bytes 131104 | tf_op jit(solution)/shard_map/ppermute | solution.py:450
  18.7 3.2 %collective-permute-start.6 = (bf16[2,256,128]{2,1,0:T(8,128)(2,1)S(1)}, bf16[2,256,128]{2,1,0:T(8,128)(2,1)S(1)}, u32[]{:S(2)}, u32[]{:S(2)}) collective-permute-start(bf16[2,256,128]{2,1,0:T(8,128)(2,1)S(1)} %pad_maximum_fusion), channel_id=1, source_target_pairs={{0,0},{6,1},{8,2},{14,3},{2,4},{5,5},{11,6},{12,7},{3,8},{4,9},{10... | collective-permute-start | bytes 393224 | tf_op jit(solution)/shard_map/ppermute | solution.py:450
  21.9 0.1 collective-permute-start.5
  21.9 0.0 collective-permute-done.3.refs_2_
  22.0 2.9 %collective-permute-start.4 = (bf16[256,128]{1,0:T(8,128)(2,1)S(1)}, bf16[256,128]{1,0:T(8,128)(2,1)S(1)}, u32[]{:S(2)}, u32[]{:S(2)}) collective-permute-start(bf16[256,128]{1,0:T(8,128)(2,1)S(1)} %collective-permute-done.3.refs_2_), channel_id=1, source_target_pairs={{1,0},{0,1},{3,2},{2,3},{5,4},{4,5},{7,6},{6,7},{9,8},{8,9},{11,10... | collective-permute-start | bytes 196616 | tf_op jit(solution)/shard_map/ppermute | solution.py:450
  24.8 0.9 %collective-permute-done.4.refs_3_ = bf16[256,128]{1,0:T(8,128)(2,1)S(1)} collective-permute-done((bf16[256,128]{1,0:T(8,128)(2,1)S(1)}, bf16[256,128]{1,0:T(8,128)(2,1)S(1)}, u32[]{:S(2)}, u32[]{:S(2)}) %collective-permute-start.4) | collective-permute-done | bytes 65568 | tf_op jit(solution)/shard_map/ppermute | solution.py:450
  25.7 5.7 %collective-permute-done.6.refs_4_ = bf16[2,256,128]{2,1,0:T(8,128)(2,1)S(1)} collective-permute-done((bf16[2,256,128]{2,1,0:T(8,128)(2,1)S(1)}, bf16[2,256,128]{2,1,0:T(8,128)(2,1)S(1)}, u32[]{:S(2)}, u32[]{:S(2)}) %collective-permute-start.6) | collective-permute-done | bytes 131104 | tf_op jit(solution)/shard_map/ppermute | solution.py:450
  31.5 0.0 copy-done.7
  31.5 0.7 %shard_map.151 = (f32[256,128]{1,0:T(8,128)S(1)}, f32[256,128]{1,0:T(8,128)S(1)}) custom-call(bf16[2,256,128]{2,1,0:T(8,128)(2,1)S(1)} %get-tuple-element.26.refs_0_, bf16[2,256,128]{2,1,0:T(8,128)(2,1)S(1)} %collective-permute-done.2.refs_1_, bf16[256,128]{1,0:T(8,128)(2,1)S(1)} %collective-permute-done.3.refs_2_, ...), custom_call_target="tpu_custom_call" | custom-call | flops 67108864 | bytes 1048576 | tf_op jit(solution)/shard_map/pallas_call | solution.py:399
  32.2 0.0 collective-permute-done.5.refs_4_
  32.2 0.0 copy-done.1
  32.2 0.0 copy-done.2
  32.3 0.0 copy-done.8
  32.3 1.9 %shard_map.152 = bf16[16,16,128]{2,1,0:T(8,128)(2,1)} custom-call(bf16[2,256,128]{2,1,0:T(8,128)(2,1)S(1)} %get-tuple-element.26.refs_0_, bf16[2,256,128]{2,1,0:T(8,128)(2,1)S(1)} %collective-permute-done.2.refs_1_, bf16[256,128]{1,0:T(8,128)(2,1)S(1)} %collective-permute-done.3.refs_2_, bf16[256,128]{1,0:T(8,128)(2,1)S(1)} %collective-permute-done.4.refs_3_, ...), custom_call_target="tpu_custom_call" | custom-call | flops 134217728 | bytes 2097152 | tf_op jit(solution)/shard_map/pallas_call | solution.py:410
  (3 shorter events, 0.0 us)
Async XLA Ops:
  0.0 1.6 %copy-start.12 = (bf16[256,16,256]{2,1,0:T(8,128)(2,1)S(1)}, bf16[256,16,256]{2,1,0:T(8,128)(2,1)}, u32[]{:S(2)}) copy-start(bf16[256,16,256]{2,1,0:T(8,128)(2,1)} %x_ref.3) | copy-start | bytes 6291460
  0.0 0.9 %copy-start.13 = (bf16[256,32]{0,1:T(8,128)(2,1)S(1)}, bf16[256,32]{0,1:T(8,128)(2,1)}, u32[]{:S(2)}) copy-start(bf16[256,32]{0,1:T(8,128)(2,1)} %param.21) | copy-start | bytes 49156
  1.6 5.6 %copy-start.14 = (bf16[256,32]{0,1:T(8,128)(2,1)S(1)}, bf16[256,32]{0,1:T(8,128)(2,1)}, u32[]{:S(2)}) copy-start(bf16[256,32]{0,1:T(8,128)(2,1)} %param.20) | copy-start | bytes 49156
  3.5 3.8 %copy-start.3 = (s32[256,64]{0,1:T(8,128)S(1)}, s32[256,64]{0,1:T(8,128)}, u32[]{:S(2)}) copy-start(s32[256,64]{0,1:T(8,128)} %param.16) | copy-start | bytes 196612
  3.5 12.5 %collective-permute-start = (bf16[2,256,128]{2,1,0:T(8,128)(2,1)S(1)}, bf16[2,256,128]{2,1,0:T(8,128)(2,1)S(1)}, u32[]{:S(2)}, u32[]{:S(2)}) collective-permute-start(bf16[2,256,128]{2,1,0:T(8,128)(2,1)S(1)} %get-tuple-element.19), channel_id=1, source_target_pairs={{0,0},{6,1},{8,2},{14,3},{2,4},{5,5},{11,6},{12,7},{3,8},{4,9},{10... | collective-permute-start | bytes 393224 | tf_op jit(solution)/shard_map/ppermute | solution.py:450
  7.1 8.9 %collective-permute-start.1 = (bf16[2,256,128]{2,1,0:T(8,128)(2,1)S(1)}, bf16[2,256,128]{2,1,0:T(8,128)(2,1)S(1)}, u32[]{:S(2)}, u32[]{:S(2)}) collective-permute-start(bf16[2,256,128]{2,1,0:T(8,128)(2,1)S(1)} %get-tuple-element.20), channel_id=1, source_target_pairs={{2,0},{4,1},{10,2},{12,3},{0,4},{7,5},{9,6},{14,7},{1,8},{6,9},{8,... | collective-permute-start | bytes 393224 | tf_op jit(solution)/shard_map/ppermute | solution.py:450
  7.3 2.2 %copy-start = (f32[32,32,128]{2,1,0:T(8,128)S(1)}, f32[32,32,128]{2,1,0:T(8,128)}, u32[]{:S(2)}) copy-start(f32[32,32,128]{2,1,0:T(8,128)} %proj_ref.1) | copy-start | bytes 1572868
  7.3 2.2 %copy-start.4 = (bf16[16,16,128]{2,1,0:T(8,128)(2,1)S(1)}, bf16[16,16,128]{2,1,0:T(8,128)(2,1)}, u32[]{:S(2)}) copy-start(bf16[16,16,128]{2,1,0:T(8,128)(2,1)} %pair_ref.1) | copy-start | bytes 196612
  7.3 2.2 %copy-start.9 = (bf16[66,128]{1,0:T(8,128)(2,1)S(1)}, bf16[66,128]{1,0:T(8,128)(2,1)}, u32[]{:S(2)}) copy-start(bf16[66,128]{1,0:T(8,128)(2,1)} %table_ref.1) | copy-start | bytes 50692
  7.3 2.2 %copy-start.10 = (s32[64]{0:T(128)S(1)}, s32[64]{0:T(128)}, u32[]{:S(2)}) copy-start(s32[64]{0:T(128)} %param.18) | copy-start | bytes 772
  7.3 2.2 %copy-start.11 = (s32[64]{0:T(128)S(1)}, s32[64]{0:T(128)}, u32[]{:S(2)}) copy-start(s32[64]{0:T(128)} %param.19) | copy-start | bytes 772
  7.3 8.7 %copy-start.5 = (bf16[128,256]{1,0:T(8,128)(2,1)S(1)}, bf16[128,256]{1,0:T(8,128)(2,1)}, u32[]{:S(2)}) copy-start(bf16[128,256]{1,0:T(8,128)(2,1)} %refs_7_.1) | copy-start | bytes 196612
  7.4 8.7 %copy-start.6 = (bf16[128,256]{1,0:T(8,128)(2,1)S(1)}, bf16[128,256]{1,0:T(8,128)(2,1)}, u32[]{:S(2)}) copy-start(bf16[128,256]{1,0:T(8,128)(2,1)} %refs_8_.2) | copy-start | bytes 196612
  9.4 22.0 %copy-start.7 = (bf16[128,128]{1,0:T(8,128)(2,1)S(1)}, bf16[128,128]{1,0:T(8,128)(2,1)}, u32[]{:S(2)}) copy-start(bf16[128,128]{1,0:T(8,128)(2,1)} %refs_6_.1) | copy-start | bytes 98308
  9.4 22.8 %copy-start.1 = (bf16[128,512]{1,0:T(8,128)(2,1)S(1)}, bf16[128,512]{1,0:T(8,128)(2,1)}, u32[]{:S(2)}) copy-start(bf16[128,512]{1,0:T(8,128)(2,1)} %refs_9_.1) | copy-start | bytes 393220
  9.5 22.8 %copy-start.2 = (bf16[512,128]{1,0:T(8,128)(2,1)S(1)}, bf16[512,128]{1,0:T(8,128)(2,1)}, u32[]{:S(2)}) copy-start(bf16[512,128]{1,0:T(8,128)(2,1)} %refs_10_.1) | copy-start | bytes 393220
  9.5 22.8 %copy-start.8 = (bf16[128,128]{1,0:T(8,128)(2,1)S(1)}, bf16[128,128]{1,0:T(8,128)(2,1)}, u32[]{:S(2)}) copy-start(bf16[128,128]{1,0:T(8,128)(2,1)} %refs_8_.3) | copy-start | bytes 98308
  17.2 1.4 %collective-permute-start.2 = (bf16[2,256,128]{2,1,0:T(8,128)(2,1)S(1)}, bf16[2,256,128]{2,1,0:T(8,128)(2,1)S(1)}, u32[]{:S(2)}, u32[]{:S(2)}) collective-permute-start(bf16[2,256,128]{2,1,0:T(8,128)(2,1)S(1)} %get-tuple-element.26.refs_0_), channel_id=1, source_target_pairs={{1,0},{0,1},{3,2},{2,3},{5,4},{4,5},{7,6},{6,7},{9,8},{8,9},{11,10... | collective-permute-start | bytes 393224 | tf_op jit(solution)/shard_map/ppermute | solution.py:450
  17.3 4.6 %collective-permute-start.3 = (bf16[256,128]{1,0:T(8,128)(2,1)S(1)}, bf16[256,128]{1,0:T(8,128)(2,1)S(1)}, u32[]{:S(2)}, u32[]{:S(2)}) collective-permute-start(bf16[256,128]{1,0:T(8,128)(2,1)S(1)} %get-tuple-element.27), channel_id=1, source_target_pairs={{2,0},{3,1},{0,2},{1,3},{6,4},{7,5},{4,6},{5,7},{10,8},{11,9},{8,1... | collective-permute-start | bytes 196616 | tf_op jit(solution)/shard_map/ppermute | solution.py:450
  18.7 12.8 %collective-permute-start.6 = (bf16[2,256,128]{2,1,0:T(8,128)(2,1)S(1)}, bf16[2,256,128]{2,1,0:T(8,128)(2,1)S(1)}, u32[]{:S(2)}, u32[]{:S(2)}) collective-permute-start(bf16[2,256,128]{2,1,0:T(8,128)(2,1)S(1)} %pad_maximum_fusion), channel_id=1, source_target_pairs={{0,0},{6,1},{8,2},{14,3},{2,4},{5,5},{11,6},{12,7},{3,8},{4,9},{10... | collective-permute-start | bytes 393224 | tf_op jit(solution)/shard_map/ppermute | solution.py:450
  21.9 10.4 %collective-permute-start.5 = (bf16[2,256,128]{2,1,0:T(8,128)(2,1)S(1)}, bf16[2,256,128]{2,1,0:T(8,128)(2,1)S(1)}, u32[]{:S(2)}, u32[]{:S(2)}) collective-permute-start(bf16[2,256,128]{2,1,0:T(8,128)(2,1)S(1)} %pad_maximum_fusion), channel_id=1, source_target_pairs={{2,0},{4,1},{10,2},{12,3},{0,4},{7,5},{9,6},{14,7},{1,8},{6,9},{8,... | collective-permute-start | bytes 393224 | tf_op jit(solution)/shard_map/ppermute | solution.py:450
  22.0 3.8 %collective-permute-start.4 = (bf16[256,128]{1,0:T(8,128)(2,1)S(1)}, bf16[256,128]{1,0:T(8,128)(2,1)S(1)}, u32[]{:S(2)}, u32[]{:S(2)}) collective-permute-start(bf16[256,128]{1,0:T(8,128)(2,1)S(1)} %collective-permute-done.3.refs_2_), channel_id=1, source_target_pairs={{1,0},{0,1},{3,2},{2,3},{5,4},{4,5},{7,6},{6,7},{9,8},{8,9},{11,10... | collective-permute-start | bytes 196616 | tf_op jit(solution)/shard_map/ppermute | solution.py:450

commit v20 on v18

--- a/solution.py
+++ b/solution.py
@@ -9,7 +9,7 @@
 
 REL_CLIP = 32
 LANES = 128
-PARTS = 2
+PARTS = 1
 EPSILON = 1e-05
 BF16 = jnp.bfloat16
 F32 = jnp.float32
@@ -22,6 +22,15 @@
     centered = values - average
     spread = jnp.mean(centered * centered, axis=-1, keepdims=True)
     return centered * lax.rsqrt(spread + EPSILON)
+
+
+def matmul_norm(values):
+    channels = values.shape[-1]
+    share = jnp.full((channels, LANES), 1.0 / channels, BF16)
+    wide = values.astype(F32)
+    centered = wide - dot(values, share)
+    spread = dot((centered * centered).astype(BF16), share)
+    return (centered * lax.rsqrt(spread + EPSILON)).astype(BF16)
 
 
 def dot(left, right):
@@ -375,10 +384,10 @@
     (start_ref, one_ref, gate_ref, out_ref, up_ref, down_ref, result_ref, left_scr, sum_scr) = refs
     add_terms(sum_scr, start_ref, lefts, rights, steps, ratio, cols, left_scr)
     one = one_ref[...].astype(F32)
-    hidden = layer_norm(sum_scr[...].astype(BF16).astype(F32)).astype(BF16)
-    two = (one + gate_ref[...] * dot(hidden, out_ref[...])).astype(BF16).astype(F32)
-    wide = jnp.maximum(dot(layer_norm(two).astype(BF16), up_ref[...]), 0.0).astype(BF16)
-    result = (two + dot(wide, down_ref[...])).astype(BF16)
+    hidden = matmul_norm(sum_scr[...].astype(BF16))
+    two = (one + gate_ref[...] * dot(hidden, out_ref[...])).astype(BF16)
+    wide = jnp.maximum(dot(matmul_norm(two), up_ref[...]), 0.0).astype(BF16)
+    result = (two.astype(F32) + dot(wide, down_ref[...])).astype(BF16)
     result_ref[...] = result.reshape(result_ref.shape)
 
 

time: 32.8 us -> 32.5 us (level)
  the two profiles are of different devices: /device:TPU:1 before, /device:TPU:3 now
where the time goes in v20:
time: 32.5 us; the launch traced here: 32.3 us
  starting transfers between devices  12.5 us (38%)
  Pallas kernels  8.98 us (28%)
  waiting for transfers between devices  8.94 us (28%)
  local copies, waits for them, and re-layouts  1.62 us (5%)
    ppermute x6, starting transfers between devices, fetch(): return lax.ppermute(values, ('dap', 'sub'), perm)  12.5 us
    ppermute x6, waiting for transfers between devices, fetch(): return lax.ppermute(values, ('dap', 'sub'), perm)  8.94 us
    pallas_call x2, Pallas kernels, factor(): pl.pallas_call(functools.partial(factor_kernel, mask is not None, hidden)...  3.96 us
    pallas_call x1, Pallas kernels, triangle_update(): pl.pallas_call(functools.partial(last_kernel, late, twos, ratio, cols), o...  2.03 us
    unnamed x30, local copies, waits for them, and re-layouts  1.61 us
    pallas_call x1, Pallas kernels, pair_update(): pl.pallas_call(functools.partial(pair_kernel, ratio, hidden), out_shape=(...  1.19 us
    pallas_call x1, Pallas kernels, prepare(): pl.pallas_call(prepare_kernel, out_shape=(jax.ShapeDtypeStruct((zl.shape[...  0.94 us
    pallas_call x1, Pallas kernels, triangle_update(): pl.pallas_call(functools.partial(first_kernel, early, twos, ratio, cols),...  0.73 us
  transfers between devices with their start and end apart: 6, of which 5 were waited for; matrix products, arithmetic and copies ran while one was open for 0% of the time, Pallas kernels for 12%

profile of v20, /device:TPU:3, one launch (start us, length us, event | category | flops | bytes accessed | tf_op | source)
XLA Modules:
  0.0 32.3 jit_solution(6396880963460310283)
XLA Ops:
  0.0 0.0 copy-start.12
  0.0 0.0 copy-start.13
  0.0 0.9 %copy-done.13 = bf16[256,32]{0,1:T(8,128)(2,1)S(1)} copy-done((bf16[256,32]{0,1:T(8,128)(2,1)S(1)}, bf16[256,32]{0,1:T(8,128)(2,1)}, u32[]{:S(2)}) %copy-start.13) | copy-done | bytes 16408
  0.9 0.1 shard_map.148.weight_ref
  0.9 0.7 %copy-done.12 = bf16[256,16,256]{2,1,0:T(8,128)(2,1)S(1)} copy-done((bf16[256,16,256]{2,1,0:T(8,128)(2,1)S(1)}, bf16[256,16,256]{2,1,0:T(8,128)(2,1)}, u32[]{:S(2)}) %copy-start.12) | copy-done | bytes 2097176
  1.6 0.0 copy-start.14
  1.6 1.9 %shard_map.149 = bf16[4,256,128]{2,1,0:T(8,128)(2,1)S(1)} custom-call(bf16[256,16,256]{2,1,0:T(8,128)(2,1)S(1)} %copy-done.12, bf16[256,128]{1,0:T(8,128)(2,1)S(1)} %shard_map.148.weight_ref), custom_call_target="tpu_custom_call" | custom-call | flops 1073741824 | bytes 4194304 | tf_op jit(solution)/shard_map/pallas_call | solution.py:124
  3.5 0.0 copy-start.3
  3.5 4.9 %collective-permute-start = (bf16[4,256,128]{2,1,0:T(8,128)(2,1)S(1)}, bf16[4,256,128]{2,1,0:T(8,128)(2,1)S(1)}, u32[]{:S(2)}, u32[]{:S(2)}) collective-permute-start(bf16[4,256,128]{2,1,0:T(8,128)(2,1)S(1)} %shard_map.149), channel_id=1, source_target_pairs={{0,0},{6,1},{8,2},{14,3},{2,4},{5,5},{11,6},{12,7},{3,8},{4,9},{10... | collective-permute-start | bytes 786440 | tf_op jit(solution)/shard_map/ppermute | solution.py:459
  8.4 0.0 copy-done.14
  8.4 0.1 shard_map.145.weight_ref
  8.5 0.0 copy-start
  8.5 0.0 copy-start.4
  8.5 0.0 copy-start.9
  8.5 0.0 copy-start.10
  8.5 0.0 copy-start.11
  8.6 0.0 copy-done.3
  8.6 0.0 copy-start.5
  8.6 0.0 copy-start.6
  8.6 2.1 %shard_map.146.zl_ref = bf16[4,256,128]{2,1,0:T(8,128)(2,1)S(1)} custom-call(bf16[256,16,256]{2,1,0:T(8,128)(2,1)S(1)} %copy-done.12, bf16[256,128]{1,0:T(8,128)(2,1)S(1)} %shard_map.145.weight_ref, s32[64,256]{1,0:T(8,128)S(1)} %bitcast.5), custom_call_target="tpu_custom_call" | custom-call | flops 1073741824 | bytes 4194304 | tf_op jit(solution)/shard_map/pallas_call | solution.py:124
  10.7 0.0 copy-start.7
  10.7 0.0 copy-start.1
  10.7 0.0 copy-start.2
  10.7 0.0 copy-start.8
  10.7 0.0 copy-done
  10.7 0.0 copy-done.4
  10.7 0.0 copy-done.9
  10.7 0.0 copy-done.10
  10.8 0.0 copy-done.11
  10.8 0.9 %shard_map.147 = (bf16[2,512,128]{2,1,0:T(8,128)(2,1)S(1)}, f32[256,128]{1,0:T(8,128)S(1)}, f32[256,128]{1,0:T(8,128)S(1)}, f32[256,128]{1,0:T(8,128)S(1)}, bf16...) custom-call(bf16[4,256,128]{2,1,0:T(8,128)(2,1)S(1)} %shard_map.146.zl_ref, s32[64,256]{1,0:T(8,128)S(1)} %bitcast.6, ...), custom_call_target="tpu_custom_call" | custom-call | flops 134217728 | bytes 2097152 | tf_op jit(solution)/shard_map/pallas_call | solution.py:197
  11.7 2.4 %collective-permute-done.refs_0_ = bf16[4,256,128]{2,1,0:T(8,128)(2,1)S(1)} collective-permute-done((bf16[4,256,128]{2,1,0:T(8,128)(2,1)S(1)}, bf16[4,256,128]{2,1,0:T(8,128)(2,1)S(1)}, u32[]{:S(2)}, u32[]{:S(2)}) %collective-permute-start) | collective-permute-done | bytes 262176 | tf_op jit(solution)/shard_map/ppermute | solution.py:459
  14.1 0.0 copy-done.5
  14.1 0.0 copy-done.6
  14.1 1.2 %shard_map.150 = (bf16[2,256,128]{2,1,0:T(8,128)(2,1)S(1)}, bf16[256,128]{1,0:T(8,128)(2,1)S(1)}, bf16[256,128]{1,0:T(8,128)(2,1)S(1)}) custom-call(bf16[2,512,128]{2,1,0:T(8,128)(2,1)S(1)} %get-tuple-element.16.zlt_ref, bf16[4,256,128]{2,1,0:T(8,128)(2,1)S(1)} %collective-permute-done.refs_0_, bf16[4,256,128]{2,1,0:T(8,128)(2,1)S(1)} %get-tuple-element.17.refs_1_, ...), custom_call_target="tpu_custom_call" | custom-call | flops 268435456 | bytes 2097152 | tf_op jit(solution)/shard_map/pallas_call | solution.py:287
  15.3 3.2 %collective-permute-start.1 = (bf16[2,256,128]{2,1,0:T(8,128)(2,1)S(1)}, bf16[2,256,128]{2,1,0:T(8,128)(2,1)S(1)}, u32[]{:S(2)}, u32[]{:S(2)}) collective-permute-start(bf16[2,256,128]{2,1,0:T(8,128)(2,1)S(1)} %get-tuple-element.22.refs_0_), channel_id=1, source_target_pairs={{1,0},{0,1},{3,2},{2,3},{5,4},{4,5},{7,6},{6,7},{9,8},{8,9},{11,10... | collective-permute-start | bytes 393224 | tf_op jit(solution)/shard_map/ppermute | solution.py:459
  18.5 0.0 collective-permute-start.2
  18.5 1.0 %collective-permute-done.1.refs_1_ = bf16[2,256,128]{2,1,0:T(8,128)(2,1)S(1)} collective-permute-done((bf16[2,256,128]{2,1,0:T(8,128)(2,1)S(1)}, bf16[2,256,128]{2,1,0:T(8,128)(2,1)S(1)}, u32[]{:S(2)}, u32[]{:S(2)}) %collective-permute-start.1) | collective-permute-done | bytes 131104 | tf_op jit(solution)/shard_map/ppermute | solution.py:459
  19.5 2.4 %collective-permute-start.5 = (bf16[2,256,128]{2,1,0:T(8,128)(2,1)S(1)}, bf16[2,256,128]{2,1,0:T(8,128)(2,1)S(1)}, u32[]{:S(2)}, u32[]{:S(2)}) collective-permute-start(bf16[2,256,128]{2,1,0:T(8,128)(2,1)S(1)} %pad_maximum_fusion), channel_id=1, source_target_pairs={{2,0},{4,1},{10,2},{12,3},{0,4},{7,5},{9,6},{14,7},{1,8},{6,9},{8,... | collective-permute-start | bytes 393224 | tf_op jit(solution)/shard_map/ppermute | solution.py:459
  21.9 1.9 %collective-permute-start.4 = (bf16[2,256,128]{2,1,0:T(8,128)(2,1)S(1)}, bf16[2,256,128]{2,1,0:T(8,128)(2,1)S(1)}, u32[]{:S(2)}, u32[]{:S(2)}) collective-permute-start(bf16[2,256,128]{2,1,0:T(8,128)(2,1)S(1)} %pad_maximum_fusion), channel_id=1, source_target_pairs={{0,0},{6,1},{8,2},{14,3},{2,4},{5,5},{11,6},{12,7},{3,8},{4,9},{10... | collective-permute-start | bytes 393224 | tf_op jit(solution)/shard_map/ppermute | solution.py:459
  23.8 0.0 collective-permute-done.2.refs_2_
  23.8 0.1 collective-permute-start.3
  23.9 1.2 %collective-permute-done.3.refs_3_ = bf16[256,128]{1,0:T(8,128)(2,1)S(1)} collective-permute-done((bf16[256,128]{1,0:T(8,128)(2,1)S(1)}, bf16[256,128]{1,0:T(8,128)(2,1)S(1)}, u32[]{:S(2)}, u32[]{:S(2)}) %collective-permute-start.3) | collective-permute-done | bytes 65568 | tf_op jit(solution)/shard_map/ppermute | solution.py:459
  25.1 1.5 %collective-permute-done.5.refs_4_ = bf16[2,256,128]{2,1,0:T(8,128)(2,1)S(1)} collective-permute-done((bf16[2,256,128]{2,1,0:T(8,128)(2,1)S(1)}, bf16[2,256,128]{2,1,0:T(8,128)(2,1)S(1)}, u32[]{:S(2)}, u32[]{:S(2)}) %collective-permute-start.5) | collective-permute-done | bytes 131104 | tf_op jit(solution)/shard_map/ppermute | solution.py:459
  26.6 0.0 copy-done.7
  26.6 0.7 %shard_map.151 = (f32[256,128]{1,0:T(8,128)S(1)}, f32[256,128]{1,0:T(8,128)S(1)}) custom-call(bf16[2,256,128]{2,1,0:T(8,128)(2,1)S(1)} %get-tuple-element.22.refs_0_, bf16[2,256,128]{2,1,0:T(8,128)(2,1)S(1)} %collective-permute-done.1.refs_1_, bf16[256,128]{1,0:T(8,128)(2,1)S(1)} %collective-permute-done.2.refs_2_, ...), custom_call_target="tpu_custom_call" | custom-call | flops 67108864 | bytes 1048576 | tf_op jit(solution)/shard_map/pallas_call | solution.py:408
  27.4 2.8 %collective-permute-done.4.refs_4_ = bf16[2,256,128]{2,1,0:T(8,128)(2,1)S(1)} collective-permute-done((bf16[2,256,128]{2,1,0:T(8,128)(2,1)S(1)}, bf16[2,256,128]{2,1,0:T(8,128)(2,1)S(1)}, u32[]{:S(2)}, u32[]{:S(2)}) %collective-permute-start.4) | collective-permute-done | bytes 131104 | tf_op jit(solution)/shard_map/ppermute | solution.py:459
  30.2 0.0 copy-done.1
  30.2 0.0 copy-done.2
  30.2 0.0 copy-done.8
  30.2 2.0 %shard_map.152 = bf16[16,16,128]{2,1,0:T(8,128)(2,1)} custom-call(bf16[2,256,128]{2,1,0:T(8,128)(2,1)S(1)} %get-tuple-element.22.refs_0_, bf16[2,256,128]{2,1,0:T(8,128)(2,1)S(1)} %collective-permute-done.1.refs_1_, bf16[256,128]{1,0:T(8,128)(2,1)S(1)} %collective-permute-done.2.refs_2_, bf16[256,128]{1,0:T(8,128)(2,1)S(1)} %collective-permute-done.3.refs_3_, ...), custom_call_target="tpu_custom_call" | custom-call | flops 134217728 | bytes 2097152 | tf_op jit(solution)/shard_map/pallas_call | solution.py:419
  (3 shorter events, 0.0 us)
Async XLA Ops:
  0.0 1.6 %copy-start.12 = (bf16[256,16,256]{2,1,0:T(8,128)(2,1)S(1)}, bf16[256,16,256]{2,1,0:T(8,128)(2,1)}, u32[]{:S(2)}) copy-start(bf16[256,16,256]{2,1,0:T(8,128)(2,1)} %x_ref.3) | copy-start | bytes 6291460
  0.0 0.9 %copy-start.13 = (bf16[256,32]{0,1:T(8,128)(2,1)S(1)}, bf16[256,32]{0,1:T(8,128)(2,1)}, u32[]{:S(2)}) copy-start(bf16[256,32]{0,1:T(8,128)(2,1)} %param.21) | copy-start | bytes 49156
  1.6 6.8 %copy-start.14 = (bf16[256,32]{0,1:T(8,128)(2,1)S(1)}, bf16[256,32]{0,1:T(8,128)(2,1)}, u32[]{:S(2)}) copy-start(bf16[256,32]{0,1:T(8,128)(2,1)} %param.20) | copy-start | bytes 49156
  3.5 5.0 %copy-start.3 = (s32[256,64]{0,1:T(8,128)S(1)}, s32[256,64]{0,1:T(8,128)}, u32[]{:S(2)}) copy-start(s32[256,64]{0,1:T(8,128)} %param.16) | copy-start | bytes 196612
  3.5 10.6 %collective-permute-start = (bf16[4,256,128]{2,1,0:T(8,128)(2,1)S(1)}, bf16[4,256,128]{2,1,0:T(8,128)(2,1)S(1)}, u32[]{:S(2)}, u32[]{:S(2)}) collective-permute-start(bf16[4,256,128]{2,1,0:T(8,128)(2,1)S(1)} %shard_map.149), channel_id=1, source_target_pairs={{0,0},{6,1},{8,2},{14,3},{2,4},{5,5},{11,6},{12,7},{3,8},{4,9},{10... | collective-permute-start | bytes 786440 | tf_op jit(solution)/shard_map/ppermute | solution.py:459
  8.5 2.2 %copy-start = (f32[32,32,128]{2,1,0:T(8,128)S(1)}, f32[32,32,128]{2,1,0:T(8,128)}, u32[]{:S(2)}) copy-start(f32[32,32,128]{2,1,0:T(8,128)} %proj_ref.1) | copy-start | bytes 1572868
  8.5 2.2 %copy-start.4 = (bf16[16,16,128]{2,1,0:T(8,128)(2,1)S(1)}, bf16[16,16,128]{2,1,0:T(8,128)(2,1)}, u32[]{:S(2)}) copy-start(bf16[16,16,128]{2,1,0:T(8,128)(2,1)} %pair_ref.1) | copy-start | bytes 196612
  8.5 2.2 %copy-start.9 = (bf16[66,128]{1,0:T(8,128)(2,1)S(1)}, bf16[66,128]{1,0:T(8,128)(2,1)}, u32[]{:S(2)}) copy-start(bf16[66,128]{1,0:T(8,128)(2,1)} %table_ref.1) | copy-start | bytes 50692
  8.5 2.2 %copy-start.10 = (s32[64]{0:T(128)S(1)}, s32[64]{0:T(128)}, u32[]{:S(2)}) copy-start(s32[64]{0:T(128)} %param.18) | copy-start | bytes 772
  8.5 2.2 %copy-start.11 = (s32[64]{0:T(128)S(1)}, s32[64]{0:T(128)}, u32[]{:S(2)}) copy-start(s32[64]{0:T(128)} %param.19) | copy-start | bytes 772
  8.6 5.5 %copy-start.5 = (bf16[128,256]{1,0:T(8,128)(2,1)S(1)}, bf16[128,256]{1,0:T(8,128)(2,1)}, u32[]{:S(2)}) copy-start(bf16[128,256]{1,0:T(8,128)(2,1)} %refs_6_.2) | copy-start | bytes 196612
  8.6 5.5 %copy-start.6 = (bf16[128,256]{1,0:T(8,128)(2,1)S(1)}, bf16[128,256]{1,0:T(8,128)(2,1)}, u32[]{:S(2)}) copy-start(bf16[128,256]{1,0:T(8,128)(2,1)} %refs_7_.1) | copy-start | bytes 196612
  10.7 16.0 %copy-start.7 = (bf16[128,128]{1,0:T(8,128)(2,1)S(1)}, bf16[128,128]{1,0:T(8,128)(2,1)}, u32[]{:S(2)}) copy-start(bf16[128,128]{1,0:T(8,128)(2,1)} %refs_6_.3) | copy-start | bytes 98308
  10.7 19.6 %copy-start.1 = (bf16[128,512]{1,0:T(8,128)(2,1)S(1)}, bf16[128,512]{1,0:T(8,128)(2,1)}, u32[]{:S(2)}) copy-start(bf16[128,512]{1,0:T(8,128)(2,1)} %refs_9_.1) | copy-start | bytes 393220
  10.7 19.5 %copy-start.2 = (bf16[512,128]{1,0:T(8,128)(2,1)S(1)}, bf16[512,128]{1,0:T(8,128)(2,1)}, u32[]{:S(2)}) copy-start(bf16[512,128]{1,0:T(8,128)(2,1)} %refs_10_.1) | copy-start | bytes 393220
  10.7 19.5 %copy-start.8 = (bf16[128,128]{1,0:T(8,128)(2,1)S(1)}, bf16[128,128]{1,0:T(8,128)(2,1)}, u32[]{:S(2)}) copy-start(bf16[128,128]{1,0:T(8,128)(2,1)} %refs_8_.1) | copy-start | bytes 98308
  15.3 4.2 %collective-permute-start.1 = (bf16[2,256,128]{2,1,0:T(8,128)(2,1)S(1)}, bf16[2,256,128]{2,1,0:T(8,128)(2,1)S(1)}, u32[]{:S(2)}, u32[]{:S(2)}) collective-permute-start(bf16[2,256,128]{2,1,0:T(8,128)(2,1)S(1)} %get-tuple-element.22.refs_0_), channel_id=1, source_target_pairs={{1,0},{0,1},{3,2},{2,3},{5,4},{4,5},{7,6},{6,7},{9,8},{8,9},{11,10... | collective-permute-start | bytes 393224 | tf_op jit(solution)/shard_map/ppermute | solution.py:459
  18.5 5.3 %collective-permute-start.2 = (bf16[256,128]{1,0:T(8,128)(2,1)S(1)}, bf16[256,128]{1,0:T(8,128)(2,1)S(1)}, u32[]{:S(2)}, u32[]{:S(2)}) collective-permute-start(bf16[256,128]{1,0:T(8,128)(2,1)S(1)} %get-tuple-element.23), channel_id=1, source_target_pairs={{2,0},{3,1},{0,2},{1,3},{6,4},{7,5},{4,6},{5,7},{10,8},{11,9},{8,1... | collective-permute-start | bytes 196616 | tf_op jit(solution)/shard_map/ppermute | solution.py:459
  19.5 7.1 %collective-permute-start.5 = (bf16[2,256,128]{2,1,0:T(8,128)(2,1)S(1)}, bf16[2,256,128]{2,1,0:T(8,128)(2,1)S(1)}, u32[]{:S(2)}, u32[]{:S(2)}) collective-permute-start(bf16[2,256,128]{2,1,0:T(8,128)(2,1)S(1)} %pad_maximum_fusion), channel_id=1, source_target_pairs={{2,0},{4,1},{10,2},{12,3},{0,4},{7,5},{9,6},{14,7},{1,8},{6,9},{8,... | collective-permute-start | bytes 393224 | tf_op jit(solution)/shard_map/ppermute | solution.py:459
  21.9 8.4 %collective-permute-start.4 = (bf16[2,256,128]{2,1,0:T(8,128)(2,1)S(1)}, bf16[2,256,128]{2,1,0:T(8,128)(2,1)S(1)}, u32[]{:S(2)}, u32[]{:S(2)}) collective-permute-start(bf16[2,256,128]{2,1,0:T(8,128)(2,1)S(1)} %pad_maximum_fusion), channel_id=1, source_target_pairs={{0,0},{6,1},{8,2},{14,3},{2,4},{5,5},{11,6},{12,7},{3,8},{4,9},{10... | collective-permute-start | bytes 393224 | tf_op jit(solution)/shard_map/ppermute | solution.py:459
  23.8 1.3 %collective-permute-start.3 = (bf16[256,128]{1,0:T(8,128)(2,1)S(1)}, bf16[256,128]{1,0:T(8,128)(2,1)S(1)}, u32[]{:S(2)}, u32[]{:S(2)}) collective-permute-start(bf16[256,128]{1,0:T(8,128)(2,1)S(1)} %collective-permute-done.2.refs_2_), channel_id=1, source_target_pairs={{1,0},{0,1},{3,2},{2,3},{5,4},{4,5},{7,6},{6,7},{9,8},{8,9},{11,10... | collective-permute-start | bytes 196616 | tf_op jit(solution)/shard_map/ppermute | solution.py:459

commit v21 on v18

--- a/solution.py
+++ b/solution.py
@@ -9,7 +9,7 @@
 
 REL_CLIP = 32
 LANES = 128
-PARTS = 2
+PARTS = 1
 EPSILON = 1e-05
 BF16 = jnp.bfloat16
 F32 = jnp.float32
@@ -53,19 +53,41 @@
 
 
 def repeat_kernel(weight_ref, out_ref):
-    rep = LANES // weight_ref.shape[0]
-    out_ref[...] = jnp.concatenate([weight_ref[...]] * rep, axis=0).T
+    hidden, channels = weight_ref.shape
+    rep = LANES // hidden
+    wide = jnp.concatenate([weight_ref[...]] * rep, axis=0).T
+    block = over(iota((channels, LANES), 1), hidden)
+    for k in range(rep):
+        out_ref[k * channels : (k + 1) * channels, :] = jnp.where(block == k, wide, 0)
 
 
 def repeat_weight(weight):
+    hidden, channels = weight.shape
     return pl.pallas_call(
         repeat_kernel,
-        out_shape=jax.ShapeDtypeStruct((weight.shape[1], LANES), BF16),
+        out_shape=jax.ShapeDtypeStruct((channels * LANES // hidden, LANES), BF16),
         in_specs=[vmem()],
         out_specs=vmem(),
         compiler_params=pltpu.CompilerParams(vmem_limit_bytes=2 << 20),
         cost_estimate=pl.CostEstimate(flops=1 << 30, bytes_accessed=1 << 17, transcendentals=0),
     )(weight)
+
+
+def exchange(s0, s1, s2, s3):
+    lane = iota(s0.shape, 1)
+    block = LANES // 4
+    odd = within(over(lane, block), 2) == 1
+    upper = over(lane, 2 * block) == 1
+    t0 = jnp.where(upper, pltpu.roll(s2, 2 * block, 1), s0)
+    t1 = jnp.where(upper, pltpu.roll(s3, 2 * block, 1), s1)
+    t2 = jnp.where(upper, s2, pltpu.roll(s0, 2 * block, 1))
+    t3 = jnp.where(upper, s3, pltpu.roll(s1, 2 * block, 1))
+    return (
+        jnp.where(odd, pltpu.roll(t1, block, 1), t0),
+        jnp.where(odd, t1, pltpu.roll(t0, 3 * block, 1)),
+        jnp.where(odd, pltpu.roll(t3, block, 1), t2),
+        jnp.where(odd, t3, pltpu.roll(t2, 3 * block, 1)),
+    )
 
 
 def factor_kernel(masked, hidden, x_ref, weight_ref, *refs):
@@ -76,48 +98,60 @@
     _, rows, channels = x_ref.shape
     rep = rows // groups
     width = rows * hidden
-    step = y_scr.shape[1] // rows
+    steps, step = y_scr.shape[0], y_scr.shape[1] // rows
+    quarter = seqs // rep
+    weight = weight_ref[...]
+    sums = dot(jnp.ones((8, channels * rep), BF16), weight)[:1]
     share = jnp.full((channels, LANES), 1.0 / channels, BF16)
-    w = jnp.concatenate([weight_ref[...], share], axis=1)
-    sums = dot(jnp.ones((8, channels), BF16), weight_ref[...])[:1]
-    block = over(iota((step, LANES), 1), hidden)
-    if mask_ref is not None:
+    side = (rep * LANES, LANES)
+    own = over(iota(side, 0), LANES) == over(iota(side, 1), hidden)
+    own = jnp.where(own, 1.0 / channels, 0.0).astype(BF16)
+    block = over(iota((step * rows, LANES), 1), hidden)
+    if masked:
         residues = mask_ref.shape[0]
         column = lax.axis_index("dap") * rows + over(iota((residues, width), 1), hidden)
         lanes_of = (iota((residues, width), 0) == column).astype(BF16)
         live = dot_tn(mask_ref[...].astype(BF16), lanes_of)
-    for turn in range(seqs // step):
-        x = x_ref[turn * step : (turn + 1) * step].reshape(step * rows, channels)
-        y = dot(x, w)
-        mean = y[:, LANES:]
-        square = jnp.zeros_like(mean)
-        for half in range(channels // LANES):
-            centered = x[:, half * LANES : (half + 1) * LANES].astype(F32) - mean
-            square = square + centered * centered
-        scale = lax.rsqrt(dot(square.astype(BF16), share[:LANES]) + EPSILON)
-        y_scr[turn] = (y[:, :LANES] - mean * sums) * scale
-        here = slice(turn * step, (turn + 1) * step)
+    for turn in range(steps):
+        inputs, squares, mean = [], [], None
+        for part in range(rep):
+            first = part * quarter + turn * step
+            x = x_ref[first : first + step].reshape(step * rows, channels)
+            inputs.append(x)
+            average = dot(x, share)
+            mean = average if mean is None else jnp.where(block == part, average, mean)
+            square = jnp.zeros_like(average)
+            for half in range(channels // LANES):
+                centered = x[:, half * LANES : (half + 1) * LANES].astype(F32) - average
+                square = square + centered * centered
+            squares.append(square.astype(BF16))
+        y = dot(jnp.concatenate(inputs, axis=1), weight)
+        scale = lax.rsqrt(dot(jnp.concatenate(squares, axis=1), own) + EPSILON)
+        y_scr[turn] = (y - mean * sums) * scale
         for group in range(groups):
-            z = y_scr[turn, pl.ds(group * rep, step, stride=rows), :]
-            for k in range(1, rep):
-                next_z = y_scr[turn, pl.ds(group * rep + k, step, stride=rows), :]
-                z = jnp.where(block == k, next_z, z)
-            if mask_ref is not None:
-                z = z * live[here, group * LANES : (group + 1) * LANES]
-            z_refs[group // each][group % each, here, :] = z.astype(BF16)
+            taken = [
+                y_scr[turn, pl.ds(group * rep + k, step, stride=rows), :] for k in range(rep)
+            ]
+            for part, z in enumerate(exchange(*taken)):
+                first = part * quarter + turn * step
+                here = slice(first, first + step)
+                if masked:
+                    z = z * live[here, group * LANES : (group + 1) * LANES]
+                z_refs[group // each][group % each, here, :] = z.astype(BF16)
 
 
 def factor(alignment, weight, hidden, parts, mask=None):
     seqs, rows, channels = alignment.shape
-    step = seqs // 2
+    steps = 2
     operands = (alignment, weight) if mask is None else (alignment, weight, mask)
     shape = jax.ShapeDtypeStruct((rows * hidden // LANES // parts, seqs, LANES), BF16)
+    packed = seqs * rows * hidden // LANES
     return pl.pallas_call(
         functools.partial(factor_kernel, mask is not None, hidden),
         out_shape=(shape,) * parts,
         in_specs=[vmem()] * len(operands),
         out_specs=[vmem()] * parts,
-        scratch_shapes=[pltpu.VMEM((seqs // step, step * rows, LANES), F32)],
+        scratch_shapes=[pltpu.VMEM((steps, packed // steps, LANES), F32)],
         compiler_params=pltpu.CompilerParams(vmem_limit_bytes=24 << 20),
         cost_estimate=pl.CostEstimate(
             flops=2 * seqs * rows * channels * 512, bytes_accessed=seqs << 14, transcendentals=0
@@ -217,10 +251,6 @@
     rows = zlt_ref.shape[1] // hidden
     rep = LANES // hidden
     me = lax.axis_index("dap")
-    lane = iota((rows, LANES), 1)
-    odd = (lane // hidden) % 2 == 1
-    upper = lane // (2 * hidden) == 1
-    half = 2 * hidden
     left = jnp.concatenate([zlt_ref[part] for part in range(zlt_ref.shape[0])], axis=1)
     for step in range(ratio):
         block = lax.rem(me + step, ratio)
@@ -237,17 +267,7 @@
                     outer[(quad * rep + k) * rows : (quad * rep + k + 1) * rows, lanes]
                     for k in range(rep)
                 )
-                t0 = jnp.where(upper, pltpu.roll(s2, half, 1), s0)
-                t1 = jnp.where(upper, pltpu.roll(s3, half, 1), s1)
-                t2 = jnp.where(upper, s2, pltpu.roll(s0, half, 1))
-                t3 = jnp.where(upper, s3, pltpu.roll(s1, half, 1))
-                back = LANES - hidden
-                found = (
-                    jnp.where(odd, pltpu.roll(t1, hidden, 1), t0),
-                    jnp.where(odd, t1, pltpu.roll(t0, back, 1)),
-                    jnp.where(odd, pltpu.roll(t3, hidden, 1), t2),
-                    jnp.where(odd, t3, pltpu.roll(t2, back, 1)),
-                )
+                found = exchange(s0, s1, s2, s3)
                 for k in range(rep):
                     first = block * rows * rows + (group * rep + k) * rows
                     if ratio == 1:

time: 32.8 us -> 32.4 us (0.988)
  the two profiles are of different devices: /device:TPU:1 before, /device:TPU:3 now
where the time goes in v21:
time: 32.4 us; the launch traced here: 32.1 us
  starting transfers between devices  12.5 us (39%)
  waiting for transfers between devices  9.07 us (28%)
  Pallas kernels  8.72 us (27%)
  local copies, waits for them, and re-layouts  1.6 us (5%)
    ppermute x6, starting transfers between devices, fetch(): return lax.ppermute(values, ('dap', 'sub'), perm)  12.5 us
    ppermute x6, waiting for transfers between devices, fetch(): return lax.ppermute(values, ('dap', 'sub'), perm)  9.07 us
    pallas_call x2, Pallas kernels, factor(): pl.pallas_call(functools.partial(factor_kernel, mask is not None, hidden)...  3.81 us
    pallas_call x1, Pallas kernels, triangle_update(): pl.pallas_call(functools.partial(last_kernel, late, twos, ratio, cols), o...  1.87 us
    unnamed x30, local copies, waits for them, and re-layouts  1.59 us
    pallas_call x1, Pallas kernels, pair_update(): pl.pallas_call(functools.partial(pair_kernel, ratio, hidden), out_shape=(...  1.19 us
    pallas_call x1, Pallas kernels, prepare(): pl.pallas_call(prepare_kernel, out_shape=(jax.ShapeDtypeStruct((zl.shape[...  0.94 us
    pallas_call x1, Pallas kernels, triangle_update(): pl.pallas_call(functools.partial(first_kernel, early, twos, ratio, cols),...  0.73 us
  transfers between devices with their start and end apart: 6, of which 5 were waited for; matrix products, arithmetic and copies ran while one was open for 0% of the time, Pallas kernels for 11%

profile of v21, /device:TPU:3, one launch (start us, length us, event | category | flops | bytes accessed | tf_op | source)
XLA Modules:
  0.0 32.1 jit_solution(346775055738156928)
XLA Ops:
  0.0 0.0 copy-start.12
  0.0 0.0 copy-start.13
  0.0 0.9 %copy-done.13 = bf16[256,32]{0,1:T(8,128)(2,1)S(1)} copy-done((bf16[256,32]{0,1:T(8,128)(2,1)S(1)}, bf16[256,32]{0,1:T(8,128)(2,1)}, u32[]{:S(2)}) %copy-start.13) | copy-done | bytes 16408
  0.9 0.1 shard_map.148.weight_ref
  1.0 0.6 %copy-done.12 = bf16[256,16,256]{2,1,0:T(8,128)(2,1)S(1)} copy-done((bf16[256,16,256]{2,1,0:T(8,128)(2,1)S(1)}, bf16[256,16,256]{2,1,0:T(8,128)(2,1)}, u32[]{:S(2)}) %copy-start.12) | copy-done | bytes 2097176
  1.6 0.0 copy-start.14
  1.6 1.9 %shard_map.149 = bf16[4,256,128]{2,1,0:T(8,128)(2,1)S(1)} custom-call(bf16[256,16,256]{2,1,0:T(8,128)(2,1)S(1)} %copy-done.12, bf16[1024,128]{1,0:T(8,128)(2,1)S(1)} %shard_map.148.weight_ref), custom_call_target="tpu_custom_call" | custom-call | flops 1073741824 | bytes 4194304 | tf_op jit(solution)/shard_map/pallas_call | solution.py:149
  3.5 0.0 copy-start.3
  3.5 4.9 %collective-permute-start = (bf16[4,256,128]{2,1,0:T(8,128)(2,1)S(1)}, bf16[4,256,128]{2,1,0:T(8,128)(2,1)S(1)}, u32[]{:S(2)}, u32[]{:S(2)}) collective-permute-start(bf16[4,256,128]{2,1,0:T(8,128)(2,1)S(1)} %shard_map.149), channel_id=1, source_target_pairs={{0,0},{6,1},{8,2},{14,3},{2,4},{5,5},{11,6},{12,7},{3,8},{4,9},{10... | collective-permute-start | bytes 786440 | tf_op jit(solution)/shard_map/ppermute | solution.py:470
  8.4 0.0 copy-done.14
  8.4 0.1 shard_map.145.weight_ref
  8.5 0.0 copy-start
  8.5 0.0 copy-start.4
  8.6 0.0 copy-start.9
  8.6 0.0 copy-start.10
  8.6 0.0 copy-start.11
  8.6 0.0 copy-done.3
  8.6 0.0 copy-start.5
  8.6 0.0 copy-start.6
  8.6 1.9 %shard_map.146.zl_ref = bf16[4,256,128]{2,1,0:T(8,128)(2,1)S(1)} custom-call(bf16[256,16,256]{2,1,0:T(8,128)(2,1)S(1)} %copy-done.12, bf16[1024,128]{1,0:T(8,128)(2,1)S(1)} %shard_map.145.weight_ref, s32[64,256]{1,0:T(8,128)S(1)} %bitcast.5), custom_call_target="tpu_custom_call" | custom-call | flops 1073741824 | bytes 4194304 | tf_op jit(solution)/shard_map/pallas_call | solution.py:149
  10.5 0.0 copy-start.7
  10.5 0.0 copy-start.1
  10.6 0.0 copy-start.2
  10.6 0.0 copy-start.8
  10.6 0.0 copy-done
  10.6 0.0 copy-done.4
  10.6 0.0 copy-done.9
  10.6 0.0 copy-done.10
  10.6 0.0 copy-done.11
  10.6 0.9 %shard_map.147 = (bf16[2,512,128]{2,1,0:T(8,128)(2,1)S(1)}, f32[256,128]{1,0:T(8,128)S(1)}, f32[256,128]{1,0:T(8,128)S(1)}, f32[256,128]{1,0:T(8,128)S(1)}, bf16...) custom-call(bf16[4,256,128]{2,1,0:T(8,128)(2,1)S(1)} %shard_map.146.zl_ref, s32[64,256]{1,0:T(8,128)S(1)} %bitcast.6, ...), custom_call_target="tpu_custom_call" | custom-call | flops 134217728 | bytes 2097152 | tf_op jit(solution)/shard_map/pallas_call | solution.py:222
  11.6 2.5 %collective-permute-done.refs_0_ = bf16[4,256,128]{2,1,0:T(8,128)(2,1)S(1)} collective-permute-done((bf16[4,256,128]{2,1,0:T(8,128)(2,1)S(1)}, bf16[4,256,128]{2,1,0:T(8,128)(2,1)S(1)}, u32[]{:S(2)}, u32[]{:S(2)}) %collective-permute-start) | collective-permute-done | bytes 262176 | tf_op jit(solution)/shard_map/ppermute | solution.py:470
  14.1 0.0 copy-done.5
  14.1 0.0 copy-done.6
  14.1 1.2 %shard_map.150 = (bf16[2,256,128]{2,1,0:T(8,128)(2,1)S(1)}, bf16[256,128]{1,0:T(8,128)(2,1)S(1)}, bf16[256,128]{1,0:T(8,128)(2,1)S(1)}) custom-call(bf16[2,512,128]{2,1,0:T(8,128)(2,1)S(1)} %get-tuple-element.16.zlt_ref, bf16[4,256,128]{2,1,0:T(8,128)(2,1)S(1)} %collective-permute-done.refs_0_, bf16[4,256,128]{2,1,0:T(8,128)(2,1)S(1)} %get-tuple-element.17.refs_1_, ...), custom_call_target="tpu_custom_call" | custom-call | flops 268435456 | bytes 2097152 | tf_op jit(solution)/shard_map/pallas_call | solution.py:298
  15.3 3.2 %collective-permute-start.1 = (bf16[2,256,128]{2,1,0:T(8,128)(2,1)S(1)}, bf16[2,256,128]{2,1,0:T(8,128)(2,1)S(1)}, u32[]{:S(2)}, u32[]{:S(2)}) collective-permute-start(bf16[2,256,128]{2,1,0:T(8,128)(2,1)S(1)} %get-tuple-element.22.refs_0_), channel_id=1, source_target_pairs={{1,0},{0,1},{3,2},{2,3},{5,4},{4,5},{7,6},{6,7},{9,8},{8,9},{11,10... | collective-permute-start | bytes 393224 | tf_op jit(solution)/shard_map/ppermute | solution.py:470
  18.5 0.0 collective-permute-start.2
  18.5 1.0 %collective-permute-done.1.refs_1_ = bf16[2,256,128]{2,1,0:T(8,128)(2,1)S(1)} collective-permute-done((bf16[2,256,128]{2,1,0:T(8,128)(2,1)S(1)}, bf16[2,256,128]{2,1,0:T(8,128)(2,1)S(1)}, u32[]{:S(2)}, u32[]{:S(2)}) %collective-permute-start.1) | collective-permute-done | bytes 131104 | tf_op jit(solution)/shard_map/ppermute | solution.py:470
  19.5 2.4 %collective-permute-start.5 = (bf16[2,256,128]{2,1,0:T(8,128)(2,1)S(1)}, bf16[2,256,128]{2,1,0:T(8,128)(2,1)S(1)}, u32[]{:S(2)}, u32[]{:S(2)}) collective-permute-start(bf16[2,256,128]{2,1,0:T(8,128)(2,1)S(1)} %pad_maximum_fusion), channel_id=1, source_target_pairs={{2,0},{4,1},{10,2},{12,3},{0,4},{7,5},{9,6},{14,7},{1,8},{6,9},{8,... | collective-permute-start | bytes 393224 | tf_op jit(solution)/shard_map/ppermute | solution.py:470
  21.9 1.9 %collective-permute-start.4 = (bf16[2,256,128]{2,1,0:T(8,128)(2,1)S(1)}, bf16[2,256,128]{2,1,0:T(8,128)(2,1)S(1)}, u32[]{:S(2)}, u32[]{:S(2)}) collective-permute-start(bf16[2,256,128]{2,1,0:T(8,128)(2,1)S(1)} %pad_maximum_fusion), channel_id=1, source_target_pairs={{0,0},{6,1},{8,2},{14,3},{2,4},{5,5},{11,6},{12,7},{3,8},{4,9},{10... | collective-permute-start | bytes 393224 | tf_op jit(solution)/shard_map/ppermute | solution.py:470
  23.8 0.0 collective-permute-done.2.refs_2_
  23.8 0.1 collective-permute-start.3
  23.9 1.2 %collective-permute-done.3.refs_3_ = bf16[256,128]{1,0:T(8,128)(2,1)S(1)} collective-permute-done((bf16[256,128]{1,0:T(8,128)(2,1)S(1)}, bf16[256,128]{1,0:T(8,128)(2,1)S(1)}, u32[]{:S(2)}, u32[]{:S(2)}) %collective-permute-start.3) | collective-permute-done | bytes 65568 | tf_op jit(solution)/shard_map/ppermute | solution.py:470
  25.1 1.5 %collective-permute-done.5.refs_4_ = bf16[2,256,128]{2,1,0:T(8,128)(2,1)S(1)} collective-permute-done((bf16[2,256,128]{2,1,0:T(8,128)(2,1)S(1)}, bf16[2,256,128]{2,1,0:T(8,128)(2,1)S(1)}, u32[]{:S(2)}, u32[]{:S(2)}) %collective-permute-start.5) | collective-permute-done | bytes 131104 | tf_op jit(solution)/shard_map/ppermute | solution.py:470
  26.6 0.0 copy-done.7
  26.6 0.7 %shard_map.151 = (f32[256,128]{1,0:T(8,128)S(1)}, f32[256,128]{1,0:T(8,128)S(1)}) custom-call(bf16[2,256,128]{2,1,0:T(8,128)(2,1)S(1)} %get-tuple-element.22.refs_0_, bf16[2,256,128]{2,1,0:T(8,128)(2,1)S(1)} %collective-permute-done.1.refs_1_, bf16[256,128]{1,0:T(8,128)(2,1)S(1)} %collective-permute-done.2.refs_2_, ...), custom_call_target="tpu_custom_call" | custom-call | flops 67108864 | bytes 1048576 | tf_op jit(solution)/shard_map/pallas_call | solution.py:419
  27.4 2.9 %collective-permute-done.4.refs_4_ = bf16[2,256,128]{2,1,0:T(8,128)(2,1)S(1)} collective-permute-done((bf16[2,256,128]{2,1,0:T(8,128)(2,1)S(1)}, bf16[2,256,128]{2,1,0:T(8,128)(2,1)S(1)}, u32[]{:S(2)}, u32[]{:S(2)}) %collective-permute-start.4) | collective-permute-done | bytes 131104 | tf_op jit(solution)/shard_map/ppermute | solution.py:470
  30.2 0.0 copy-done.1
  30.2 0.0 copy-done.2
  30.2 0.0 copy-done.8
  30.2 1.9 %shard_map.152 = bf16[16,16,128]{2,1,0:T(8,128)(2,1)} custom-call(bf16[2,256,128]{2,1,0:T(8,128)(2,1)S(1)} %get-tuple-element.22.refs_0_, bf16[2,256,128]{2,1,0:T(8,128)(2,1)S(1)} %collective-permute-done.1.refs_1_, bf16[256,128]{1,0:T(8,128)(2,1)S(1)} %collective-permute-done.2.refs_2_, bf16[256,128]{1,0:T(8,128)(2,1)S(1)} %collective-permute-done.3.refs_3_, ...), custom_call_target="tpu_custom_call" | custom-call | flops 134217728 | bytes 2097152 | tf_op jit(solution)/shard_map/pallas_call | solution.py:430
  (3 shorter events, 0.0 us)
Async XLA Ops:
  0.0 1.6 %copy-start.12 = (bf16[256,16,256]{2,1,0:T(8,128)(2,1)S(1)}, bf16[256,16,256]{2,1,0:T(8,128)(2,1)}, u32[]{:S(2)}) copy-start(bf16[256,16,256]{2,1,0:T(8,128)(2,1)} %x_ref.3) | copy-start | bytes 6291460
  0.0 0.9 %copy-start.13 = (bf16[256,32]{0,1:T(8,128)(2,1)S(1)}, bf16[256,32]{0,1:T(8,128)(2,1)}, u32[]{:S(2)}) copy-start(bf16[256,32]{0,1:T(8,128)(2,1)} %param.21) | copy-start | bytes 49156
  1.6 6.8 %copy-start.14 = (bf16[256,32]{0,1:T(8,128)(2,1)S(1)}, bf16[256,32]{0,1:T(8,128)(2,1)}, u32[]{:S(2)}) copy-start(bf16[256,32]{0,1:T(8,128)(2,1)} %param.20) | copy-start | bytes 49156
  3.5 5.1 %copy-start.3 = (s32[256,64]{0,1:T(8,128)S(1)}, s32[256,64]{0,1:T(8,128)}, u32[]{:S(2)}) copy-start(s32[256,64]{0,1:T(8,128)} %param.16) | copy-start | bytes 196612
  3.5 10.6 %collective-permute-start = (bf16[4,256,128]{2,1,0:T(8,128)(2,1)S(1)}, bf16[4,256,128]{2,1,0:T(8,128)(2,1)S(1)}, u32[]{:S(2)}, u32[]{:S(2)}) collective-permute-start(bf16[4,256,128]{2,1,0:T(8,128)(2,1)S(1)} %shard_map.149), channel_id=1, source_target_pairs={{0,0},{6,1},{8,2},{14,3},{2,4},{5,5},{11,6},{12,7},{3,8},{4,9},{10... | collective-permute-start | bytes 786440 | tf_op jit(solution)/shard_map/ppermute | solution.py:470
  8.5 2.1 %copy-start = (f32[32,32,128]{2,1,0:T(8,128)S(1)}, f32[32,32,128]{2,1,0:T(8,128)}, u32[]{:S(2)}) copy-start(f32[32,32,128]{2,1,0:T(8,128)} %proj_ref.1) | copy-start | bytes 1572868
  8.5 2.1 %copy-start.4 = (bf16[16,16,128]{2,1,0:T(8,128)(2,1)S(1)}, bf16[16,16,128]{2,1,0:T(8,128)(2,1)}, u32[]{:S(2)}) copy-start(bf16[16,16,128]{2,1,0:T(8,128)(2,1)} %pair_ref.1) | copy-start | bytes 196612
  8.6 2.1 %copy-start.9 = (bf16[66,128]{1,0:T(8,128)(2,1)S(1)}, bf16[66,128]{1,0:T(8,128)(2,1)}, u32[]{:S(2)}) copy-start(bf16[66,128]{1,0:T(8,128)(2,1)} %table_ref.1) | copy-start | bytes 50692
  8.6 2.0 %copy-start.10 = (s32[64]{0:T(128)S(1)}, s32[64]{0:T(128)}, u32[]{:S(2)}) copy-start(s32[64]{0:T(128)} %param.18) | copy-start | bytes 772
  8.6 2.0 %copy-start.11 = (s32[64]{0:T(128)S(1)}, s32[64]{0:T(128)}, u32[]{:S(2)}) copy-start(s32[64]{0:T(128)} %param.19) | copy-start | bytes 772
  8.6 5.5 %copy-start.5 = (bf16[128,256]{1,0:T(8,128)(2,1)S(1)}, bf16[128,256]{1,0:T(8,128)(2,1)}, u32[]{:S(2)}) copy-start(bf16[128,256]{1,0:T(8,128)(2,1)} %refs_6_.2) | copy-start | bytes 196612
  8.6 5.5 %copy-start.6 = (bf16[128,256]{1,0:T(8,128)(2,1)S(1)}, bf16[128,256]{1,0:T(8,128)(2,1)}, u32[]{:S(2)}) copy-start(bf16[128,256]{1,0:T(8,128)(2,1)} %refs_7_.1) | copy-start | bytes 196612
  10.5 16.1 %copy-start.7 = (bf16[128,128]{1,0:T(8,128)(2,1)S(1)}, bf16[128,128]{1,0:T(8,128)(2,1)}, u32[]{:S(2)}) copy-start(bf16[128,128]{1,0:T(8,128)(2,1)} %refs_6_.3) | copy-start | bytes 98308
  10.5 19.7 %copy-start.1 = (bf16[128,512]{1,0:T(8,128)(2,1)S(1)}, bf16[128,512]{1,0:T(8,128)(2,1)}, u32[]{:S(2)}) copy-start(bf16[128,512]{1,0:T(8,128)(2,1)} %refs_9_.1) | copy-start | bytes 393220
  10.6 19.7 %copy-start.2 = (bf16[512,128]{1,0:T(8,128)(2,1)S(1)}, bf16[512,128]{1,0:T(8,128)(2,1)}, u32[]{:S(2)}) copy-start(bf16[512,128]{1,0:T(8,128)(2,1)} %refs_10_.1) | copy-start | bytes 393220
  10.6 19.7 %copy-start.8 = (bf16[128,128]{1,0:T(8,128)(2,1)S(1)}, bf16[128,128]{1,0:T(8,128)(2,1)}, u32[]{:S(2)}) copy-start(bf16[128,128]{1,0:T(8,128)(2,1)} %refs_8_.1) | copy-start | bytes 98308
  15.3 4.2 %collective-permute-start.1 = (bf16[2,256,128]{2,1,0:T(8,128)(2,1)S(1)}, bf16[2,256,128]{2,1,0:T(8,128)(2,1)S(1)}, u32[]{:S(2)}, u32[]{:S(2)}) collective-permute-start(bf16[2,256,128]{2,1,0:T(8,128)(2,1)S(1)} %get-tuple-element.22.refs_0_), channel_id=1, source_target_pairs={{1,0},{0,1},{3,2},{2,3},{5,4},{4,5},{7,6},{6,7},{9,8},{8,9},{11,10... | collective-permute-start | bytes 393224 | tf_op jit(solution)/shard_map/ppermute | solution.py:470
  18.5 5.3 %collective-permute-start.2 = (bf16[256,128]{1,0:T(8,128)(2,1)S(1)}, bf16[256,128]{1,0:T(8,128)(2,1)S(1)}, u32[]{:S(2)}, u32[]{:S(2)}) collective-permute-start(bf16[256,128]{1,0:T(8,128)(2,1)S(1)} %get-tuple-element.23), channel_id=1, source_target_pairs={{2,0},{3,1},{0,2},{1,3},{6,4},{7,5},{4,6},{5,7},{10,8},{11,9},{8,1... | collective-permute-start | bytes 196616 | tf_op jit(solution)/shard_map/ppermute | solution.py:470
  19.5 7.1 %collective-permute-start.5 = (bf16[2,256,128]{2,1,0:T(8,128)(2,1)S(1)}, bf16[2,256,128]{2,1,0:T(8,128)(2,1)S(1)}, u32[]{:S(2)}, u32[]{:S(2)}) collective-permute-start(bf16[2,256,128]{2,1,0:T(8,128)(2,1)S(1)} %pad_maximum_fusion), channel_id=1, source_target_pairs={{2,0},{4,1},{10,2},{12,3},{0,4},{7,5},{9,6},{14,7},{1,8},{6,9},{8,... | collective-permute-start | bytes 393224 | tf_op jit(solution)/shard_map/ppermute | solution.py:470
  21.9 8.4 %collective-permute-start.4 = (bf16[2,256,128]{2,1,0:T(8,128)(2,1)S(1)}, bf16[2,256,128]{2,1,0:T(8,128)(2,1)S(1)}, u32[]{:S(2)}, u32[]{:S(2)}) collective-permute-start(bf16[2,256,128]{2,1,0:T(8,128)(2,1)S(1)} %pad_maximum_fusion), channel_id=1, source_target_pairs={{0,0},{6,1},{8,2},{14,3},{2,4},{5,5},{11,6},{12,7},{3,8},{4,9},{10... | collective-permute-start | bytes 393224 | tf_op jit(solution)/shard_map/ppermute | solution.py:470
  23.8 1.3 %collective-permute-start.3 = (bf16[256,128]{1,0:T(8,128)(2,1)S(1)}, bf16[256,128]{1,0:T(8,128)(2,1)S(1)}, u32[]{:S(2)}, u32[]{:S(2)}) collective-permute-start(bf16[256,128]{1,0:T(8,128)(2,1)S(1)} %collective-permute-done.2.refs_2_), channel_id=1, source_target_pairs={{1,0},{0,1},{3,2},{2,3},{5,4},{4,5},{7,6},{6,7},{9,8},{8,9},{11,10... | collective-permute-start | bytes 196616 | tf_op jit(solution)/shard_map/ppermute | solution.py:470

commit v22 on v21

--- a/solution.py
+++ b/solution.py
@@ -53,19 +53,14 @@
 
 
 def repeat_kernel(weight_ref, out_ref):
-    hidden, channels = weight_ref.shape
-    rep = LANES // hidden
-    wide = jnp.concatenate([weight_ref[...]] * rep, axis=0).T
-    block = over(iota((channels, LANES), 1), hidden)
-    for k in range(rep):
-        out_ref[k * channels : (k + 1) * channels, :] = jnp.where(block == k, wide, 0)
+    rep = LANES // weight_ref.shape[0]
+    out_ref[...] = jnp.concatenate([weight_ref[...]] * rep, axis=0).T
 
 
 def repeat_weight(weight):
-    hidden, channels = weight.shape
     return pl.pallas_call(
         repeat_kernel,
-        out_shape=jax.ShapeDtypeStruct((channels * LANES // hidden, LANES), BF16),
+        out_shape=jax.ShapeDtypeStruct((weight.shape[1], LANES), BF16),
         in_specs=[vmem()],
         out_specs=vmem(),
         compiler_params=pltpu.CompilerParams(vmem_limit_bytes=2 << 20),
@@ -100,9 +95,9 @@
     width = rows * hidden
     steps, step = y_scr.shape[0], y_scr.shape[1] // rows
     quarter = seqs // rep
-    weight = weight_ref[...]
-    sums = dot(jnp.ones((8, channels * rep), BF16), weight)[:1]
     share = jnp.full((channels, LANES), 1.0 / channels, BF16)
+    weight = jnp.concatenate([weight_ref[...], share], axis=1)
+    sums = dot(jnp.ones((8, channels), BF16), weight_ref[...])[:1]
     side = (rep * LANES, LANES)
     own = over(iota(side, 0), LANES) == over(iota(side, 1), hidden)
     own = jnp.where(own, 1.0 / channels, 0.0).astype(BF16)
@@ -113,19 +108,19 @@
         lanes_of = (iota((residues, width), 0) == column).astype(BF16)
         live = dot_tn(mask_ref[...].astype(BF16), lanes_of)
     for turn in range(steps):
-        inputs, squares, mean = [], [], None
+        squares, y, mean = [], None, None
         for part in range(rep):
             first = part * quarter + turn * step
             x = x_ref[first : first + step].reshape(step * rows, channels)
-            inputs.append(x)
-            average = dot(x, share)
-            mean = average if mean is None else jnp.where(block == part, average, mean)
+            both = dot(x, weight)
+            product, average = both[:, :LANES], both[:, LANES:]
+            y = product if part == 0 else jnp.where(block == part, product, y)
+            mean = average if part == 0 else jnp.where(block == part, average, mean)
             square = jnp.zeros_like(average)
             for half in range(channels // LANES):
                 centered = x[:, half * LANES : (half + 1) * LANES].astype(F32) - average
                 square = square + centered * centered
             squares.append(square.astype(BF16))
-        y = dot(jnp.concatenate(inputs, axis=1), weight)
         scale = lax.rsqrt(dot(jnp.concatenate(squares, axis=1), own) + EPSILON)
         y_scr[turn] = (y - mean * sums) * scale
         for group in range(groups):

time: 32.4 us -> 32 us (0.988)
  Pallas kernels: 8.72 us -> 7.93 us
  waiting for transfers between devices: 9.07 us -> 9.43 us
    pallas_call x2, Pallas kernels: 3.81 us -> 3.06 us  [factor(): pl.pallas_call(functools.partial(factor_kernel, mask is not None, hidden)...]
    ppermute x6, waiting for transfers between devices: 9.07 us -> 9.43 us  [fetch(): return lax.ppermute(values, ('dap', 'sub'), perm)]
  transfers between devices with their start and end apart: 6 -> 6, of which waited for: 5 -> 5; matrix products, arithmetic and copies ran while one was open for 0% -> 0% of each run, Pallas kernels for 11% -> 10%
where the time goes in v22:
time: 32 us; the launch traced here: 31.7 us
  starting transfers between devices  12.5 us (39%)
  waiting for transfers between devices  9.43 us (29%)
  Pallas kernels  7.93 us (25%)
  local copies, waits for them, and re-layouts  1.62 us (5%)
    ppermute x6, starting transfers between devices, fetch(): return lax.ppermute(values, ('dap', 'sub'), perm)  12.5 us
    ppermute x6, waiting for transfers between devices, fetch(): return lax.ppermute(values, ('dap', 'sub'), perm)  9.43 us
    pallas_call x2, Pallas kernels, factor(): pl.pallas_call(functools.partial(factor_kernel, mask is not None, hidden)...  3.06 us
    pallas_call x1, Pallas kernels, triangle_update(): pl.pallas_call(functools.partial(last_kernel, late, twos, ratio, cols), o...  1.87 us
    unnamed x30, local copies, waits for them, and re-layouts  1.61 us
    pallas_call x1, Pallas kernels, pair_update(): pl.pallas_call(functools.partial(pair_kernel, ratio, hidden), out_shape=(...  1.19 us
    pallas_call x1, Pallas kernels, prepare(): pl.pallas_call(prepare_kernel, out_shape=(jax.ShapeDtypeStruct((zl.shape[...  0.94 us
    pallas_call x1, Pallas kernels, triangle_update(): pl.pallas_call(functools.partial(first_kernel, early, twos, ratio, cols),...  0.73 us
  transfers between devices with their start and end apart: 6, of which 5 were waited for; matrix products, arithmetic and copies ran while one was open for 0% of the time, Pallas kernels for 10%

profile of v22, /device:TPU:3, one launch (start us, length us, event | category | flops | bytes accessed | tf_op | source)
XLA Modules:
  0.0 31.7 jit_solution(3993517061382599687)
XLA Ops:
  0.0 0.0 copy-start.12
  0.0 0.0 copy-start.13
  0.0 0.9 %copy-done.13 = bf16[256,32]{0,1:T(8,128)(2,1)S(1)} copy-done((bf16[256,32]{0,1:T(8,128)(2,1)S(1)}, bf16[256,32]{0,1:T(8,128)(2,1)}, u32[]{:S(2)}) %copy-start.13) | copy-done | bytes 16408
  0.9 0.1 shard_map.148.weight_ref
  0.9 0.7 %copy-done.12 = bf16[256,16,256]{2,1,0:T(8,128)(2,1)S(1)} copy-done((bf16[256,16,256]{2,1,0:T(8,128)(2,1)S(1)}, bf16[256,16,256]{2,1,0:T(8,128)(2,1)}, u32[]{:S(2)}) %copy-start.12) | copy-done | bytes 2097176
  1.6 0.0 copy-start.14
  1.6 1.5 %shard_map.149 = bf16[4,256,128]{2,1,0:T(8,128)(2,1)S(1)} custom-call(bf16[256,16,256]{2,1,0:T(8,128)(2,1)S(1)} %copy-done.12, bf16[256,128]{1,0:T(8,128)(2,1)S(1)} %shard_map.148.weight_ref), custom_call_target="tpu_custom_call" | custom-call | flops 1073741824 | bytes 4194304 | tf_op jit(solution)/shard_map/pallas_call | solution.py:144
  3.1 0.0 copy-start.3
  3.1 4.9 %collective-permute-start = (bf16[4,256,128]{2,1,0:T(8,128)(2,1)S(1)}, bf16[4,256,128]{2,1,0:T(8,128)(2,1)S(1)}, u32[]{:S(2)}, u32[]{:S(2)}) collective-permute-start(bf16[4,256,128]{2,1,0:T(8,128)(2,1)S(1)} %shard_map.149), channel_id=1, source_target_pairs={{0,0},{6,1},{8,2},{14,3},{2,4},{5,5},{11,6},{12,7},{3,8},{4,9},{10... | collective-permute-start | bytes 786440 | tf_op jit(solution)/shard_map/ppermute | solution.py:465
  8.0 0.0 copy-done.14
  8.0 0.1 shard_map.145.weight_ref
  8.1 0.0 copy-start
  8.1 0.0 copy-start.4
  8.1 0.0 copy-start.9
  8.1 0.0 copy-start.10
  8.1 0.0 copy-start.11
  8.2 0.0 copy-done.3
  8.2 0.0 copy-start.5
  8.2 0.0 copy-start.6
  8.2 1.6 %shard_map.146.zl_ref = bf16[4,256,128]{2,1,0:T(8,128)(2,1)S(1)} custom-call(bf16[256,16,256]{2,1,0:T(8,128)(2,1)S(1)} %copy-done.12, bf16[256,128]{1,0:T(8,128)(2,1)S(1)} %shard_map.145.weight_ref, s32[64,256]{1,0:T(8,128)S(1)} %bitcast.5), custom_call_target="tpu_custom_call" | custom-call | flops 1073741824 | bytes 4194304 | tf_op jit(solution)/shard_map/pallas_call | solution.py:144
  9.8 0.0 copy-start.7
  9.8 0.0 copy-start.1
  9.8 0.0 copy-start.2
  9.8 0.0 copy-start.8
  9.8 0.0 copy-done
  9.8 0.0 copy-done.4
  9.8 0.0 copy-done.9
  9.8 0.0 copy-done.10
  9.8 0.0 copy-done.11
  9.9 0.9 %shard_map.147 = (bf16[2,512,128]{2,1,0:T(8,128)(2,1)S(1)}, f32[256,128]{1,0:T(8,128)S(1)}, f32[256,128]{1,0:T(8,128)S(1)}, f32[256,128]{1,0:T(8,128)S(1)}, bf16...) custom-call(bf16[4,256,128]{2,1,0:T(8,128)(2,1)S(1)} %shard_map.146.zl_ref, s32[64,256]{1,0:T(8,128)S(1)} %bitcast.6, ...), custom_call_target="tpu_custom_call" | custom-call | flops 134217728 | bytes 2097152 | tf_op jit(solution)/shard_map/pallas_call | solution.py:217
  10.8 2.9 %collective-permute-done.refs_0_ = bf16[4,256,128]{2,1,0:T(8,128)(2,1)S(1)} collective-permute-done((bf16[4,256,128]{2,1,0:T(8,128)(2,1)S(1)}, bf16[4,256,128]{2,1,0:T(8,128)(2,1)S(1)}, u32[]{:S(2)}, u32[]{:S(2)}) %collective-permute-start) | collective-permute-done | bytes 262176 | tf_op jit(solution)/shard_map/ppermute | solution.py:465
  13.7 0.0 copy-done.5
  13.7 0.0 copy-done.6
  13.7 1.2 %shard_map.150 = (bf16[2,256,128]{2,1,0:T(8,128)(2,1)S(1)}, bf16[256,128]{1,0:T(8,128)(2,1)S(1)}, bf16[256,128]{1,0:T(8,128)(2,1)S(1)}) custom-call(bf16[2,512,128]{2,1,0:T(8,128)(2,1)S(1)} %get-tuple-element.16.zlt_ref, bf16[4,256,128]{2,1,0:T(8,128)(2,1)S(1)} %collective-permute-done.refs_0_, bf16[4,256,128]{2,1,0:T(8,128)(2,1)S(1)} %get-tuple-element.17.refs_1_, ...), custom_call_target="tpu_custom_call" | custom-call | flops 268435456 | bytes 2097152 | tf_op jit(solution)/shard_map/pallas_call | solution.py:293
  14.9 3.2 %collective-permute-start.1 = (bf16[2,256,128]{2,1,0:T(8,128)(2,1)S(1)}, bf16[2,256,128]{2,1,0:T(8,128)(2,1)S(1)}, u32[]{:S(2)}, u32[]{:S(2)}) collective-permute-start(bf16[2,256,128]{2,1,0:T(8,128)(2,1)S(1)} %get-tuple-element.22.refs_0_), channel_id=1, source_target_pairs={{1,0},{0,1},{3,2},{2,3},{5,4},{4,5},{7,6},{6,7},{9,8},{8,9},{11,10... | collective-permute-start | bytes 393224 | tf_op jit(solution)/shard_map/ppermute | solution.py:465
  18.1 0.0 collective-permute-start.2
  18.1 1.0 %collective-permute-done.1.refs_1_ = bf16[2,256,128]{2,1,0:T(8,128)(2,1)S(1)} collective-permute-done((bf16[2,256,128]{2,1,0:T(8,128)(2,1)S(1)}, bf16[2,256,128]{2,1,0:T(8,128)(2,1)S(1)}, u32[]{:S(2)}, u32[]{:S(2)}) %collective-permute-start.1) | collective-permute-done | bytes 131104 | tf_op jit(solution)/shard_map/ppermute | solution.py:465
  19.1 2.4 %collective-permute-start.5 = (bf16[2,256,128]{2,1,0:T(8,128)(2,1)S(1)}, bf16[2,256,128]{2,1,0:T(8,128)(2,1)S(1)}, u32[]{:S(2)}, u32[]{:S(2)}) collective-permute-start(bf16[2,256,128]{2,1,0:T(8,128)(2,1)S(1)} %pad_maximum_fusion), channel_id=1, source_target_pairs={{2,0},{4,1},{10,2},{12,3},{0,4},{7,5},{9,6},{14,7},{1,8},{6,9},{8,... | collective-permute-start | bytes 393224 | tf_op jit(solution)/shard_map/ppermute | solution.py:465
  21.4 1.9 %collective-permute-start.4 = (bf16[2,256,128]{2,1,0:T(8,128)(2,1)S(1)}, bf16[2,256,128]{2,1,0:T(8,128)(2,1)S(1)}, u32[]{:S(2)}, u32[]{:S(2)}) collective-permute-start(bf16[2,256,128]{2,1,0:T(8,128)(2,1)S(1)} %pad_maximum_fusion), channel_id=1, source_target_pairs={{0,0},{6,1},{8,2},{14,3},{2,4},{5,5},{11,6},{12,7},{3,8},{4,9},{10... | collective-permute-start | bytes 393224 | tf_op jit(solution)/shard_map/ppermute | solution.py:465
  23.4 0.0 collective-permute-done.2.refs_2_
  23.4 0.1 collective-permute-start.3
  23.5 1.2 %collective-permute-done.3.refs_3_ = bf16[256,128]{1,0:T(8,128)(2,1)S(1)} collective-permute-done((bf16[256,128]{1,0:T(8,128)(2,1)S(1)}, bf16[256,128]{1,0:T(8,128)(2,1)S(1)}, u32[]{:S(2)}, u32[]{:S(2)}) %collective-permute-start.3) | collective-permute-done | bytes 65568 | tf_op jit(solution)/shard_map/ppermute | solution.py:465
  24.7 1.5 %collective-permute-done.5.refs_4_ = bf16[2,256,128]{2,1,0:T(8,128)(2,1)S(1)} collective-permute-done((bf16[2,256,128]{2,1,0:T(8,128)(2,1)S(1)}, bf16[2,256,128]{2,1,0:T(8,128)(2,1)S(1)}, u32[]{:S(2)}, u32[]{:S(2)}) %collective-permute-start.5) | collective-permute-done | bytes 131104 | tf_op jit(solution)/shard_map/ppermute | solution.py:465
  26.2 0.0 copy-done.7
  26.2 0.7 %shard_map.151 = (f32[256,128]{1,0:T(8,128)S(1)}, f32[256,128]{1,0:T(8,128)S(1)}) custom-call(bf16[2,256,128]{2,1,0:T(8,128)(2,1)S(1)} %get-tuple-element.22.refs_0_, bf16[2,256,128]{2,1,0:T(8,128)(2,1)S(1)} %collective-permute-done.1.refs_1_, bf16[256,128]{1,0:T(8,128)(2,1)S(1)} %collective-permute-done.2.refs_2_, ...), custom_call_target="tpu_custom_call" | custom-call | flops 67108864 | bytes 1048576 | tf_op jit(solution)/shard_map/pallas_call | solution.py:414
  27.0 2.9 %collective-permute-done.4.refs_4_ = bf16[2,256,128]{2,1,0:T(8,128)(2,1)S(1)} collective-permute-done((bf16[2,256,128]{2,1,0:T(8,128)(2,1)S(1)}, bf16[2,256,128]{2,1,0:T(8,128)(2,1)S(1)}, u32[]{:S(2)}, u32[]{:S(2)}) %collective-permute-start.4) | collective-permute-done | bytes 131104 | tf_op jit(solution)/shard_map/ppermute | solution.py:465
  29.8 0.0 copy-done.1
  29.8 0.0 copy-done.2
  29.8 0.0 copy-done.8
  29.8 1.9 %shard_map.152 = bf16[16,16,128]{2,1,0:T(8,128)(2,1)} custom-call(bf16[2,256,128]{2,1,0:T(8,128)(2,1)S(1)} %get-tuple-element.22.refs_0_, bf16[2,256,128]{2,1,0:T(8,128)(2,1)S(1)} %collective-permute-done.1.refs_1_, bf16[256,128]{1,0:T(8,128)(2,1)S(1)} %collective-permute-done.2.refs_2_, bf16[256,128]{1,0:T(8,128)(2,1)S(1)} %collective-permute-done.3.refs_3_, ...), custom_call_target="tpu_custom_call" | custom-call | flops 134217728 | bytes 2097152 | tf_op jit(solution)/shard_map/pallas_call | solution.py:425
  (3 shorter events, 0.0 us)
Async XLA Ops:
  0.0 1.6 %copy-start.12 = (bf16[256,16,256]{2,1,0:T(8,128)(2,1)S(1)}, bf16[256,16,256]{2,1,0:T(8,128)(2,1)}, u32[]{:S(2)}) copy-start(bf16[256,16,256]{2,1,0:T(8,128)(2,1)} %x_ref.3) | copy-start | bytes 6291460
  0.0 0.9 %copy-start.13 = (bf16[256,32]{0,1:T(8,128)(2,1)S(1)}, bf16[256,32]{0,1:T(8,128)(2,1)}, u32[]{:S(2)}) copy-start(bf16[256,32]{0,1:T(8,128)(2,1)} %param.21) | copy-start | bytes 49156
  1.6 6.4 %copy-start.14 = (bf16[256,32]{0,1:T(8,128)(2,1)S(1)}, bf16[256,32]{0,1:T(8,128)(2,1)}, u32[]{:S(2)}) copy-start(bf16[256,32]{0,1:T(8,128)(2,1)} %param.20) | copy-start | bytes 49156
  3.1 5.0 %copy-start.3 = (s32[256,64]{0,1:T(8,128)S(1)}, s32[256,64]{0,1:T(8,128)}, u32[]{:S(2)}) copy-start(s32[256,64]{0,1:T(8,128)} %param.16) | copy-start | bytes 196612
  3.1 10.6 %collective-permute-start = (bf16[4,256,128]{2,1,0:T(8,128)(2,1)S(1)}, bf16[4,256,128]{2,1,0:T(8,128)(2,1)S(1)}, u32[]{:S(2)}, u32[]{:S(2)}) collective-permute-start(bf16[4,256,128]{2,1,0:T(8,128)(2,1)S(1)} %shard_map.149), channel_id=1, source_target_pairs={{0,0},{6,1},{8,2},{14,3},{2,4},{5,5},{11,6},{12,7},{3,8},{4,9},{10... | collective-permute-start | bytes 786440 | tf_op jit(solution)/shard_map/ppermute | solution.py:465
  8.1 1.7 %copy-start = (f32[32,32,128]{2,1,0:T(8,128)S(1)}, f32[32,32,128]{2,1,0:T(8,128)}, u32[]{:S(2)}) copy-start(f32[32,32,128]{2,1,0:T(8,128)} %proj_ref.1) | copy-start | bytes 1572868
  8.1 1.7 %copy-start.4 = (bf16[16,16,128]{2,1,0:T(8,128)(2,1)S(1)}, bf16[16,16,128]{2,1,0:T(8,128)(2,1)}, u32[]{:S(2)}) copy-start(bf16[16,16,128]{2,1,0:T(8,128)(2,1)} %pair_ref.1) | copy-start | bytes 196612
  8.1 1.7 %copy-start.9 = (bf16[66,128]{1,0:T(8,128)(2,1)S(1)}, bf16[66,128]{1,0:T(8,128)(2,1)}, u32[]{:S(2)}) copy-start(bf16[66,128]{1,0:T(8,128)(2,1)} %table_ref.1) | copy-start | bytes 50692
  8.1 1.7 %copy-start.10 = (s32[64]{0:T(128)S(1)}, s32[64]{0:T(128)}, u32[]{:S(2)}) copy-start(s32[64]{0:T(128)} %param.18) | copy-start | bytes 772
  8.1 1.7 %copy-start.11 = (s32[64]{0:T(128)S(1)}, s32[64]{0:T(128)}, u32[]{:S(2)}) copy-start(s32[64]{0:T(128)} %param.19) | copy-start | bytes 772
  8.2 5.5 %copy-start.5 = (bf16[128,256]{1,0:T(8,128)(2,1)S(1)}, bf16[128,256]{1,0:T(8,128)(2,1)}, u32[]{:S(2)}) copy-start(bf16[128,256]{1,0:T(8,128)(2,1)} %refs_6_.2) | copy-start | bytes 196612
  8.2 5.5 %copy-start.6 = (bf16[128,256]{1,0:T(8,128)(2,1)S(1)}, bf16[128,256]{1,0:T(8,128)(2,1)}, u32[]{:S(2)}) copy-start(bf16[128,256]{1,0:T(8,128)(2,1)} %refs_7_.1) | copy-start | bytes 196612
  9.8 16.5 %copy-start.7 = (bf16[128,128]{1,0:T(8,128)(2,1)S(1)}, bf16[128,128]{1,0:T(8,128)(2,1)}, u32[]{:S(2)}) copy-start(bf16[128,128]{1,0:T(8,128)(2,1)} %refs_6_.3) | copy-start | bytes 98308
  9.8 20.0 %copy-start.1 = (bf16[128,512]{1,0:T(8,128)(2,1)S(1)}, bf16[128,512]{1,0:T(8,128)(2,1)}, u32[]{:S(2)}) copy-start(bf16[128,512]{1,0:T(8,128)(2,1)} %refs_9_.1) | copy-start | bytes 393220
  9.8 20.0 %copy-start.2 = (bf16[512,128]{1,0:T(8,128)(2,1)S(1)}, bf16[512,128]{1,0:T(8,128)(2,1)}, u32[]{:S(2)}) copy-start(bf16[512,128]{1,0:T(8,128)(2,1)} %refs_10_.1) | copy-start | bytes 393220
  9.8 20.0 %copy-start.8 = (bf16[128,128]{1,0:T(8,128)(2,1)S(1)}, bf16[128,128]{1,0:T(8,128)(2,1)}, u32[]{:S(2)}) copy-start(bf16[128,128]{1,0:T(8,128)(2,1)} %refs_8_.1) | copy-start | bytes 98308
  14.9 4.2 %collective-permute-start.1 = (bf16[2,256,128]{2,1,0:T(8,128)(2,1)S(1)}, bf16[2,256,128]{2,1,0:T(8,128)(2,1)S(1)}, u32[]{:S(2)}, u32[]{:S(2)}) collective-permute-start(bf16[2,256,128]{2,1,0:T(8,128)(2,1)S(1)} %get-tuple-element.22.refs_0_), channel_id=1, source_target_pairs={{1,0},{0,1},{3,2},{2,3},{5,4},{4,5},{7,6},{6,7},{9,8},{8,9},{11,10... | collective-permute-start | bytes 393224 | tf_op jit(solution)/shard_map/ppermute | solution.py:465
  18.1 5.3 %collective-permute-start.2 = (bf16[256,128]{1,0:T(8,128)(2,1)S(1)}, bf16[256,128]{1,0:T(8,128)(2,1)S(1)}, u32[]{:S(2)}, u32[]{:S(2)}) collective-permute-start(bf16[256,128]{1,0:T(8,128)(2,1)S(1)} %get-tuple-element.23), channel_id=1, source_target_pairs={{2,0},{3,1},{0,2},{1,3},{6,4},{7,5},{4,6},{5,7},{10,8},{11,9},{8,1... | collective-permute-start | bytes 196616 | tf_op jit(solution)/shard_map/ppermute | solution.py:465
  19.1 7.1 %collective-permute-start.5 = (bf16[2,256,128]{2,1,0:T(8,128)(2,1)S(1)}, bf16[2,256,128]{2,1,0:T(8,128)(2,1)S(1)}, u32[]{:S(2)}, u32[]{:S(2)}) collective-permute-start(bf16[2,256,128]{2,1,0:T(8,128)(2,1)S(1)} %pad_maximum_fusion), channel_id=1, source_target_pairs={{2,0},{4,1},{10,2},{12,3},{0,4},{7,5},{9,6},{14,7},{1,8},{6,9},{8,... | collective-permute-start | bytes 393224 | tf_op jit(solution)/shard_map/ppermute | solution.py:465
  21.4 8.4 %collective-permute-start.4 = (bf16[2,256,128]{2,1,0:T(8,128)(2,1)S(1)}, bf16[2,256,128]{2,1,0:T(8,128)(2,1)S(1)}, u32[]{:S(2)}, u32[]{:S(2)}) collective-permute-start(bf16[2,256,128]{2,1,0:T(8,128)(2,1)S(1)} %pad_maximum_fusion), channel_id=1, source_target_pairs={{0,0},{6,1},{8,2},{14,3},{2,4},{5,5},{11,6},{12,7},{3,8},{4,9},{10... | collective-permute-start | bytes 393224 | tf_op jit(solution)/shard_map/ppermute | solution.py:465
  23.4 1.3 %collective-permute-start.3 = (bf16[256,128]{1,0:T(8,128)(2,1)S(1)}, bf16[256,128]{1,0:T(8,128)(2,1)S(1)}, u32[]{:S(2)}, u32[]{:S(2)}) collective-permute-start(bf16[256,128]{1,0:T(8,128)(2,1)S(1)} %collective-permute-done.2.refs_2_), channel_id=1, source_target_pairs={{1,0},{0,1},{3,2},{2,3},{5,4},{4,5},{7,6},{6,7},{9,8},{8,9},{11,10... | collective-permute-start | bytes 196616 | tf_op jit(solution)/shard_map/ppermute | solution.py:465

commit v23 on v22

--- a/solution.py
+++ b/solution.py
@@ -310,7 +310,7 @@
     return sub + 1 - 2 * (sub % 2)
 
 
-SENDERS = ((0, 2, 3, 1), (2, 1, 0, 3), (0, 3, 2, 1), (2, 0, 1, 3))
+SENDERS = ((3, 0, 2, 1), (0, 3, 2, 1), (2, 0, 1, 3), (2, 0, 3, 1))
 
 
 def sender(a, b, subs, ratio):

time: 32 us -> 30.3 us (0.947)
  the two profiles are of different devices: /device:TPU:3 before, /device:TPU:2 now
where the time goes in v23:
time: 30.3 us; the launch traced here: 30 us
  waiting for transfers between devices  11.6 us (38%)
  starting transfers between devices  8.55 us (28%)
  Pallas kernels  7.93 us (26%)
  local copies, waits for them, and re-layouts  1.62 us (5%)
    ppermute x6, waiting for transfers between devices, fetch(): return lax.ppermute(values, ('dap', 'sub'), perm)  11.6 us
    ppermute x6, starting transfers between devices, fetch(): return lax.ppermute(values, ('dap', 'sub'), perm)  8.55 us
    pallas_call x2, Pallas kernels, factor(): pl.pallas_call(functools.partial(factor_kernel, mask is not None, hidden)...  3.06 us
    pallas_call x1, Pallas kernels, triangle_update(): pl.pallas_call(functools.partial(last_kernel, late, twos, ratio, cols), o...  1.87 us
    unnamed x30, local copies, waits for them, and re-layouts  1.61 us
    pallas_call x1, Pallas kernels, pair_update(): pl.pallas_call(functools.partial(pair_kernel, ratio, hidden), out_shape=(...  1.19 us
    pallas_call x1, Pallas kernels, prepare(): pl.pallas_call(prepare_kernel, out_shape=(jax.ShapeDtypeStruct((zl.shape[...  0.94 us
    pallas_call x1, Pallas kernels, triangle_update(): pl.pallas_call(functools.partial(first_kernel, early, twos, ratio, cols),...  0.73 us
  transfers between devices with their start and end apart: 6, of which 4 were waited for; matrix products, arithmetic and copies ran while one was open for 0% of the time, Pallas kernels for 11%

profile of v23, /device:TPU:2, one launch (start us, length us, event | category | flops | bytes accessed | tf_op | source)
XLA Modules:
  0.0 30.0 jit_solution(1355221985700723142)
XLA Ops:
  0.0 0.0 copy-start.12
  0.0 0.0 copy-start.13
  0.0 0.9 %copy-done.13 = bf16[256,32]{0,1:T(8,128)(2,1)S(1)} copy-done((bf16[256,32]{0,1:T(8,128)(2,1)S(1)}, bf16[256,32]{0,1:T(8,128)(2,1)}, u32[]{:S(2)}) %copy-start.13) | copy-done | bytes 16408
  0.9 0.1 shard_map.148.weight_ref
  0.9 0.7 %copy-done.12 = bf16[256,16,256]{2,1,0:T(8,128)(2,1)S(1)} copy-done((bf16[256,16,256]{2,1,0:T(8,128)(2,1)S(1)}, bf16[256,16,256]{2,1,0:T(8,128)(2,1)}, u32[]{:S(2)}) %copy-start.12) | copy-done | bytes 2097176
  1.6 0.0 copy-start.14
  1.6 1.5 %shard_map.149 = bf16[4,256,128]{2,1,0:T(8,128)(2,1)S(1)} custom-call(bf16[256,16,256]{2,1,0:T(8,128)(2,1)S(1)} %copy-done.12, bf16[256,128]{1,0:T(8,128)(2,1)S(1)} %shard_map.148.weight_ref), custom_call_target="tpu_custom_call" | custom-call | flops 1073741824 | bytes 4194304 | tf_op jit(solution)/shard_map/pallas_call | solution.py:144
  3.1 0.0 copy-start.3
  3.1 2.6 %collective-permute-start = (bf16[4,256,128]{2,1,0:T(8,128)(2,1)S(1)}, bf16[4,256,128]{2,1,0:T(8,128)(2,1)S(1)}, u32[]{:S(2)}, u32[]{:S(2)}) collective-permute-start(bf16[4,256,128]{2,1,0:T(8,128)(2,1)S(1)} %shard_map.149), channel_id=1, source_target_pairs={{3,0},{4,1},{10,2},{14,3},{0,4},{7,5},{8,6},{12,7},{2,8},{6,9},{9,... | collective-permute-start | bytes 786440 | tf_op jit(solution)/shard_map/ppermute | solution.py:465
  5.7 0.0 copy-done.14
  5.7 0.1 shard_map.145.weight_ref
  5.8 0.0 copy-start
  5.8 0.0 copy-start.4
  5.8 0.0 copy-start.9
  5.8 0.0 copy-start.10
  5.9 0.0 copy-start.11
  5.9 0.0 copy-done.3
  5.9 0.0 copy-start.5
  5.9 0.0 copy-start.6
  5.9 1.6 %shard_map.146.zl_ref = bf16[4,256,128]{2,1,0:T(8,128)(2,1)S(1)} custom-call(bf16[256,16,256]{2,1,0:T(8,128)(2,1)S(1)} %copy-done.12, bf16[256,128]{1,0:T(8,128)(2,1)S(1)} %shard_map.145.weight_ref, s32[64,256]{1,0:T(8,128)S(1)} %bitcast.5), custom_call_target="tpu_custom_call" | custom-call | flops 1073741824 | bytes 4194304 | tf_op jit(solution)/shard_map/pallas_call | solution.py:144
  7.5 0.0 copy-start.7
  7.5 0.0 copy-start.1
  7.5 0.0 copy-start.2
  7.5 0.0 copy-start.8
  7.5 0.0 copy-done
  7.5 0.0 copy-done.4
  7.5 0.0 copy-done.9
  7.6 0.0 copy-done.10
  7.6 0.0 copy-done.11
  7.6 0.9 %shard_map.147 = (bf16[2,512,128]{2,1,0:T(8,128)(2,1)S(1)}, f32[256,128]{1,0:T(8,128)S(1)}, f32[256,128]{1,0:T(8,128)S(1)}, f32[256,128]{1,0:T(8,128)S(1)}, bf16...) custom-call(bf16[4,256,128]{2,1,0:T(8,128)(2,1)S(1)} %shard_map.146.zl_ref, s32[64,256]{1,0:T(8,128)S(1)} %bitcast.6, ...), custom_call_target="tpu_custom_call" | custom-call | flops 134217728 | bytes 2097152 | tf_op jit(solution)/shard_map/pallas_call | solution.py:217
  8.5 4.7 %collective-permute-done.refs_0_ = bf16[4,256,128]{2,1,0:T(8,128)(2,1)S(1)} collective-permute-done((bf16[4,256,128]{2,1,0:T(8,128)(2,1)S(1)}, bf16[4,256,128]{2,1,0:T(8,128)(2,1)S(1)}, u32[]{:S(2)}, u32[]{:S(2)}) %collective-permute-start) | collective-permute-done | bytes 262176 | tf_op jit(solution)/shard_map/ppermute | solution.py:465
  13.3 0.0 copy-done.5
  13.3 0.0 copy-done.6
  13.3 1.2 %shard_map.150 = (bf16[2,256,128]{2,1,0:T(8,128)(2,1)S(1)}, bf16[256,128]{1,0:T(8,128)(2,1)S(1)}, bf16[256,128]{1,0:T(8,128)(2,1)S(1)}) custom-call(bf16[2,512,128]{2,1,0:T(8,128)(2,1)S(1)} %get-tuple-element.16.zlt_ref, bf16[4,256,128]{2,1,0:T(8,128)(2,1)S(1)} %collective-permute-done.refs_0_, bf16[4,256,128]{2,1,0:T(8,128)(2,1)S(1)} %get-tuple-element.17.refs_1_, ...), custom_call_target="tpu_custom_call" | custom-call | flops 268435456 | bytes 2097152 | tf_op jit(solution)/shard_map/pallas_call | solution.py:293
  14.5 0.1 collective-permute-start.1
  14.6 0.1 collective-permute-start.2
  14.6 1.2 %collective-permute-done.1.refs_1_ = bf16[2,256,128]{2,1,0:T(8,128)(2,1)S(1)} collective-permute-done((bf16[2,256,128]{2,1,0:T(8,128)(2,1)S(1)}, bf16[2,256,128]{2,1,0:T(8,128)(2,1)S(1)}, u32[]{:S(2)}, u32[]{:S(2)}) %collective-permute-start.1) | collective-permute-done | bytes 131104 | tf_op jit(solution)/shard_map/ppermute | solution.py:465
  15.9 3.7 %collective-permute-start.5 = (bf16[2,256,128]{2,1,0:T(8,128)(2,1)S(1)}, bf16[2,256,128]{2,1,0:T(8,128)(2,1)S(1)}, u32[]{:S(2)}, u32[]{:S(2)}) collective-permute-start(bf16[2,256,128]{2,1,0:T(8,128)(2,1)S(1)} %pad_maximum_fusion), channel_id=1, source_target_pairs={{1,0},{6,1},{8,2},{12,3},{2,4},{5,5},{10,6},{14,7},{0,8},{4,9},{11... | collective-permute-start | bytes 393224 | tf_op jit(solution)/shard_map/ppermute | solution.py:465
  19.6 2.1 %collective-permute-start.4 = (bf16[2,256,128]{2,1,0:T(8,128)(2,1)S(1)}, bf16[2,256,128]{2,1,0:T(8,128)(2,1)S(1)}, u32[]{:S(2)}, u32[]{:S(2)}) collective-permute-start(bf16[2,256,128]{2,1,0:T(8,128)(2,1)S(1)} %pad_maximum_fusion), channel_id=1, source_target_pairs={{3,0},{4,1},{10,2},{14,3},{0,4},{7,5},{8,6},{12,7},{2,8},{6,9},{9,... | collective-permute-start | bytes 393224 | tf_op jit(solution)/shard_map/ppermute | solution.py:465
  21.7 0.0 collective-permute-done.2.refs_2_
  21.7 0.0 collective-permute-start.3
  21.7 1.3 %collective-permute-done.3.refs_3_ = bf16[256,128]{1,0:T(8,128)(2,1)S(1)} collective-permute-done((bf16[256,128]{1,0:T(8,128)(2,1)S(1)}, bf16[256,128]{1,0:T(8,128)(2,1)S(1)}, u32[]{:S(2)}, u32[]{:S(2)}) %collective-permute-start.3) | collective-permute-done | bytes 65568 | tf_op jit(solution)/shard_map/ppermute | solution.py:465
  23.0 4.4 %collective-permute-done.5.refs_4_ = bf16[2,256,128]{2,1,0:T(8,128)(2,1)S(1)} collective-permute-done((bf16[2,256,128]{2,1,0:T(8,128)(2,1)S(1)}, bf16[2,256,128]{2,1,0:T(8,128)(2,1)S(1)}, u32[]{:S(2)}, u32[]{:S(2)}) %collective-permute-start.5) | collective-permute-done | bytes 131104 | tf_op jit(solution)/shard_map/ppermute | solution.py:465
  27.4 0.0 copy-done.7
  27.4 0.7 %shard_map.151 = (f32[256,128]{1,0:T(8,128)S(1)}, f32[256,128]{1,0:T(8,128)S(1)}) custom-call(bf16[2,256,128]{2,1,0:T(8,128)(2,1)S(1)} %get-tuple-element.22.refs_0_, bf16[2,256,128]{2,1,0:T(8,128)(2,1)S(1)} %collective-permute-done.1.refs_1_, bf16[256,128]{1,0:T(8,128)(2,1)S(1)} %collective-permute-done.2.refs_2_, ...), custom_call_target="tpu_custom_call" | custom-call | flops 67108864 | bytes 1048576 | tf_op jit(solution)/shard_map/pallas_call | solution.py:414
  28.1 0.0 collective-permute-done.4.refs_4_
  28.1 0.0 copy-done.1
  28.1 0.0 copy-done.2
  28.1 0.0 copy-done.8
  28.2 1.9 %shard_map.152 = bf16[16,16,128]{2,1,0:T(8,128)(2,1)} custom-call(bf16[2,256,128]{2,1,0:T(8,128)(2,1)S(1)} %get-tuple-element.22.refs_0_, bf16[2,256,128]{2,1,0:T(8,128)(2,1)S(1)} %collective-permute-done.1.refs_1_, bf16[256,128]{1,0:T(8,128)(2,1)S(1)} %collective-permute-done.2.refs_2_, bf16[256,128]{1,0:T(8,128)(2,1)S(1)} %collective-permute-done.3.refs_3_, ...), custom_call_target="tpu_custom_call" | custom-call | flops 134217728 | bytes 2097152 | tf_op jit(solution)/shard_map/pallas_call | solution.py:425
  (3 shorter events, 0.0 us)
Async XLA Ops:
  0.0 1.6 %copy-start.12 = (bf16[256,16,256]{2,1,0:T(8,128)(2,1)S(1)}, bf16[256,16,256]{2,1,0:T(8,128)(2,1)}, u32[]{:S(2)}) copy-start(bf16[256,16,256]{2,1,0:T(8,128)(2,1)} %x_ref.3) | copy-start | bytes 6291460
  0.0 0.9 %copy-start.13 = (bf16[256,32]{0,1:T(8,128)(2,1)S(1)}, bf16[256,32]{0,1:T(8,128)(2,1)}, u32[]{:S(2)}) copy-start(bf16[256,32]{0,1:T(8,128)(2,1)} %param.21) | copy-start | bytes 49156
  1.6 4.1 %copy-start.14 = (bf16[256,32]{0,1:T(8,128)(2,1)S(1)}, bf16[256,32]{0,1:T(8,128)(2,1)}, u32[]{:S(2)}) copy-start(bf16[256,32]{0,1:T(8,128)(2,1)} %param.20) | copy-start | bytes 49156
  3.1 2.8 %copy-start.3 = (s32[256,64]{0,1:T(8,128)S(1)}, s32[256,64]{0,1:T(8,128)}, u32[]{:S(2)}) copy-start(s32[256,64]{0,1:T(8,128)} %param.16) | copy-start | bytes 196612
  3.1 10.1 %collective-permute-start = (bf16[4,256,128]{2,1,0:T(8,128)(2,1)S(1)}, bf16[4,256,128]{2,1,0:T(8,128)(2,1)S(1)}, u32[]{:S(2)}, u32[]{:S(2)}) collective-permute-start(bf16[4,256,128]{2,1,0:T(8,128)(2,1)S(1)} %shard_map.149), channel_id=1, source_target_pairs={{3,0},{4,1},{10,2},{14,3},{0,4},{7,5},{8,6},{12,7},{2,8},{6,9},{9,... | collective-permute-start | bytes 786440 | tf_op jit(solution)/shard_map/ppermute | solution.py:465
  5.8 1.7 %copy-start = (f32[32,32,128]{2,1,0:T(8,128)S(1)}, f32[32,32,128]{2,1,0:T(8,128)}, u32[]{:S(2)}) copy-start(f32[32,32,128]{2,1,0:T(8,128)} %proj_ref.1) | copy-start | bytes 1572868
  5.8 1.7 %copy-start.4 = (bf16[16,16,128]{2,1,0:T(8,128)(2,1)S(1)}, bf16[16,16,128]{2,1,0:T(8,128)(2,1)}, u32[]{:S(2)}) copy-start(bf16[16,16,128]{2,1,0:T(8,128)(2,1)} %pair_ref.1) | copy-start | bytes 196612
  5.8 1.7 %copy-start.9 = (bf16[66,128]{1,0:T(8,128)(2,1)S(1)}, bf16[66,128]{1,0:T(8,128)(2,1)}, u32[]{:S(2)}) copy-start(bf16[66,128]{1,0:T(8,128)(2,1)} %table_ref.1) | copy-start | bytes 50692
  5.8 1.7 %copy-start.10 = (s32[64]{0:T(128)S(1)}, s32[64]{0:T(128)}, u32[]{:S(2)}) copy-start(s32[64]{0:T(128)} %param.18) | copy-start | bytes 772
  5.9 1.7 %copy-start.11 = (s32[64]{0:T(128)S(1)}, s32[64]{0:T(128)}, u32[]{:S(2)}) copy-start(s32[64]{0:T(128)} %param.19) | copy-start | bytes 772
  5.9 7.4 %copy-start.5 = (bf16[128,256]{1,0:T(8,128)(2,1)S(1)}, bf16[128,256]{1,0:T(8,128)(2,1)}, u32[]{:S(2)}) copy-start(bf16[128,256]{1,0:T(8,128)(2,1)} %refs_6_.2) | copy-start | bytes 196612
  5.9 7.4 %copy-start.6 = (bf16[128,256]{1,0:T(8,128)(2,1)S(1)}, bf16[128,256]{1,0:T(8,128)(2,1)}, u32[]{:S(2)}) copy-start(bf16[128,256]{1,0:T(8,128)(2,1)} %refs_7_.1) | copy-start | bytes 196612
  7.5 19.9 %copy-start.7 = (bf16[128,128]{1,0:T(8,128)(2,1)S(1)}, bf16[128,128]{1,0:T(8,128)(2,1)}, u32[]{:S(2)}) copy-start(bf16[128,128]{1,0:T(8,128)(2,1)} %refs_6_.3) | copy-start | bytes 98308
  7.5 20.6 %copy-start.1 = (bf16[128,512]{1,0:T(8,128)(2,1)S(1)}, bf16[128,512]{1,0:T(8,128)(2,1)}, u32[]{:S(2)}) copy-start(bf16[128,512]{1,0:T(8,128)(2,1)} %refs_9_.1) | copy-start | bytes 393220
  7.5 20.6 %copy-start.2 = (bf16[512,128]{1,0:T(8,128)(2,1)S(1)}, bf16[512,128]{1,0:T(8,128)(2,1)}, u32[]{:S(2)}) copy-start(bf16[512,128]{1,0:T(8,128)(2,1)} %refs_10_.1) | copy-start | bytes 393220
  7.5 20.6 %copy-start.8 = (bf16[128,128]{1,0:T(8,128)(2,1)S(1)}, bf16[128,128]{1,0:T(8,128)(2,1)}, u32[]{:S(2)}) copy-start(bf16[128,128]{1,0:T(8,128)(2,1)} %refs_8_.1) | copy-start | bytes 98308
  14.5 1.4 %collective-permute-start.1 = (bf16[2,256,128]{2,1,0:T(8,128)(2,1)S(1)}, bf16[2,256,128]{2,1,0:T(8,128)(2,1)S(1)}, u32[]{:S(2)}, u32[]{:S(2)}) collective-permute-start(bf16[2,256,128]{2,1,0:T(8,128)(2,1)S(1)} %get-tuple-element.22.refs_0_), channel_id=1, source_target_pairs={{1,0},{0,1},{3,2},{2,3},{5,4},{4,5},{7,6},{6,7},{9,8},{8,9},{11,10... | collective-permute-start | bytes 393224 | tf_op jit(solution)/shard_map/ppermute | solution.py:465
  14.6 7.1 %collective-permute-start.2 = (bf16[256,128]{1,0:T(8,128)(2,1)S(1)}, bf16[256,128]{1,0:T(8,128)(2,1)S(1)}, u32[]{:S(2)}, u32[]{:S(2)}) collective-permute-start(bf16[256,128]{1,0:T(8,128)(2,1)S(1)} %get-tuple-element.23), channel_id=1, source_target_pairs={{2,0},{3,1},{0,2},{1,3},{6,4},{7,5},{4,6},{5,7},{10,8},{11,9},{8,1... | collective-permute-start | bytes 196616 | tf_op jit(solution)/shard_map/ppermute | solution.py:465
  15.9 11.5 %collective-permute-start.5 = (bf16[2,256,128]{2,1,0:T(8,128)(2,1)S(1)}, bf16[2,256,128]{2,1,0:T(8,128)(2,1)S(1)}, u32[]{:S(2)}, u32[]{:S(2)}) collective-permute-start(bf16[2,256,128]{2,1,0:T(8,128)(2,1)S(1)} %pad_maximum_fusion), channel_id=1, source_target_pairs={{1,0},{6,1},{8,2},{12,3},{2,4},{5,5},{10,6},{14,7},{0,8},{4,9},{11... | collective-permute-start | bytes 393224 | tf_op jit(solution)/shard_map/ppermute | solution.py:465
  19.6 8.5 %collective-permute-start.4 = (bf16[2,256,128]{2,1,0:T(8,128)(2,1)S(1)}, bf16[2,256,128]{2,1,0:T(8,128)(2,1)S(1)}, u32[]{:S(2)}, u32[]{:S(2)}) collective-permute-start(bf16[2,256,128]{2,1,0:T(8,128)(2,1)S(1)} %pad_maximum_fusion), channel_id=1, source_target_pairs={{3,0},{4,1},{10,2},{14,3},{0,4},{7,5},{8,6},{12,7},{2,8},{6,9},{9,... | collective-permute-start | bytes 393224 | tf_op jit(solution)/shard_map/ppermute | solution.py:465
  21.7 1.3 %collective-permute-start.3 = (bf16[256,128]{1,0:T(8,128)(2,1)S(1)}, bf16[256,128]{1,0:T(8,128)(2,1)S(1)}, u32[]{:S(2)}, u32[]{:S(2)}) collective-permute-start(bf16[256,128]{1,0:T(8,128)(2,1)S(1)} %collective-permute-done.2.refs_2_), channel_id=1, source_target_pairs={{1,0},{0,1},{3,2},{2,3},{5,4},{4,5},{7,6},{6,7},{9,8},{8,9},{11,10... | collective-permute-start | bytes 196616 | tf_op jit(solution)/shard_map/ppermute | solution.py:465

commit v24 on v23

--- a/solution.py
+++ b/solution.py
@@ -352,7 +352,7 @@
         else:
             totals = tuple(start[pl.ds(place, rows), :] for place in places)
         for index, step in enumerate(steps):
-            sub = lax.rem(first_sub + 2 * step, subs)
+            sub = lax.rem(first_sub + 2 * step + 2, subs)
             pair = rights[turn * len(steps) + index]
             for member, slot in enumerate((sub, other(sub))):
 
@@ -497,7 +497,7 @@
         fetch(
             right,
             lambda a, b, t=turn, m=step: (
-                owner(a, b, t), (sender(a, b, subs, ratio) + 2 * m) % subs
+                owner(a, b, t), (sender(a, b, subs, ratio) + 2 * m + 2) % subs
             ),
         )
         for turn in range(ratio)

time: 30.3 us -> 29.6 us (0.977)
  the two profiles are of different devices: /device:TPU:2 before, /device:TPU:6 now
where the time goes in v24:
time: 29.6 us; the launch traced here: 29.3 us
  waiting for transfers between devices  10 us (34%)
  starting transfers between devices  9.49 us (32%)
  Pallas kernels  7.92 us (27%)
  local copies, waits for them, and re-layouts  1.62 us (5%)
    ppermute x6, waiting for transfers between devices, fetch(): return lax.ppermute(values, ('dap', 'sub'), perm)  10 us
    ppermute x6, starting transfers between devices, fetch(): return lax.ppermute(values, ('dap', 'sub'), perm)  9.49 us
    pallas_call x2, Pallas kernels, factor(): pl.pallas_call(functools.partial(factor_kernel, mask is not None, hidden)...  3.06 us
    pallas_call x1, Pallas kernels, triangle_update(): pl.pallas_call(functools.partial(last_kernel, late, twos, ratio, cols), o...  1.87 us
    unnamed x30, local copies, waits for them, and re-layouts  1.61 us
    pallas_call x1, Pallas kernels, pair_update(): pl.pallas_call(functools.partial(pair_kernel, ratio, hidden), out_shape=(...  1.19 us
    pallas_call x1, Pallas kernels, prepare(): pl.pallas_call(prepare_kernel, out_shape=(jax.ShapeDtypeStruct((zl.shape[...  0.94 us
    pallas_call x1, Pallas kernels, triangle_update(): pl.pallas_call(functools.partial(first_kernel, early, twos, ratio, cols),...  0.73 us
  transfers between devices with their start and end apart: 6, of which 4 were waited for; matrix products, arithmetic and copies ran while one was open for 0% of the time, Pallas kernels for 11%

profile of v24, /device:TPU:6, one launch (start us, length us, event | category | flops | bytes accessed | tf_op | source)
XLA Modules:
  0.0 29.3 jit_solution(5639102404187901144)
XLA Ops:
  0.0 0.0 copy-start.12
  0.0 0.0 copy-start.13
  0.0 0.9 %copy-done.13 = bf16[256,32]{0,1:T(8,128)(2,1)S(1)} copy-done((bf16[256,32]{0,1:T(8,128)(2,1)S(1)}, bf16[256,32]{0,1:T(8,128)(2,1)}, u32[]{:S(2)}) %copy-start.13) | copy-done | bytes 16408
  0.9 0.1 shard_map.148.weight_ref
  0.9 0.7 %copy-done.12 = bf16[256,16,256]{2,1,0:T(8,128)(2,1)S(1)} copy-done((bf16[256,16,256]{2,1,0:T(8,128)(2,1)S(1)}, bf16[256,16,256]{2,1,0:T(8,128)(2,1)}, u32[]{:S(2)}) %copy-start.12) | copy-done | bytes 2097176
  1.6 0.0 copy-start.14
  1.6 1.5 %shard_map.149 = bf16[4,256,128]{2,1,0:T(8,128)(2,1)S(1)} custom-call(bf16[256,16,256]{2,1,0:T(8,128)(2,1)S(1)} %copy-done.12, bf16[256,128]{1,0:T(8,128)(2,1)S(1)} %shard_map.148.weight_ref), custom_call_target="tpu_custom_call" | custom-call | flops 1073741824 | bytes 4194304 | tf_op jit(solution)/shard_map/pallas_call | solution.py:144
  3.1 0.0 copy-start.3
  3.1 2.6 %collective-permute-start = (bf16[4,256,128]{2,1,0:T(8,128)(2,1)S(1)}, bf16[4,256,128]{2,1,0:T(8,128)(2,1)S(1)}, u32[]{:S(2)}, u32[]{:S(2)}) collective-permute-start(bf16[4,256,128]{2,1,0:T(8,128)(2,1)S(1)} %shard_map.149), channel_id=1, source_target_pairs={{3,0},{4,1},{10,2},{14,3},{0,4},{7,5},{8,6},{12,7},{2,8},{6,9},{9,... | collective-permute-start | bytes 786440 | tf_op jit(solution)/shard_map/ppermute | solution.py:465
  5.7 0.0 copy-done.14
  5.7 0.1 shard_map.145.weight_ref
  5.8 0.0 copy-start
  5.8 0.0 copy-start.4
  5.8 0.0 copy-start.9
  5.8 0.0 copy-start.10
  5.9 0.0 copy-start.11
  5.9 0.0 copy-done.3
  5.9 0.0 copy-start.5
  5.9 0.0 copy-start.6
  5.9 1.6 %shard_map.146.zl_ref = bf16[4,256,128]{2,1,0:T(8,128)(2,1)S(1)} custom-call(bf16[256,16,256]{2,1,0:T(8,128)(2,1)S(1)} %copy-done.12, bf16[256,128]{1,0:T(8,128)(2,1)S(1)} %shard_map.145.weight_ref, s32[64,256]{1,0:T(8,128)S(1)} %bitcast.5), custom_call_target="tpu_custom_call" | custom-call | flops 1073741824 | bytes 4194304 | tf_op jit(solution)/shard_map/pallas_call | solution.py:144
  7.5 0.0 copy-start.7
  7.5 0.0 copy-start.1
  7.5 0.0 copy-start.2
  7.5 0.0 copy-start.8
  7.5 0.0 copy-done
  7.5 0.0 copy-done.4
  7.5 0.0 copy-done.9
  7.6 0.0 copy-done.10
  7.6 0.0 copy-done.11
  7.6 0.9 %shard_map.147 = (bf16[2,512,128]{2,1,0:T(8,128)(2,1)S(1)}, f32[256,128]{1,0:T(8,128)S(1)}, f32[256,128]{1,0:T(8,128)S(1)}, f32[256,128]{1,0:T(8,128)S(1)}, bf16...) custom-call(bf16[4,256,128]{2,1,0:T(8,128)(2,1)S(1)} %shard_map.146.zl_ref, s32[64,256]{1,0:T(8,128)S(1)} %bitcast.6, ...), custom_call_target="tpu_custom_call" | custom-call | flops 134217728 | bytes 2097152 | tf_op jit(solution)/shard_map/pallas_call | solution.py:217
  8.5 4.7 %collective-permute-done.refs_0_ = bf16[4,256,128]{2,1,0:T(8,128)(2,1)S(1)} collective-permute-done((bf16[4,256,128]{2,1,0:T(8,128)(2,1)S(1)}, bf16[4,256,128]{2,1,0:T(8,128)(2,1)S(1)}, u32[]{:S(2)}, u32[]{:S(2)}) %collective-permute-start) | collective-permute-done | bytes 262176 | tf_op jit(solution)/shard_map/ppermute | solution.py:465
  13.3 0.0 copy-done.5
  13.3 0.0 copy-done.6
  13.3 1.2 %shard_map.150 = (bf16[2,256,128]{2,1,0:T(8,128)(2,1)S(1)}, bf16[256,128]{1,0:T(8,128)(2,1)S(1)}, bf16[256,128]{1,0:T(8,128)(2,1)S(1)}) custom-call(bf16[2,512,128]{2,1,0:T(8,128)(2,1)S(1)} %get-tuple-element.16.zlt_ref, bf16[4,256,128]{2,1,0:T(8,128)(2,1)S(1)} %collective-permute-done.refs_0_, bf16[4,256,128]{2,1,0:T(8,128)(2,1)S(1)} %get-tuple-element.17.refs_1_, ...), custom_call_target="tpu_custom_call" | custom-call | flops 268435456 | bytes 2097152 | tf_op jit(solution)/shard_map/pallas_call | solution.py:293
  14.5 0.1 collective-permute-start.1
  14.6 0.1 collective-permute-start.2
  14.6 1.2 %collective-permute-done.1.refs_1_ = bf16[2,256,128]{2,1,0:T(8,128)(2,1)S(1)} collective-permute-done((bf16[2,256,128]{2,1,0:T(8,128)(2,1)S(1)}, bf16[2,256,128]{2,1,0:T(8,128)(2,1)S(1)}, u32[]{:S(2)}, u32[]{:S(2)}) %collective-permute-start.1) | collective-permute-done | bytes 131104 | tf_op jit(solution)/shard_map/ppermute | solution.py:465
  15.9 1.5 %collective-permute-start.5 = (bf16[2,256,128]{2,1,0:T(8,128)(2,1)S(1)}, bf16[2,256,128]{2,1,0:T(8,128)(2,1)S(1)}, u32[]{:S(2)}, u32[]{:S(2)}) collective-permute-start(bf16[2,256,128]{2,1,0:T(8,128)(2,1)S(1)} %pad_maximum_fusion), channel_id=1, source_target_pairs={{3,0},{4,1},{10,2},{14,3},{0,4},{7,5},{8,6},{12,7},{2,8},{6,9},{9,... | collective-permute-start | bytes 393224 | tf_op jit(solution)/shard_map/ppermute | solution.py:465
  17.4 2.5 %collective-permute-start.4 = (bf16[2,256,128]{2,1,0:T(8,128)(2,1)S(1)}, bf16[2,256,128]{2,1,0:T(8,128)(2,1)S(1)}, u32[]{:S(2)}, u32[]{:S(2)}) collective-permute-start(bf16[2,256,128]{2,1,0:T(8,128)(2,1)S(1)} %pad_maximum_fusion), channel_id=1, source_target_pairs={{1,0},{6,1},{8,2},{12,3},{2,4},{5,5},{10,6},{14,7},{0,8},{4,9},{11... | collective-permute-start | bytes 393224 | tf_op jit(solution)/shard_map/ppermute | solution.py:465
  19.9 0.0 collective-permute-done.2.refs_2_
  19.9 2.8 %collective-permute-start.3 = (bf16[256,128]{1,0:T(8,128)(2,1)S(1)}, bf16[256,128]{1,0:T(8,128)(2,1)S(1)}, u32[]{:S(2)}, u32[]{:S(2)}) collective-permute-start(bf16[256,128]{1,0:T(8,128)(2,1)S(1)} %collective-permute-done.2.refs_2_), channel_id=1, source_target_pairs={{1,0},{0,1},{3,2},{2,3},{5,4},{4,5},{7,6},{6,7},{9,8},{8,9},{11,10... | collective-permute-start | bytes 196616 | tf_op jit(solution)/shard_map/ppermute | solution.py:465
  22.6 0.9 %collective-permute-done.3.refs_3_ = bf16[256,128]{1,0:T(8,128)(2,1)S(1)} collective-permute-done((bf16[256,128]{1,0:T(8,128)(2,1)S(1)}, bf16[256,128]{1,0:T(8,128)(2,1)S(1)}, u32[]{:S(2)}, u32[]{:S(2)}) %collective-permute-start.3) | collective-permute-done | bytes 65568 | tf_op jit(solution)/shard_map/ppermute | solution.py:465
  23.5 0.0 collective-permute-done.5.refs_4_
  23.6 0.0 copy-done.7
  23.6 0.7 %shard_map.151 = (f32[256,128]{1,0:T(8,128)S(1)}, f32[256,128]{1,0:T(8,128)S(1)}) custom-call(bf16[2,256,128]{2,1,0:T(8,128)(2,1)S(1)} %get-tuple-element.22.refs_0_, bf16[2,256,128]{2,1,0:T(8,128)(2,1)S(1)} %collective-permute-done.1.refs_1_, bf16[256,128]{1,0:T(8,128)(2,1)S(1)} %collective-permute-done.2.refs_2_, ...), custom_call_target="tpu_custom_call" | custom-call | flops 67108864 | bytes 1048576 | tf_op jit(solution)/shard_map/pallas_call | solution.py:414
  24.3 3.2 %collective-permute-done.4.refs_4_ = bf16[2,256,128]{2,1,0:T(8,128)(2,1)S(1)} collective-permute-done((bf16[2,256,128]{2,1,0:T(8,128)(2,1)S(1)}, bf16[2,256,128]{2,1,0:T(8,128)(2,1)S(1)}, u32[]{:S(2)}, u32[]{:S(2)}) %collective-permute-start.4) | collective-permute-done | bytes 131104 | tf_op jit(solution)/shard_map/ppermute | solution.py:465
  27.5 0.0 copy-done.1
  27.5 0.0 copy-done.2
  27.5 0.0 copy-done.8
  27.5 1.9 %shard_map.152 = bf16[16,16,128]{2,1,0:T(8,128)(2,1)} custom-call(bf16[2,256,128]{2,1,0:T(8,128)(2,1)S(1)} %get-tuple-element.22.refs_0_, bf16[2,256,128]{2,1,0:T(8,128)(2,1)S(1)} %collective-permute-done.1.refs_1_, bf16[256,128]{1,0:T(8,128)(2,1)S(1)} %collective-permute-done.2.refs_2_, bf16[256,128]{1,0:T(8,128)(2,1)S(1)} %collective-permute-done.3.refs_3_, ...), custom_call_target="tpu_custom_call" | custom-call | flops 134217728 | bytes 2097152 | tf_op jit(solution)/shard_map/pallas_call | solution.py:425
  (3 shorter events, 0.0 us)
Async XLA Ops:
  0.0 1.6 %copy-start.12 = (bf16[256,16,256]{2,1,0:T(8,128)(2,1)S(1)}, bf16[256,16,256]{2,1,0:T(8,128)(2,1)}, u32[]{:S(2)}) copy-start(bf16[256,16,256]{2,1,0:T(8,128)(2,1)} %x_ref.3) | copy-start | bytes 6291460
  0.0 0.9 %copy-start.13 = (bf16[256,32]{0,1:T(8,128)(2,1)S(1)}, bf16[256,32]{0,1:T(8,128)(2,1)}, u32[]{:S(2)}) copy-start(bf16[256,32]{0,1:T(8,128)(2,1)} %param.21) | copy-start | bytes 49156
  1.6 4.1 %copy-start.14 = (bf16[256,32]{0,1:T(8,128)(2,1)S(1)}, bf16[256,32]{0,1:T(8,128)(2,1)}, u32[]{:S(2)}) copy-start(bf16[256,32]{0,1:T(8,128)(2,1)} %param.20) | copy-start | bytes 49156
  3.1 2.8 %copy-start.3 = (s32[256,64]{0,1:T(8,128)S(1)}, s32[256,64]{0,1:T(8,128)}, u32[]{:S(2)}) copy-start(s32[256,64]{0,1:T(8,128)} %param.16) | copy-start | bytes 196612
  3.1 10.1 %collective-permute-start = (bf16[4,256,128]{2,1,0:T(8,128)(2,1)S(1)}, bf16[4,256,128]{2,1,0:T(8,128)(2,1)S(1)}, u32[]{:S(2)}, u32[]{:S(2)}) collective-permute-start(bf16[4,256,128]{2,1,0:T(8,128)(2,1)S(1)} %shard_map.149), channel_id=1, source_target_pairs={{3,0},{4,1},{10,2},{14,3},{0,4},{7,5},{8,6},{12,7},{2,8},{6,9},{9,... | collective-permute-start | bytes 786440 | tf_op jit(solution)/shard_map/ppermute | solution.py:465
  5.8 1.7 %copy-start = (f32[32,32,128]{2,1,0:T(8,128)S(1)}, f32[32,32,128]{2,1,0:T(8,128)}, u32[]{:S(2)}) copy-start(f32[32,32,128]{2,1,0:T(8,128)} %proj_ref.1) | copy-start | bytes 1572868
  5.8 1.7 %copy-start.4 = (bf16[16,16,128]{2,1,0:T(8,128)(2,1)S(1)}, bf16[16,16,128]{2,1,0:T(8,128)(2,1)}, u32[]{:S(2)}) copy-start(bf16[16,16,128]{2,1,0:T(8,128)(2,1)} %pair_ref.1) | copy-start | bytes 196612
  5.8 1.7 %copy-start.9 = (bf16[66,128]{1,0:T(8,128)(2,1)S(1)}, bf16[66,128]{1,0:T(8,128)(2,1)}, u32[]{:S(2)}) copy-start(bf16[66,128]{1,0:T(8,128)(2,1)} %table_ref.1) | copy-start | bytes 50692
  5.8 1.7 %copy-start.10 = (s32[64]{0:T(128)S(1)}, s32[64]{0:T(128)}, u32[]{:S(2)}) copy-start(s32[64]{0:T(128)} %param.18) | copy-start | bytes 772
  5.9 1.7 %copy-start.11 = (s32[64]{0:T(128)S(1)}, s32[64]{0:T(128)}, u32[]{:S(2)}) copy-start(s32[64]{0:T(128)} %param.19) | copy-start | bytes 772
  5.9 7.4 %copy-start.5 = (bf16[128,256]{1,0:T(8,128)(2,1)S(1)}, bf16[128,256]{1,0:T(8,128)(2,1)}, u32[]{:S(2)}) copy-start(bf16[128,256]{1,0:T(8,128)(2,1)} %refs_6_.2) | copy-start | bytes 196612
  5.9 7.4 %copy-start.6 = (bf16[128,256]{1,0:T(8,128)(2,1)S(1)}, bf16[128,256]{1,0:T(8,128)(2,1)}, u32[]{:S(2)}) copy-start(bf16[128,256]{1,0:T(8,128)(2,1)} %refs_7_.1) | copy-start | bytes 196612
  7.5 16.1 %copy-start.7 = (bf16[128,128]{1,0:T(8,128)(2,1)S(1)}, bf16[128,128]{1,0:T(8,128)(2,1)}, u32[]{:S(2)}) copy-start(bf16[128,128]{1,0:T(8,128)(2,1)} %refs_6_.3) | copy-start | bytes 98308
  7.5 20.0 %copy-start.1 = (bf16[128,512]{1,0:T(8,128)(2,1)S(1)}, bf16[128,512]{1,0:T(8,128)(2,1)}, u32[]{:S(2)}) copy-start(bf16[128,512]{1,0:T(8,128)(2,1)} %refs_9_.1) | copy-start | bytes 393220
  7.5 20.0 %copy-start.2 = (bf16[512,128]{1,0:T(8,128)(2,1)S(1)}, bf16[512,128]{1,0:T(8,128)(2,1)}, u32[]{:S(2)}) copy-start(bf16[512,128]{1,0:T(8,128)(2,1)} %refs_10_.1) | copy-start | bytes 393220
  7.5 20.0 %copy-start.8 = (bf16[128,128]{1,0:T(8,128)(2,1)S(1)}, bf16[128,128]{1,0:T(8,128)(2,1)}, u32[]{:S(2)}) copy-start(bf16[128,128]{1,0:T(8,128)(2,1)} %refs_8_.1) | copy-start | bytes 98308
  14.5 1.4 %collective-permute-start.1 = (bf16[2,256,128]{2,1,0:T(8,128)(2,1)S(1)}, bf16[2,256,128]{2,1,0:T(8,128)(2,1)S(1)}, u32[]{:S(2)}, u32[]{:S(2)}) collective-permute-start(bf16[2,256,128]{2,1,0:T(8,128)(2,1)S(1)} %get-tuple-element.22.refs_0_), channel_id=1, source_target_pairs={{1,0},{0,1},{3,2},{2,3},{5,4},{4,5},{7,6},{6,7},{9,8},{8,9},{11,10... | collective-permute-start | bytes 393224 | tf_op jit(solution)/shard_map/ppermute | solution.py:465
  14.6 5.3 %collective-permute-start.2 = (bf16[256,128]{1,0:T(8,128)(2,1)S(1)}, bf16[256,128]{1,0:T(8,128)(2,1)S(1)}, u32[]{:S(2)}, u32[]{:S(2)}) collective-permute-start(bf16[256,128]{1,0:T(8,128)(2,1)S(1)} %get-tuple-element.23), channel_id=1, source_target_pairs={{2,0},{3,1},{0,2},{1,3},{6,4},{7,5},{4,6},{5,7},{10,8},{11,9},{8,1... | collective-permute-start | bytes 196616 | tf_op jit(solution)/shard_map/ppermute | solution.py:465
  15.9 7.7 %collective-permute-start.5 = (bf16[2,256,128]{2,1,0:T(8,128)(2,1)S(1)}, bf16[2,256,128]{2,1,0:T(8,128)(2,1)S(1)}, u32[]{:S(2)}, u32[]{:S(2)}) collective-permute-start(bf16[2,256,128]{2,1,0:T(8,128)(2,1)S(1)} %pad_maximum_fusion), channel_id=1, source_target_pairs={{3,0},{4,1},{10,2},{14,3},{0,4},{7,5},{8,6},{12,7},{2,8},{6,9},{9,... | collective-permute-start | bytes 393224 | tf_op jit(solution)/shard_map/ppermute | solution.py:465
  17.4 10.1 %collective-permute-start.4 = (bf16[2,256,128]{2,1,0:T(8,128)(2,1)S(1)}, bf16[2,256,128]{2,1,0:T(8,128)(2,1)S(1)}, u32[]{:S(2)}, u32[]{:S(2)}) collective-permute-start(bf16[2,256,128]{2,1,0:T(8,128)(2,1)S(1)} %pad_maximum_fusion), channel_id=1, source_target_pairs={{1,0},{6,1},{8,2},{12,3},{2,4},{5,5},{10,6},{14,7},{0,8},{4,9},{11... | collective-permute-start | bytes 393224 | tf_op jit(solution)/shard_map/ppermute | solution.py:465
  19.9 3.7 %collective-permute-start.3 = (bf16[256,128]{1,0:T(8,128)(2,1)S(1)}, bf16[256,128]{1,0:T(8,128)(2,1)S(1)}, u32[]{:S(2)}, u32[]{:S(2)}) collective-permute-start(bf16[256,128]{1,0:T(8,128)(2,1)S(1)} %collective-permute-done.2.refs_2_), channel_id=1, source_target_pairs={{1,0},{0,1},{3,2},{2,3},{5,4},{4,5},{7,6},{6,7},{9,8},{8,9},{11,10... | collective-permute-start | bytes 196616 | tf_op jit(solution)/shard_map/ppermute | solution.py:465

commit v25 on v24

--- a/solution.py
+++ b/solution.py
@@ -311,11 +311,12 @@
 
 
 SENDERS = ((3, 0, 2, 1), (0, 3, 2, 1), (2, 0, 1, 3), (2, 0, 3, 1))
-
-
-def sender(a, b, subs, ratio):
+PAIR_SENDERS = ((3, 0, 2, 1), (0, 3, 1, 2), (0, 2, 1, 3), (2, 0, 3, 1))
+
+
+def sender(a, b, subs, ratio, table):
     if (subs, ratio) == (4, 1):
-        return SENDERS[b][a]
+        return table[b][a]
     return a // ratio
 
 
@@ -323,7 +324,7 @@
     if (subs, ratio) != (4, 1):
         return a // ratio
     found = 0
-    for col, places in enumerate(SENDERS):
+    for col, places in enumerate(PAIR_SENDERS):
         for row, place in enumerate(places):
             found = jnp.where((a == row) & (b == col), place, found)
     return found
@@ -474,7 +475,7 @@
         fetch(
             zr[part],
             lambda a, b, t=turn, p=part: (
-                owner(a, b, t), (sender(a, b, subs, ratio) + 2 * p) % subs
+                owner(a, b, t), (sender(a, b, subs, ratio, SENDERS) + 2 * p) % subs
             ),
         )
         for turn in range(ratio)
@@ -497,7 +498,8 @@
         fetch(
             right,
             lambda a, b, t=turn, m=step: (
-                owner(a, b, t), (sender(a, b, subs, ratio) + 2 * m + 2) % subs
+                owner(a, b, t),
+                (sender(a, b, subs, ratio, PAIR_SENDERS) + 2 * m + 2) % subs,
             ),
         )
         for turn in range(ratio)

time: 29.6 us -> 29 us (0.980)
  the two profiles are of different devices: /device:TPU:6 before, /device:TPU:1 now
where the time goes in v25:
time: 29 us; the launch traced here: 28.7 us
  starting transfers between devices  14.2 us (49%)
  Pallas kernels  7.92 us (27%)
  waiting for transfers between devices  4.67 us (16%)
  local copies, waits for them, and re-layouts  1.62 us (6%)
    ppermute x6, starting transfers between devices, fetch(): return lax.ppermute(values, ('dap', 'sub'), perm)  14.2 us
    ppermute x6, waiting for transfers between devices, fetch(): return lax.ppermute(values, ('dap', 'sub'), perm)  4.67 us
    pallas_call x2, Pallas kernels, factor(): pl.pallas_call(functools.partial(factor_kernel, mask is not None, hidden)...  3.05 us
    pallas_call x1, Pallas kernels, triangle_update(): pl.pallas_call(functools.partial(last_kernel, late, twos, ratio, cols), o...  1.87 us
    unnamed x30, local copies, waits for them, and re-layouts  1.61 us
    pallas_call x1, Pallas kernels, pair_update(): pl.pallas_call(functools.partial(pair_kernel, ratio, hidden), out_shape=(...  1.19 us
    pallas_call x1, Pallas kernels, prepare(): pl.pallas_call(prepare_kernel, out_shape=(jax.ShapeDtypeStruct((zl.shape[...  0.94 us
    pallas_call x1, Pallas kernels, triangle_update(): pl.pallas_call(functools.partial(first_kernel, early, twos, ratio, cols),...  0.74 us
  transfers between devices with their start and end apart: 6, of which 3 were waited for; matrix products, arithmetic and copies ran while one was open for 0% of the time, Pallas kernels for 12%

profile of v25, /device:TPU:1, one launch (start us, length us, event | category | flops | bytes accessed | tf_op | source)
XLA Modules:
  0.0 28.7 jit_solution(1153673858484974769)
XLA Ops:
  0.0 0.0 copy-start.12
  0.0 0.0 copy-start.13
  0.0 0.9 %copy-done.13 = bf16[256,32]{0,1:T(8,128)(2,1)S(1)} copy-done((bf16[256,32]{0,1:T(8,128)(2,1)S(1)}, bf16[256,32]{0,1:T(8,128)(2,1)}, u32[]{:S(2)}) %copy-start.13) | copy-done | bytes 16408
  0.9 0.1 shard_map.148.weight_ref
  0.9 0.7 %copy-done.12 = bf16[256,16,256]{2,1,0:T(8,128)(2,1)S(1)} copy-done((bf16[256,16,256]{2,1,0:T(8,128)(2,1)S(1)}, bf16[256,16,256]{2,1,0:T(8,128)(2,1)}, u32[]{:S(2)}) %copy-start.12) | copy-done | bytes 2097176
  1.6 0.0 copy-start.14
  1.6 1.5 %shard_map.149 = bf16[4,256,128]{2,1,0:T(8,128)(2,1)S(1)} custom-call(bf16[256,16,256]{2,1,0:T(8,128)(2,1)S(1)} %copy-done.12, bf16[256,128]{1,0:T(8,128)(2,1)S(1)} %shard_map.148.weight_ref), custom_call_target="tpu_custom_call" | custom-call | flops 1073741824 | bytes 4194304 | tf_op jit(solution)/shard_map/pallas_call | solution.py:144
  3.1 0.0 copy-start.3
  3.1 4.8 %collective-permute-start = (bf16[4,256,128]{2,1,0:T(8,128)(2,1)S(1)}, bf16[4,256,128]{2,1,0:T(8,128)(2,1)S(1)}, u32[]{:S(2)}, u32[]{:S(2)}) collective-permute-start(bf16[4,256,128]{2,1,0:T(8,128)(2,1)S(1)} %shard_map.149), channel_id=1, source_target_pairs={{3,0},{4,1},{10,2},{14,3},{0,4},{7,5},{8,6},{12,7},{2,8},{6,9},{9,... | collective-permute-start | bytes 786440 | tf_op jit(solution)/shard_map/ppermute | solution.py:466
  7.9 0.0 copy-done.14
  7.9 0.1 shard_map.145.weight_ref
  8.0 0.0 copy-start
  8.0 0.0 copy-start.4
  8.0 0.0 copy-start.9
  8.0 0.0 copy-start.10
  8.0 0.0 copy-start.11
  8.0 0.0 copy-done.3
  8.0 0.0 copy-start.5
  8.0 0.0 copy-start.6
  8.1 1.6 %shard_map.146.zl_ref = bf16[4,256,128]{2,1,0:T(8,128)(2,1)S(1)} custom-call(bf16[256,16,256]{2,1,0:T(8,128)(2,1)S(1)} %copy-done.12, bf16[256,128]{1,0:T(8,128)(2,1)S(1)} %shard_map.145.weight_ref, s32[64,256]{1,0:T(8,128)S(1)} %bitcast.5), custom_call_target="tpu_custom_call" | custom-call | flops 1073741824 | bytes 4194304 | tf_op jit(solution)/shard_map/pallas_call | solution.py:144
  9.6 0.0 copy-start.7
  9.6 0.0 copy-start.1
  9.7 0.0 copy-start.2
  9.7 0.0 copy-start.8
  9.7 0.0 copy-done
  9.7 0.0 copy-done.4
  9.7 0.0 copy-done.9
  9.7 0.0 copy-done.10
  9.7 0.0 copy-done.11
  9.7 0.9 %shard_map.147 = (bf16[2,512,128]{2,1,0:T(8,128)(2,1)S(1)}, f32[256,128]{1,0:T(8,128)S(1)}, f32[256,128]{1,0:T(8,128)S(1)}, f32[256,128]{1,0:T(8,128)S(1)}, bf16...) custom-call(bf16[4,256,128]{2,1,0:T(8,128)(2,1)S(1)} %shard_map.146.zl_ref, s32[64,256]{1,0:T(8,128)S(1)} %bitcast.6, ...), custom_call_target="tpu_custom_call" | custom-call | flops 134217728 | bytes 2097152 | tf_op jit(solution)/shard_map/pallas_call | solution.py:217
  10.7 1.9 %collective-permute-done.refs_0_ = bf16[4,256,128]{2,1,0:T(8,128)(2,1)S(1)} collective-permute-done((bf16[4,256,128]{2,1,0:T(8,128)(2,1)S(1)}, bf16[4,256,128]{2,1,0:T(8,128)(2,1)S(1)}, u32[]{:S(2)}, u32[]{:S(2)}) %collective-permute-start) | collective-permute-done | bytes 262176 | tf_op jit(solution)/shard_map/ppermute | solution.py:466
  12.6 0.0 copy-done.5
  12.6 0.0 copy-done.6
  12.6 1.2 %shard_map.150 = (bf16[2,256,128]{2,1,0:T(8,128)(2,1)S(1)}, bf16[256,128]{1,0:T(8,128)(2,1)S(1)}, bf16[256,128]{1,0:T(8,128)(2,1)S(1)}) custom-call(bf16[2,512,128]{2,1,0:T(8,128)(2,1)S(1)} %get-tuple-element.16.zlt_ref, bf16[4,256,128]{2,1,0:T(8,128)(2,1)S(1)} %collective-permute-done.refs_0_, bf16[4,256,128]{2,1,0:T(8,128)(2,1)S(1)} %get-tuple-element.17.refs_1_, ...), custom_call_target="tpu_custom_call" | custom-call | flops 268435456 | bytes 2097152 | tf_op jit(solution)/shard_map/pallas_call | solution.py:293
  13.8 0.1 collective-permute-start.1
  13.9 3.4 %collective-permute-start.2 = (bf16[256,128]{1,0:T(8,128)(2,1)S(1)}, bf16[256,128]{1,0:T(8,128)(2,1)S(1)}, u32[]{:S(2)}, u32[]{:S(2)}) collective-permute-start(bf16[256,128]{1,0:T(8,128)(2,1)S(1)} %get-tuple-element.23), channel_id=1, source_target_pairs={{2,0},{3,1},{0,2},{1,3},{6,4},{7,5},{4,6},{5,7},{10,8},{11,9},{8,1... | collective-permute-start | bytes 196616 | tf_op jit(solution)/shard_map/ppermute | solution.py:466
  17.3 0.0 collective-permute-done.1.refs_1_
  17.3 2.2 %collective-permute-start.5 = (bf16[2,256,128]{2,1,0:T(8,128)(2,1)S(1)}, bf16[2,256,128]{2,1,0:T(8,128)(2,1)S(1)}, u32[]{:S(2)}, u32[]{:S(2)}) collective-permute-start(bf16[2,256,128]{2,1,0:T(8,128)(2,1)S(1)} %pad_maximum_fusion), channel_id=1, source_target_pairs={{3,0},{4,1},{8,2},{14,3},{0,4},{7,5},{10,6},{12,7},{2,8},{5,9},{9,... | collective-permute-start | bytes 393224 | tf_op jit(solution)/shard_map/ppermute | solution.py:466
  19.5 1.9 %collective-permute-start.4 = (bf16[2,256,128]{2,1,0:T(8,128)(2,1)S(1)}, bf16[2,256,128]{2,1,0:T(8,128)(2,1)S(1)}, u32[]{:S(2)}, u32[]{:S(2)}) collective-permute-start(bf16[2,256,128]{2,1,0:T(8,128)(2,1)S(1)} %pad_maximum_fusion), channel_id=1, source_target_pairs={{1,0},{6,1},{10,2},{12,3},{2,4},{5,5},{8,6},{14,7},{0,8},{7,9},{11... | collective-permute-start | bytes 393224 | tf_op jit(solution)/shard_map/ppermute | solution.py:466
  21.5 0.0 collective-permute-done.2.refs_2_
  21.5 1.8 %collective-permute-start.3 = (bf16[256,128]{1,0:T(8,128)(2,1)S(1)}, bf16[256,128]{1,0:T(8,128)(2,1)S(1)}, u32[]{:S(2)}, u32[]{:S(2)}) collective-permute-start(bf16[256,128]{1,0:T(8,128)(2,1)S(1)} %collective-permute-done.2.refs_2_), channel_id=1, source_target_pairs={{1,0},{0,1},{3,2},{2,3},{5,4},{4,5},{7,6},{6,7},{9,8},{8,9},{11,10... | collective-permute-start | bytes 196616 | tf_op jit(solution)/shard_map/ppermute | solution.py:466
  23.3 0.9 %collective-permute-done.3.refs_3_ = bf16[256,128]{1,0:T(8,128)(2,1)S(1)} collective-permute-done((bf16[256,128]{1,0:T(8,128)(2,1)S(1)}, bf16[256,128]{1,0:T(8,128)(2,1)S(1)}, u32[]{:S(2)}, u32[]{:S(2)}) %collective-permute-start.3) | collective-permute-done | bytes 65568 | tf_op jit(solution)/shard_map/ppermute | solution.py:466
  24.2 0.0 collective-permute-done.5.refs_4_
  24.2 0.0 copy-done.7
  24.2 0.7 %shard_map.151 = (f32[256,128]{1,0:T(8,128)S(1)}, f32[256,128]{1,0:T(8,128)S(1)}) custom-call(bf16[2,256,128]{2,1,0:T(8,128)(2,1)S(1)} %get-tuple-element.22.refs_0_, bf16[2,256,128]{2,1,0:T(8,128)(2,1)S(1)} %collective-permute-done.1.refs_1_, bf16[256,128]{1,0:T(8,128)(2,1)S(1)} %collective-permute-done.2.refs_2_, ...), custom_call_target="tpu_custom_call" | custom-call | flops 67108864 | bytes 1048576 | tf_op jit(solution)/shard_map/pallas_call | solution.py:415
  25.0 1.9 %collective-permute-done.4.refs_4_ = bf16[2,256,128]{2,1,0:T(8,128)(2,1)S(1)} collective-permute-done((bf16[2,256,128]{2,1,0:T(8,128)(2,1)S(1)}, bf16[2,256,128]{2,1,0:T(8,128)(2,1)S(1)}, u32[]{:S(2)}, u32[]{:S(2)}) %collective-permute-start.4) | collective-permute-done | bytes 131104 | tf_op jit(solution)/shard_map/ppermute | solution.py:466
  26.8 0.0 copy-done.1
  26.8 0.0 copy-done.2
  26.8 0.0 copy-done.8
  26.8 1.9 %shard_map.152 = bf16[16,16,128]{2,1,0:T(8,128)(2,1)} custom-call(bf16[2,256,128]{2,1,0:T(8,128)(2,1)S(1)} %get-tuple-element.22.refs_0_, bf16[2,256,128]{2,1,0:T(8,128)(2,1)S(1)} %collective-permute-done.1.refs_1_, bf16[256,128]{1,0:T(8,128)(2,1)S(1)} %collective-permute-done.2.refs_2_, bf16[256,128]{1,0:T(8,128)(2,1)S(1)} %collective-permute-done.3.refs_3_, ...), custom_call_target="tpu_custom_call" | custom-call | flops 134217728 | bytes 2097152 | tf_op jit(solution)/shard_map/pallas_call | solution.py:426
  (3 shorter events, 0.0 us)
Async XLA Ops:
  0.0 1.6 %copy-start.12 = (bf16[256,16,256]{2,1,0:T(8,128)(2,1)S(1)}, bf16[256,16,256]{2,1,0:T(8,128)(2,1)}, u32[]{:S(2)}) copy-start(bf16[256,16,256]{2,1,0:T(8,128)(2,1)} %x_ref.3) | copy-start | bytes 6291460
  0.0 0.9 %copy-start.13 = (bf16[256,32]{0,1:T(8,128)(2,1)S(1)}, bf16[256,32]{0,1:T(8,128)(2,1)}, u32[]{:S(2)}) copy-start(bf16[256,32]{0,1:T(8,128)(2,1)} %param.21) | copy-start | bytes 49156
  1.6 6.3 %copy-start.14 = (bf16[256,32]{0,1:T(8,128)(2,1)S(1)}, bf16[256,32]{0,1:T(8,128)(2,1)}, u32[]{:S(2)}) copy-start(bf16[256,32]{0,1:T(8,128)(2,1)} %param.20) | copy-start | bytes 49156
  3.1 4.9 %copy-start.3 = (s32[256,64]{0,1:T(8,128)S(1)}, s32[256,64]{0,1:T(8,128)}, u32[]{:S(2)}) copy-start(s32[256,64]{0,1:T(8,128)} %param.16) | copy-start | bytes 196612
  3.1 9.4 %collective-permute-start = (bf16[4,256,128]{2,1,0:T(8,128)(2,1)S(1)}, bf16[4,256,128]{2,1,0:T(8,128)(2,1)S(1)}, u32[]{:S(2)}, u32[]{:S(2)}) collective-permute-start(bf16[4,256,128]{2,1,0:T(8,128)(2,1)S(1)} %shard_map.149), channel_id=1, source_target_pairs={{3,0},{4,1},{10,2},{14,3},{0,4},{7,5},{8,6},{12,7},{2,8},{6,9},{9,... | collective-permute-start | bytes 786440 | tf_op jit(solution)/shard_map/ppermute | solution.py:466
  8.0 1.7 %copy-start = (f32[32,32,128]{2,1,0:T(8,128)S(1)}, f32[32,32,128]{2,1,0:T(8,128)}, u32[]{:S(2)}) copy-start(f32[32,32,128]{2,1,0:T(8,128)} %proj_ref.1) | copy-start | bytes 1572868
  8.0 1.7 %copy-start.4 = (bf16[16,16,128]{2,1,0:T(8,128)(2,1)S(1)}, bf16[16,16,128]{2,1,0:T(8,128)(2,1)}, u32[]{:S(2)}) copy-start(bf16[16,16,128]{2,1,0:T(8,128)(2,1)} %pair_ref.1) | copy-start | bytes 196612
  8.0 1.7 %copy-start.9 = (bf16[66,128]{1,0:T(8,128)(2,1)S(1)}, bf16[66,128]{1,0:T(8,128)(2,1)}, u32[]{:S(2)}) copy-start(bf16[66,128]{1,0:T(8,128)(2,1)} %table_ref.1) | copy-start | bytes 50692
  8.0 1.7 %copy-start.10 = (s32[64]{0:T(128)S(1)}, s32[64]{0:T(128)}, u32[]{:S(2)}) copy-start(s32[64]{0:T(128)} %param.18) | copy-start | bytes 772
  8.0 1.7 %copy-start.11 = (s32[64]{0:T(128)S(1)}, s32[64]{0:T(128)}, u32[]{:S(2)}) copy-start(s32[64]{0:T(128)} %param.19) | copy-start | bytes 772
  8.0 4.5 %copy-start.5 = (bf16[128,256]{1,0:T(8,128)(2,1)S(1)}, bf16[128,256]{1,0:T(8,128)(2,1)}, u32[]{:S(2)}) copy-start(bf16[128,256]{1,0:T(8,128)(2,1)} %refs_6_.2) | copy-start | bytes 196612
  8.0 4.5 %copy-start.6 = (bf16[128,256]{1,0:T(8,128)(2,1)S(1)}, bf16[128,256]{1,0:T(8,128)(2,1)}, u32[]{:S(2)}) copy-start(bf16[128,256]{1,0:T(8,128)(2,1)} %refs_7_.1) | copy-start | bytes 196612
  9.6 14.6 %copy-start.7 = (bf16[128,128]{1,0:T(8,128)(2,1)S(1)}, bf16[128,128]{1,0:T(8,128)(2,1)}, u32[]{:S(2)}) copy-start(bf16[128,128]{1,0:T(8,128)(2,1)} %refs_6_.3) | copy-start | bytes 98308
  9.6 17.2 %copy-start.1 = (bf16[128,512]{1,0:T(8,128)(2,1)S(1)}, bf16[128,512]{1,0:T(8,128)(2,1)}, u32[]{:S(2)}) copy-start(bf16[128,512]{1,0:T(8,128)(2,1)} %refs_9_.1) | copy-start | bytes 393220
  9.7 17.2 %copy-start.2 = (bf16[512,128]{1,0:T(8,128)(2,1)S(1)}, bf16[512,128]{1,0:T(8,128)(2,1)}, u32[]{:S(2)}) copy-start(bf16[512,128]{1,0:T(8,128)(2,1)} %refs_10_.1) | copy-start | bytes 393220
  9.7 17.2 %copy-start.8 = (bf16[128,128]{1,0:T(8,128)(2,1)S(1)}, bf16[128,128]{1,0:T(8,128)(2,1)}, u32[]{:S(2)}) copy-start(bf16[128,128]{1,0:T(8,128)(2,1)} %refs_8_.1) | copy-start | bytes 98308
  13.8 3.5 %collective-permute-start.1 = (bf16[2,256,128]{2,1,0:T(8,128)(2,1)S(1)}, bf16[2,256,128]{2,1,0:T(8,128)(2,1)S(1)}, u32[]{:S(2)}, u32[]{:S(2)}) collective-permute-start(bf16[2,256,128]{2,1,0:T(8,128)(2,1)S(1)} %get-tuple-element.22.refs_0_), channel_id=1, source_target_pairs={{1,0},{0,1},{3,2},{2,3},{5,4},{4,5},{7,6},{6,7},{9,8},{8,9},{11,10... | collective-permute-start | bytes 393224 | tf_op jit(solution)/shard_map/ppermute | solution.py:466
  13.9 7.6 %collective-permute-start.2 = (bf16[256,128]{1,0:T(8,128)(2,1)S(1)}, bf16[256,128]{1,0:T(8,128)(2,1)S(1)}, u32[]{:S(2)}, u32[]{:S(2)}) collective-permute-start(bf16[256,128]{1,0:T(8,128)(2,1)S(1)} %get-tuple-element.23), channel_id=1, source_target_pairs={{2,0},{3,1},{0,2},{1,3},{6,4},{7,5},{4,6},{5,7},{10,8},{11,9},{8,1... | collective-permute-start | bytes 196616 | tf_op jit(solution)/shard_map/ppermute | solution.py:466
  17.3 6.9 %collective-permute-start.5 = (bf16[2,256,128]{2,1,0:T(8,128)(2,1)S(1)}, bf16[2,256,128]{2,1,0:T(8,128)(2,1)S(1)}, u32[]{:S(2)}, u32[]{:S(2)}) collective-permute-start(bf16[2,256,128]{2,1,0:T(8,128)(2,1)S(1)} %pad_maximum_fusion), channel_id=1, source_target_pairs={{3,0},{4,1},{8,2},{14,3},{0,4},{7,5},{10,6},{12,7},{2,8},{5,9},{9,... | collective-permute-start | bytes 393224 | tf_op jit(solution)/shard_map/ppermute | solution.py:466
  19.5 7.3 %collective-permute-start.4 = (bf16[2,256,128]{2,1,0:T(8,128)(2,1)S(1)}, bf16[2,256,128]{2,1,0:T(8,128)(2,1)S(1)}, u32[]{:S(2)}, u32[]{:S(2)}) collective-permute-start(bf16[2,256,128]{2,1,0:T(8,128)(2,1)S(1)} %pad_maximum_fusion), channel_id=1, source_target_pairs={{1,0},{6,1},{10,2},{12,3},{2,4},{5,5},{8,6},{14,7},{0,8},{7,9},{11... | collective-permute-start | bytes 393224 | tf_op jit(solution)/shard_map/ppermute | solution.py:466
  21.5 2.7 %collective-permute-start.3 = (bf16[256,128]{1,0:T(8,128)(2,1)S(1)}, bf16[256,128]{1,0:T(8,128)(2,1)S(1)}, u32[]{:S(2)}, u32[]{:S(2)}) collective-permute-start(bf16[256,128]{1,0:T(8,128)(2,1)S(1)} %collective-permute-done.2.refs_2_), channel_id=1, source_target_pairs={{1,0},{0,1},{3,2},{2,3},{5,4},{4,5},{7,6},{6,7},{9,8},{8,9},{11,10... | collective-permute-start | bytes 196616 | tf_op jit(solution)/shard_map/ppermute | solution.py:466

commit v26 on v25

--- a/solution.py
+++ b/solution.py
@@ -9,7 +9,7 @@
 
 REL_CLIP = 32
 LANES = 128
-PARTS = 1
+PARTS = 2
 EPSILON = 1e-05
 BF16 = jnp.bfloat16
 F32 = jnp.float32

time: 29 us -> 31.2 us (1.076)
  waiting for transfers between devices: 4.67 us -> 6.33 us
  starting transfers between devices: 14.2 us -> 14.8 us
    ppermute x6 -> x7, waiting for transfers between devices: 4.67 us -> 6.33 us  [fetch(): return lax.ppermute(values, ('dap', 'sub'), perm)]
    ppermute x6 -> x7, starting transfers between devices: 14.2 us -> 14.8 us  [fetch(): return lax.ppermute(values, ('dap', 'sub'), perm)]
  transfers between devices with their start and end apart: 6 -> 7, of which waited for: 3 -> 3; matrix products, arithmetic and copies ran while one was open for 0% -> 0% of each run, Pallas kernels for 12% -> 11%
where the time goes in v26:
time: 31.2 us; the launch traced here: 30.9 us
  starting transfers between devices  14.8 us (47%)
  Pallas kernels  7.91 us (25%)
  waiting for transfers between devices  6.33 us (20%)
  local copies, waits for them, and re-layouts  1.62 us (5%)
    ppermute x7, starting transfers between devices, fetch(): return lax.ppermute(values, ('dap', 'sub'), perm)  14.8 us
    ppermute x7, waiting for transfers between devices, fetch(): return lax.ppermute(values, ('dap', 'sub'), perm)  6.33 us
    pallas_call x2, Pallas kernels, factor(): pl.pallas_call(functools.partial(factor_kernel, mask is not None, hidden)...  3.05 us
    pallas_call x1, Pallas kernels, triangle_update(): pl.pallas_call(functools.partial(last_kernel, late, twos, ratio, cols), o...  1.87 us
    unnamed x30, local copies, waits for them, and re-layouts  1.61 us
    pallas_call x1, Pallas kernels, pair_update(): pl.pallas_call(functools.partial(pair_kernel, ratio, hidden), out_shape=(...  1.19 us
    pallas_call x1, Pallas kernels, prepare(): pl.pallas_call(prepare_kernel, out_shape=(jax.ShapeDtypeStruct((zl.shape[...  0.94 us
    pallas_call x1, Pallas kernels, triangle_update(): pl.pallas_call(functools.partial(first_kernel, early, twos, ratio, cols),...  0.73 us
  transfers between devices with their start and end apart: 7, of which 3 were waited for; matrix products, arithmetic and copies ran while one was open for 0% of the time, Pallas kernels for 11%

profile of v26, /device:TPU:1, one launch (start us, length us, event | category | flops | bytes accessed | tf_op | source)
XLA Modules:
  0.0 30.9 jit_solution(17180641839387353832)
XLA Ops:
  0.0 0.0 copy-start.12
  0.0 0.0 copy-start.13
  0.0 0.9 %copy-done.13 = bf16[256,32]{0,1:T(8,128)(2,1)S(1)} copy-done((bf16[256,32]{0,1:T(8,128)(2,1)S(1)}, bf16[256,32]{0,1:T(8,128)(2,1)}, u32[]{:S(2)}) %copy-start.13) | copy-done | bytes 16408
  0.9 0.1 shard_map.148.weight_ref
  0.9 0.7 %copy-done.12 = bf16[256,16,256]{2,1,0:T(8,128)(2,1)S(1)} copy-done((bf16[256,16,256]{2,1,0:T(8,128)(2,1)S(1)}, bf16[256,16,256]{2,1,0:T(8,128)(2,1)}, u32[]{:S(2)}) %copy-start.12) | copy-done | bytes 2097176
  1.6 0.0 copy-start.14
  1.6 1.5 %shard_map.149 = (bf16[2,256,128]{2,1,0:T(8,128)(2,1)S(1)}, bf16[2,256,128]{2,1,0:T(8,128)(2,1)S(1)}) custom-call(bf16[256,16,256]{2,1,0:T(8,128)(2,1)S(1)} %copy-done.12, bf16[256,128]{1,0:T(8,128)(2,1)S(1)} %shard_map.148.weight_ref), custom_call_target="tpu_custom_call" | custom-call | flops 1073741824 | bytes 4194304 | tf_op jit(solution)/shard_map/pallas_call | solution.py:144
  3.1 0.0 copy-start.3
  3.1 4.8 %collective-permute-start = (bf16[2,256,128]{2,1,0:T(8,128)(2,1)S(1)}, bf16[2,256,128]{2,1,0:T(8,128)(2,1)S(1)}, u32[]{:S(2)}, u32[]{:S(2)}) collective-permute-start(bf16[2,256,128]{2,1,0:T(8,128)(2,1)S(1)} %get-tuple-element.19), channel_id=1, source_target_pairs={{3,0},{4,1},{10,2},{14,3},{0,4},{7,5},{8,6},{12,7},{2,8},{6,9},{9,... | collective-permute-start | bytes 393224 | tf_op jit(solution)/shard_map/ppermute | solution.py:466
  7.9 1.9 %collective-permute-start.1 = (bf16[2,256,128]{2,1,0:T(8,128)(2,1)S(1)}, bf16[2,256,128]{2,1,0:T(8,128)(2,1)S(1)}, u32[]{:S(2)}, u32[]{:S(2)}) collective-permute-start(bf16[2,256,128]{2,1,0:T(8,128)(2,1)S(1)} %get-tuple-element.20), channel_id=1, source_target_pairs={{1,0},{6,1},{8,2},{12,3},{2,4},{5,5},{10,6},{14,7},{0,8},{4,9},{11... | collective-permute-start | bytes 393224 | tf_op jit(solution)/shard_map/ppermute | solution.py:466
  9.8 0.0 copy-done.14
  9.8 0.1 shard_map.145.weight_ref
  9.9 0.0 copy-start
  9.9 0.0 copy-start.4
  9.9 0.0 copy-start.9
  9.9 0.0 copy-start.10
  9.9 0.0 copy-start.11
  9.9 0.0 copy-done.3
  10.0 0.0 copy-start.5
  10.0 0.0 copy-start.6
  10.0 1.6 %shard_map.146.zl_ref = bf16[4,256,128]{2,1,0:T(8,128)(2,1)S(1)} custom-call(bf16[256,16,256]{2,1,0:T(8,128)(2,1)S(1)} %copy-done.12, bf16[256,128]{1,0:T(8,128)(2,1)S(1)} %shard_map.145.weight_ref, s32[64,256]{1,0:T(8,128)S(1)} %bitcast.5), custom_call_target="tpu_custom_call" | custom-call | flops 1073741824 | bytes 4194304 | tf_op jit(solution)/shard_map/pallas_call | solution.py:144
  11.5 0.0 copy-start.7
  11.6 0.0 copy-start.1
  11.6 0.0 copy-start.2
  11.6 0.0 copy-start.8
  11.6 0.0 copy-done
  11.6 0.0 copy-done.4
  11.6 0.0 copy-done.9
  11.6 0.0 copy-done.10
  11.6 0.0 copy-done.11
  11.6 0.9 %shard_map.147 = (bf16[2,512,128]{2,1,0:T(8,128)(2,1)S(1)}, f32[256,128]{1,0:T(8,128)S(1)}, f32[256,128]{1,0:T(8,128)S(1)}, f32[256,128]{1,0:T(8,128)S(1)}, bf16...) custom-call(bf16[4,256,128]{2,1,0:T(8,128)(2,1)S(1)} %shard_map.146.zl_ref, s32[64,256]{1,0:T(8,128)S(1)} %bitcast.6, ...), custom_call_target="tpu_custom_call" | custom-call | flops 134217728 | bytes 2097152 | tf_op jit(solution)/shard_map/pallas_call | solution.py:217
  12.6 0.0 collective-permute-done.refs_0_
  12.6 2.5 %collective-permute-done.1.refs_1_ = bf16[2,256,128]{2,1,0:T(8,128)(2,1)S(1)} collective-permute-done((bf16[2,256,128]{2,1,0:T(8,128)(2,1)S(1)}, bf16[2,256,128]{2,1,0:T(8,128)(2,1)S(1)}, u32[]{:S(2)}, u32[]{:S(2)}) %collective-permute-start.1) | collective-permute-done | bytes 131104 | tf_op jit(solution)/shard_map/ppermute | solution.py:466
  15.1 0.0 copy-done.5
  15.1 0.0 copy-done.6
  15.1 1.2 %shard_map.150 = (bf16[2,256,128]{2,1,0:T(8,128)(2,1)S(1)}, bf16[256,128]{1,0:T(8,128)(2,1)S(1)}, bf16[256,128]{1,0:T(8,128)(2,1)S(1)}) custom-call(bf16[2,512,128]{2,1,0:T(8,128)(2,1)S(1)} %get-tuple-element.18.zlt_ref, bf16[2,256,128]{2,1,0:T(8,128)(2,1)S(1)} %collective-permute-done.refs_0_, bf16[2,256,128]{2,1,0:T(8,128)(2,1)S(1)} %collective-permute-done.1.refs_1_, ...), custom_call_target="tpu_custom_call" | custom-call | flops 268435456 | bytes 2097152 | tf_op jit(solution)/shard_map/pallas_call | solution.py:293
  16.3 0.1 collective-permute-start.2
  16.4 2.0 %collective-permute-start.3 = (bf16[256,128]{1,0:T(8,128)(2,1)S(1)}, bf16[256,128]{1,0:T(8,128)(2,1)S(1)}, u32[]{:S(2)}, u32[]{:S(2)}) collective-permute-start(bf16[256,128]{1,0:T(8,128)(2,1)S(1)} %get-tuple-element.27), channel_id=1, source_target_pairs={{2,0},{3,1},{0,2},{1,3},{6,4},{7,5},{4,6},{5,7},{10,8},{11,9},{8,1... | collective-permute-start | bytes 196616 | tf_op jit(solution)/shard_map/ppermute | solution.py:466
  18.4 0.0 collective-permute-done.2.refs_1_
  18.4 2.2 %collective-permute-start.6 = (bf16[2,256,128]{2,1,0:T(8,128)(2,1)S(1)}, bf16[2,256,128]{2,1,0:T(8,128)(2,1)S(1)}, u32[]{:S(2)}, u32[]{:S(2)}) collective-permute-start(bf16[2,256,128]{2,1,0:T(8,128)(2,1)S(1)} %pad_maximum_fusion), channel_id=1, source_target_pairs={{3,0},{4,1},{8,2},{14,3},{0,4},{7,5},{10,6},{12,7},{2,8},{5,9},{9,... | collective-permute-start | bytes 393224 | tf_op jit(solution)/shard_map/ppermute | solution.py:466
  20.6 1.9 %collective-permute-start.5 = (bf16[2,256,128]{2,1,0:T(8,128)(2,1)S(1)}, bf16[2,256,128]{2,1,0:T(8,128)(2,1)S(1)}, u32[]{:S(2)}, u32[]{:S(2)}) collective-permute-start(bf16[2,256,128]{2,1,0:T(8,128)(2,1)S(1)} %pad_maximum_fusion), channel_id=1, source_target_pairs={{1,0},{6,1},{10,2},{12,3},{2,4},{5,5},{8,6},{14,7},{0,8},{7,9},{11... | collective-permute-start | bytes 393224 | tf_op jit(solution)/shard_map/ppermute | solution.py:466
  22.6 0.0 collective-permute-done.3.refs_2_
  22.6 1.9 %collective-permute-start.4 = (bf16[256,128]{1,0:T(8,128)(2,1)S(1)}, bf16[256,128]{1,0:T(8,128)(2,1)S(1)}, u32[]{:S(2)}, u32[]{:S(2)}) collective-permute-start(bf16[256,128]{1,0:T(8,128)(2,1)S(1)} %collective-permute-done.3.refs_2_), channel_id=1, source_target_pairs={{1,0},{0,1},{3,2},{2,3},{5,4},{4,5},{7,6},{6,7},{9,8},{8,9},{11,10... | collective-permute-start | bytes 196616 | tf_op jit(solution)/shard_map/ppermute | solution.py:466
  24.4 0.9 %collective-permute-done.4.refs_3_ = bf16[256,128]{1,0:T(8,128)(2,1)S(1)} collective-permute-done((bf16[256,128]{1,0:T(8,128)(2,1)S(1)}, bf16[256,128]{1,0:T(8,128)(2,1)S(1)}, u32[]{:S(2)}, u32[]{:S(2)}) %collective-permute-start.4) | collective-permute-done | bytes 65568 | tf_op jit(solution)/shard_map/ppermute | solution.py:466
  25.3 0.0 collective-permute-done.6.refs_4_
  25.3 0.0 copy-done.7
  25.3 0.7 %shard_map.151 = (f32[256,128]{1,0:T(8,128)S(1)}, f32[256,128]{1,0:T(8,128)S(1)}) custom-call(bf16[2,256,128]{2,1,0:T(8,128)(2,1)S(1)} %get-tuple-element.26.refs_0_, bf16[2,256,128]{2,1,0:T(8,128)(2,1)S(1)} %collective-permute-done.2.refs_1_, bf16[256,128]{1,0:T(8,128)(2,1)S(1)} %collective-permute-done.3.refs_2_, ...), custom_call_target="tpu_custom_call" | custom-call | flops 67108864 | bytes 1048576 | tf_op jit(solution)/shard_map/pallas_call | solution.py:415
  26.1 3.0 %collective-permute-done.5.refs_4_ = bf16[2,256,128]{2,1,0:T(8,128)(2,1)S(1)} collective-permute-done((bf16[2,256,128]{2,1,0:T(8,128)(2,1)S(1)}, bf16[2,256,128]{2,1,0:T(8,128)(2,1)S(1)}, u32[]{:S(2)}, u32[]{:S(2)}) %collective-permute-start.5) | collective-permute-done | bytes 131104 | tf_op jit(solution)/shard_map/ppermute | solution.py:466
  29.0 0.0 copy-done.1
  29.0 0.0 copy-done.2
  29.0 0.0 copy-done.8
  29.0 1.9 %shard_map.152 = bf16[16,16,128]{2,1,0:T(8,128)(2,1)} custom-call(bf16[2,256,128]{2,1,0:T(8,128)(2,1)S(1)} %get-tuple-element.26.refs_0_, bf16[2,256,128]{2,1,0:T(8,128)(2,1)S(1)} %collective-permute-done.2.refs_1_, bf16[256,128]{1,0:T(8,128)(2,1)S(1)} %collective-permute-done.3.refs_2_, bf16[256,128]{1,0:T(8,128)(2,1)S(1)} %collective-permute-done.4.refs_3_, ...), custom_call_target="tpu_custom_call" | custom-call | flops 134217728 | bytes 2097152 | tf_op jit(solution)/shard_map/pallas_call | solution.py:426
  (3 shorter events, 0.0 us)
Async XLA Ops:
  0.0 1.6 %copy-start.12 = (bf16[256,16,256]{2,1,0:T(8,128)(2,1)S(1)}, bf16[256,16,256]{2,1,0:T(8,128)(2,1)}, u32[]{:S(2)}) copy-start(bf16[256,16,256]{2,1,0:T(8,128)(2,1)} %x_ref.3) | copy-start | bytes 6291460
  0.0 0.9 %copy-start.13 = (bf16[256,32]{0,1:T(8,128)(2,1)S(1)}, bf16[256,32]{0,1:T(8,128)(2,1)}, u32[]{:S(2)}) copy-start(bf16[256,32]{0,1:T(8,128)(2,1)} %param.21) | copy-start | bytes 49156
  1.6 8.2 %copy-start.14 = (bf16[256,32]{0,1:T(8,128)(2,1)S(1)}, bf16[256,32]{0,1:T(8,128)(2,1)}, u32[]{:S(2)}) copy-start(bf16[256,32]{0,1:T(8,128)(2,1)} %param.20) | copy-start | bytes 49156
  3.1 6.8 %copy-start.3 = (s32[256,64]{0,1:T(8,128)S(1)}, s32[256,64]{0,1:T(8,128)}, u32[]{:S(2)}) copy-start(s32[256,64]{0,1:T(8,128)} %param.16) | copy-start | bytes 196612
  3.1 9.5 %collective-permute-start = (bf16[2,256,128]{2,1,0:T(8,128)(2,1)S(1)}, bf16[2,256,128]{2,1,0:T(8,128)(2,1)S(1)}, u32[]{:S(2)}, u32[]{:S(2)}) collective-permute-start(bf16[2,256,128]{2,1,0:T(8,128)(2,1)S(1)} %get-tuple-element.19), channel_id=1, source_target_pairs={{3,0},{4,1},{10,2},{14,3},{0,4},{7,5},{8,6},{12,7},{2,8},{6,9},{9,... | collective-permute-start | bytes 393224 | tf_op jit(solution)/shard_map/ppermute | solution.py:466
  7.9 7.2 %collective-permute-start.1 = (bf16[2,256,128]{2,1,0:T(8,128)(2,1)S(1)}, bf16[2,256,128]{2,1,0:T(8,128)(2,1)S(1)}, u32[]{:S(2)}, u32[]{:S(2)}) collective-permute-start(bf16[2,256,128]{2,1,0:T(8,128)(2,1)S(1)} %get-tuple-element.20), channel_id=1, source_target_pairs={{1,0},{6,1},{8,2},{12,3},{2,4},{5,5},{10,6},{14,7},{0,8},{4,9},{11... | collective-permute-start | bytes 393224 | tf_op jit(solution)/shard_map/ppermute | solution.py:466
  9.9 1.7 %copy-start = (f32[32,32,128]{2,1,0:T(8,128)S(1)}, f32[32,32,128]{2,1,0:T(8,128)}, u32[]{:S(2)}) copy-start(f32[32,32,128]{2,1,0:T(8,128)} %proj_ref.1) | copy-start | bytes 1572868
  9.9 1.7 %copy-start.4 = (bf16[16,16,128]{2,1,0:T(8,128)(2,1)S(1)}, bf16[16,16,128]{2,1,0:T(8,128)(2,1)}, u32[]{:S(2)}) copy-start(bf16[16,16,128]{2,1,0:T(8,128)(2,1)} %pair_ref.1) | copy-start | bytes 196612
  9.9 1.7 %copy-start.9 = (bf16[66,128]{1,0:T(8,128)(2,1)S(1)}, bf16[66,128]{1,0:T(8,128)(2,1)}, u32[]{:S(2)}) copy-start(bf16[66,128]{1,0:T(8,128)(2,1)} %table_ref.1) | copy-start | bytes 50692
  9.9 1.7 %copy-start.10 = (s32[64]{0:T(128)S(1)}, s32[64]{0:T(128)}, u32[]{:S(2)}) copy-start(s32[64]{0:T(128)} %param.18) | copy-start | bytes 772
  9.9 1.7 %copy-start.11 = (s32[64]{0:T(128)S(1)}, s32[64]{0:T(128)}, u32[]{:S(2)}) copy-start(s32[64]{0:T(128)} %param.19) | copy-start | bytes 772
  10.0 5.1 %copy-start.5 = (bf16[128,256]{1,0:T(8,128)(2,1)S(1)}, bf16[128,256]{1,0:T(8,128)(2,1)}, u32[]{:S(2)}) copy-start(bf16[128,256]{1,0:T(8,128)(2,1)} %refs_7_.1) | copy-start | bytes 196612
  10.0 5.1 %copy-start.6 = (bf16[128,256]{1,0:T(8,128)(2,1)S(1)}, bf16[128,256]{1,0:T(8,128)(2,1)}, u32[]{:S(2)}) copy-start(bf16[128,256]{1,0:T(8,128)(2,1)} %refs_8_.2) | copy-start | bytes 196612
  11.5 13.8 %copy-start.7 = (bf16[128,128]{1,0:T(8,128)(2,1)S(1)}, bf16[128,128]{1,0:T(8,128)(2,1)}, u32[]{:S(2)}) copy-start(bf16[128,128]{1,0:T(8,128)(2,1)} %refs_6_.1) | copy-start | bytes 98308
  11.6 17.5 %copy-start.1 = (bf16[128,512]{1,0:T(8,128)(2,1)S(1)}, bf16[128,512]{1,0:T(8,128)(2,1)}, u32[]{:S(2)}) copy-start(bf16[128,512]{1,0:T(8,128)(2,1)} %refs_9_.1) | copy-start | bytes 393220
  11.6 17.5 %copy-start.2 = (bf16[512,128]{1,0:T(8,128)(2,1)S(1)}, bf16[512,128]{1,0:T(8,128)(2,1)}, u32[]{:S(2)}) copy-start(bf16[512,128]{1,0:T(8,128)(2,1)} %refs_10_.1) | copy-start | bytes 393220
  11.6 17.5 %copy-start.8 = (bf16[128,128]{1,0:T(8,128)(2,1)S(1)}, bf16[128,128]{1,0:T(8,128)(2,1)}, u32[]{:S(2)}) copy-start(bf16[128,128]{1,0:T(8,128)(2,1)} %refs_8_.3) | copy-start | bytes 98308
  16.3 2.1 %collective-permute-start.2 = (bf16[2,256,128]{2,1,0:T(8,128)(2,1)S(1)}, bf16[2,256,128]{2,1,0:T(8,128)(2,1)S(1)}, u32[]{:S(2)}, u32[]{:S(2)}) collective-permute-start(bf16[2,256,128]{2,1,0:T(8,128)(2,1)S(1)} %get-tuple-element.26.refs_0_), channel_id=1, source_target_pairs={{1,0},{0,1},{3,2},{2,3},{5,4},{4,5},{7,6},{6,7},{9,8},{8,9},{11,10... | collective-permute-start | bytes 393224 | tf_op jit(solution)/shard_map/ppermute | solution.py:466
  16.4 6.2 %collective-permute-start.3 = (bf16[256,128]{1,0:T(8,128)(2,1)S(1)}, bf16[256,128]{1,0:T(8,128)(2,1)S(1)}, u32[]{:S(2)}, u32[]{:S(2)}) collective-permute-start(bf16[256,128]{1,0:T(8,128)(2,1)S(1)} %get-tuple-element.27), channel_id=1, source_target_pairs={{2,0},{3,1},{0,2},{1,3},{6,4},{7,5},{4,6},{5,7},{10,8},{11,9},{8,1... | collective-permute-start | bytes 196616 | tf_op jit(solution)/shard_map/ppermute | solution.py:466
  18.4 6.9 %collective-permute-start.6 = (bf16[2,256,128]{2,1,0:T(8,128)(2,1)S(1)}, bf16[2,256,128]{2,1,0:T(8,128)(2,1)S(1)}, u32[]{:S(2)}, u32[]{:S(2)}) collective-permute-start(bf16[2,256,128]{2,1,0:T(8,128)(2,1)S(1)} %pad_maximum_fusion), channel_id=1, source_target_pairs={{3,0},{4,1},{8,2},{14,3},{0,4},{7,5},{10,6},{12,7},{2,8},{5,9},{9,... | collective-permute-start | bytes 393224 | tf_op jit(solution)/shard_map/ppermute | solution.py:466
  20.6 8.4 %collective-permute-start.5 = (bf16[2,256,128]{2,1,0:T(8,128)(2,1)S(1)}, bf16[2,256,128]{2,1,0:T(8,128)(2,1)S(1)}, u32[]{:S(2)}, u32[]{:S(2)}) collective-permute-start(bf16[2,256,128]{2,1,0:T(8,128)(2,1)S(1)} %pad_maximum_fusion), channel_id=1, source_target_pairs={{1,0},{6,1},{10,2},{12,3},{2,4},{5,5},{8,6},{14,7},{0,8},{7,9},{11... | collective-permute-start | bytes 393224 | tf_op jit(solution)/shard_map/ppermute | solution.py:466
  22.6 2.8 %collective-permute-start.4 = (bf16[256,128]{1,0:T(8,128)(2,1)S(1)}, bf16[256,128]{1,0:T(8,128)(2,1)S(1)}, u32[]{:S(2)}, u32[]{:S(2)}) collective-permute-start(bf16[256,128]{1,0:T(8,128)(2,1)S(1)} %collective-permute-done.3.refs_2_), channel_id=1, source_target_pairs={{1,0},{0,1},{3,2},{2,3},{5,4},{4,5},{7,6},{6,7},{9,8},{8,9},{11,10... | collective-permute-start | bytes 196616 | tf_op jit(solution)/shard_map/ppermute | solution.py:466

commit v27 on v25

--- a/solution.py
+++ b/solution.py
@@ -310,8 +310,7 @@
     return sub + 1 - 2 * (sub % 2)
 
 
-SENDERS = ((3, 0, 2, 1), (0, 3, 2, 1), (2, 0, 1, 3), (2, 0, 3, 1))
-PAIR_SENDERS = ((3, 0, 2, 1), (0, 3, 1, 2), (0, 2, 1, 3), (2, 0, 3, 1))
+SENDERS = ((3, 0, 2, 1), (0, 3, 1, 2), (0, 2, 1, 3), (2, 0, 3, 1))
 
 
 def sender(a, b, subs, ratio, table):
@@ -324,7 +323,7 @@
     if (subs, ratio) != (4, 1):
         return a // ratio
     found = 0
-    for col, places in enumerate(PAIR_SENDERS):
+    for col, places in enumerate(SENDERS):
         for row, place in enumerate(places):
             found = jnp.where((a == row) & (b == col), place, found)
     return found
@@ -499,7 +498,7 @@
             right,
             lambda a, b, t=turn, m=step: (
                 owner(a, b, t),
-                (sender(a, b, subs, ratio, PAIR_SENDERS) + 2 * m + 2) % subs,
+                (sender(a, b, subs, ratio, SENDERS) + 2 * m + 2) % subs,
             ),
         )
         for turn in range(ratio)

time: 29 us -> 30.6 us (1.055)
  starting transfers between devices: 14.2 us -> 15.1 us
  waiting for transfers between devices: 4.67 us -> 5.4 us
    ppermute x6, starting transfers between devices: 14.2 us -> 15.1 us  [fetch(): return lax.ppermute(values, ('dap', 'sub'), perm)]
    ppermute x6, waiting for transfers between devices: 4.67 us -> 5.4 us  [fetch(): return lax.ppermute(values, ('dap', 'sub'), perm)]
  transfers between devices with their start and end apart: 6 -> 6, of which waited for: 3 -> 3; matrix products, arithmetic and copies ran while one was open for 0% -> 0% of each run, Pallas kernels for 12% -> 11%
where the time goes in v27:
time: 30.6 us; the launch traced here: 30.3 us
  starting transfers between devices  15.1 us (49%)
  Pallas kernels  7.92 us (26%)
  waiting for transfers between devices  5.4 us (18%)
  local copies, waits for them, and re-layouts  1.62 us (5%)
    ppermute x6, starting transfers between devices, fetch(): return lax.ppermute(values, ('dap', 'sub'), perm)  15.1 us
    ppermute x6, waiting for transfers between devices, fetch(): return lax.ppermute(values, ('dap', 'sub'), perm)  5.4 us
    pallas_call x2, Pallas kernels, factor(): pl.pallas_call(functools.partial(factor_kernel, mask is not None, hidden)...  3.06 us
    pallas_call x1, Pallas kernels, triangle_update(): pl.pallas_call(functools.partial(last_kernel, late, twos, ratio, cols), o...  1.87 us
    unnamed x30, local copies, waits for them, and re-layouts  1.61 us
    pallas_call x1, Pallas kernels, pair_update(): pl.pallas_call(functools.partial(pair_kernel, ratio, hidden), out_shape=(...  1.19 us
    pallas_call x1, Pallas kernels, prepare(): pl.pallas_call(prepare_kernel, out_shape=(jax.ShapeDtypeStruct((zl.shape[...  0.94 us
    pallas_call x1, Pallas kernels, triangle_update(): pl.pallas_call(functools.partial(first_kernel, early, twos, ratio, cols),...  0.73 us
  transfers between devices with their start and end apart: 6, of which 3 were waited for; matrix products, arithmetic and copies ran while one was open for 0% of the time, Pallas kernels for 11%

profile of v27, /device:TPU:1, one launch (start us, length us, event | category | flops | bytes accessed | tf_op | source)
XLA Modules:
  0.0 30.3 jit_solution(8438215550005160682)
XLA Ops:
  0.0 0.0 copy-start.12
  0.0 0.0 copy-start.13
  0.0 0.9 %copy-done.13 = bf16[256,32]{0,1:T(8,128)(2,1)S(1)} copy-done((bf16[256,32]{0,1:T(8,128)(2,1)S(1)}, bf16[256,32]{0,1:T(8,128)(2,1)}, u32[]{:S(2)}) %copy-start.13) | copy-done | bytes 16408
  0.9 0.1 shard_map.148.weight_ref
  0.9 0.7 %copy-done.12 = bf16[256,16,256]{2,1,0:T(8,128)(2,1)S(1)} copy-done((bf16[256,16,256]{2,1,0:T(8,128)(2,1)S(1)}, bf16[256,16,256]{2,1,0:T(8,128)(2,1)}, u32[]{:S(2)}) %copy-start.12) | copy-done | bytes 2097176
  1.6 0.0 copy-start.14
  1.6 1.5 %shard_map.149 = bf16[4,256,128]{2,1,0:T(8,128)(2,1)S(1)} custom-call(bf16[256,16,256]{2,1,0:T(8,128)(2,1)S(1)} %copy-done.12, bf16[256,128]{1,0:T(8,128)(2,1)S(1)} %shard_map.148.weight_ref), custom_call_target="tpu_custom_call" | custom-call | flops 1073741824 | bytes 4194304 | tf_op jit(solution)/shard_map/pallas_call | solution.py:144
  3.1 0.0 copy-start.3
  3.1 4.8 %collective-permute-start = (bf16[4,256,128]{2,1,0:T(8,128)(2,1)S(1)}, bf16[4,256,128]{2,1,0:T(8,128)(2,1)S(1)}, u32[]{:S(2)}, u32[]{:S(2)}) collective-permute-start(bf16[4,256,128]{2,1,0:T(8,128)(2,1)S(1)} %shard_map.149), channel_id=1, source_target_pairs={{3,0},{4,1},{8,2},{14,3},{0,4},{7,5},{10,6},{12,7},{2,8},{5,9},{9,... | collective-permute-start | bytes 786440 | tf_op jit(solution)/shard_map/ppermute | solution.py:465
  7.9 0.0 copy-done.14
  7.9 0.1 shard_map.145.weight_ref
  8.0 0.0 copy-start
  8.0 0.0 copy-start.4
  8.0 0.0 copy-start.9
  8.0 0.0 copy-start.10
  8.0 0.0 copy-start.11
  8.0 0.0 copy-done.3
  8.0 0.0 copy-start.5
  8.0 0.0 copy-start.6
  8.1 1.6 %shard_map.146.zl_ref = bf16[4,256,128]{2,1,0:T(8,128)(2,1)S(1)} custom-call(bf16[256,16,256]{2,1,0:T(8,128)(2,1)S(1)} %copy-done.12, bf16[256,128]{1,0:T(8,128)(2,1)S(1)} %shard_map.145.weight_ref, s32[64,256]{1,0:T(8,128)S(1)} %bitcast.5), custom_call_target="tpu_custom_call" | custom-call | flops 1073741824 | bytes 4194304 | tf_op jit(solution)/shard_map/pallas_call | solution.py:144
  9.6 0.0 copy-start.7
  9.6 0.0 copy-start.1
  9.7 0.0 copy-start.2
  9.7 0.0 copy-start.8
  9.7 0.0 copy-done
  9.7 0.0 copy-done.4
  9.7 0.0 copy-done.9
  9.7 0.0 copy-done.10
  9.7 0.0 copy-done.11
  9.7 0.9 %shard_map.147 = (bf16[2,512,128]{2,1,0:T(8,128)(2,1)S(1)}, f32[256,128]{1,0:T(8,128)S(1)}, f32[256,128]{1,0:T(8,128)S(1)}, f32[256,128]{1,0:T(8,128)S(1)}, bf16...) custom-call(bf16[4,256,128]{2,1,0:T(8,128)(2,1)S(1)} %shard_map.146.zl_ref, s32[64,256]{1,0:T(8,128)S(1)} %bitcast.6, ...), custom_call_target="tpu_custom_call" | custom-call | flops 134217728 | bytes 2097152 | tf_op jit(solution)/shard_map/pallas_call | solution.py:217
  10.7 1.9 %collective-permute-done.refs_0_ = bf16[4,256,128]{2,1,0:T(8,128)(2,1)S(1)} collective-permute-done((bf16[4,256,128]{2,1,0:T(8,128)(2,1)S(1)}, bf16[4,256,128]{2,1,0:T(8,128)(2,1)S(1)}, u32[]{:S(2)}, u32[]{:S(2)}) %collective-permute-start) | collective-permute-done | bytes 262176 | tf_op jit(solution)/shard_map/ppermute | solution.py:465
  12.6 0.0 copy-done.5
  12.6 0.0 copy-done.6
  12.6 1.2 %shard_map.150 = (bf16[2,256,128]{2,1,0:T(8,128)(2,1)S(1)}, bf16[256,128]{1,0:T(8,128)(2,1)S(1)}, bf16[256,128]{1,0:T(8,128)(2,1)S(1)}) custom-call(bf16[2,512,128]{2,1,0:T(8,128)(2,1)S(1)} %get-tuple-element.16.zlt_ref, bf16[4,256,128]{2,1,0:T(8,128)(2,1)S(1)} %collective-permute-done.refs_0_, bf16[4,256,128]{2,1,0:T(8,128)(2,1)S(1)} %get-tuple-element.17.refs_1_, ...), custom_call_target="tpu_custom_call" | custom-call | flops 268435456 | bytes 2097152 | tf_op jit(solution)/shard_map/pallas_call | solution.py:293
  13.8 0.1 collective-permute-start.1
  13.9 4.3 %collective-permute-start.2 = (bf16[256,128]{1,0:T(8,128)(2,1)S(1)}, bf16[256,128]{1,0:T(8,128)(2,1)S(1)}, u32[]{:S(2)}, u32[]{:S(2)}) collective-permute-start(bf16[256,128]{1,0:T(8,128)(2,1)S(1)} %get-tuple-element.23), channel_id=1, source_target_pairs={{2,0},{3,1},{0,2},{1,3},{6,4},{7,5},{4,6},{5,7},{10,8},{11,9},{8,1... | collective-permute-start | bytes 196616 | tf_op jit(solution)/shard_map/ppermute | solution.py:465
  18.2 0.0 collective-permute-done.1.refs_1_
  18.2 2.3 %collective-permute-start.5 = (bf16[2,256,128]{2,1,0:T(8,128)(2,1)S(1)}, bf16[2,256,128]{2,1,0:T(8,128)(2,1)S(1)}, u32[]{:S(2)}, u32[]{:S(2)}) collective-permute-start(bf16[2,256,128]{2,1,0:T(8,128)(2,1)S(1)} %pad_maximum_fusion), channel_id=1, source_target_pairs={{3,0},{4,1},{8,2},{14,3},{0,4},{7,5},{10,6},{12,7},{2,8},{5,9},{9,... | collective-permute-start | bytes 393224 | tf_op jit(solution)/shard_map/ppermute | solution.py:465
  20.5 1.9 %collective-permute-start.4 = (bf16[2,256,128]{2,1,0:T(8,128)(2,1)S(1)}, bf16[2,256,128]{2,1,0:T(8,128)(2,1)S(1)}, u32[]{:S(2)}, u32[]{:S(2)}) collective-permute-start(bf16[2,256,128]{2,1,0:T(8,128)(2,1)S(1)} %pad_maximum_fusion), channel_id=1, source_target_pairs={{1,0},{6,1},{10,2},{12,3},{2,4},{5,5},{8,6},{14,7},{0,8},{7,9},{11... | collective-permute-start | bytes 393224 | tf_op jit(solution)/shard_map/ppermute | solution.py:465
  22.4 0.0 collective-permute-done.2.refs_2_
  22.4 1.8 %collective-permute-start.3 = (bf16[256,128]{1,0:T(8,128)(2,1)S(1)}, bf16[256,128]{1,0:T(8,128)(2,1)S(1)}, u32[]{:S(2)}, u32[]{:S(2)}) collective-permute-start(bf16[256,128]{1,0:T(8,128)(2,1)S(1)} %collective-permute-done.2.refs_2_), channel_id=1, source_target_pairs={{1,0},{0,1},{3,2},{2,3},{5,4},{4,5},{7,6},{6,7},{9,8},{8,9},{11,10... | collective-permute-start | bytes 196616 | tf_op jit(solution)/shard_map/ppermute | solution.py:465
  24.2 0.9 %collective-permute-done.3.refs_3_ = bf16[256,128]{1,0:T(8,128)(2,1)S(1)} collective-permute-done((bf16[256,128]{1,0:T(8,128)(2,1)S(1)}, bf16[256,128]{1,0:T(8,128)(2,1)S(1)}, u32[]{:S(2)}, u32[]{:S(2)}) %collective-permute-start.3) | collective-permute-done | bytes 65568 | tf_op jit(solution)/shard_map/ppermute | solution.py:465
  25.1 0.0 collective-permute-done.5.refs_4_
  25.1 0.0 copy-done.7
  25.1 0.7 %shard_map.151 = (f32[256,128]{1,0:T(8,128)S(1)}, f32[256,128]{1,0:T(8,128)S(1)}) custom-call(bf16[2,256,128]{2,1,0:T(8,128)(2,1)S(1)} %get-tuple-element.22.refs_0_, bf16[2,256,128]{2,1,0:T(8,128)(2,1)S(1)} %collective-permute-done.1.refs_1_, bf16[256,128]{1,0:T(8,128)(2,1)S(1)} %collective-permute-done.2.refs_2_, ...), custom_call_target="tpu_custom_call" | custom-call | flops 67108864 | bytes 1048576 | tf_op jit(solution)/shard_map/pallas_call | solution.py:414
  25.9 2.6 %collective-permute-done.4.refs_4_ = bf16[2,256,128]{2,1,0:T(8,128)(2,1)S(1)} collective-permute-done((bf16[2,256,128]{2,1,0:T(8,128)(2,1)S(1)}, bf16[2,256,128]{2,1,0:T(8,128)(2,1)S(1)}, u32[]{:S(2)}, u32[]{:S(2)}) %collective-permute-start.4) | collective-permute-done | bytes 131104 | tf_op jit(solution)/shard_map/ppermute | solution.py:465
  28.5 0.0 copy-done.1
  28.5 0.0 copy-done.2
  28.5 0.0 copy-done.8
  28.5 1.9 %shard_map.152 = bf16[16,16,128]{2,1,0:T(8,128)(2,1)} custom-call(bf16[2,256,128]{2,1,0:T(8,128)(2,1)S(1)} %get-tuple-element.22.refs_0_, bf16[2,256,128]{2,1,0:T(8,128)(2,1)S(1)} %collective-permute-done.1.refs_1_, bf16[256,128]{1,0:T(8,128)(2,1)S(1)} %collective-permute-done.2.refs_2_, bf16[256,128]{1,0:T(8,128)(2,1)S(1)} %collective-permute-done.3.refs_3_, ...), custom_call_target="tpu_custom_call" | custom-call | flops 134217728 | bytes 2097152 | tf_op jit(solution)/shard_map/pallas_call | solution.py:425
  (3 shorter events, 0.0 us)
Async XLA Ops:
  0.0 1.6 %copy-start.12 = (bf16[256,16,256]{2,1,0:T(8,128)(2,1)S(1)}, bf16[256,16,256]{2,1,0:T(8,128)(2,1)}, u32[]{:S(2)}) copy-start(bf16[256,16,256]{2,1,0:T(8,128)(2,1)} %x_ref.3) | copy-start | bytes 6291460
  0.0 0.9 %copy-start.13 = (bf16[256,32]{0,1:T(8,128)(2,1)S(1)}, bf16[256,32]{0,1:T(8,128)(2,1)}, u32[]{:S(2)}) copy-start(bf16[256,32]{0,1:T(8,128)(2,1)} %param.21) | copy-start | bytes 49156
  1.6 6.3 %copy-start.14 = (bf16[256,32]{0,1:T(8,128)(2,1)S(1)}, bf16[256,32]{0,1:T(8,128)(2,1)}, u32[]{:S(2)}) copy-start(bf16[256,32]{0,1:T(8,128)(2,1)} %param.20) | copy-start | bytes 49156
  3.1 4.9 %copy-start.3 = (s32[256,64]{0,1:T(8,128)S(1)}, s32[256,64]{0,1:T(8,128)}, u32[]{:S(2)}) copy-start(s32[256,64]{0,1:T(8,128)} %param.16) | copy-start | bytes 196612
  3.1 9.4 %collective-permute-start = (bf16[4,256,128]{2,1,0:T(8,128)(2,1)S(1)}, bf16[4,256,128]{2,1,0:T(8,128)(2,1)S(1)}, u32[]{:S(2)}, u32[]{:S(2)}) collective-permute-start(bf16[4,256,128]{2,1,0:T(8,128)(2,1)S(1)} %shard_map.149), channel_id=1, source_target_pairs={{3,0},{4,1},{8,2},{14,3},{0,4},{7,5},{10,6},{12,7},{2,8},{5,9},{9,... | collective-permute-start | bytes 786440 | tf_op jit(solution)/shard_map/ppermute | solution.py:465
  8.0 1.7 %copy-start = (f32[32,32,128]{2,1,0:T(8,128)S(1)}, f32[32,32,128]{2,1,0:T(8,128)}, u32[]{:S(2)}) copy-start(f32[32,32,128]{2,1,0:T(8,128)} %proj_ref.1) | copy-start | bytes 1572868
  8.0 1.7 %copy-start.4 = (bf16[16,16,128]{2,1,0:T(8,128)(2,1)S(1)}, bf16[16,16,128]{2,1,0:T(8,128)(2,1)}, u32[]{:S(2)}) copy-start(bf16[16,16,128]{2,1,0:T(8,128)(2,1)} %pair_ref.1) | copy-start | bytes 196612
  8.0 1.7 %copy-start.9 = (bf16[66,128]{1,0:T(8,128)(2,1)S(1)}, bf16[66,128]{1,0:T(8,128)(2,1)}, u32[]{:S(2)}) copy-start(bf16[66,128]{1,0:T(8,128)(2,1)} %table_ref.1) | copy-start | bytes 50692
  8.0 1.7 %copy-start.10 = (s32[64]{0:T(128)S(1)}, s32[64]{0:T(128)}, u32[]{:S(2)}) copy-start(s32[64]{0:T(128)} %param.18) | copy-start | bytes 772
  8.0 1.7 %copy-start.11 = (s32[64]{0:T(128)S(1)}, s32[64]{0:T(128)}, u32[]{:S(2)}) copy-start(s32[64]{0:T(128)} %param.19) | copy-start | bytes 772
  8.0 4.5 %copy-start.5 = (bf16[128,256]{1,0:T(8,128)(2,1)S(1)}, bf16[128,256]{1,0:T(8,128)(2,1)}, u32[]{:S(2)}) copy-start(bf16[128,256]{1,0:T(8,128)(2,1)} %refs_6_.2) | copy-start | bytes 196612
  8.0 4.5 %copy-start.6 = (bf16[128,256]{1,0:T(8,128)(2,1)S(1)}, bf16[128,256]{1,0:T(8,128)(2,1)}, u32[]{:S(2)}) copy-start(bf16[128,256]{1,0:T(8,128)(2,1)} %refs_7_.1) | copy-start | bytes 196612
  9.6 15.5 %copy-start.7 = (bf16[128,128]{1,0:T(8,128)(2,1)S(1)}, bf16[128,128]{1,0:T(8,128)(2,1)}, u32[]{:S(2)}) copy-start(bf16[128,128]{1,0:T(8,128)(2,1)} %refs_6_.3) | copy-start | bytes 98308
  9.6 18.8 %copy-start.1 = (bf16[128,512]{1,0:T(8,128)(2,1)S(1)}, bf16[128,512]{1,0:T(8,128)(2,1)}, u32[]{:S(2)}) copy-start(bf16[128,512]{1,0:T(8,128)(2,1)} %refs_9_.1) | copy-start | bytes 393220
  9.7 18.8 %copy-start.2 = (bf16[512,128]{1,0:T(8,128)(2,1)S(1)}, bf16[512,128]{1,0:T(8,128)(2,1)}, u32[]{:S(2)}) copy-start(bf16[512,128]{1,0:T(8,128)(2,1)} %refs_10_.1) | copy-start | bytes 393220
  9.7 18.8 %copy-start.8 = (bf16[128,128]{1,0:T(8,128)(2,1)S(1)}, bf16[128,128]{1,0:T(8,128)(2,1)}, u32[]{:S(2)}) copy-start(bf16[128,128]{1,0:T(8,128)(2,1)} %refs_8_.1) | copy-start | bytes 98308
  13.8 4.4 %collective-permute-start.1 = (bf16[2,256,128]{2,1,0:T(8,128)(2,1)S(1)}, bf16[2,256,128]{2,1,0:T(8,128)(2,1)S(1)}, u32[]{:S(2)}, u32[]{:S(2)}) collective-permute-start(bf16[2,256,128]{2,1,0:T(8,128)(2,1)S(1)} %get-tuple-element.22.refs_0_), channel_id=1, source_target_pairs={{1,0},{0,1},{3,2},{2,3},{5,4},{4,5},{7,6},{6,7},{9,8},{8,9},{11,10... | collective-permute-start | bytes 393224 | tf_op jit(solution)/shard_map/ppermute | solution.py:465
  13.9 8.5 %collective-permute-start.2 = (bf16[256,128]{1,0:T(8,128)(2,1)S(1)}, bf16[256,128]{1,0:T(8,128)(2,1)S(1)}, u32[]{:S(2)}, u32[]{:S(2)}) collective-permute-start(bf16[256,128]{1,0:T(8,128)(2,1)S(1)} %get-tuple-element.23), channel_id=1, source_target_pairs={{2,0},{3,1},{0,2},{1,3},{6,4},{7,5},{4,6},{5,7},{10,8},{11,9},{8,1... | collective-permute-start | bytes 196616 | tf_op jit(solution)/shard_map/ppermute | solution.py:465
  18.2 6.9 %collective-permute-start.5 = (bf16[2,256,128]{2,1,0:T(8,128)(2,1)S(1)}, bf16[2,256,128]{2,1,0:T(8,128)(2,1)S(1)}, u32[]{:S(2)}, u32[]{:S(2)}) collective-permute-start(bf16[2,256,128]{2,1,0:T(8,128)(2,1)S(1)} %pad_maximum_fusion), channel_id=1, source_target_pairs={{3,0},{4,1},{8,2},{14,3},{0,4},{7,5},{10,6},{12,7},{2,8},{5,9},{9,... | collective-permute-start | bytes 393224 | tf_op jit(solution)/shard_map/ppermute | solution.py:465
  20.5 8.0 %collective-permute-start.4 = (bf16[2,256,128]{2,1,0:T(8,128)(2,1)S(1)}, bf16[2,256,128]{2,1,0:T(8,128)(2,1)S(1)}, u32[]{:S(2)}, u32[]{:S(2)}) collective-permute-start(bf16[2,256,128]{2,1,0:T(8,128)(2,1)S(1)} %pad_maximum_fusion), channel_id=1, source_target_pairs={{1,0},{6,1},{10,2},{12,3},{2,4},{5,5},{8,6},{14,7},{0,8},{7,9},{11... | collective-permute-start | bytes 393224 | tf_op jit(solution)/shard_map/ppermute | solution.py:465
  22.4 2.7 %collective-permute-start.3 = (bf16[256,128]{1,0:T(8,128)(2,1)S(1)}, bf16[256,128]{1,0:T(8,128)(2,1)S(1)}, u32[]{:S(2)}, u32[]{:S(2)}) collective-permute-start(bf16[256,128]{1,0:T(8,128)(2,1)S(1)} %collective-permute-done.2.refs_2_), channel_id=1, source_target_pairs={{1,0},{0,1},{3,2},{2,3},{5,4},{4,5},{7,6},{6,7},{9,8},{8,9},{11,10... | collective-permute-start | bytes 196616 | tf_op jit(solution)/shard_map/ppermute | solution.py:465
